TPU v7x, 32 devices: a whole 2x2x4 slice. The times are simulated.
32 devices in a mesh: groups: 2 (over y), shard: 8 (over z, x), sub: 2 (over core).
Axes of the slice: x: 2, y: 2, z: 4, core: 2. Of those that a mesh axis runs over, the one named last changes fastest.
Arguments:
- queries: bfloat16 [32, 32, 128], P(('groups', 'shard', 'sub')), parts along dimension 0, may hold values from -6 to 6
- candidates: int32 [32, 62], P(('groups', 'shard', 'sub')), parts along dimension 0, may hold values from 0 to 1023, as said below
- token_codes: int32 [2048, 128], P(('groups', 'shard', 'sub')), parts along dimension 0, may hold values from 0 to 16383
- residuals: bfloat16 [2048, 128, 128], P(('groups', 'shard', 'sub')), parts along dimension 0, may hold values from -0.3984375 to 0.3984375
- lengths: int32 [2048], P(('groups', 'shard', 'sub')), parts along dimension 0, may hold values from 9 to 128
- centroids: bfloat16 [262144, 128], P(('groups', 'shard', 'sub')), parts along dimension 0, may hold values from -0.5 to 0.5
Outputs:
- scores: float32 [32, 62], P(('groups', 'shard', 'sub')), parts along dimension 0
There are 2 independent parts, one for each index of `groups`. A program takes and returns all parts, laid end to end along the dimension named above; each array names one. Nothing has to cross between parts.
Inputs may be any that keep to these rules, and one draw needn't show every extreme that they name: `candidates`: each row names 62 different passages, at most 4 of them among one device's passages (passage p lies on the device of index p // 64 along shard+sub). So the rows of one device name at most 4 passages of one device and 8 of one shard; in every draw both devices of one shard receive exactly these numbers from the rows of every device.
All inputs are finite; a program needn't handle non-finite values.
Results may differ from a plain program's by a relative error of at most 0.00033.
Values may be sent and summed in bfloat16 or wider, within the bound.
No kernel may reach another device: no remote copies, remote signals or barrier semaphores. Data moves between devices by JAX's collectives and lax.ppermute only.
A program may use at most 64 MiB of HBM per device.

v0:
```python
import math

import jax
import jax.numpy as jnp
from jax import lax
from jax.sharding import PartitionSpec as P

QUERY_DEVICE_MAX = 4


def normalize_rows(vectors):
    total = lax.optimization_barrier(jnp.sum(vectors * vectors, axis=-1, keepdims=True))
    return (vectors * lax.rsqrt(total + 1e-06)).astype(jnp.bfloat16)


def decode_tokens(token_codes, residuals, table_rows):
    vectors = jnp.take(table_rows, token_codes, axis=0).astype(jnp.float32) + residuals.astype(
        jnp.float32
    )
    return normalize_rows(vectors)


def score_slots(slot_table, per_dest, gathered, embedded, lengths, local_queries):
    sources, slot_width = slot_table.shape
    token_count = gathered.shape[1]
    width = gathered.shape[2]
    slot_len = embedded.shape[1]
    clipped = jnp.maximum(slot_table, 0)
    query_local = clipped // per_dest
    passage_index = clipped % per_dest
    live_slots = (slot_table >= 0).astype(jnp.int32)
    group = math.gcd(sources, max(1, 128 // slot_width))
    block_count = sources // group
    rows = group * slot_width
    query_sets = gathered.reshape(block_count, group, local_queries, token_count, width)
    embedded_flat = embedded.reshape(per_dest, slot_len * width)
    local_numbers = jnp.arange(local_queries, dtype=jnp.int32)
    passage_numbers = jnp.arange(per_dest, dtype=jnp.int32)

    def compute_block(pieces):
        query_part, local_part, passage_part, live_part = pieces
        query_pick = (local_part[:, :, None] == local_numbers[None, None, :]).astype(jnp.bfloat16)
        query_block = (
            jnp.einsum("gsl,gltd->gstd", query_pick, query_part, preferred_element_type=jnp.float32)
            .astype(jnp.bfloat16)
            .reshape(rows, token_count, width)
        )
        passage_hits = passage_part.reshape(rows)[:, None] == passage_numbers[None, :]
        passage_pick = passage_hits.astype(jnp.bfloat16)
        passage_block = (
            jnp.dot(passage_pick, embedded_flat, preferred_element_type=jnp.float32)
            .astype(jnp.bfloat16)
            .reshape(rows, slot_len, width)
        )
        slot_lengths = jnp.sum(passage_hits.astype(jnp.int32) * lengths[None, :], axis=1)
        similar = jnp.einsum(
            "btd,bjd->btj", query_block, passage_block, preferred_element_type=jnp.float32
        )
        usable = jnp.arange(slot_len)[None, :] < slot_lengths[:, None]
        largest = jnp.max(jnp.where(usable[:, None, :], similar, -jnp.inf), axis=2)
        return jnp.sum(largest, axis=1).reshape(group, slot_width)

    def one_block(pieces):
        return compute_block(pieces)

    result = lax.map(
        one_block,
        (
            query_sets,
            query_local.reshape(block_count, group, slot_width),
            passage_index.reshape(block_count, group, slot_width),
            live_slots.reshape(block_count, group, slot_width),
        ),
    )
    return result.reshape(sources, slot_width)


def body(queries, candidates, token_codes, residuals, lengths, centroids):
    local_queries = queries.shape[0]
    normed = normalize_rows(queries.astype(jnp.float32))
    shards = lax.axis_size("shard")
    halves = lax.axis_size("sub")
    own_passages = token_codes.shape[0]
    table_rows = lax.all_gather(centroids, "sub", axis=0, tiled=True)
    gathered = lax.all_gather(normed, ("shard", "sub"), axis=0, tiled=True)
    targets = shards * halves
    embedded = decode_tokens(token_codes, residuals, table_rows)
    per_query = QUERY_DEVICE_MAX * (own_passages // own_passages)
    capacity = per_query * local_queries
    cand_count = candidates.shape[1]
    target_numbers = jnp.arange(targets, dtype=jnp.int32)
    rank_numbers = jnp.arange(per_query, dtype=jnp.int32)
    positions = jnp.arange(cand_count, dtype=jnp.int32)

    def plan_query(pieces):
        cand_row, query_number = pieces
        target_of = cand_row // own_passages
        same_target = (target_of[:, None] == target_of[None, :]) & (
            positions[:, None] > positions[None, :]
        )
        rank_of = jnp.sum(same_target.astype(jnp.int32), axis=1)
        target_hot = (target_of[:, None] == target_numbers[None, :]).astype(jnp.int32)
        rank_hot = (rank_of[:, None] == rank_numbers[None, :]).astype(jnp.int32)
        packed = query_number * own_passages + cand_row % own_passages + 1
        filled = (
            jnp.einsum(
                "ct,ck->tk",
                target_hot * packed[:, None],
                rank_hot,
                preferred_element_type=jnp.int32,
            )
            - 1
        )
        return (filled, target_hot, rank_hot)

    query_numbers = jnp.arange(local_queries, dtype=jnp.int32)
    filled, target_hot, rank_hot = lax.map(plan_query, (candidates, query_numbers))
    outgoing = jnp.transpose(filled, (1, 0, 2)).reshape(targets, capacity)
    incoming = lax.all_to_all(
        lax.all_to_all(
            outgoing.reshape(shards, halves, capacity),
            "shard",
            split_axis=0,
            concat_axis=0,
            tiled=True,
        ),
        "sub",
        split_axis=1,
        concat_axis=1,
        tiled=True,
    ).reshape(targets, capacity)
    slot_scores = score_slots(incoming, own_passages, gathered, embedded, lengths, local_queries)
    returned = lax.all_to_all(
        lax.all_to_all(
            slot_scores.reshape(shards, halves, capacity),
            "shard",
            split_axis=0,
            concat_axis=0,
            tiled=True,
        ),
        "sub",
        split_axis=1,
        concat_axis=1,
        tiled=True,
    ).reshape(targets, capacity)
    returned_sets = jnp.transpose(returned.reshape(targets, local_queries, per_query), (1, 0, 2))

    def read_query(pieces):
        values, hot_targets, hot_ranks = pieces
        picked = jnp.dot(hot_targets.astype(jnp.float32), values, precision=lax.Precision.HIGHEST)
        return jnp.sum(picked * hot_ranks.astype(jnp.float32), axis=1)

    return lax.map(read_query, (returned_sets, target_hot, rank_hot))


def solution(mesh):
    placed = (
        P(("groups", "shard", "sub"), None, None),
        P(("groups", "shard", "sub"), None),
        P(("groups", "shard", "sub"), None),
        P(("groups", "shard", "sub"), None, None),
        P(("groups", "shard", "sub")),
        P(("groups", "shard", "sub"), None),
    )
    return jax.shard_map(
        body,
        mesh=mesh,
        in_specs=placed,
        out_specs=P(("groups", "shard", "sub"), None),
        check_vma=False,
    )
```

profile of v0, /device:TPU:0, one launch (start us, length us, event | category | flops | bytes accessed | tf_op | source)
XLA Modules:
  0.0 98.9 jit_solution(13039822681004205671)
XLA Ops:
  6.6 0.7 all-gather.2.cloned.1.call-update
  7.3 0.2 convert_reduce_fusion
  7.5 0.2 convolution_add_fusion
  7.7 0.7 copy.37
  8.4 7.3 %all-to-all-start = ((s32[8,2,4]{2,1,0:T(2,128)}), s32[8,2,4]{2,1,0:T(2,128)S(1)}, u32[]{:S(2)}, u32[]{:S(2)}) async-start(s32[8,2,4]{2,1,0:T(2,128)} %bitcast.2), calls=%async_computation | async-start | bytes 16384 | tf_op jit(solution)/shard_map/all_to_all | solution.py:120
  15.7 0.1 fusion.11
  15.8 0.1 fusion.12
  15.9 22.2 %all_gather.6 = bf16[16,32,128]{2,1,0:T(8,128)(2,1)S(1)} all-gather(bf16[1,32,128]{2,1,0:T(8,128)(2,1)S(1)} %fusion.12), channel_id=1, replica_groups=mesh['groups'=2,'shard'=8,'sub'=2] {'shard','sub'}, dimensions={0}, use_global_device_ids=true | all-gather | bytes 139264 | tf_op jit(solution)/shard_map/all_gather | solution.py:85
  38.1 0.1 copy.38
  38.2 3.7 %all_to_all.20 = s32[8,2,4]{0,2,1:T(4,128)S(1)} all-to-all(s32[8,2,4]{0,2,1:T(4,128)S(1)} %copy.38), channel_id=1, replica_groups=mesh['groups'=2,'shard'=8,'sub'=2] {'sub'}, dimensions={1} | all-to-all | bytes 512 | tf_op jit(solution)/shard_map/all_to_all | solution.py:119
  41.9 0.1 copy.40
  42.0 0.1 and.63
  42.1 0.1 copy.39
  42.2 0.1 rem.76
  42.3 0.1 copy.41
  42.4 0.1 copy.42
  42.5 0.1 copy.44
  42.6 0.2 select_reduce_fusion
  42.8 0.2 multiply_convert_fusion.1
  43.0 24.6 %gather_fusion = bf16[8192,128]{1,0:T(8,128)(2,1)S(1)} fusion(bf16[16384,128]{1,0:T(8,128)(2,1)} %all-gather.2.cloned.1.call-done, s32[8192]{0:T(1024)S(1)} %bitcast_clamp_fusion), kind=kCustom, calls=%fused_computation | custom fusion | bytes 4227072 | tf_op jit(solution)/shard_map/jit(_take)/gather | solution.py:17
  67.7 4.2 %multiply_reduce_fusion = f32[64,128]{1,0:T(8,128)S(1)} fusion(bf16[64,128,128]{2,1,0:T(8,128)(2,1)} %param.9, bf16[64,128,128]{2,1,0:T(8,128)(2,1)S(1)} %bitcast.46, pred[64,128]{1,0:T(8,128)(4,1)S(1)} %compare_and_fusion), kind=kLoop, calls=%fused_computation.3 | loop fusion | flops 6283264 | bytes 4235264 | tf_op jit(solution)/shard_map/reduce_sum | solution.py:12
  71.9 2.8 %multiply_convert_fusion = bf16[64,128,128]{2,1,0:T(8,128)(2,1)S(1)} fusion(bf16[64,128,128]{2,1,0:T(8,128)(2,1)S(1)} %copy-done, f32[64,128]{1,0:T(8,128)S(1)} %rsqrt_bitcast_fusion, pred[64,128]{1,0:T(8,128)(4,1)S(1)} %compare_and_fusion, bf16[8192,128]{1,0:T(8,128)(2,1)S(1)} %gather_fusion), kind=kLoop, calls=%fused_computation.2 | loop fusion | flops 6291456 | bytes 6332416 | tf_op jit(solution)/shard_map/convert_element_type | solution.py:13
  74.7 1.7 %fusion.2 = bf16[8,8,128,128]{3,1,2,0:T(8,128)(2,1)S(1)} fusion(bf16[8,8,128,128]{3,2,1,0:T(8,128)(2,1)S(1)} %bitcast.47, s32[64]{0:T(128)S(1)} %and_select_fusion), kind=kOutput, calls=%fused_computation.8 | convolution fusion | flops 135270400 | bytes 4194560 | tf_op jit(solution)/shard_map/while/body/eval_jaxpr/dot_general | solution.py:51
  76.4 0.6 copy.50
  77.0 1.3 %fusion.5 = f32[64,32]{1,0:T(8,128)S(1)} fusion(bf16[64,32,128]{2,1,0:T(8,128)(2,1)S(1)} %bitcast.49, bf16[64,128,128]{2,1,0:T(8,128)(2,1)S(1)} %bitcast.48, pred[64,128]{1,0:T(8,128)(4,1)S(1)} %iota_compare_fusion.3), kind=kOutput, calls=%fused_computation.10 | convolution fusion | flops 67631104 | bytes 2637824 | tf_op jit(solution)/shard_map/while/body/eval_jaxpr/btd,bjd->btj/dot_general | solution.py:56
  78.3 0.1 reduce_sum.62
  78.4 0.1 reshape_reshape.3
  78.5 8.9 %all_to_all.21 = f32[8,2,4]{2,1,0:T(2,128)S(1)} all-to-all(f32[8,2,4]{2,1,0:T(2,128)S(1)} %reshape_reshape.3), channel_id=1, replica_groups=mesh['groups'=2,'shard'=8,'sub'=2] {'shard'}, dimensions={0} | all-to-all | bytes 512 | tf_op jit(solution)/shard_map/all_to_all | solution.py:134
  87.4 0.1 copy.46
  87.5 3.7 %all_to_all.22 = f32[8,2,4]{0,2,1:T(4,128)S(1)} all-to-all(f32[8,2,4]{0,2,1:T(4,128)S(1)} %copy.46), channel_id=1, replica_groups=mesh['groups'=2,'shard'=8,'sub'=2] {'sub'}, dimensions={1} | all-to-all | bytes 512 | tf_op jit(solution)/shard_map/all_to_all | solution.py:133
  91.2 0.1 copy.47
  91.2 0.8 fusion.6
  (25 shorter events, 0.3 us)
Async XLA Ops:
  6.5 0.7 copy-start.3
  6.5 9.1 %copy-start.2 = (bf16[1,32,128]{2,1,0:T(8,128)(2,1)S(1)}, bf16[1,32,128]{2,1,0:T(8,128)(2,1)}, u32[]{:S(2)}) copy-start(bf16[1,32,128]{2,1,0:T(8,128)(2,1)} %param.6) | copy-start | bytes 24580
  6.5 9.3 %copy-start.1 = (s32[64,128]{1,0:T(8,128)S(1)}, s32[64,128]{1,0:T(8,128)}, u32[]{:S(2)}) copy-start(s32[64,128]{1,0:T(8,128)} %param.8) | copy-start | bytes 98308
  6.5 36.0 %copy-start.4 = (s32[64]{0:T(128)S(1)}, s32[64]{0:T(128)}, u32[]{:S(2)}) copy-start(s32[64]{0:T(128)} %param.10) | copy-start | bytes 772
  6.5 36.5 %all-gather.2.cloned.1.call-start = ((), (), s32[]{:S(2)}) async-start(), calls=%async_computation.4 | async-start | bytes 6291456 | tf_op jit(solution)/shard_map/all_gather | solution.py:84
  8.4 29.7 %all-to-all-start = ((s32[8,2,4]{2,1,0:T(2,128)}), s32[8,2,4]{2,1,0:T(2,128)S(1)}, u32[]{:S(2)}, u32[]{:S(2)}) async-start(s32[8,2,4]{2,1,0:T(2,128)} %bitcast.2), calls=%async_computation | async-start | bytes 16384 | tf_op jit(solution)/shard_map/all_to_all | solution.py:120
  67.7 4.2 %copy-start = (bf16[64,128,128]{2,1,0:T(8,128)(2,1)S(1)}, bf16[64,128,128]{2,1,0:T(8,128)(2,1)}, u32[]{:S(2)}) copy-start(bf16[64,128,128]{2,1,0:T(8,128)(2,1)} %param.9) | copy-start | bytes 6291460
Sparse Core Ops, SparseCore 0:
  8.9 16.3 all-gather.1
where the time goes:
time: 99.2 us; the launch traced here: 98.9 us
  blocking collectives  38.4 us (39%)
  local copies, waits for them, and re-layouts  26.9 us (27%)
  between operations  13.6 us (14%)
  other arithmetic  7.99 us (8%)
  starting transfers between devices  7.29 us (7%)
  matrix products  3.97 us (4%)
    gather x1, local copies, waits for them, and re-layouts, decode_tokens(): jnp.take(table_rows, token_codes, axis=0).astype(jnp.float32)  24.6 us
    all_gather x1, blocking collectives, body(): gathered = lax.all_gather(normed, ('shard', 'sub'), axis=0, tiled=True)  22.2 us
    all_to_all x1, blocking collectives, body(): lax.all_to_all(slot_scores.reshape(shards, halves, capacity), 'shard', sp...  8.88 us
    all_to_all x1, starting transfers between devices, body(): lax.all_to_all(outgoing.reshape(shards, halves, capacity), 'shard', split...  7.25 us
    reduce_sum x2, other arithmetic, normalize_rows(): jnp.sum(vectors * vectors, axis=-1, keepdims=True)  4.31 us
    all_to_all x1, blocking collectives, body(): lax.all_to_all(lax.all_to_all(outgoing.reshape(shards, halves, capacity),...  3.68 us
    all_to_all x1, blocking collectives, body(): lax.all_to_all(lax.all_to_all(slot_scores.reshape(shards, halves, capacit...  3.68 us
    convert_element_type x2, other arithmetic, normalize_rows(): return (vectors * lax.rsqrt(total + 1e-06)).astype(jnp.bfloat16)  2.86 us
  transfers between devices with their start and end apart: 2, of which 0 were waited for; matrix products, arithmetic and copies ran while one was open for 3% of the time, Pallas kernels for 0%

commit v1 on v0

v1 whole, which is shorter than its diff:
```python
import functools

import jax
import jax.numpy as jnp
from jax import lax
from jax.experimental import pallas as pl
from jax.experimental.pallas import tpu as pltpu
from jax.sharding import PartitionSpec as P

CHUNK = 16
QUERY_BLOCK = 512


def normalized(vectors):
    total = jnp.sum(vectors * vectors, axis=-1, keepdims=True)
    return (vectors * lax.rsqrt(total + 1e-06)).astype(jnp.bfloat16)


def score_kernel(
    token_count,
    half_ref,
    codes_ref,
    lengths_ref,
    queries_ref,
    own_ref,
    other_ref,
    residuals_ref,
    out_ref,
    staged,
    table,
    residual_rows,
    rows,
    embedded,
    turned,
    largest,
    sems,
):
    passages, slots, width = residuals_ref.shape
    half_rows = own_ref.shape[0]
    half = half_ref[0]
    own_copy = pltpu.make_async_copy(own_ref, staged.at[0], sems.at[0])
    other_copy = pltpu.make_async_copy(other_ref, staged.at[1], sems.at[1])
    residual_copy = pltpu.make_async_copy(residuals_ref, residual_rows, sems.at[2])
    own_copy.start()
    other_copy.start()
    residual_copy.start()

    query_tokens = queries_ref.shape[0]
    block = min(QUERY_BLOCK, query_tokens)
    blocks = query_tokens // block

    def turn(b, carry):
        at = pl.ds(pl.multiple_of(b * block, block), block)
        vectors = normalized(queries_ref[at, :].astype(jnp.float32))
        turned[b] = vectors.astype(jnp.float32).T.astype(jnp.bfloat16)
        return carry

    lax.fori_loop(0, blocks, turn, 0)

    step = 256

    def widen(source, base):
        def body(i, carry):
            start = pl.multiple_of(i * step, step)
            table[pl.ds(pl.multiple_of(base + start, step), step), :] = staged[
                source, pl.ds(start, step), :
            ].astype(jnp.float32)
            return carry

        lax.fori_loop(0, half_rows // step, body, 0)

    own_copy.wait()
    widen(0, half * half_rows)
    other_copy.wait()
    widen(1, (1 - half) * half_rows)
    residual_copy.wait()

    slot_numbers = lax.broadcasted_iota(jnp.int32, (slots, width), 0)

    def decode(p, carry):
        length = lengths_ref[p]

        def fetch(c, inner):
            base = pl.multiple_of(c * CHUNK, CHUNK)
            for k in range(CHUNK):
                code = codes_ref[p, base + k]
                rows[pl.ds(base + k, 1), :] = table[pl.ds(code, 1), :]
            return inner

        lax.fori_loop(0, (length + CHUNK - 1) // CHUNK, fetch, 0)
        vectors = rows[...] + residual_rows[p].astype(jnp.float32)
        vectors = jnp.where(slot_numbers < length, vectors, vectors[0:1, :])
        embedded[p] = normalized(vectors)
        return carry

    lax.fori_loop(0, passages, decode, 0)

    def score(i, carry):
        b = i // passages
        p = i % passages
        similar = jnp.dot(embedded[p], turned[b], preferred_element_type=jnp.float32)
        largest[b, pl.ds(p, 1), :] = jnp.max(similar, axis=0, keepdims=True)
        return carry

    lax.fori_loop(0, blocks * passages, score, 0)

    per_block = block // token_count
    owner = lax.broadcasted_iota(jnp.int32, (per_block, block), 0)
    token_of = lax.broadcasted_iota(jnp.int32, (per_block, block), 1) // token_count
    summing = (owner == token_of).astype(jnp.float32)

    def total(b, carry):
        sums = lax.dot_general(
            summing,
            largest[b],
            (((1,), (1,)), ((), ())),
            precision=lax.Precision.HIGHEST,
            preferred_element_type=jnp.float32,
        )
        out_ref[pl.ds(pl.multiple_of(b * per_block, per_block), per_block), :] = sums
        return carry

    lax.fori_loop(0, blocks, total, 0)


def score_all(half, token_codes, lengths, query_rows, own, other, residuals, token_count):
    passages, slots, width = residuals.shape
    half_rows = own.shape[0]
    query_tokens = query_rows.shape[0]
    block = min(QUERY_BLOCK, query_tokens)
    blocks = query_tokens // block
    smem = pl.BlockSpec(memory_space=pltpu.SMEM)
    vmem = pl.BlockSpec(memory_space=pltpu.VMEM)
    hbm = pl.BlockSpec(memory_space=pl.ANY)
    return pl.pallas_call(
        functools.partial(score_kernel, token_count),
        out_shape=jax.ShapeDtypeStruct((query_tokens // token_count, passages), jnp.float32),
        in_specs=[smem, smem, smem, vmem, hbm, hbm, hbm],
        out_specs=vmem,
        scratch_shapes=[
            pltpu.VMEM((2, half_rows, width), jnp.bfloat16),
            pltpu.VMEM((2 * half_rows, width), jnp.float32),
            pltpu.VMEM((passages, slots, width), jnp.bfloat16),
            pltpu.VMEM((slots, width), jnp.float32),
            pltpu.VMEM((passages, slots, width), jnp.bfloat16),
            pltpu.VMEM((blocks, width, block), jnp.bfloat16),
            pltpu.VMEM((blocks, passages, block), jnp.float32),
            pltpu.SemaphoreType.DMA((3,)),
        ],
        compiler_params=pltpu.CompilerParams(vmem_limit_bytes=48 * 1024 * 1024),
    )(half, token_codes, lengths, query_rows, own, other, residuals)


def body(queries, candidates, token_codes, residuals, lengths, centroids):
    local_queries, token_count, width = queries.shape
    targets = lax.axis_size("shard") * lax.axis_size("sub")
    passages = token_codes.shape[0]
    other = lax.ppermute(centroids, "sub", [(0, 1), (1, 0)])
    sent = jnp.broadcast_to(queries[None], (targets,) + queries.shape)
    gathered = lax.all_to_all(sent, ("shard", "sub"), split_axis=0, concat_axis=0, tiled=True)
    query_rows = gathered.reshape(targets * local_queries * token_count, width)
    half = lax.axis_index("sub").astype(jnp.int32).reshape(1)
    scores = score_all(
        half, token_codes, lengths, query_rows, centroids, other, residuals, token_count
    )
    returned = lax.all_to_all(
        scores.reshape(targets, local_queries, passages),
        ("shard", "sub"),
        split_axis=0,
        concat_axis=0,
        tiled=True,
    )
    known = jnp.transpose(returned, (1, 0, 2)).reshape(local_queries, targets * passages)
    numbers = jnp.arange(targets * passages, dtype=jnp.int32)
    hits = candidates[:, :, None] == numbers[None, None, :]
    return jnp.sum(jnp.where(hits, known[:, None, :], 0.0), axis=2)


def solution(mesh):
    placed = (
        P(("groups", "shard", "sub"), None, None),
        P(("groups", "shard", "sub"), None),
        P(("groups", "shard", "sub"), None),
        P(("groups", "shard", "sub"), None, None),
        P(("groups", "shard", "sub")),
        P(("groups", "shard", "sub"), None),
    )
    return jax.shard_map(
        body,
        mesh=mesh,
        in_specs=placed,
        out_specs=P(("groups", "shard", "sub"), None),
        check_vma=False,
    )
```

time: 99.2 us -> 66.4 us (0.67)
  Pallas kernels: 0 us -> 34.2 us
  blocking collectives: 38.4 us -> 9.17 us
  local copies, waits for them, and re-layouts: 26.9 us -> 4.94 us
  between operations: 13.6 us -> 0.03 us
  waiting for transfers between devices: 0.7 us -> 7.93 us
  other arithmetic: 7.99 us -> 2.13 us
  matrix products: 3.97 us -> 0 us
    pallas_call x0 -> x1, Pallas kernels: none -> 34.2 us  [score_all(): pl.pallas_call(functools.partial(score_kernel, token_count), out_shape=ja...]
    gather x1 -> x0, local copies, waits for them, and re-layouts: 24.6 us -> none  [decode_tokens(): jnp.take(table_rows, token_codes, axis=0).astype(jnp.float32)]
    all_gather x1 -> x0, blocking collectives: 22.2 us -> none  [body(): gathered = lax.all_gather(normed, ('shard', 'sub'), axis=0, tiled=True)]
    all_to_all x1, waiting for transfers between devices: 0.01 us -> 7.93 us  [body(): lax.all_to_all(sent, ('shard', 'sub'), split_axis=0, concat_axis=0, tiled...]
    all_to_all x3 -> x1, blocking collectives: 16.2 us -> 9.17 us  [body(): lax.all_to_all(scores.reshape(targets, local_queries, passages), ('shard'...]
    dot_general x4 -> x0, matrix products: 3.97 us -> none  [the longest x1 1.68 us: compute_block(): jnp.dot(passage_pick, embedded_flat, preferred_element_type=jnp.float32)]
    reduce_sum x5 -> x1, other arithmetic: 4.79 us -> 1.46 us  [body(): return jnp.sum(jnp.where(hits, known[:, None, :], 0.0), axis=2)]
    convert_element_type x3 -> x0, other arithmetic: 3.02 us -> none  [the longest x2 2.86 us: normalize_rows(): return (vectors * lax.rsqrt(total + 1e-06)).astype(jnp.bfloat16)]
  transfers between devices with their start and end apart: 2 -> 2, of which waited for: 0 -> 1; matrix products, arithmetic and copies ran while one was open for 3% -> 2% of each run, Pallas kernels for 0% -> 0%
where the time goes in v1:
time: 66.4 us; the launch traced here: 65.9 us
  Pallas kernels  34.2 us (52%)
  blocking collectives  9.17 us (14%)
  waiting for transfers between devices  7.93 us (12%)
  starting transfers between devices  7.47 us (11%)
  local copies, waits for them, and re-layouts  4.94 us (7%)
  other arithmetic  2.13 us (3%)
    pallas_call x1, Pallas kernels, score_all(): pl.pallas_call(functools.partial(score_kernel, token_count), out_shape=ja...  34.2 us
    all_to_all x1, blocking collectives, body(): lax.all_to_all(scores.reshape(targets, local_queries, passages), ('shard'...  9.17 us
    all_to_all x1, waiting for transfers between devices, body(): lax.all_to_all(sent, ('shard', 'sub'), split_axis=0, concat_axis=0, tiled...  7.93 us
    all_to_all x1, starting transfers between devices, body(): lax.all_to_all(sent, ('shard', 'sub'), split_axis=0, concat_axis=0, tiled...  7.02 us
    unnamed x8, local copies, waits for them, and re-layouts  3.01 us
    reduce_sum x1, other arithmetic, body(): return jnp.sum(jnp.where(hits, known[:, None, :], 0.0), axis=2)  1.46 us
    broadcast_in_dim x1, local copies, waits for them, and re-layouts, body(): sent = jnp.broadcast_to(queries[None], (targets,) + queries.shape)  1.35 us
  transfers between devices with their start and end apart: 2, of which 1 were waited for; matrix products, arithmetic and copies ran while one was open for 2% of the time, Pallas kernels for 0%

profile of v1, /device:TPU:0, one launch (start us, length us, event | category | flops | bytes accessed | tf_op | source)
XLA Modules:
  0.0 65.9 jit_solution(18245809427423997885)
XLA Ops:
  0.0 0.5 collective-permute-start
  0.5 1.3 %broadcast_in_dim.25 = bf16[16,1,32,128]{3,2,1,0:T(8,128)(2,1)} broadcast(bf16[32,128]{1,0:T(8,128)(2,1)} %bitcast.10), dimensions={2,3} | broadcast | bytes 139264 | tf_op jit(solution)/shard_map/broadcast_in_dim | solution.py:159
  1.8 7.0 %all-to-all-start = ((bf16[16,1,32,128]{3,2,1,0:T(8,128)(2,1)}), bf16[16,1,32,128]{3,2,1,0:T(8,128)(2,1)S(1)}, u32[]{:S(2)}, u32[]{:S(2)}) async-start(bf16[16,1,32,128]{3,2,1,0:T(8,128)(2,1)} %broadcast_in_dim.25), calls=%async_computation | async-start | bytes 262144 | tf_op jit(solution)/shard_map/all_to_all | solution.py:160
  8.8 7.9 %all-to-all-done = bf16[16,1,32,128]{3,2,1,0:T(8,128)(2,1)S(1)} async-done(((bf16[16,1,32,128]{3,2,1,0:T(8,128)(2,1)}), bf16[16,1,32,128]{3,2,1,0:T(8,128)(2,1)S(1)}, u32[]{:S(2)}, u32[]{:S(2)}) %all-to-all-start) | async-done | bytes 131104 | tf_op jit(solution)/shard_map/all_to_all | solution.py:160
  16.8 0.0 collective-permute-done.other_ref
  16.8 0.0 copy-start
  16.8 1.6 %copy-done = bf16[8192,128]{1,0:T(8,128)(2,1)S(1)} copy-done((bf16[8192,128]{1,0:T(8,128)(2,1)S(1)}, bf16[8192,128]{1,0:T(8,128)(2,1)}, u32[]{:S(2)}) %copy-start) | copy-done | bytes 2097176
  18.4 0.0 copy-start.1
  18.4 0.8 %copy-done.1 = s32[64,128]{1,0:T(8,128)S(1)} copy-done((s32[64,128]{1,0:T(8,128)S(1)}, s32[64,128]{1,0:T(8,128)}, u32[]{:S(2)}) %copy-start.1) | copy-done | bytes 32792
  19.1 0.0 copy-start.2
  19.1 0.7 copy-done.2
  19.8 0.0 copy-start.3
  19.8 34.2 %shard_map.67 = f32[16,64]{1,0:T(8,128)S(1)} custom-call(s32[1]{0:T(128)} %bitcast.1.half_ref, s32[64,128]{1,0:T(8,128)S(1)} %copy-done.1, s32[64]{0:T(128)S(1)} %copy-done.2, bf16[512,128]{1,0:T(8,128)(2,1)S(1)} %bitcast.8, bf16[8192,128]{1,0:T(8,128)(2,1)S(1)} %copy-done, bf16[8192,128]{1,0:T(8,128)(2,1)S(1)} %collective-permute-done.other_ref, ...), custom_call_target="tpu_custom_call" | custom-call | tf_op jit(solution)/shard_map/pallas_call | solution.py:135
  54.0 9.2 %all_to_all.10 = f32[16,1,64]{2,1,0:T(1,128)S(1)} all-to-all(f32[16,1,64]{2,1,0:T(1,128)S(1)} %bitcast.9), channel_id=1, replica_groups=mesh['groups'=2,'shard'=8,'sub'=2] {'shard','sub'}, dimensions={0} | all-to-all | bytes 8192 | tf_op jit(solution)/shard_map/all_to_all | solution.py:166
  63.1 0.5 broadcast.59
  63.6 0.7 %reduce.4 = f32[16,64]{1,0:T(8,128)S(1)} reduce(f32[16,1,64]{2,1,0:T(1,128)S(1)} %all_to_all.10, f32[]{:T(128)} %broadcast.59), dimensions={1}, to_apply=%all_to_all.7.reduce_sub_computation.3 | reduce | bytes 8196 | tf_op jit(solution)/shard_map/all_to_all | solution.py:166
  64.3 0.1 broadcast_in_dim.26
  64.4 0.0 copy-done.3
  64.4 1.5 %fusion = f32[62]{0:T(128)} fusion(s32[62]{0:T(128)S(1)} %bitcast.11, f32[1024]{0:T(1024)S(1)} %broadcast_in_dim.26), kind=kLoop, calls=%fused_computation.1 | loop fusion | flops 190402 | bytes 4592 | tf_op jit(solution)/shard_map/reduce_sum | solution.py:176
Async XLA Ops:
  0.0 16.8 %collective-permute-start = (bf16[8192,128]{1,0:T(8,128)(2,1)}, bf16[8192,128]{1,0:T(8,128)(2,1)S(1)}, u32[]{:S(2)}, u32[]{:S(2)}) collective-permute-start(bf16[8192,128]{1,0:T(8,128)(2,1)} %own_ref.1), channel_id=1, source_target_pairs={{0,1},{1,0},{2,3},{3,2},{4,5},{5,4},{6,7},{7,6},{8,9},{9,8},{10,11... | collective-permute-start | bytes 6291464 | tf_op jit(solution)/shard_map/ppermute | solution.py:158
  1.8 15.0 %all-to-all-start = ((bf16[16,1,32,128]{3,2,1,0:T(8,128)(2,1)}), bf16[16,1,32,128]{3,2,1,0:T(8,128)(2,1)S(1)}, u32[]{:S(2)}, u32[]{:S(2)}) async-start(bf16[16,1,32,128]{3,2,1,0:T(8,128)(2,1)} %broadcast_in_dim.25), calls=%async_computation | async-start | bytes 262144 | tf_op jit(solution)/shard_map/all_to_all | solution.py:160
  16.8 1.6 %copy-start = (bf16[8192,128]{1,0:T(8,128)(2,1)S(1)}, bf16[8192,128]{1,0:T(8,128)(2,1)}, u32[]{:S(2)}) copy-start(bf16[8192,128]{1,0:T(8,128)(2,1)} %own_ref.1) | copy-start | bytes 6291460
  18.4 0.8 %copy-start.1 = (s32[64,128]{1,0:T(8,128)S(1)}, s32[64,128]{1,0:T(8,128)}, u32[]{:S(2)}) copy-start(s32[64,128]{1,0:T(8,128)} %codes_ref.1) | copy-start | bytes 98308
  19.1 0.7 copy-start.2
  19.8 44.6 %copy-start.3 = (s32[1,62]{1,0:T(1,128)S(1)}, s32[1,62]{1,0:T(1,128)}, u32[]{:S(2)}) copy-start(s32[1,62]{1,0:T(1,128)} %param.7) | copy-start | bytes 748

commit v2 on v1

v2 whole, which is shorter than its diff:
```python
import functools

import jax
import jax.numpy as jnp
from jax import lax
from jax.experimental import pallas as pl
from jax.experimental.pallas import tpu as pltpu
from jax.sharding import PartitionSpec as P

CHUNK = 32
GROUP = 8
BATCH = 16
QUERY_BLOCK = 512
ROUND_BITS = 2


def normalized(vectors):
    total = jnp.sum(vectors * vectors, axis=-1, keepdims=True)
    return (vectors * lax.rsqrt(total + 1e-06)).astype(jnp.bfloat16)


def score_kernel(
    token_count,
    half_ref,
    codes_hbm,
    lengths_hbm,
    queries_ref,
    own_ref,
    other_ref,
    residuals_ref,
    out_ref,
    codes_ref,
    lengths_ref,
    owner_ref,
    staged,
    table,
    residual_rows,
    rows,
    embedded,
    turned,
    largest,
    sems,
):
    passages, slots, width = residuals_ref.shape
    half_rows = own_ref.shape[0]
    half = half_ref[0]
    own_copy = pltpu.make_async_copy(own_ref, staged.at[0], sems.at[0])
    other_copy = pltpu.make_async_copy(other_ref, staged.at[1], sems.at[1])
    residual_copy = pltpu.make_async_copy(residuals_ref, residual_rows, sems.at[2])
    codes_copy = pltpu.make_async_copy(codes_hbm, codes_ref, sems.at[3])
    lengths_copy = pltpu.make_async_copy(lengths_hbm, lengths_ref, sems.at[4])
    lengths_copy.start()
    codes_copy.start()
    own_copy.start()
    other_copy.start()
    residual_copy.start()

    query_tokens = queries_ref.shape[0]
    block = min(QUERY_BLOCK, query_tokens)
    blocks = query_tokens // block

    def turn(b, carry):
        at = pl.ds(pl.multiple_of(b * block, block), block)
        vectors = normalized(queries_ref[at, :].astype(jnp.float32))
        turned[b] = vectors.astype(jnp.float32).T.astype(jnp.bfloat16)
        return carry

    lax.fori_loop(0, blocks, turn, 0)

    step = 256

    def widen(source, base):
        def body(i, carry):
            start = pl.multiple_of(i * step, step)
            table[pl.ds(pl.multiple_of(base + start, step), step), :] = staged[
                source, pl.ds(start, step), :
            ].astype(jnp.float32)
            return carry

        lax.fori_loop(0, half_rows // step, body, 0)

    own_copy.wait()
    widen(0, half * half_rows)
    lengths_copy.wait()
    codes_copy.wait()

    def count(p, chunks):
        return chunks + (lengths_ref[p] + CHUNK - 1) // CHUNK

    chunks = lax.fori_loop(0, passages, count, 0)
    other_copy.wait()
    widen(1, (1 - half) * half_rows)
    residual_copy.wait()

    slot_numbers = lax.broadcasted_iota(jnp.int32, (CHUNK, width), 0)

    def decode(i, carry):
        p, start, last_p, last_start = carry
        last_at = pl.ds(pl.multiple_of(last_start, CHUNK), CHUNK)
        vectors = rows[...] + residual_rows[last_p, last_at, :].astype(jnp.float32)
        live = slot_numbers < lengths_ref[last_p] - last_start
        vectors = jnp.where(live, vectors, vectors[0:1, :])
        done = jnp.maximum(i - 1, 0)
        embedded[pl.ds(pl.multiple_of(done * CHUNK, CHUNK), CHUNK), :] = normalized(vectors)
        owner_ref[done] = last_p
        for k in range(0, CHUNK, BATCH):
            fetched = [
                table[pl.ds(codes_ref[p, start + k + j], 1), :] for j in range(BATCH)
            ]
            for j in range(BATCH):
                rows[pl.ds(k + j, 1), :] = fetched[j]
        more = start + CHUNK < lengths_ref[p]
        next_p = jnp.where(more, p, jnp.minimum(p + 1, passages - 1))
        next_start = jnp.where(more, start + CHUNK, 0)
        return next_p, next_start, p, start

    lax.fori_loop(0, chunks + 1, decode, (0, 0, 0, 0))
    for k in range(GROUP):
        owner_ref[chunks + k] = passages

    groups = (chunks + GROUP - 1) // GROUP

    def score_block(b, carry):
        largest[...] = jnp.full(largest.shape, -jnp.inf, jnp.float32)

        def score(g, inner):
            at = pl.ds(pl.multiple_of(g * GROUP * CHUNK, GROUP * CHUNK), GROUP * CHUNK)
            similar = jnp.dot(embedded[at, :], turned[b], preferred_element_type=jnp.float32)
            parts = jnp.max(similar.reshape(GROUP, CHUNK // 8, 8, block), axis=1)
            for k in range(GROUP):
                p = owner_ref[g * GROUP + k]
                largest[p] = jnp.maximum(largest[p], parts[k])
            return inner

        lax.fori_loop(0, groups, score, 0)
        per_block = block // token_count
        owner = lax.broadcasted_iota(jnp.int32, (per_block, block), 0)
        token_of = lax.broadcasted_iota(jnp.int32, (per_block, block), 1) // token_count
        summing = (owner == token_of).astype(jnp.float32)
        sums = lax.dot_general(
            summing,
            jnp.max(largest[0:passages], axis=1),
            (((1,), (1,)), ((), ())),
            precision=lax.Precision.HIGHEST,
            preferred_element_type=jnp.float32,
        )
        out_ref[pl.ds(pl.multiple_of(b * per_block, per_block), per_block), :] = sums
        return carry

    lax.fori_loop(0, blocks, score_block, 0)


def score_all(half, token_codes, lengths, query_rows, own, other, residuals, token_count):
    passages, slots, width = residuals.shape
    half_rows = own.shape[0]
    query_tokens = query_rows.shape[0]
    block = min(QUERY_BLOCK, query_tokens)
    blocks = query_tokens // block
    most = passages * (slots // CHUNK) + GROUP
    smem = pl.BlockSpec(memory_space=pltpu.SMEM)
    vmem = pl.BlockSpec(memory_space=pltpu.VMEM)
    hbm = pl.BlockSpec(memory_space=pl.ANY)
    return pl.pallas_call(
        functools.partial(score_kernel, token_count),
        out_shape=jax.ShapeDtypeStruct((query_tokens // token_count, passages), jnp.float32),
        in_specs=[smem, hbm, hbm, vmem, hbm, hbm, hbm],
        out_specs=vmem,
        scratch_shapes=[
            pltpu.SMEM(token_codes.shape, jnp.int32),
            pltpu.SMEM(lengths.shape, jnp.int32),
            pltpu.SMEM((most,), jnp.int32),
            pltpu.VMEM((2, half_rows, width), jnp.bfloat16),
            pltpu.VMEM((2 * half_rows, width), jnp.float32),
            pltpu.VMEM((passages, slots, width), jnp.bfloat16),
            pltpu.VMEM((CHUNK, width), jnp.float32),
            pltpu.VMEM((most * CHUNK, width), jnp.bfloat16),
            pltpu.VMEM((blocks, width, block), jnp.bfloat16),
            pltpu.VMEM((passages + 1, 8, block), jnp.float32),
            pltpu.SemaphoreType.DMA((5,)),
        ],
        compiler_params=pltpu.CompilerParams(vmem_limit_bytes=60 * 1024 * 1024),
    )(half, token_codes, lengths, query_rows, own, other, residuals)


def rounds_of(targets):
    first = 0
    bits = targets.bit_length() - 1
    while first < bits:
        taken = min(ROUND_BITS, bits - first)
        yield first, taken
        first += taken


def partner(targets, offset):
    return [(device, device ^ offset) for device in range(targets)]


def gather_relative(own, targets):
    held = own[None]
    for first, taken in rounds_of(targets):
        parts = [held]
        for value in range(1, 1 << taken):
            pairs = partner(targets, value << first)
            parts.append(lax.ppermute(held, ("shard", "sub"), pairs))
        held = jnp.concatenate(parts, axis=0)
    return held


def return_relative(blocks, targets):
    held = blocks.reshape((targets, 1) + blocks.shape[1:])
    for first, taken in rounds_of(targets):
        split = held.reshape((-1, 1 << taken) + held.shape[1:])
        parts = [split[:, 0]]
        for value in range(1, 1 << taken):
            pairs = partner(targets, value << first)
            parts.append(lax.ppermute(split[:, value], ("shard", "sub"), pairs))
        held = jnp.concatenate(parts, axis=1)
    return held[0]


def body(queries, candidates, token_codes, residuals, lengths, centroids):
    local_queries, token_count, width = queries.shape
    targets = lax.axis_size("shard") * lax.axis_size("sub")
    passages = token_codes.shape[0]
    half = lax.axis_index("sub").astype(jnp.int32)
    me = lax.axis_index("shard").astype(jnp.int32) * lax.axis_size("sub") + half
    other = lax.ppermute(centroids, "sub", [(0, 1), (1, 0)])
    gathered = gather_relative(queries, targets)
    query_rows = gathered.reshape(targets * local_queries * token_count, width)
    scores = score_all(
        half.reshape(1), token_codes, lengths, query_rows, centroids, other, residuals, token_count
    )
    returned = return_relative(scores.reshape(targets, local_queries, passages), targets)
    known = jnp.transpose(returned, (1, 0, 2)).reshape(local_queries, targets * passages)
    relative = ((candidates // passages) ^ me) * passages + candidates % passages
    numbers = jnp.arange(targets * passages, dtype=jnp.int32)
    hits = relative[:, :, None] == numbers[None, None, :]
    return jnp.sum(jnp.where(hits, known[:, None, :], 0.0), axis=2)


def solution(mesh):
    placed = (
        P(("groups", "shard", "sub"), None, None),
        P(("groups", "shard", "sub"), None),
        P(("groups", "shard", "sub"), None),
        P(("groups", "shard", "sub"), None, None),
        P(("groups", "shard", "sub")),
        P(("groups", "shard", "sub"), None),
    )
    return jax.shard_map(
        body,
        mesh=mesh,
        in_specs=placed,
        out_specs=P(("groups", "shard", "sub"), None),
        check_vma=False,
    )
```

time: 66.4 us -> 59.4 us (0.89); the launches traced: 65.9 us -> 59.6 us
  blocking collectives: 9.17 us -> 0 us
  Pallas kernels: 34.2 us -> 26.3 us
  starting transfers between devices: 7.47 us -> 14.9 us
  waiting for transfers between devices: 7.93 us -> 13.1 us
  local copies, waits for them, and re-layouts: 4.94 us -> 3.04 us
    ppermute x0 -> x12, starting transfers between devices: none -> 14.4 us  [the longest x6 7.27 us: return_relative(): parts.append(lax.ppermute(split[:, value], ('shard', 'sub'), pairs))]
    ppermute x0 -> x12, waiting for transfers between devices: none -> 13.1 us  [the longest x6 7.01 us: gather_relative(): parts.append(lax.ppermute(held, ('shard', 'sub'), pairs))]
    all_to_all x1 -> x0, blocking collectives: 9.17 us -> none  [body(): lax.all_to_all(scores.reshape(targets, local_queries, passages), ('shard'...]
    all_to_all x1 -> x0, waiting for transfers between devices: 7.93 us -> none  [body(): lax.all_to_all(sent, ('shard', 'sub'), split_axis=0, concat_axis=0, tiled...]
    pallas_call x1, Pallas kernels: 34.2 us -> 26.3 us  [score_all(): pl.pallas_call(functools.partial(score_kernel, token_count), out_shape=ja...]
    all_to_all x1 -> x0, starting transfers between devices: 7.02 us -> none  [body(): lax.all_to_all(sent, ('shard', 'sub'), split_axis=0, concat_axis=0, tiled...]
    broadcast_in_dim x1 -> x0, local copies, waits for them, and re-layouts: 1.35 us -> none  [body(): sent = jnp.broadcast_to(queries[None], (targets,) + queries.shape)]
    unnamed x8 -> x12, local copies, waits for them, and re-layouts: 3.01 us -> 2.09 us
  transfers between devices with their start and end apart: 2 -> 13, of which waited for: 1 -> 8; matrix products, arithmetic and copies ran while one was open for 2% -> 2% of each run, Pallas kernels for 0% -> 0%
where the time goes in v2:
time: 59.4 us; the launch traced here: 59.6 us
  Pallas kernels  26.3 us (44%)
  starting transfers between devices  14.9 us (25%)
  waiting for transfers between devices  13.1 us (22%)
  local copies, waits for them, and re-layouts  3.04 us (5%)
  other arithmetic  2.2 us (4%)
    pallas_call x1, Pallas kernels, score_all(): pl.pallas_call(functools.partial(score_kernel, token_count), out_shape=ja...  26.3 us
    ppermute x6, starting transfers between devices, return_relative(): parts.append(lax.ppermute(split[:, value], ('shard', 'sub'), pairs))  7.27 us
    ppermute x6, starting transfers between devices, gather_relative(): parts.append(lax.ppermute(held, ('shard', 'sub'), pairs))  7.14 us
    ppermute x6, waiting for transfers between devices, gather_relative(): parts.append(lax.ppermute(held, ('shard', 'sub'), pairs))  7.01 us
    ppermute x6, waiting for transfers between devices, return_relative(): parts.append(lax.ppermute(split[:, value], ('shard', 'sub'), pairs))  6.06 us
    unnamed x12, local copies, waits for them, and re-layouts  2.09 us
    reduce_sum x1, other arithmetic, body(): return jnp.sum(jnp.where(hits, known[:, None, :], 0.0), axis=2)  1.47 us
  transfers between devices with their start and end apart: 13, of which 8 were waited for; matrix products, arithmetic and copies ran while one was open for 2% of the time, Pallas kernels for 0%

profile of v2, /device:TPU:0, one launch (start us, length us, event | category | flops | bytes accessed | tf_op | source)
XLA Modules:
  0.0 59.6 jit_solution(5603893879660940779)
XLA Ops:
  0.0 0.5 collective-permute-start.6
  0.5 2.6 %collective-permute-start.2 = (bf16[1,1,32,128]{3,2,1,0:T(8,128)(2,1)}, bf16[1,1,32,128]{3,2,1,0:T(8,128)(2,1)S(1)}, u32[]{:S(2)}, u32[]{:S(2)}) collective-permute-start(bf16[1,1,32,128]{3,2,1,0:T(8,128)(2,1)} %bitcast.36), channel_id=1, source_target_pairs={{0,3},{1,2},{2,1},{3,0},{4,7},{5,6},{6,5},{7,4},{8,11},{9,10},{10,... | collective-permute-start | bytes 24584 | tf_op jit(solution)/shard_map/ppermute | solution.py:204
  3.1 0.0 collective-permute-start.1
  3.1 0.1 collective-permute-start
  3.2 0.7 %constant_dynamic-update-slice_fusion.6 = bf16[16,1,32,128]{3,2,1,0:T(8,128)(2,1)S(1)} fusion(bf16[1,32,128]{2,1,0:T(8,128)(2,1)} %param.6), kind=kLoop, calls=%fused_computation.9 | loop fusion | bytes 16384
  3.9 0.7 %collective-permute-done.2 = bf16[1,1,32,128]{3,2,1,0:T(8,128)(2,1)S(1)} collective-permute-done((bf16[1,1,32,128]{3,2,1,0:T(8,128)(2,1)}, bf16[1,1,32,128]{3,2,1,0:T(8,128)(2,1)S(1)}, u32[]{:S(2)}, u32[]{:S(2)}) %collective-permute-start.2) | collective-permute-done | bytes 8224 | tf_op jit(solution)/shard_map/ppermute | solution.py:204
  4.6 2.3 %collective-permute-done.1 = bf16[1,1,32,128]{3,2,1,0:T(8,128)(2,1)S(1)} collective-permute-done((bf16[1,1,32,128]{3,2,1,0:T(8,128)(2,1)}, bf16[1,1,32,128]{3,2,1,0:T(8,128)(2,1)S(1)}, u32[]{:S(2)}, u32[]{:S(2)}) %collective-permute-start.1) | collective-permute-done | bytes 8224 | tf_op jit(solution)/shard_map/ppermute | solution.py:204
  6.9 0.0 collective-permute-done
  6.9 0.7 %pad_maximum_fusion = bf16[4,1,32,128]{3,2,1,0:T(8,128)(2,1)S(1)} fusion(bf16[1,1,32,128]{3,2,1,0:T(8,128)(2,1)S(1)} %collective-permute-done.2, bf16[1,1,32,128]{3,2,1,0:T(8,128)(2,1)S(1)} %collective-permute-done.1, bf16[1,1,32,128]{3,2,1,0:T(8,128)(2,1)S(1)} %collective-permute-done, bf16[1,1,32,128]{3,2,1,0:T(8,128)(2,1)} %bitcast.39), kind=kLoop, calls=%fused_computation.2 | loop fusion | flops 49152 | bytes 65536 | tf_op jit(solution)/shard_map/concatenate | solution.py:205
  7.6 3.6 %collective-permute-start.5 = (bf16[4,1,32,128]{3,2,1,0:T(8,128)(2,1)S(1)}, bf16[4,1,32,128]{3,2,1,0:T(8,128)(2,1)S(1)}, u32[]{:S(2)}, u32[]{:S(2)}) collective-permute-start(bf16[4,1,32,128]{3,2,1,0:T(8,128)(2,1)S(1)} %pad_maximum_fusion), channel_id=1, source_target_pairs={{0,12},{1,13},{2,14},{3,15},{4,8},{5,9},{6,10},{7,11},{8,4},{9,5},... | collective-permute-start | bytes 98312 | tf_op jit(solution)/shard_map/ppermute | solution.py:204
  11.2 0.0 collective-permute-start.4
  11.2 0.8 %collective-permute-start.3 = (bf16[4,1,32,128]{3,2,1,0:T(8,128)(2,1)S(1)}, bf16[4,1,32,128]{3,2,1,0:T(8,128)(2,1)S(1)}, u32[]{:S(2)}, u32[]{:S(2)}) collective-permute-start(bf16[4,1,32,128]{3,2,1,0:T(8,128)(2,1)S(1)} %pad_maximum_fusion), channel_id=1, source_target_pairs={{0,4},{1,5},{2,6},{3,7},{4,0},{5,1},{6,2},{7,3},{8,12},{9,13},{10,... | collective-permute-start | bytes 98312 | tf_op jit(solution)/shard_map/ppermute | solution.py:204
  12.0 3.1 %collective-permute-done.3 = bf16[4,1,32,128]{3,2,1,0:T(8,128)(2,1)S(1)} collective-permute-done((bf16[4,1,32,128]{3,2,1,0:T(8,128)(2,1)S(1)}, bf16[4,1,32,128]{3,2,1,0:T(8,128)(2,1)S(1)}, u32[]{:S(2)}, u32[]{:S(2)}) %collective-permute-start.3) | collective-permute-done | bytes 32800 | tf_op jit(solution)/shard_map/ppermute | solution.py:204
  15.2 0.9 %collective-permute-done.4 = bf16[4,1,32,128]{3,2,1,0:T(8,128)(2,1)S(1)} collective-permute-done((bf16[4,1,32,128]{3,2,1,0:T(8,128)(2,1)S(1)}, bf16[4,1,32,128]{3,2,1,0:T(8,128)(2,1)S(1)}, u32[]{:S(2)}, u32[]{:S(2)}) %collective-permute-start.4) | collective-permute-done | bytes 32800 | tf_op jit(solution)/shard_map/ppermute | solution.py:204
  16.1 0.0 collective-permute-done.5
  16.1 0.0 collective-permute-done.6.other_ref
  16.1 0.6 %copy-done.1 = bf16[16,1,32,128]{3,2,1,0:T(8,128)(2,1)} copy-done((bf16[16,1,32,128]{3,2,1,0:T(8,128)(2,1)}, bf16[16,1,32,128]{3,2,1,0:T(8,128)(2,1)S(1)}, u32[]{:S(2)}) %copy-start.1) | copy-done | bytes 131096
  16.7 0.7 %copy-done = bf16[8192,128]{1,0:T(8,128)(2,1)} copy-done((bf16[8192,128]{1,0:T(8,128)(2,1)}, bf16[8192,128]{1,0:T(8,128)(2,1)S(1)}, u32[]{:S(2)}) %copy-start) | copy-done | bytes 2097176
  17.4 26.3 %shard_map.64 = f32[16,64]{1,0:T(8,128)} custom-call(s32[1]{0:T(128)} %bitcast.1.half_ref, s32[64,128]{1,0:T(8,128)} %codes_hbm.1, s32[64]{0:T(128)} %lengths_hbm.1, bf16[512,128]{1,0:T(8,128)(2,1)} %bitcast.34, bf16[8192,128]{1,0:T(8,128)(2,1)} %own_ref.1, bf16[8192,128]{1,0:T(8,128)(2,1)} %copy-done, bf16[64,128,128]{2,1,0:T(8,128)(2,1)} %residuals_ref.1), custom_call_target="tpu_custom_call" | custom-call | tf_op jit(solution)/shard_map/pallas_call | solution.py:163
  43.8 0.9 %fusion.4 = (f32[4,1,1,1,64]{4,1,0,3,2:T(1,128)S(1)}, f32[4,1,1,1,64]{4,1,0,3,2:T(1,128)S(1)}, f32[4,1,1,1,64]{4,1,0,3,2:T(1,128)S(1)}, f32[4,1,1,1,64]{4,1,0,3,2:T(1,128)S(1)}) fusion(f32[4,4,1,1,64]{4,1,0,3,2:T(4,128)} %bitcast.35), kind=kLoop, calls=%fused_computation.20 | loop fusion | bytes 8192 | tf_op jit(solution)/shard_map/slice | solution.py:213
  44.6 0.1 collective-permute-start.7
  44.7 0.1 collective-permute-start.9
  44.8 2.1 %collective-permute-start.8 = (f32[4,1,1,64]{3,0,2,1:T(4,128)S(1)}, f32[4,1,1,64]{3,0,2,1:T(4,128)S(1)}, u32[]{:S(2)}, u32[]{:S(2)}) collective-permute-start(f32[4,1,1,64]{3,0,2,1:T(4,128)S(1)} %bitcast.42), channel_id=1, source_target_pairs={{0,2},{1,3},{2,0},{3,1},{4,6},{5,7},{6,4},{7,5},{8,10},{9,11},{10,... | collective-permute-start | bytes 3080 | tf_op jit(solution)/shard_map/ppermute | solution.py:216
  46.9 0.0 collective-permute-done.7
  46.9 0.9 %collective-permute-done.9 = f32[4,1,1,64]{3,0,2,1:T(4,128)S(1)} collective-permute-done((f32[4,1,1,64]{3,0,2,1:T(4,128)S(1)}, f32[4,1,1,64]{3,0,2,1:T(4,128)S(1)}, u32[]{:S(2)}, u32[]{:S(2)}) %collective-permute-start.9) | collective-permute-done | bytes 1056 | tf_op jit(solution)/shard_map/ppermute | solution.py:216
  47.8 0.7 %collective-permute-done.8 = f32[4,1,1,64]{3,0,2,1:T(4,128)S(1)} collective-permute-done((f32[4,1,1,64]{3,0,2,1:T(4,128)S(1)}, f32[4,1,1,64]{3,0,2,1:T(4,128)S(1)}, u32[]{:S(2)}, u32[]{:S(2)}) %collective-permute-start.8) | collective-permute-done | bytes 1056 | tf_op jit(solution)/shard_map/ppermute | solution.py:216
  48.5 0.1 collective-permute-start.10
  48.6 5.0 %collective-permute-start.12 = (f32[1,4,1,64]{3,1,2,0:T(4,128)S(1)}, f32[1,4,1,64]{3,1,2,0:T(4,128)S(1)}, u32[]{:S(2)}, u32[]{:S(2)}) collective-permute-start(f32[1,4,1,64]{3,1,2,0:T(4,128)S(1)} %bitcast.46), channel_id=1, source_target_pairs={{0,12},{1,13},{2,14},{3,15},{4,8},{5,9},{6,10},{7,11},{8,4},{9,5},... | collective-permute-start | bytes 3080 | tf_op jit(solution)/shard_map/ppermute | solution.py:216
  53.6 1.6 %collective-permute-done.12 = f32[1,4,1,64]{3,1,2,0:T(4,128)S(1)} collective-permute-done((f32[1,4,1,64]{3,1,2,0:T(4,128)S(1)}, f32[1,4,1,64]{3,1,2,0:T(4,128)S(1)}, u32[]{:S(2)}, u32[]{:S(2)}) %collective-permute-start.12) | collective-permute-done | bytes 1056 | tf_op jit(solution)/shard_map/ppermute | solution.py:216
  55.1 2.9 %collective-permute-done.11 = f32[1,4,1,64]{3,1,2,0:T(4,128)S(1)} collective-permute-done((f32[1,4,1,64]{3,1,2,0:T(4,128)S(1)}, f32[1,4,1,64]{3,1,2,0:T(4,128)S(1)}, u32[]{:S(2)}, u32[]{:S(2)}) %collective-permute-start.11) | collective-permute-done | bytes 1056 | tf_op jit(solution)/shard_map/ppermute | solution.py:216
  58.0 0.1 broadcast_in_dim.20
  58.1 1.5 %fusion = f32[62]{0:T(128)} fusion(s32[62]{0:T(128)S(1)} %fusion.2, f32[1024]{0:T(1024)S(1)} %broadcast_in_dim.20), kind=kLoop, calls=%fused_computation.1 | loop fusion | flops 190402 | bytes 4592 | tf_op jit(solution)/shard_map/reduce_sum | solution.py:238
  (16 shorter events, 0.1 us)
Async XLA Ops:
  0.0 16.1 %collective-permute-start.6 = (bf16[8192,128]{1,0:T(8,128)(2,1)}, bf16[8192,128]{1,0:T(8,128)(2,1)S(1)}, u32[]{:S(2)}, u32[]{:S(2)}) collective-permute-start(bf16[8192,128]{1,0:T(8,128)(2,1)} %own_ref.1), channel_id=1, source_target_pairs={{0,1},{1,0},{2,3},{3,2},{4,5},{5,4},{6,7},{7,6},{8,9},{9,8},{10,11... | collective-permute-start | bytes 6291464 | tf_op jit(solution)/shard_map/ppermute | solution.py:227
  0.5 4.2 %collective-permute-start.2 = (bf16[1,1,32,128]{3,2,1,0:T(8,128)(2,1)}, bf16[1,1,32,128]{3,2,1,0:T(8,128)(2,1)S(1)}, u32[]{:S(2)}, u32[]{:S(2)}) collective-permute-start(bf16[1,1,32,128]{3,2,1,0:T(8,128)(2,1)} %bitcast.36), channel_id=1, source_target_pairs={{0,3},{1,2},{2,1},{3,0},{4,7},{5,6},{6,5},{7,4},{8,11},{9,10},{10,... | collective-permute-start | bytes 24584 | tf_op jit(solution)/shard_map/ppermute | solution.py:204
  3.1 3.9 %collective-permute-start.1 = (bf16[1,1,32,128]{3,2,1,0:T(8,128)(2,1)}, bf16[1,1,32,128]{3,2,1,0:T(8,128)(2,1)S(1)}, u32[]{:S(2)}, u32[]{:S(2)}) collective-permute-start(bf16[1,1,32,128]{3,2,1,0:T(8,128)(2,1)} %bitcast.37), channel_id=1, source_target_pairs={{0,2},{1,3},{2,0},{3,1},{4,6},{5,7},{6,4},{7,5},{8,10},{9,11},{10,... | collective-permute-start | bytes 24584 | tf_op jit(solution)/shard_map/ppermute | solution.py:204
  3.1 3.9 %collective-permute-start = (bf16[1,1,32,128]{3,2,1,0:T(8,128)(2,1)}, bf16[1,1,32,128]{3,2,1,0:T(8,128)(2,1)S(1)}, u32[]{:S(2)}, u32[]{:S(2)}) collective-permute-start(bf16[1,1,32,128]{3,2,1,0:T(8,128)(2,1)} %bitcast.38), channel_id=1, source_target_pairs={{0,1},{1,0},{2,3},{3,2},{4,5},{5,4},{6,7},{7,6},{8,9},{9,8},{10,11... | collective-permute-start | bytes 24584 | tf_op jit(solution)/shard_map/ppermute | solution.py:204
  7.6 8.4 %collective-permute-start.5 = (bf16[4,1,32,128]{3,2,1,0:T(8,128)(2,1)S(1)}, bf16[4,1,32,128]{3,2,1,0:T(8,128)(2,1)S(1)}, u32[]{:S(2)}, u32[]{:S(2)}) collective-permute-start(bf16[4,1,32,128]{3,2,1,0:T(8,128)(2,1)S(1)} %pad_maximum_fusion), channel_id=1, source_target_pairs={{0,12},{1,13},{2,14},{3,15},{4,8},{5,9},{6,10},{7,11},{8,4},{9,5},... | collective-permute-start | bytes 98312 | tf_op jit(solution)/shard_map/ppermute | solution.py:204
  11.2 4.8 %collective-permute-start.4 = (bf16[4,1,32,128]{3,2,1,0:T(8,128)(2,1)S(1)}, bf16[4,1,32,128]{3,2,1,0:T(8,128)(2,1)S(1)}, u32[]{:S(2)}, u32[]{:S(2)}) collective-permute-start(bf16[4,1,32,128]{3,2,1,0:T(8,128)(2,1)S(1)} %pad_maximum_fusion), channel_id=1, source_target_pairs={{0,8},{1,9},{2,10},{3,11},{4,12},{5,13},{6,14},{7,15},{8,0},{9,1},... | collective-permute-start | bytes 98312 | tf_op jit(solution)/shard_map/ppermute | solution.py:204
  11.2 3.9 %collective-permute-start.3 = (bf16[4,1,32,128]{3,2,1,0:T(8,128)(2,1)S(1)}, bf16[4,1,32,128]{3,2,1,0:T(8,128)(2,1)S(1)}, u32[]{:S(2)}, u32[]{:S(2)}) collective-permute-start(bf16[4,1,32,128]{3,2,1,0:T(8,128)(2,1)S(1)} %pad_maximum_fusion), channel_id=1, source_target_pairs={{0,4},{1,5},{2,6},{3,7},{4,0},{5,1},{6,2},{7,3},{8,12},{9,13},{10,... | collective-permute-start | bytes 98312 | tf_op jit(solution)/shard_map/ppermute | solution.py:204
  16.1 0.6 %copy-start.1 = (bf16[16,1,32,128]{3,2,1,0:T(8,128)(2,1)}, bf16[16,1,32,128]{3,2,1,0:T(8,128)(2,1)S(1)}, u32[]{:S(2)}) copy-start(bf16[16,1,32,128]{3,2,1,0:T(8,128)(2,1)S(1)} %constant_dynamic-update-slice_fusion) | copy-start | bytes 393220
  16.1 1.4 %copy-start = (bf16[8192,128]{1,0:T(8,128)(2,1)}, bf16[8192,128]{1,0:T(8,128)(2,1)S(1)}, u32[]{:S(2)}) copy-start(bf16[8192,128]{1,0:T(8,128)(2,1)S(1)} %collective-permute-done.6.other_ref) | copy-start | bytes 6291460
  17.4 36.1 %copy-start.2 = (s32[1,62]{1,0:T(1,128)S(1)}, s32[1,62]{1,0:T(1,128)}, u32[]{:S(2)}) copy-start(s32[1,62]{1,0:T(1,128)} %param.7) | copy-start | bytes 748
  44.6 2.2 %collective-permute-start.7 = (f32[4,1,1,64]{3,0,2,1:T(4,128)S(1)}, f32[4,1,1,64]{3,0,2,1:T(4,128)S(1)}, u32[]{:S(2)}, u32[]{:S(2)}) collective-permute-start(f32[4,1,1,64]{3,0,2,1:T(4,128)S(1)} %bitcast.44), channel_id=1, source_target_pairs={{0,1},{1,0},{2,3},{3,2},{4,5},{5,4},{6,7},{7,6},{8,9},{9,8},{10,11... | collective-permute-start | bytes 3080 | tf_op jit(solution)/shard_map/ppermute | solution.py:216
  44.7 3.1 %collective-permute-start.9 = (f32[4,1,1,64]{3,0,2,1:T(4,128)S(1)}, f32[4,1,1,64]{3,0,2,1:T(4,128)S(1)}, u32[]{:S(2)}, u32[]{:S(2)}) collective-permute-start(f32[4,1,1,64]{3,0,2,1:T(4,128)S(1)} %bitcast.43), channel_id=1, source_target_pairs={{0,3},{1,2},{2,1},{3,0},{4,7},{5,6},{6,5},{7,4},{8,11},{9,10},{10,... | collective-permute-start | bytes 3080 | tf_op jit(solution)/shard_map/ppermute | solution.py:216
  44.8 3.7 %collective-permute-start.8 = (f32[4,1,1,64]{3,0,2,1:T(4,128)S(1)}, f32[4,1,1,64]{3,0,2,1:T(4,128)S(1)}, u32[]{:S(2)}, u32[]{:S(2)}) collective-permute-start(f32[4,1,1,64]{3,0,2,1:T(4,128)S(1)} %bitcast.42), channel_id=1, source_target_pairs={{0,2},{1,3},{2,0},{3,1},{4,6},{5,7},{6,4},{7,5},{8,10},{9,11},{10,... | collective-permute-start | bytes 3080 | tf_op jit(solution)/shard_map/ppermute | solution.py:216
  48.5 5.1 %collective-permute-start.10 = (f32[1,4,1,64]{3,1,2,0:T(4,128)S(1)}, f32[1,4,1,64]{3,1,2,0:T(4,128)S(1)}, u32[]{:S(2)}, u32[]{:S(2)}) collective-permute-start(f32[1,4,1,64]{3,1,2,0:T(4,128)S(1)} %bitcast.47), channel_id=1, source_target_pairs={{0,4},{1,5},{2,6},{3,7},{4,0},{5,1},{6,2},{7,3},{8,12},{9,13},{10,... | collective-permute-start | bytes 3080 | tf_op jit(solution)/shard_map/ppermute | solution.py:216
  48.6 6.6 %collective-permute-start.12 = (f32[1,4,1,64]{3,1,2,0:T(4,128)S(1)}, f32[1,4,1,64]{3,1,2,0:T(4,128)S(1)}, u32[]{:S(2)}, u32[]{:S(2)}) collective-permute-start(f32[1,4,1,64]{3,1,2,0:T(4,128)S(1)} %bitcast.46), channel_id=1, source_target_pairs={{0,12},{1,13},{2,14},{3,15},{4,8},{5,9},{6,10},{7,11},{8,4},{9,5},... | collective-permute-start | bytes 3080 | tf_op jit(solution)/shard_map/ppermute | solution.py:216
  53.5 4.5 %collective-permute-start.11 = (f32[1,4,1,64]{3,1,2,0:T(4,128)S(1)}, f32[1,4,1,64]{3,1,2,0:T(4,128)S(1)}, u32[]{:S(2)}, u32[]{:S(2)}) collective-permute-start(f32[1,4,1,64]{3,1,2,0:T(4,128)S(1)} %bitcast.45), channel_id=1, source_target_pairs={{0,8},{1,9},{2,10},{3,11},{4,12},{5,13},{6,14},{7,15},{8,0},{9,1},... | collective-permute-start | bytes 3080 | tf_op jit(solution)/shard_map/ppermute | solution.py:216

commit v3 on v1

v3 whole, which is shorter than its diff:
```python
import functools

import jax
import jax.numpy as jnp
from jax import lax
from jax.experimental import pallas as pl
from jax.experimental.pallas import tpu as pltpu
from jax.sharding import PartitionSpec as P

CHUNK = 32
GROUP = 8
QUERY_BLOCK = 512
SMEM = pl.BlockSpec(memory_space=pltpu.SMEM)
VMEM = pl.BlockSpec(memory_space=pltpu.VMEM)
HBM = pl.BlockSpec(memory_space=pltpu.HBM)


def normalized(vectors):
    total = jnp.sum(vectors * vectors, axis=-1, keepdims=True)
    return (vectors * lax.rsqrt(total + 1e-06)).astype(jnp.bfloat16)


def decode_kernel(
    half_ref,
    codes_hbm,
    lengths_hbm,
    own_ref,
    other_ref,
    residuals_ref,
    embedded,
    owner_ref,
    codes_ref,
    lengths_ref,
    at_ref,
    live_ref,
    staged,
    table,
    residual_rows,
    rows,
    sems,
):
    passages = lengths_ref.shape[0]
    slots = codes_ref.shape[0] // passages
    half_rows, width = own_ref.shape
    half = half_ref[0]
    lengths_copy = pltpu.make_async_copy(lengths_hbm, lengths_ref, sems.at[2])
    codes_copy = pltpu.make_async_copy(codes_hbm, codes_ref, sems.at[3])
    own_copy = pltpu.make_async_copy(own_ref, staged, sems.at[0])
    residual_copy = pltpu.make_async_copy(residuals_ref, residual_rows, sems.at[1])
    lengths_copy.start()
    codes_copy.start()
    own_copy.start()
    residual_copy.start()

    lengths_copy.wait()

    def listing(p, chunks):
        length = lengths_ref[p]
        for k in range(slots // CHUNK):
            at_ref[chunks + k] = p * slots + k * CHUNK
            live_ref[chunks + k] = length - k * CHUNK
            owner_ref[chunks + k] = p
        return chunks + (length + CHUNK - 1) // CHUNK

    chunks = lax.fori_loop(0, passages, listing, 0)
    for k in range(GROUP):
        at_ref[chunks + k] = 0
        live_ref[chunks + k] = CHUNK
        owner_ref[chunks + k] = passages
    groups = (chunks + GROUP - 1) // GROUP
    owner_ref[owner_ref.shape[0] - 1] = groups

    step = 256

    def widen(source, base):
        def body(i, carry):
            start = pl.multiple_of(i * step, step)
            table[pl.ds(pl.multiple_of(base + start, step), step), :] = source[
                pl.ds(start, step), :
            ].astype(jnp.float32)
            return carry

        lax.fori_loop(0, half_rows // step, body, 0)

    widen(other_ref, (1 - half) * half_rows)
    own_copy.wait()
    widen(staged, half * half_rows)
    codes_copy.wait()
    residual_copy.wait()

    slot_numbers = lax.broadcasted_iota(jnp.int32, (CHUNK, width), 0)
    single = table.reshape(2 * half_rows, 1, width)

    def decode(g, carry):
        before = jnp.maximum(g - 1, 0)
        done = []
        for k in range(GROUP):
            i = before * GROUP + k
            own = pl.ds(pl.multiple_of(at_ref[i], CHUNK), CHUNK)
            vectors = rows[pl.ds(k * CHUNK, CHUNK), :] + residual_rows[own, :].astype(jnp.float32)
            vectors = jnp.where(slot_numbers < live_ref[i], vectors, vectors[0:1, :])
            done.append(normalized(vectors))
            at = at_ref[g * GROUP + k]
            for j in range(CHUNK):
                rows[pl.ds(k * CHUNK + j, 1), :] = single[codes_ref[at + j]]
        for k in range(GROUP):
            start = pl.multiple_of((before * GROUP + k) * CHUNK, CHUNK)
            embedded[pl.ds(start, CHUNK), :] = done[k]
        return carry

    lax.fori_loop(0, groups + 1, decode, 0)


def decode_all(half, token_codes, lengths, own, other, residuals):
    passages, slots, width = residuals.shape
    half_rows = own.shape[0]
    most = passages * (slots // CHUNK) + 2 * GROUP
    return pl.pallas_call(
        decode_kernel,
        out_shape=(
            jax.ShapeDtypeStruct((most * CHUNK, width), jnp.bfloat16),
            jax.ShapeDtypeStruct((most + 1,), jnp.int32),
        ),
        in_specs=[SMEM, HBM, HBM, HBM, VMEM, HBM],
        out_specs=(VMEM, SMEM),
        scratch_shapes=[
            pltpu.SMEM((passages * slots,), jnp.int32),
            pltpu.SMEM((passages,), jnp.int32),
            pltpu.SMEM((most,), jnp.int32),
            pltpu.SMEM((most,), jnp.int32),
            pltpu.VMEM((half_rows, width), jnp.bfloat16),
            pltpu.VMEM((2 * half_rows, width), jnp.float32),
            pltpu.VMEM((passages * slots, width), jnp.bfloat16),
            pltpu.VMEM((GROUP * CHUNK, width), jnp.float32),
            pltpu.SemaphoreType.DMA((4,)),
        ],
        compiler_params=pltpu.CompilerParams(vmem_limit_bytes=40 * 1024 * 1024),
        cost_estimate=pl.CostEstimate(flops=10**7, bytes_accessed=40 * 10**6, transcendentals=0),
        name="decode",
    )(
        half,
        token_codes.reshape(passages * slots),
        lengths,
        own,
        other,
        residuals.reshape(passages * slots, width),
    )


def score_kernel(token_count, passages, owner_ref, queries_ref, embedded, out_ref, turned, largest):
    query_tokens = queries_ref.shape[0]
    block = min(QUERY_BLOCK, query_tokens)
    blocks = query_tokens // block
    groups = owner_ref[owner_ref.shape[0] - 1]
    per_block = block // token_count
    owner = lax.broadcasted_iota(jnp.int32, (per_block, block), 0)
    token_of = lax.broadcasted_iota(jnp.int32, (per_block, block), 1) // token_count
    summing = (owner == token_of).astype(jnp.float32)

    def score_block(b, carry):
        at = pl.ds(pl.multiple_of(b * block, block), block)
        vectors = normalized(queries_ref[at, :].astype(jnp.float32))
        turned[...] = vectors.astype(jnp.float32).T.astype(jnp.bfloat16)
        largest[...] = jnp.full(largest.shape, -jnp.inf, jnp.float32)

        def score(g, inner):
            at = pl.ds(pl.multiple_of(g * GROUP * CHUNK, GROUP * CHUNK), GROUP * CHUNK)
            similar = jnp.dot(embedded[at, :], turned[...], preferred_element_type=jnp.float32)
            parts = jnp.max(similar.reshape(GROUP, CHUNK // 8, 8, block), axis=1)
            for k in range(GROUP):
                p = owner_ref[g * GROUP + k]
                largest[p] = jnp.maximum(largest[p], parts[k])
            return inner

        lax.fori_loop(0, groups, score, 0)
        sums = lax.dot_general(
            summing,
            jnp.max(largest[0:passages], axis=1),
            (((1,), (1,)), ((), ())),
            precision=lax.Precision.HIGHEST,
            preferred_element_type=jnp.float32,
        )
        out_ref[pl.ds(pl.multiple_of(b * per_block, per_block), per_block), :] = sums
        return carry

    lax.fori_loop(0, blocks, score_block, 0)


def score_all(owner, query_rows, embedded, passages, token_count):
    query_tokens, width = query_rows.shape
    block = min(QUERY_BLOCK, query_tokens)
    return pl.pallas_call(
        functools.partial(score_kernel, token_count, passages),
        out_shape=jax.ShapeDtypeStruct((query_tokens // token_count, passages), jnp.float32),
        in_specs=[SMEM, VMEM, VMEM],
        out_specs=VMEM,
        scratch_shapes=[
            pltpu.VMEM((width, block), jnp.bfloat16),
            pltpu.VMEM((passages + 1, 8, block), jnp.float32),
        ],
        compiler_params=pltpu.CompilerParams(vmem_limit_bytes=32 * 1024 * 1024),
        name="score",
    )(owner, query_rows, embedded)


def body(queries, candidates, token_codes, residuals, lengths, centroids):
    local_queries, token_count, width = queries.shape
    targets = lax.axis_size("shard") * lax.axis_size("sub")
    passages = token_codes.shape[0]
    half = lax.axis_index("sub").astype(jnp.int32)
    other = lax.ppermute(centroids, "sub", [(0, 1), (1, 0)])
    sent = jnp.broadcast_to(queries[None], (targets,) + queries.shape)
    gathered = lax.all_to_all(sent, ("shard", "sub"), split_axis=0, concat_axis=0, tiled=True)
    query_rows = gathered.reshape(targets * local_queries * token_count, width)
    embedded, owner = decode_all(half.reshape(1), token_codes, lengths, centroids, other, residuals)
    scores = score_all(owner, query_rows, embedded, passages, token_count)
    returned = lax.all_to_all(
        scores.reshape(targets, local_queries, passages),
        ("shard", "sub"),
        split_axis=0,
        concat_axis=0,
        tiled=True,
    )
    known = jnp.transpose(returned, (1, 0, 2)).reshape(local_queries, targets * passages)
    numbers = jnp.arange(targets * passages, dtype=jnp.int32)
    hits = candidates[:, :, None] == numbers[None, None, :]
    return jnp.sum(jnp.where(hits, known[:, None, :], 0.0), axis=2)


def solution(mesh):
    placed = (
        P(("groups", "shard", "sub"), None, None),
        P(("groups", "shard", "sub"), None),
        P(("groups", "shard", "sub"), None),
        P(("groups", "shard", "sub"), None, None),
        P(("groups", "shard", "sub")),
        P(("groups", "shard", "sub"), None),
    )
    return jax.shard_map(
        body,
        mesh=mesh,
        in_specs=placed,
        out_specs=P(("groups", "shard", "sub"), None),
        check_vma=False,
    )
```

time: 66.4 us -> 47.6 us (0.72)
  Pallas kernels: 34.2 us -> 15.1 us
  waiting for transfers between devices: 7.93 us -> 0.01 us
  local copies, waits for them, and re-layouts: 4.94 us -> 9.47 us
  blocking collectives: 9.17 us -> 12.8 us
    pallas_call x1 -> x2, Pallas kernels: 34.2 us -> 15.1 us  [the longest x1 9.35 us: decode_all(): pl.pallas_call(decode_kernel, out_shape=(jax.ShapeDtypeStruct((most * CHU...]
    all_to_all x1, waiting for transfers between devices: 7.93 us -> 0.01 us  [body(): lax.all_to_all(sent, ('shard', 'sub'), split_axis=0, concat_axis=0, tiled...]
    unnamed x8 -> x14, local copies, waits for them, and re-layouts: 3.01 us -> 7.52 us
    all_to_all x1, blocking collectives: 9.17 us -> 12.8 us  [body(): lax.all_to_all(scores.reshape(targets, local_queries, passages), ('shard'...]
  transfers between devices with their start and end apart: 2 -> 2, of which waited for: 1 -> 0; matrix products, arithmetic and copies ran while one was open for 2% -> 3% of each run, Pallas kernels for 0% -> 20%
where the time goes in v3:
time: 47.6 us; the launch traced here: 47 us
  Pallas kernels  15.1 us (32%)
  blocking collectives  12.8 us (27%)
  local copies, waits for them, and re-layouts  9.47 us (20%)
  starting transfers between devices  7.47 us (16%)
  other arithmetic  2.13 us (4%)
    all_to_all x1, blocking collectives, body(): lax.all_to_all(scores.reshape(targets, local_queries, passages), ('shard'...  12.8 us
    pallas_call x1, Pallas kernels, decode_all(): pl.pallas_call(decode_kernel, out_shape=(jax.ShapeDtypeStruct((most * CHU...  9.35 us
    unnamed x14, local copies, waits for them, and re-layouts  7.52 us
    all_to_all x1, starting transfers between devices, body(): lax.all_to_all(sent, ('shard', 'sub'), split_axis=0, concat_axis=0, tiled...  7.02 us
    pallas_call x1, Pallas kernels, score_all(): pl.pallas_call(functools.partial(score_kernel, token_count, passages), ou...  5.74 us
    reduce_sum x1, other arithmetic, body(): return jnp.sum(jnp.where(hits, known[:, None, :], 0.0), axis=2)  1.46 us
    broadcast_in_dim x1, local copies, waits for them, and re-layouts, body(): sent = jnp.broadcast_to(queries[None], (targets,) + queries.shape)  1.37 us
  transfers between devices with their start and end apart: 2, of which 0 were waited for; matrix products, arithmetic and copies ran while one was open for 3% of the time, Pallas kernels for 20%

profile of v3, /device:TPU:0, one launch (start us, length us, event | category | flops | bytes accessed | tf_op | source)
XLA Modules:
  0.0 47.0 jit_solution(9365944610609859012)
XLA Ops:
  0.0 0.5 collective-permute-start
  0.5 1.4 %broadcast_in_dim.25 = bf16[16,1,32,128]{3,2,1,0:T(8,128)(2,1)} broadcast(bf16[32,128]{1,0:T(8,128)(2,1)} %bitcast.14), dimensions={2,3} | broadcast | bytes 139264 | tf_op jit(solution)/shard_map/broadcast_in_dim | solution.py:212
  1.8 7.0 %all-to-all-start = ((bf16[16,1,32,128]{3,2,1,0:T(8,128)(2,1)}), bf16[16,1,32,128]{3,2,1,0:T(8,128)(2,1)S(1)}, u32[]{:S(2)}, u32[]{:S(2)}) async-start(bf16[16,1,32,128]{3,2,1,0:T(8,128)(2,1)} %broadcast_in_dim.25), calls=%async_computation | async-start | bytes 262144 | tf_op jit(solution)/shard_map/all_to_all | solution.py:213
  8.8 0.0 collective-permute-done.other_ref
  8.9 0.0 copy-start.2
  8.9 1.3 %copy-done.2 = bf16[8192,128]{1,0:T(8,128)(2,1)} copy-done((bf16[8192,128]{1,0:T(8,128)(2,1)}, bf16[8192,128]{1,0:T(8,128)(2,1)S(1)}, u32[]{:S(2)}) %copy-start.2) | copy-done | bytes 2097176
  10.2 0.0 copy-start
  10.2 1.6 %copy-done = bf16[8192,128]{1,0:T(8,128)(2,1)S(1)} copy-done((bf16[8192,128]{1,0:T(8,128)(2,1)S(1)}, bf16[8192,128]{1,0:T(8,128)(2,1)}, u32[]{:S(2)}) %copy-start) | copy-done | bytes 2097176
  11.8 0.0 copy-start.1
  11.8 1.6 %copy-done.1 = bf16[64,128,128]{2,1,0:T(8,128)(2,1)S(1)} copy-done((bf16[64,128,128]{2,1,0:T(8,128)(2,1)S(1)}, bf16[64,128,128]{2,1,0:T(8,128)(2,1)}, u32[]{:S(2)}) %copy-start.1) | copy-done | bytes 2097176
  13.4 0.0 copy-start.3
  13.4 1.6 %copy-done.3 = bf16[8192,128]{1,0:T(8,128)(2,1)S(1)} copy-done((bf16[8192,128]{1,0:T(8,128)(2,1)S(1)}, bf16[8192,128]{1,0:T(8,128)(2,1)}, u32[]{:S(2)}) %copy-start.3) | copy-done | bytes 2097176
  15.0 0.0 copy-start.4
  15.0 0.8 %copy-done.4 = s32[64,128]{1,0:T(8,128)S(1)} copy-done((s32[64,128]{1,0:T(8,128)S(1)}, s32[64,128]{1,0:T(8,128)}, u32[]{:S(2)}) %copy-start.4) | copy-done | bytes 32792
  15.7 0.0 copy-start.5
  15.7 0.7 %copy-done.5 = s32[64]{0:T(128)S(1)} copy-done((s32[64]{0:T(128)S(1)}, s32[64]{0:T(128)}, u32[]{:S(2)}) %copy-start.5) | copy-done | bytes 280
  16.4 9.4 %decode.1 = (bf16[8704,128]{1,0:T(8,128)(2,1)S(1)}, s32[273]{0:T(512)S(1)}) custom-call(s32[1]{0:T(128)} %bitcast.1.half_ref, s32[8192]{0:T(1024)S(1)} %bitcast.12, s32[64]{0:T(128)S(1)} %copy-done.5, bf16[8192,128]{1,0:T(8,128)(2,1)S(1)} %copy-done, bf16[8192,128]{1,0:T(8,128)(2,1)S(1)} %copy-done.3, bf16[8192,128]{1,0:T(8,128)(2,1)S(1)} %bitcast.10), custom_call_target="tpu_custom_call" | custom-call | flops 10000000 | bytes 40000000 | tf_op jit(solution)/shard_map/decode/pallas_call | solution.py:118
  25.8 0.0 copy-start.6
  25.8 0.0 all-to-all-done
  25.8 5.7 %score.1 = f32[16,64]{1,0:T(8,128)S(1)} custom-call(s32[273]{0:T(512)S(1)} %get-tuple-element.7.owner_ref, bf16[512,128]{1,0:T(8,128)(2,1)S(1)} %bitcast.11, bf16[8704,128]{1,0:T(8,128)(2,1)S(1)} %get-tuple-element.8.embedded), custom_call_target="tpu_custom_call" | custom-call | tf_op jit(solution)/shard_map/score/pallas_call | solution.py:192
  31.5 12.8 %all_to_all.10 = f32[16,1,64]{2,1,0:T(1,128)S(1)} all-to-all(f32[16,1,64]{2,1,0:T(1,128)S(1)} %bitcast.13), channel_id=1, replica_groups=mesh['groups'=2,'shard'=8,'sub'=2] {'shard','sub'}, dimensions={0} | all-to-all | bytes 8192 | tf_op jit(solution)/shard_map/all_to_all | solution.py:217
  44.3 0.5 %broadcast.59 = f32[]{:T(128)} broadcast(f32[]{:T(128)} %constant.12), dimensions={} | broadcast | bytes 8 | tf_op jit(solution)/shard_map/all_to_all | solution.py:217
  44.8 0.7 %reduce.4 = f32[16,64]{1,0:T(8,128)S(1)} reduce(f32[16,1,64]{2,1,0:T(1,128)S(1)} %all_to_all.10, f32[]{:T(128)} %broadcast.59), dimensions={1}, to_apply=%all_to_all.7.reduce_sub_computation.3 | reduce | bytes 8196 | tf_op jit(solution)/shard_map/all_to_all | solution.py:217
  45.5 0.1 broadcast_in_dim.26
  45.5 0.0 copy-done.6
  45.5 1.5 %fusion = f32[62]{0:T(128)} fusion(s32[62]{0:T(128)S(1)} %bitcast.15, f32[1024]{0:T(1024)S(1)} %broadcast_in_dim.26), kind=kLoop, calls=%fused_computation.1 | loop fusion | flops 190402 | bytes 4592 | tf_op jit(solution)/shard_map/reduce_sum | solution.py:227
Async XLA Ops:
  0.0 8.9 %collective-permute-start = (bf16[8192,128]{1,0:T(8,128)(2,1)}, bf16[8192,128]{1,0:T(8,128)(2,1)S(1)}, u32[]{:S(2)}, u32[]{:S(2)}) collective-permute-start(bf16[8192,128]{1,0:T(8,128)(2,1)} %own_ref.1), channel_id=1, source_target_pairs={{0,1},{1,0},{2,3},{3,2},{4,5},{5,4},{6,7},{7,6},{8,9},{9,8},{10,11... | collective-permute-start | bytes 6291464 | tf_op jit(solution)/shard_map/ppermute | solution.py:211
  1.8 23.9 %all-to-all-start = ((bf16[16,1,32,128]{3,2,1,0:T(8,128)(2,1)}), bf16[16,1,32,128]{3,2,1,0:T(8,128)(2,1)S(1)}, u32[]{:S(2)}, u32[]{:S(2)}) async-start(bf16[16,1,32,128]{3,2,1,0:T(8,128)(2,1)} %broadcast_in_dim.25), calls=%async_computation | async-start | bytes 262144 | tf_op jit(solution)/shard_map/all_to_all | solution.py:213
  8.9 1.3 %copy-start.2 = (bf16[8192,128]{1,0:T(8,128)(2,1)}, bf16[8192,128]{1,0:T(8,128)(2,1)S(1)}, u32[]{:S(2)}) copy-start(bf16[8192,128]{1,0:T(8,128)(2,1)S(1)} %collective-permute-done.other_ref) | copy-start | bytes 6291460
  10.2 1.6 %copy-start = (bf16[8192,128]{1,0:T(8,128)(2,1)S(1)}, bf16[8192,128]{1,0:T(8,128)(2,1)}, u32[]{:S(2)}) copy-start(bf16[8192,128]{1,0:T(8,128)(2,1)} %own_ref.1) | copy-start | bytes 6291460
  11.8 1.6 %copy-start.1 = (bf16[64,128,128]{2,1,0:T(8,128)(2,1)S(1)}, bf16[64,128,128]{2,1,0:T(8,128)(2,1)}, u32[]{:S(2)}) copy-start(bf16[64,128,128]{2,1,0:T(8,128)(2,1)} %param.9) | copy-start | bytes 6291460
  13.4 1.6 %copy-start.3 = (bf16[8192,128]{1,0:T(8,128)(2,1)S(1)}, bf16[8192,128]{1,0:T(8,128)(2,1)}, u32[]{:S(2)}) copy-start(bf16[8192,128]{1,0:T(8,128)(2,1)} %copy-done.2) | copy-start | bytes 6291460
  15.0 0.8 %copy-start.4 = (s32[64,128]{1,0:T(8,128)S(1)}, s32[64,128]{1,0:T(8,128)}, u32[]{:S(2)}) copy-start(s32[64,128]{1,0:T(8,128)} %param.8) | copy-start | bytes 98308
  15.7 0.7 %copy-start.5 = (s32[64]{0:T(128)S(1)}, s32[64]{0:T(128)}, u32[]{:S(2)}) copy-start(s32[64]{0:T(128)} %lengths_hbm.1) | copy-start | bytes 772
  25.8 19.8 %copy-start.6 = (s32[1,62]{1,0:T(1,128)S(1)}, s32[1,62]{1,0:T(1,128)}, u32[]{:S(2)}) copy-start(s32[1,62]{1,0:T(1,128)} %param.7) | copy-start | bytes 748

commit v4 on v3

--- a/solution.py
+++ b/solution.py
@@ -9,6 +9,7 @@
 
 CHUNK = 32
 GROUP = 8
+SCORE_GROUP = 16
 QUERY_BLOCK = 512
 SMEM = pl.BlockSpec(memory_space=pltpu.SMEM)
 VMEM = pl.BlockSpec(memory_space=pltpu.VMEM)
@@ -63,12 +64,12 @@
         return chunks + (length + CHUNK - 1) // CHUNK
 
     chunks = lax.fori_loop(0, passages, listing, 0)
-    for k in range(GROUP):
+    for k in range(SCORE_GROUP):
         at_ref[chunks + k] = 0
         live_ref[chunks + k] = CHUNK
         owner_ref[chunks + k] = passages
     groups = (chunks + GROUP - 1) // GROUP
-    owner_ref[owner_ref.shape[0] - 1] = groups
+    owner_ref[owner_ref.shape[0] - 1] = chunks
 
     step = 256
 
@@ -111,10 +112,14 @@
     lax.fori_loop(0, groups + 1, decode, 0)
 
 
+def pinned(array):
+    return pltpu.with_memory_space_constraint(array, pltpu.HBM)
+
+
 def decode_all(half, token_codes, lengths, own, other, residuals):
     passages, slots, width = residuals.shape
     half_rows = own.shape[0]
-    most = passages * (slots // CHUNK) + 2 * GROUP
+    most = passages * (slots // CHUNK) + 2 * SCORE_GROUP
     return pl.pallas_call(
         decode_kernel,
         out_shape=(
@@ -139,11 +144,11 @@
         name="decode",
     )(
         half,
-        token_codes.reshape(passages * slots),
-        lengths,
-        own,
+        pinned(token_codes.reshape(passages * slots)),
+        pinned(lengths),
+        pinned(own),
         other,
-        residuals.reshape(passages * slots, width),
+        pinned(residuals.reshape(passages * slots, width)),
     )
 
 
@@ -151,7 +156,8 @@
     query_tokens = queries_ref.shape[0]
     block = min(QUERY_BLOCK, query_tokens)
     blocks = query_tokens // block
-    groups = owner_ref[owner_ref.shape[0] - 1]
+    chunks = owner_ref[owner_ref.shape[0] - 1]
+    groups = (chunks + SCORE_GROUP - 1) // SCORE_GROUP
     per_block = block // token_count
     owner = lax.broadcasted_iota(jnp.int32, (per_block, block), 0)
     token_of = lax.broadcasted_iota(jnp.int32, (per_block, block), 1) // token_count
@@ -164,11 +170,11 @@
         largest[...] = jnp.full(largest.shape, -jnp.inf, jnp.float32)
 
         def score(g, inner):
-            at = pl.ds(pl.multiple_of(g * GROUP * CHUNK, GROUP * CHUNK), GROUP * CHUNK)
+            at = pl.ds(pl.multiple_of(g * SCORE_GROUP * CHUNK, SCORE_GROUP * CHUNK), SCORE_GROUP * CHUNK)
             similar = jnp.dot(embedded[at, :], turned[...], preferred_element_type=jnp.float32)
-            parts = jnp.max(similar.reshape(GROUP, CHUNK // 8, 8, block), axis=1)
-            for k in range(GROUP):
-                p = owner_ref[g * GROUP + k]
+            parts = jnp.max(similar.reshape(SCORE_GROUP, CHUNK // 8, 8, block), axis=1)
+            for k in range(SCORE_GROUP):
+                p = owner_ref[g * SCORE_GROUP + k]
                 largest[p] = jnp.maximum(largest[p], parts[k])
             return inner
 
@@ -203,28 +209,55 @@
     )(owner, query_rows, embedded)
 
 
+def pick_kernel(passages, candidates_ref, returned_ref, out_ref):
+    local_queries, count = candidates_ref.shape
+    targets = returned_ref.shape[0]
+    passage_numbers = lax.broadcasted_iota(jnp.int32, (passages, count), 0)
+    target_numbers = lax.broadcasted_iota(jnp.int32, (targets, count), 0)
+    for q in range(local_queries):
+        wanted = candidates_ref[q : q + 1, :]
+        target = wanted // passages
+        hits = (passage_numbers == wanted - target * passages).astype(jnp.float32)
+        picked = jnp.dot(
+            returned_ref[:, q * passages : (q + 1) * passages],
+            hits,
+            precision=lax.Precision.HIGHEST,
+            preferred_element_type=jnp.float32,
+        )
+        kept = jnp.where(target_numbers == target, picked, 0.0)
+        out_ref[q : q + 1, :] = jnp.sum(kept, axis=0, keepdims=True)
+
+
+def pick(candidates, returned, passages):
+    return pl.pallas_call(
+        functools.partial(pick_kernel, passages),
+        out_shape=jax.ShapeDtypeStruct(candidates.shape, jnp.float32),
+        in_specs=[VMEM, VMEM],
+        out_specs=VMEM,
+        name="pick",
+    )(candidates, returned)
+
+
 def body(queries, candidates, token_codes, residuals, lengths, centroids):
     local_queries, token_count, width = queries.shape
     targets = lax.axis_size("shard") * lax.axis_size("sub")
     passages = token_codes.shape[0]
     half = lax.axis_index("sub").astype(jnp.int32)
     other = lax.ppermute(centroids, "sub", [(0, 1), (1, 0)])
-    sent = jnp.broadcast_to(queries[None], (targets,) + queries.shape)
+    own_rows = queries.reshape(1, local_queries * token_count, width)
+    sent = jnp.broadcast_to(own_rows, (targets,) + own_rows.shape[1:])
     gathered = lax.all_to_all(sent, ("shard", "sub"), split_axis=0, concat_axis=0, tiled=True)
     query_rows = gathered.reshape(targets * local_queries * token_count, width)
     embedded, owner = decode_all(half.reshape(1), token_codes, lengths, centroids, other, residuals)
     scores = score_all(owner, query_rows, embedded, passages, token_count)
     returned = lax.all_to_all(
-        scores.reshape(targets, local_queries, passages),
+        scores.reshape(targets, local_queries * passages),
         ("shard", "sub"),
         split_axis=0,
         concat_axis=0,
         tiled=True,
     )
-    known = jnp.transpose(returned, (1, 0, 2)).reshape(local_queries, targets * passages)
-    numbers = jnp.arange(targets * passages, dtype=jnp.int32)
-    hits = candidates[:, :, None] == numbers[None, None, :]
-    return jnp.sum(jnp.where(hits, known[:, None, :], 0.0), axis=2)
+    return pick(candidates, returned, passages)
 
 
 def solution(mesh):

time: 47.6 us -> 40.3 us (0.85)
  local copies, waits for them, and re-layouts: 9.47 us -> 4.29 us
  other arithmetic: 2.13 us -> 0 us
    unnamed x14 -> x4, local copies, waits for them, and re-layouts: 7.52 us -> 2.92 us
    reduce_sum x1 -> x0, other arithmetic: 1.46 us -> none  [body(): return jnp.sum(jnp.where(hits, known[:, None, :], 0.0), axis=2)]
    pallas_call x0 -> x1, Pallas kernels: none -> 1.38 us  [pick(): pl.pallas_call(functools.partial(pick_kernel, passages), out_shape=jax.Sh...]
    pallas_call x1, Pallas kernels: 5.74 us -> 4.39 us  [score_all(): pl.pallas_call(functools.partial(score_kernel, token_count, passages), ou...]
    all_to_all x1 -> x0, other arithmetic: 0.67 us -> none  [body(): lax.all_to_all(scores.reshape(targets, local_queries, passages), ('shard'...]
    all_to_all x1 -> x0, local copies, waits for them, and re-layouts: 0.51 us -> none  [body(): lax.all_to_all(scores.reshape(targets, local_queries, passages), ('shard'...]
    broadcast_in_dim x2 -> x1, local copies, waits for them, and re-layouts: 1.44 us -> 1.37 us  [body(): sent = jnp.broadcast_to(own_rows, (targets,) + own_rows.shape[1:])]
  transfers between devices with their start and end apart: 2 -> 2, of which waited for: 0 -> 0; matrix products, arithmetic and copies ran while one was open for 3% -> 3% of each run, Pallas kernels for 20% -> 24%
where the time goes in v4:
time: 40.3 us; the launch traced here: 39.5 us
  Pallas kernels  15.3 us (38%)
  blocking collectives  12.5 us (31%)
  starting transfers between devices  7.47 us (19%)
  local copies, waits for them, and re-layouts  4.29 us (11%)
    all_to_all x1, blocking collectives, body(): lax.all_to_all(scores.reshape(targets, local_queries * passages), ('shard...  12.5 us
    pallas_call x1, Pallas kernels, decode_all(): pl.pallas_call(decode_kernel, out_shape=(jax.ShapeDtypeStruct((most * CHU...  9.49 us
    all_to_all x1, starting transfers between devices, body(): lax.all_to_all(sent, ('shard', 'sub'), split_axis=0, concat_axis=0, tiled...  7.02 us
    pallas_call x1, Pallas kernels, score_all(): pl.pallas_call(functools.partial(score_kernel, token_count, passages), ou...  4.39 us
    unnamed x4, local copies, waits for them, and re-layouts  2.92 us
    pallas_call x1, Pallas kernels, pick(): pl.pallas_call(functools.partial(pick_kernel, passages), out_shape=jax.Sh...  1.38 us
    broadcast_in_dim x1, local copies, waits for them, and re-layouts, body(): sent = jnp.broadcast_to(own_rows, (targets,) + own_rows.shape[1:])  1.37 us
  transfers between devices with their start and end apart: 2, of which 0 were waited for; matrix products, arithmetic and copies ran while one was open for 3% of the time, Pallas kernels for 24%

profile of v4, /device:TPU:0, one launch (start us, length us, event | category | flops | bytes accessed | tf_op | source)
XLA Modules:
  0.0 39.5 jit_solution(13722724606916232128)
XLA Ops:
  0.0 0.5 %collective-permute-start = (bf16[8192,128]{1,0:T(8,128)(2,1)}, bf16[8192,128]{1,0:T(8,128)(2,1)S(1)}, u32[]{:S(2)}, u32[]{:S(2)}) collective-permute-start(bf16[8192,128]{1,0:T(8,128)(2,1)} %own_ref.1), channel_id=1, source_target_pairs={{0,1},{1,0},{2,3},{3,2},{4,5},{5,4},{6,7},{7,6},{8,9},{9,8},{10,11... | collective-permute-start | bytes 6291464 | tf_op jit(solution)/shard_map/ppermute | solution.py:246
  0.5 1.4 %broadcast_in_dim.8 = bf16[16,32,128]{2,1,0:T(8,128)(2,1)} broadcast(bf16[32,128]{1,0:T(8,128)(2,1)} %bitcast.14), dimensions={1,2} | broadcast | bytes 139264 | tf_op jit(solution)/shard_map/broadcast_in_dim | solution.py:248
  1.8 7.0 %all-to-all-start = ((bf16[16,32,128]{2,1,0:T(8,128)(2,1)}), bf16[16,32,128]{2,1,0:T(8,128)(2,1)S(1)}, u32[]{:S(2)}, u32[]{:S(2)}) async-start(bf16[16,32,128]{2,1,0:T(8,128)(2,1)} %broadcast_in_dim.8), calls=%async_computation | async-start | bytes 262144 | tf_op jit(solution)/shard_map/all_to_all | solution.py:249
  8.8 0.0 collective-permute-done.other_ref
  8.9 0.0 copy-start
  8.9 1.3 %copy-done = bf16[8192,128]{1,0:T(8,128)(2,1)} copy-done((bf16[8192,128]{1,0:T(8,128)(2,1)}, bf16[8192,128]{1,0:T(8,128)(2,1)S(1)}, u32[]{:S(2)}) %copy-start) | copy-done | bytes 2097176
  10.2 0.0 copy-start.1
  10.2 1.6 %copy-done.1 = bf16[8192,128]{1,0:T(8,128)(2,1)S(1)} copy-done((bf16[8192,128]{1,0:T(8,128)(2,1)S(1)}, bf16[8192,128]{1,0:T(8,128)(2,1)}, u32[]{:S(2)}) %copy-start.1) | copy-done | bytes 2097176
  11.8 9.5 %decode.1 = (bf16[9216,128]{1,0:T(8,128)(2,1)S(1)}, s32[289]{0:T(512)S(1)}) custom-call(s32[1]{0:T(128)} %bitcast.half_ref, s32[8192]{0:T(1024)} %bitcast.12, s32[64]{0:T(128)} %lengths_hbm.1, bf16[8192,128]{1,0:T(8,128)(2,1)} %own_ref.1, bf16[8192,128]{1,0:T(8,128)(2,1)S(1)} %copy-done.1, bf16[8192,128]{1,0:T(8,128)(2,1)} %bitcast.11), custom_call_target="tpu_custom_call" | custom-call | flops 10000000 | bytes 40000000 | tf_op jit(solution)/shard_map/decode/pallas_call | solution.py:123
  21.3 0.0 all-to-all-done
  21.3 4.4 %score.1 = f32[16,64]{1,0:T(8,128)S(1)} custom-call(s32[289]{0:T(512)S(1)} %get-tuple-element.7.owner_ref, bf16[512,128]{1,0:T(8,128)(2,1)S(1)} %bitcast.9, bf16[9216,128]{1,0:T(8,128)(2,1)S(1)} %get-tuple-element.8.embedded), custom_call_target="tpu_custom_call" | custom-call | tf_op jit(solution)/shard_map/score/pallas_call | solution.py:198
  25.7 12.5 %all_to_all.16 = f32[16,1,64]{2,1,0:T(1,128)} all-to-all(f32[16,1,64]{2,1,0:T(1,128)S(1)} %bitcast.10), channel_id=1, replica_groups=mesh['groups'=2,'shard'=8,'sub'=2] {'shard','sub'}, dimensions={0} | all-to-all | bytes 8192 | tf_op jit(solution)/shard_map/all_to_all | solution.py:253
  38.2 1.4 %pick.1 = f32[1,62]{1,0:T(1,128)} custom-call(s32[1,62]{1,0:T(1,128)} %candidates_ref.1, f32[16,64]{1,0:T(8,128)} %bitcast.13), custom_call_target="tpu_custom_call" | custom-call | tf_op jit(solution)/shard_map/pick/pallas_call | solution.py:232
Async XLA Ops:
  0.0 8.9 %collective-permute-start = (bf16[8192,128]{1,0:T(8,128)(2,1)}, bf16[8192,128]{1,0:T(8,128)(2,1)S(1)}, u32[]{:S(2)}, u32[]{:S(2)}) collective-permute-start(bf16[8192,128]{1,0:T(8,128)(2,1)} %own_ref.1), channel_id=1, source_target_pairs={{0,1},{1,0},{2,3},{3,2},{4,5},{5,4},{6,7},{7,6},{8,9},{9,8},{10,11... | collective-permute-start | bytes 6291464 | tf_op jit(solution)/shard_map/ppermute | solution.py:246
  1.8 19.5 %all-to-all-start = ((bf16[16,32,128]{2,1,0:T(8,128)(2,1)}), bf16[16,32,128]{2,1,0:T(8,128)(2,1)S(1)}, u32[]{:S(2)}, u32[]{:S(2)}) async-start(bf16[16,32,128]{2,1,0:T(8,128)(2,1)} %broadcast_in_dim.8), calls=%async_computation | async-start | bytes 262144 | tf_op jit(solution)/shard_map/all_to_all | solution.py:249
  8.9 1.3 %copy-start = (bf16[8192,128]{1,0:T(8,128)(2,1)}, bf16[8192,128]{1,0:T(8,128)(2,1)S(1)}, u32[]{:S(2)}) copy-start(bf16[8192,128]{1,0:T(8,128)(2,1)S(1)} %collective-permute-done.other_ref) | copy-start | bytes 6291460
  10.2 1.6 %copy-start.1 = (bf16[8192,128]{1,0:T(8,128)(2,1)S(1)}, bf16[8192,128]{1,0:T(8,128)(2,1)}, u32[]{:S(2)}) copy-start(bf16[8192,128]{1,0:T(8,128)(2,1)} %copy-done) | copy-start | bytes 6291460

commit v5 on v4

--- a/solution.py
+++ b/solution.py
@@ -7,9 +7,9 @@
 from jax.experimental.pallas import tpu as pltpu
 from jax.sharding import PartitionSpec as P
 
-CHUNK = 32
-GROUP = 8
-SCORE_GROUP = 16
+CHUNK = 16
+GROUP = 16
+SCORE_GROUP = 32
 QUERY_BLOCK = 512
 SMEM = pl.BlockSpec(memory_space=pltpu.SMEM)
 VMEM = pl.BlockSpec(memory_space=pltpu.VMEM)
@@ -60,18 +60,18 @@
         for k in range(slots // CHUNK):
             at_ref[chunks + k] = p * slots + k * CHUNK
             live_ref[chunks + k] = length - k * CHUNK
-            owner_ref[chunks + k] = p
+            owner_ref[chunks + k] = 2 * p + (1 if k == 0 else 0)
         return chunks + (length + CHUNK - 1) // CHUNK
 
     chunks = lax.fori_loop(0, passages, listing, 0)
     for k in range(SCORE_GROUP):
         at_ref[chunks + k] = 0
         live_ref[chunks + k] = CHUNK
-        owner_ref[chunks + k] = passages
+        owner_ref[chunks + k] = 2 * passages + 1
     groups = (chunks + GROUP - 1) // GROUP
     owner_ref[owner_ref.shape[0] - 1] = chunks
 
-    step = 256
+    step = min(1024, half_rows)
 
     def widen(source, base):
         def body(i, carry):
@@ -92,24 +92,36 @@
     slot_numbers = lax.broadcasted_iota(jnp.int32, (CHUNK, width), 0)
     single = table.reshape(2 * half_rows, 1, width)
 
+    def fetch(g, k):
+        at = at_ref[g * GROUP + k]
+        for j in range(CHUNK):
+            rows[pl.ds(k * CHUNK + j, 1), :] = single[codes_ref[at + j]]
+
+    def finish(g, k):
+        i = g * GROUP + k
+        at = pl.ds(pl.multiple_of(at_ref[i], CHUNK), CHUNK)
+        vectors = rows[pl.ds(k * CHUNK, CHUNK), :] + residual_rows[at, :].astype(jnp.float32)
+        vectors = jnp.where(slot_numbers < live_ref[i], vectors, vectors[0:1, :])
+        return normalized(vectors)
+
+    def keep(g, done):
+        for k in range(GROUP):
+            start = pl.multiple_of((g * GROUP + k) * CHUNK, CHUNK)
+            embedded[pl.ds(start, CHUNK), :] = done[k]
+
+    for k in range(GROUP):
+        fetch(0, k)
+
     def decode(g, carry):
-        before = jnp.maximum(g - 1, 0)
         done = []
         for k in range(GROUP):
-            i = before * GROUP + k
-            own = pl.ds(pl.multiple_of(at_ref[i], CHUNK), CHUNK)
-            vectors = rows[pl.ds(k * CHUNK, CHUNK), :] + residual_rows[own, :].astype(jnp.float32)
-            vectors = jnp.where(slot_numbers < live_ref[i], vectors, vectors[0:1, :])
-            done.append(normalized(vectors))
-            at = at_ref[g * GROUP + k]
-            for j in range(CHUNK):
-                rows[pl.ds(k * CHUNK + j, 1), :] = single[codes_ref[at + j]]
-        for k in range(GROUP):
-            start = pl.multiple_of((before * GROUP + k) * CHUNK, CHUNK)
-            embedded[pl.ds(start, CHUNK), :] = done[k]
+            done.append(finish(g - 1, k))
+            fetch(g, k)
+        keep(g - 1, done)
         return carry
 
-    lax.fori_loop(0, groups + 1, decode, 0)
+    lax.fori_loop(1, groups, decode, 0)
+    keep(groups - 1, [finish(groups - 1, k) for k in range(GROUP)])
 
 
 def pinned(array):
@@ -139,7 +151,7 @@
             pltpu.VMEM((GROUP * CHUNK, width), jnp.float32),
             pltpu.SemaphoreType.DMA((4,)),
         ],
-        compiler_params=pltpu.CompilerParams(vmem_limit_bytes=40 * 1024 * 1024),
+        compiler_params=pltpu.CompilerParams(vmem_limit_bytes=24 * 1024 * 1024),
         cost_estimate=pl.CostEstimate(flops=10**7, bytes_accessed=40 * 10**6, transcendentals=0),
         name="decode",
     )(
@@ -147,7 +159,7 @@
         pinned(token_codes.reshape(passages * slots)),
         pinned(lengths),
         pinned(own),
-        other,
+        pltpu.with_memory_space_constraint(other, pltpu.VMEM),
         pinned(residuals.reshape(passages * slots, width)),
     )
 
@@ -161,31 +173,41 @@
     per_block = block // token_count
     owner = lax.broadcasted_iota(jnp.int32, (per_block, block), 0)
     token_of = lax.broadcasted_iota(jnp.int32, (per_block, block), 1) // token_count
-    summing = (owner == token_of).astype(jnp.float32)
+    summing = (owner == token_of).astype(jnp.bfloat16)
 
     def score_block(b, carry):
         at = pl.ds(pl.multiple_of(b * block, block), block)
         vectors = normalized(queries_ref[at, :].astype(jnp.float32))
         turned[...] = vectors.astype(jnp.float32).T.astype(jnp.bfloat16)
-        largest[...] = jnp.full(largest.shape, -jnp.inf, jnp.float32)
-
-        def score(g, inner):
+
+        def score(g, so_far):
             at = pl.ds(pl.multiple_of(g * SCORE_GROUP * CHUNK, SCORE_GROUP * CHUNK), SCORE_GROUP * CHUNK)
             similar = jnp.dot(embedded[at, :], turned[...], preferred_element_type=jnp.float32)
             parts = jnp.max(similar.reshape(SCORE_GROUP, CHUNK // 8, 8, block), axis=1)
             for k in range(SCORE_GROUP):
-                p = owner_ref[g * SCORE_GROUP + k]
-                largest[p] = jnp.maximum(largest[p], parts[k])
-            return inner
-
-        lax.fori_loop(0, groups, score, 0)
-        sums = lax.dot_general(
-            summing,
-            jnp.max(largest[0:passages], axis=1),
-            (((1,), (1,)), ((), ())),
-            precision=lax.Precision.HIGHEST,
-            preferred_element_type=jnp.float32,
-        )
+                mark = owner_ref[g * SCORE_GROUP + k]
+                first = lax.rem(mark, 2) == 1
+                so_far = jnp.where(first, parts[k], jnp.maximum(so_far, parts[k]))
+                at = pl.multiple_of(lax.shift_right_logical(mark, 1) * 8, 8)
+                for lane in range(block // 128):
+                    largest[lane, pl.ds(at, 8), :] = so_far[:, lane * 128 : (lane + 1) * 128]
+            return so_far
+
+        lax.fori_loop(0, groups, score, jnp.zeros((8, block), jnp.float32))
+        kept = []
+        for lane in range(block // 128):
+            best = largest[lane, pl.ds(0, passages, stride=8), :]
+            for k in range(1, 8):
+                best = jnp.maximum(best, largest[lane, pl.ds(k, passages, stride=8), :])
+            kept.append(best)
+        best = jnp.concatenate(kept, axis=1)
+        sums = jnp.zeros((per_block, passages), jnp.float32)
+        for _ in range(3):
+            part = best.astype(jnp.bfloat16)
+            best = best - part.astype(jnp.float32)
+            sums = sums + lax.dot_general(
+                summing, part, (((1,), (1,)), ((), ())), preferred_element_type=jnp.float32
+            )
         out_ref[pl.ds(pl.multiple_of(b * per_block, per_block), per_block), :] = sums
         return carry
 
@@ -202,7 +224,7 @@
         out_specs=VMEM,
         scratch_shapes=[
             pltpu.VMEM((width, block), jnp.bfloat16),
-            pltpu.VMEM((passages + 1, 8, block), jnp.float32),
+            pltpu.VMEM((block // 128, (passages + 1) * 8, 128), jnp.float32),
         ],
         compiler_params=pltpu.CompilerParams(vmem_limit_bytes=32 * 1024 * 1024),
         name="score",
@@ -216,14 +238,14 @@
     target_numbers = lax.broadcasted_iota(jnp.int32, (targets, count), 0)
     for q in range(local_queries):
         wanted = candidates_ref[q : q + 1, :]
-        target = wanted // passages
-        hits = (passage_numbers == wanted - target * passages).astype(jnp.float32)
-        picked = jnp.dot(
-            returned_ref[:, q * passages : (q + 1) * passages],
-            hits,
-            precision=lax.Precision.HIGHEST,
-            preferred_element_type=jnp.float32,
-        )
+        target = lax.div(wanted, passages)
+        hits = (passage_numbers == wanted - target * passages).astype(jnp.bfloat16)
+        left = returned_ref[:, q * passages : (q + 1) * passages]
+        picked = jnp.zeros((targets, count), jnp.float32)
+        for _ in range(3):
+            part = left.astype(jnp.bfloat16)
+            left = left - part.astype(jnp.float32)
+            picked = picked + jnp.dot(part, hits, preferred_element_type=jnp.float32)
         kept = jnp.where(target_numbers == target, picked, 0.0)
         out_ref[q : q + 1, :] = jnp.sum(kept, axis=0, keepdims=True)
 
@@ -235,7 +257,7 @@
         in_specs=[VMEM, VMEM],
         out_specs=VMEM,
         name="pick",
-    )(candidates, returned)
+    )(candidates, pltpu.with_memory_space_constraint(returned, pltpu.VMEM))
 
 
 def body(queries, candidates, token_codes, residuals, lengths, centroids):

time: 40.3 us -> 40 us (level); the launches traced: 39.5 us -> 39.7 us
    pallas_call x1, Pallas kernels: 9.49 us -> 10.2 us  [decode_all(): pl.pallas_call(decode_kernel, out_shape=(jax.ShapeDtypeStruct((most * CHU...]
  transfers between devices with their start and end apart: 2 -> 2, of which waited for: 0 -> 0; matrix products, arithmetic and copies ran while one was open for 3% -> 3% of each run, Pallas kernels for 24% -> 26%
where the time goes in v5:
time: 40 us; the launch traced here: 39.7 us
  Pallas kernels  15.6 us (39%)
  blocking collectives  12.2 us (30%)
  starting transfers between devices  7.47 us (19%)
  local copies, waits for them, and re-layouts  4.29 us (11%)
    all_to_all x1, blocking collectives, body(): lax.all_to_all(scores.reshape(targets, local_queries * passages), ('shard...  12.2 us
    pallas_call x1, Pallas kernels, decode_all(): pl.pallas_call(decode_kernel, out_shape=(jax.ShapeDtypeStruct((most * CHU...  10.2 us
    all_to_all x1, starting transfers between devices, body(): lax.all_to_all(sent, ('shard', 'sub'), split_axis=0, concat_axis=0, tiled...  7.02 us
    pallas_call x1, Pallas kernels, score_all(): pl.pallas_call(functools.partial(score_kernel, token_count, passages), ou...  4.16 us
    unnamed x4, local copies, waits for them, and re-layouts  2.92 us
    broadcast_in_dim x1, local copies, waits for them, and re-layouts, body(): sent = jnp.broadcast_to(own_rows, (targets,) + own_rows.shape[1:])  1.37 us
    pallas_call x1, Pallas kernels, pick(): pl.pallas_call(functools.partial(pick_kernel, passages), out_shape=jax.Sh...  1.31 us
  transfers between devices with their start and end apart: 2, of which 0 were waited for; matrix products, arithmetic and copies ran while one was open for 3% of the time, Pallas kernels for 26%

profile of v5, /device:TPU:0, one launch (start us, length us, event | category | flops | bytes accessed | tf_op | source)
XLA Modules:
  0.0 39.7 jit_solution(16357899649139758523)
XLA Ops:
  0.0 0.5 %collective-permute-start = (bf16[8192,128]{1,0:T(8,128)(2,1)}, bf16[8192,128]{1,0:T(8,128)(2,1)S(1)}, u32[]{:S(2)}, u32[]{:S(2)}) collective-permute-start(bf16[8192,128]{1,0:T(8,128)(2,1)} %own_ref.1), channel_id=1, source_target_pairs={{0,1},{1,0},{2,3},{3,2},{4,5},{5,4},{6,7},{7,6},{8,9},{9,8},{10,11... | collective-permute-start | bytes 6291464 | tf_op jit(solution)/shard_map/ppermute | solution.py:268
  0.5 1.4 %broadcast_in_dim.8 = bf16[16,32,128]{2,1,0:T(8,128)(2,1)} broadcast(bf16[32,128]{1,0:T(8,128)(2,1)} %bitcast.14), dimensions={1,2} | broadcast | bytes 139264 | tf_op jit(solution)/shard_map/broadcast_in_dim | solution.py:270
  1.8 7.0 %all-to-all-start = ((bf16[16,32,128]{2,1,0:T(8,128)(2,1)}), bf16[16,32,128]{2,1,0:T(8,128)(2,1)S(1)}, u32[]{:S(2)}, u32[]{:S(2)}) async-start(bf16[16,32,128]{2,1,0:T(8,128)(2,1)} %broadcast_in_dim.8), calls=%async_computation | async-start | bytes 262144 | tf_op jit(solution)/shard_map/all_to_all | solution.py:271
  8.8 0.0 collective-permute-done.other_ref
  8.9 0.0 copy-start
  8.9 1.3 %copy-done = bf16[8192,128]{1,0:T(8,128)(2,1)} copy-done((bf16[8192,128]{1,0:T(8,128)(2,1)}, bf16[8192,128]{1,0:T(8,128)(2,1)S(1)}, u32[]{:S(2)}) %copy-start) | copy-done | bytes 2097176
  10.2 0.0 copy-start.1
  10.2 1.6 %copy-done.1 = bf16[8192,128]{1,0:T(8,128)(2,1)S(1)} copy-done((bf16[8192,128]{1,0:T(8,128)(2,1)S(1)}, bf16[8192,128]{1,0:T(8,128)(2,1)}, u32[]{:S(2)}) %copy-start.1) | copy-done | bytes 2097176
  11.8 10.2 %decode.1 = (bf16[9216,128]{1,0:T(8,128)(2,1)S(1)}, s32[577]{0:T(1024)S(1)}) custom-call(s32[1]{0:T(128)} %bitcast.half_ref, s32[8192]{0:T(1024)} %bitcast.13, s32[64]{0:T(128)} %lengths_hbm.1, bf16[8192,128]{1,0:T(8,128)(2,1)} %own_ref.1, bf16[8192,128]{1,0:T(8,128)(2,1)S(1)} %copy-done.1, bf16[8192,128]{1,0:T(8,128)(2,1)} %bitcast.12), custom_call_target="tpu_custom_call" | custom-call | flops 10000000 | bytes 40000000 | tf_op jit(solution)/shard_map/decode/pallas_call | solution.py:135
  22.0 0.0 all-to-all-done
  22.0 4.2 %score.1 = f32[16,64]{1,0:T(8,128)S(1)} custom-call(s32[577]{0:T(1024)S(1)} %get-tuple-element.7.owner_ref, bf16[512,128]{1,0:T(8,128)(2,1)S(1)} %bitcast.9, bf16[9216,128]{1,0:T(8,128)(2,1)S(1)} %get-tuple-element.8.embedded), custom_call_target="tpu_custom_call" | custom-call | tf_op jit(solution)/shard_map/score/pallas_call | solution.py:220
  26.1 12.2 %all_to_all.16 = f32[16,1,64]{2,1,0:T(1,128)S(1)} all-to-all(f32[16,1,64]{2,1,0:T(1,128)S(1)} %bitcast.10), channel_id=1, replica_groups=mesh['groups'=2,'shard'=8,'sub'=2] {'shard','sub'}, dimensions={0} | all-to-all | bytes 8192 | tf_op jit(solution)/shard_map/all_to_all | solution.py:275
  38.4 1.3 %pick.1 = f32[1,62]{1,0:T(1,128)} custom-call(s32[1,62]{1,0:T(1,128)} %candidates_ref.1, f32[16,64]{1,0:T(8,128)S(1)} %bitcast.11), custom_call_target="tpu_custom_call" | custom-call | tf_op jit(solution)/shard_map/pick/pallas_call | solution.py:254
Async XLA Ops:
  0.0 8.9 %collective-permute-start = (bf16[8192,128]{1,0:T(8,128)(2,1)}, bf16[8192,128]{1,0:T(8,128)(2,1)S(1)}, u32[]{:S(2)}, u32[]{:S(2)}) collective-permute-start(bf16[8192,128]{1,0:T(8,128)(2,1)} %own_ref.1), channel_id=1, source_target_pairs={{0,1},{1,0},{2,3},{3,2},{4,5},{5,4},{6,7},{7,6},{8,9},{9,8},{10,11... | collective-permute-start | bytes 6291464 | tf_op jit(solution)/shard_map/ppermute | solution.py:268
  1.8 20.1 %all-to-all-start = ((bf16[16,32,128]{2,1,0:T(8,128)(2,1)}), bf16[16,32,128]{2,1,0:T(8,128)(2,1)S(1)}, u32[]{:S(2)}, u32[]{:S(2)}) async-start(bf16[16,32,128]{2,1,0:T(8,128)(2,1)} %broadcast_in_dim.8), calls=%async_computation | async-start | bytes 262144 | tf_op jit(solution)/shard_map/all_to_all | solution.py:271
  8.9 1.3 %copy-start = (bf16[8192,128]{1,0:T(8,128)(2,1)}, bf16[8192,128]{1,0:T(8,128)(2,1)S(1)}, u32[]{:S(2)}) copy-start(bf16[8192,128]{1,0:T(8,128)(2,1)S(1)} %collective-permute-done.other_ref) | copy-start | bytes 6291460
  10.2 1.6 %copy-start.1 = (bf16[8192,128]{1,0:T(8,128)(2,1)S(1)}, bf16[8192,128]{1,0:T(8,128)(2,1)}, u32[]{:S(2)}) copy-start(bf16[8192,128]{1,0:T(8,128)(2,1)} %copy-done) | copy-start | bytes 6291460

commit v6 on v5

--- a/solution.py
+++ b/solution.py
@@ -10,6 +10,7 @@
 CHUNK = 16
 GROUP = 16
 SCORE_GROUP = 32
+PIECES = 4
 QUERY_BLOCK = 512
 SMEM = pl.BlockSpec(memory_space=pltpu.SMEM)
 VMEM = pl.BlockSpec(memory_space=pltpu.VMEM)
@@ -19,6 +20,12 @@
 def normalized(vectors):
     total = jnp.sum(vectors * vectors, axis=-1, keepdims=True)
     return (vectors * lax.rsqrt(total + 1e-06)).astype(jnp.bfloat16)
+
+
+def quotient(number, divisor):
+    if divisor & (divisor - 1) == 0:
+        return lax.shift_right_logical(number, divisor.bit_length() - 1)
+    return lax.div(number, divisor)
 
 
 def decode_kernel(
@@ -29,11 +36,9 @@
     other_ref,
     residuals_ref,
     embedded,
-    owner_ref,
+    at_ref,
     codes_ref,
     lengths_ref,
-    at_ref,
-    live_ref,
     staged,
     table,
     residual_rows,
@@ -41,51 +46,44 @@
     sems,
 ):
     passages = lengths_ref.shape[0]
-    slots = codes_ref.shape[0] // passages
+    tokens = codes_ref.shape[0]
+    slots = tokens // passages
     half_rows, width = own_ref.shape
     half = half_ref[0]
-    lengths_copy = pltpu.make_async_copy(lengths_hbm, lengths_ref, sems.at[2])
-    codes_copy = pltpu.make_async_copy(codes_hbm, codes_ref, sems.at[3])
-    own_copy = pltpu.make_async_copy(own_ref, staged, sems.at[0])
-    residual_copy = pltpu.make_async_copy(residuals_ref, residual_rows, sems.at[1])
+    lengths_copy = pltpu.make_async_copy(lengths_hbm, lengths_ref, sems.at[0])
+    codes_copy = pltpu.make_async_copy(codes_hbm, codes_ref, sems.at[1])
+    residual_copy = pltpu.make_async_copy(residuals_ref, residual_rows, sems.at[2])
     lengths_copy.start()
     codes_copy.start()
-    own_copy.start()
+    piece = half_rows // PIECES
+    copies = []
+    for source, ref in enumerate((own_ref, other_ref)):
+        for k in range(PIECES):
+            at = pl.ds(k * piece, piece)
+            sem = sems.at[3 + source * PIECES + k]
+            copies.append(pltpu.make_async_copy(ref.at[at], staged.at[source, at], sem))
+            copies[-1].start()
     residual_copy.start()
 
     lengths_copy.wait()
 
     def listing(p, chunks):
-        length = lengths_ref[p]
         for k in range(slots // CHUNK):
             at_ref[chunks + k] = p * slots + k * CHUNK
-            live_ref[chunks + k] = length - k * CHUNK
-            owner_ref[chunks + k] = 2 * p + (1 if k == 0 else 0)
-        return chunks + (length + CHUNK - 1) // CHUNK
-
-    chunks = lax.fori_loop(0, passages, listing, 0)
+        return chunks + quotient(lengths_ref[p] + CHUNK - 1, CHUNK)
+
+    chunks = lax.fori_loop(0, passages, listing, 0, unroll=4)
     for k in range(SCORE_GROUP):
-        at_ref[chunks + k] = 0
-        live_ref[chunks + k] = CHUNK
-        owner_ref[chunks + k] = 2 * passages + 1
-    groups = (chunks + GROUP - 1) // GROUP
-    owner_ref[owner_ref.shape[0] - 1] = chunks
-
-    step = min(1024, half_rows)
-
-    def widen(source, base):
-        def body(i, carry):
-            start = pl.multiple_of(i * step, step)
-            table[pl.ds(pl.multiple_of(base + start, step), step), :] = source[
-                pl.ds(start, step), :
-            ].astype(jnp.float32)
-            return carry
-
-        lax.fori_loop(0, half_rows // step, body, 0)
-
-    widen(other_ref, (1 - half) * half_rows)
-    own_copy.wait()
-    widen(staged, half * half_rows)
+        at_ref[chunks + k] = tokens
+    groups = quotient(chunks + GROUP - 1, GROUP)
+    at_ref[at_ref.shape[0] - 1] = chunks
+
+    for source in range(2):
+        base = (half if source == 0 else 1 - half) * half_rows
+        for k in range(PIECES):
+            copies[source * PIECES + k].wait()
+            to = pl.ds(pl.multiple_of(base + k * piece, piece), piece)
+            table[to, :] = staged[source, pl.ds(k * piece, piece), :].astype(jnp.float32)
     codes_copy.wait()
     residual_copy.wait()
 
@@ -93,15 +91,17 @@
     single = table.reshape(2 * half_rows, 1, width)
 
     def fetch(g, k):
-        at = at_ref[g * GROUP + k]
+        at = jnp.minimum(at_ref[g * GROUP + k], tokens - CHUNK)
         for j in range(CHUNK):
             rows[pl.ds(k * CHUNK + j, 1), :] = single[codes_ref[at + j]]
 
     def finish(g, k):
-        i = g * GROUP + k
-        at = pl.ds(pl.multiple_of(at_ref[i], CHUNK), CHUNK)
-        vectors = rows[pl.ds(k * CHUNK, CHUNK), :] + residual_rows[at, :].astype(jnp.float32)
-        vectors = jnp.where(slot_numbers < live_ref[i], vectors, vectors[0:1, :])
+        at = jnp.minimum(at_ref[g * GROUP + k], tokens - CHUNK)
+        p = quotient(at, slots)
+        live = lengths_ref[p] - (at - p * slots)
+        near = residual_rows[pl.ds(pl.multiple_of(at, CHUNK), CHUNK), :]
+        vectors = rows[pl.ds(k * CHUNK, CHUNK), :] + near.astype(jnp.float32)
+        vectors = jnp.where(slot_numbers < live, vectors, vectors[0:1, :])
         return normalized(vectors)
 
     def keep(g, done):
@@ -138,18 +138,16 @@
             jax.ShapeDtypeStruct((most * CHUNK, width), jnp.bfloat16),
             jax.ShapeDtypeStruct((most + 1,), jnp.int32),
         ),
-        in_specs=[SMEM, HBM, HBM, HBM, VMEM, HBM],
+        in_specs=[SMEM, HBM, HBM, HBM, HBM, HBM],
         out_specs=(VMEM, SMEM),
         scratch_shapes=[
             pltpu.SMEM((passages * slots,), jnp.int32),
             pltpu.SMEM((passages,), jnp.int32),
-            pltpu.SMEM((most,), jnp.int32),
-            pltpu.SMEM((most,), jnp.int32),
-            pltpu.VMEM((half_rows, width), jnp.bfloat16),
+            pltpu.VMEM((2, half_rows, width), jnp.bfloat16),
             pltpu.VMEM((2 * half_rows, width), jnp.float32),
             pltpu.VMEM((passages * slots, width), jnp.bfloat16),
             pltpu.VMEM((GROUP * CHUNK, width), jnp.float32),
-            pltpu.SemaphoreType.DMA((4,)),
+            pltpu.SemaphoreType.DMA((3 + 2 * PIECES,)),
         ],
         compiler_params=pltpu.CompilerParams(vmem_limit_bytes=24 * 1024 * 1024),
         cost_estimate=pl.CostEstimate(flops=10**7, bytes_accessed=40 * 10**6, transcendentals=0),
@@ -159,17 +157,17 @@
         pinned(token_codes.reshape(passages * slots)),
         pinned(lengths),
         pinned(own),
-        pltpu.with_memory_space_constraint(other, pltpu.VMEM),
+        pinned(other),
         pinned(residuals.reshape(passages * slots, width)),
     )
 
 
-def score_kernel(token_count, passages, owner_ref, queries_ref, embedded, out_ref, turned, largest):
+def score_kernel(token_count, slots, at_ref, queries_ref, embedded, out_ref, turned, largest):
+    passages = out_ref.shape[1]
     query_tokens = queries_ref.shape[0]
     block = min(QUERY_BLOCK, query_tokens)
     blocks = query_tokens // block
-    chunks = owner_ref[owner_ref.shape[0] - 1]
-    groups = (chunks + SCORE_GROUP - 1) // SCORE_GROUP
+    groups = quotient(at_ref[at_ref.shape[0] - 1] + SCORE_GROUP - 1, SCORE_GROUP)
     per_block = block // token_count
     owner = lax.broadcasted_iota(jnp.int32, (per_block, block), 0)
     token_of = lax.broadcasted_iota(jnp.int32, (per_block, block), 1) // token_count
@@ -181,14 +179,15 @@
         turned[...] = vectors.astype(jnp.float32).T.astype(jnp.bfloat16)
 
         def score(g, so_far):
-            at = pl.ds(pl.multiple_of(g * SCORE_GROUP * CHUNK, SCORE_GROUP * CHUNK), SCORE_GROUP * CHUNK)
+            size = SCORE_GROUP * CHUNK
+            at = pl.ds(pl.multiple_of(g * size, size), size)
             similar = jnp.dot(embedded[at, :], turned[...], preferred_element_type=jnp.float32)
             parts = jnp.max(similar.reshape(SCORE_GROUP, CHUNK // 8, 8, block), axis=1)
             for k in range(SCORE_GROUP):
-                mark = owner_ref[g * SCORE_GROUP + k]
-                first = lax.rem(mark, 2) == 1
-                so_far = jnp.where(first, parts[k], jnp.maximum(so_far, parts[k]))
-                at = pl.multiple_of(lax.shift_right_logical(mark, 1) * 8, 8)
+                start = at_ref[g * SCORE_GROUP + k]
+                p = quotient(start, slots)
+                so_far = jnp.where(start == p * slots, parts[k], jnp.maximum(so_far, parts[k]))
+                at = pl.multiple_of(p * 8, 8)
                 for lane in range(block // 128):
                     largest[lane, pl.ds(at, 8), :] = so_far[:, lane * 128 : (lane + 1) * 128]
             return so_far
@@ -214,11 +213,11 @@
     lax.fori_loop(0, blocks, score_block, 0)
 
 
-def score_all(owner, query_rows, embedded, passages, token_count):
+def score_all(starts, query_rows, embedded, passages, slots, token_count):
     query_tokens, width = query_rows.shape
     block = min(QUERY_BLOCK, query_tokens)
     return pl.pallas_call(
-        functools.partial(score_kernel, token_count, passages),
+        functools.partial(score_kernel, token_count, slots),
         out_shape=jax.ShapeDtypeStruct((query_tokens // token_count, passages), jnp.float32),
         in_specs=[SMEM, VMEM, VMEM],
         out_specs=VMEM,
@@ -228,7 +227,7 @@
         ],
         compiler_params=pltpu.CompilerParams(vmem_limit_bytes=32 * 1024 * 1024),
         name="score",
-    )(owner, query_rows, embedded)
+    )(starts, query_rows, embedded)
 
 
 def pick_kernel(passages, candidates_ref, returned_ref, out_ref):
@@ -238,7 +237,7 @@
     target_numbers = lax.broadcasted_iota(jnp.int32, (targets, count), 0)
     for q in range(local_queries):
         wanted = candidates_ref[q : q + 1, :]
-        target = lax.div(wanted, passages)
+        target = quotient(wanted, passages)
         hits = (passage_numbers == wanted - target * passages).astype(jnp.bfloat16)
         left = returned_ref[:, q * passages : (q + 1) * passages]
         picked = jnp.zeros((targets, count), jnp.float32)
@@ -256,6 +255,7 @@
         out_shape=jax.ShapeDtypeStruct(candidates.shape, jnp.float32),
         in_specs=[VMEM, VMEM],
         out_specs=VMEM,
+        compiler_params=pltpu.CompilerParams(vmem_limit_bytes=4 * 1024 * 1024),
         name="pick",
     )(candidates, pltpu.with_memory_space_constraint(returned, pltpu.VMEM))
 
@@ -263,15 +263,15 @@
 def body(queries, candidates, token_codes, residuals, lengths, centroids):
     local_queries, token_count, width = queries.shape
     targets = lax.axis_size("shard") * lax.axis_size("sub")
-    passages = token_codes.shape[0]
+    passages, slots = token_codes.shape
     half = lax.axis_index("sub").astype(jnp.int32)
     other = lax.ppermute(centroids, "sub", [(0, 1), (1, 0)])
     own_rows = queries.reshape(1, local_queries * token_count, width)
     sent = jnp.broadcast_to(own_rows, (targets,) + own_rows.shape[1:])
     gathered = lax.all_to_all(sent, ("shard", "sub"), split_axis=0, concat_axis=0, tiled=True)
     query_rows = gathered.reshape(targets * local_queries * token_count, width)
-    embedded, owner = decode_all(half.reshape(1), token_codes, lengths, centroids, other, residuals)
-    scores = score_all(owner, query_rows, embedded, passages, token_count)
+    embedded, starts = decode_all(half.reshape(1), token_codes, lengths, centroids, other, residuals)
+    scores = score_all(starts, query_rows, embedded, passages, slots, token_count)
     returned = lax.all_to_all(
         scores.reshape(targets, local_queries * passages),
         ("shard", "sub"),

time: 40 us -> 37.8 us (0.945); the launches traced: 39.7 us -> 37.9 us
  local copies, waits for them, and re-layouts: 4.29 us -> 2.7 us
  Pallas kernels: 15.6 us -> 14.5 us
  blocking collectives: 12.2 us -> 13.2 us
    unnamed x4, local copies, waits for them, and re-layouts: 2.92 us -> 1.34 us
    all_to_all x1, blocking collectives: 12.2 us -> 13.2 us  [body(): lax.all_to_all(scores.reshape(targets, local_queries * passages), ('shard...]
    pallas_call x1, Pallas kernels: 1.31 us -> 0.66 us  [pick(): pl.pallas_call(functools.partial(pick_kernel, passages), out_shape=jax.Sh...]
  transfers between devices with their start and end apart: 2 -> 2, of which waited for: 0 -> 0; matrix products, arithmetic and copies ran while one was open for 3% -> 4% of each run, Pallas kernels for 26% -> 26%
where the time goes in v6:
time: 37.8 us; the launch traced here: 37.9 us
  Pallas kernels  14.5 us (38%)
  blocking collectives  13.2 us (35%)
  starting transfers between devices  7.47 us (20%)
  local copies, waits for them, and re-layouts  2.7 us (7%)
    all_to_all x1, blocking collectives, body(): lax.all_to_all(scores.reshape(targets, local_queries * passages), ('shard...  13.2 us
    pallas_call x1, Pallas kernels, decode_all(): pl.pallas_call(decode_kernel, out_shape=(jax.ShapeDtypeStruct((most * CHU...  9.93 us
    all_to_all x1, starting transfers between devices, body(): lax.all_to_all(sent, ('shard', 'sub'), split_axis=0, concat_axis=0, tiled...  7.02 us
    pallas_call x1, Pallas kernels, score_all(): pl.pallas_call(functools.partial(score_kernel, token_count, slots), out_s...  3.88 us
    broadcast_in_dim x1, local copies, waits for them, and re-layouts, body(): sent = jnp.broadcast_to(own_rows, (targets,) + own_rows.shape[1:])  1.37 us
    unnamed x4, local copies, waits for them, and re-layouts  1.34 us
  transfers between devices with their start and end apart: 2, of which 0 were waited for; matrix products, arithmetic and copies ran while one was open for 4% of the time, Pallas kernels for 26%

profile of v6, /device:TPU:0, one launch (start us, length us, event | category | flops | bytes accessed | tf_op | source)
XLA Modules:
  0.0 37.9 jit_solution(2301475997314241202)
XLA Ops:
  0.0 0.5 %collective-permute-start = (bf16[8192,128]{1,0:T(8,128)(2,1)}, bf16[8192,128]{1,0:T(8,128)(2,1)S(1)}, u32[]{:S(2)}, u32[]{:S(2)}) collective-permute-start(bf16[8192,128]{1,0:T(8,128)(2,1)} %own_ref.1), channel_id=1, source_target_pairs={{0,1},{1,0},{2,3},{3,2},{4,5},{5,4},{6,7},{7,6},{8,9},{9,8},{10,11... | collective-permute-start | bytes 6291464 | tf_op jit(solution)/shard_map/ppermute | solution.py:268
  0.5 1.4 %broadcast_in_dim.8 = bf16[16,32,128]{2,1,0:T(8,128)(2,1)} broadcast(bf16[32,128]{1,0:T(8,128)(2,1)} %bitcast.14), dimensions={1,2} | broadcast | bytes 139264 | tf_op jit(solution)/shard_map/broadcast_in_dim | solution.py:270
  1.8 7.0 %all-to-all-start = ((bf16[16,32,128]{2,1,0:T(8,128)(2,1)}), bf16[16,32,128]{2,1,0:T(8,128)(2,1)S(1)}, u32[]{:S(2)}, u32[]{:S(2)}) async-start(bf16[16,32,128]{2,1,0:T(8,128)(2,1)} %broadcast_in_dim.8), calls=%async_computation | async-start | bytes 262144 | tf_op jit(solution)/shard_map/all_to_all | solution.py:271
  8.8 0.0 collective-permute-done.other_ref
  8.9 0.0 copy-start.1
  8.9 1.3 %copy-done.1 = bf16[8192,128]{1,0:T(8,128)(2,1)} copy-done((bf16[8192,128]{1,0:T(8,128)(2,1)}, bf16[8192,128]{1,0:T(8,128)(2,1)S(1)}, u32[]{:S(2)}) %copy-start.1) | copy-done | bytes 2097176
  10.2 9.9 %decode.1 = (bf16[9216,128]{1,0:T(8,128)(2,1)S(1)}, s32[577]{0:T(1024)S(1)}) custom-call(s32[1]{0:T(128)} %bitcast.half_ref, s32[8192]{0:T(1024)} %bitcast.13, s32[64]{0:T(128)} %lengths_hbm.1, bf16[8192,128]{1,0:T(8,128)(2,1)} %own_ref.1, bf16[8192,128]{1,0:T(8,128)(2,1)} %copy-done.1, bf16[8192,128]{1,0:T(8,128)(2,1)} %bitcast.12), custom_call_target="tpu_custom_call" | custom-call | flops 10000000 | bytes 40000000 | tf_op jit(solution)/shard_map/decode/pallas_call | solution.py:135
  20.1 0.0 copy-start
  20.1 0.0 all-to-all-done
  20.2 3.9 %score.1 = f32[16,64]{1,0:T(8,128)S(1)} custom-call(s32[577]{0:T(1024)S(1)} %get-tuple-element.7.at_ref, bf16[512,128]{1,0:T(8,128)(2,1)S(1)} %bitcast.9, bf16[9216,128]{1,0:T(8,128)(2,1)S(1)} %get-tuple-element.8.embedded), custom_call_target="tpu_custom_call" | custom-call | tf_op jit(solution)/shard_map/score/pallas_call | solution.py:219
  24.0 13.2 %all_to_all.16 = f32[16,1,64]{2,1,0:T(1,128)S(1)} all-to-all(f32[16,1,64]{2,1,0:T(1,128)S(1)} %bitcast.10), channel_id=1, replica_groups=mesh['groups'=2,'shard'=8,'sub'=2] {'shard','sub'}, dimensions={0} | all-to-all | bytes 8192 | tf_op jit(solution)/shard_map/all_to_all | solution.py:275
  37.2 0.0 copy-done
  37.2 0.7 %pick.1 = f32[1,62]{1,0:T(1,128)} custom-call(s32[1,62]{1,0:T(1,128)S(1)} %copy-done, f32[16,64]{1,0:T(8,128)S(1)} %bitcast.11), custom_call_target="tpu_custom_call" | custom-call | tf_op jit(solution)/shard_map/pick/pallas_call | solution.py:253
Async XLA Ops:
  0.0 8.9 %collective-permute-start = (bf16[8192,128]{1,0:T(8,128)(2,1)}, bf16[8192,128]{1,0:T(8,128)(2,1)S(1)}, u32[]{:S(2)}, u32[]{:S(2)}) collective-permute-start(bf16[8192,128]{1,0:T(8,128)(2,1)} %own_ref.1), channel_id=1, source_target_pairs={{0,1},{1,0},{2,3},{3,2},{4,5},{5,4},{6,7},{7,6},{8,9},{9,8},{10,11... | collective-permute-start | bytes 6291464 | tf_op jit(solution)/shard_map/ppermute | solution.py:268
  1.8 18.3 %all-to-all-start = ((bf16[16,32,128]{2,1,0:T(8,128)(2,1)}), bf16[16,32,128]{2,1,0:T(8,128)(2,1)S(1)}, u32[]{:S(2)}, u32[]{:S(2)}) async-start(bf16[16,32,128]{2,1,0:T(8,128)(2,1)} %broadcast_in_dim.8), calls=%async_computation | async-start | bytes 262144 | tf_op jit(solution)/shard_map/all_to_all | solution.py:271
  8.9 1.3 %copy-start.1 = (bf16[8192,128]{1,0:T(8,128)(2,1)}, bf16[8192,128]{1,0:T(8,128)(2,1)S(1)}, u32[]{:S(2)}) copy-start(bf16[8192,128]{1,0:T(8,128)(2,1)S(1)} %collective-permute-done.other_ref) | copy-start | bytes 6291460
  20.1 17.1 %copy-start = (s32[1,62]{1,0:T(1,128)S(1)}, s32[1,62]{1,0:T(1,128)}, u32[]{:S(2)}) copy-start(s32[1,62]{1,0:T(1,128)} %candidates_ref.1) | copy-start | bytes 748

commit v7 on v6

v7 whole, which is shorter than its diff:
```python
import functools

import jax
import jax.numpy as jnp
from jax import lax
from jax.experimental import pallas as pl
from jax.experimental.pallas import tpu as pltpu
from jax.sharding import PartitionSpec as P

CHUNK = 16
GROUP = 16
PIECES = 4
QUERY_BLOCK = 512
DIGIT = 128
NOBODY = 255.0
SMEM = pl.BlockSpec(memory_space=pltpu.SMEM)
VMEM = pl.BlockSpec(memory_space=pltpu.VMEM)
HBM = pl.BlockSpec(memory_space=pltpu.HBM)


def pinned(array, space=pltpu.HBM):
    return pltpu.with_memory_space_constraint(array, space)


def granted(mebibytes):
    return pltpu.CompilerParams(vmem_limit_bytes=mebibytes * 1024 * 1024)


def quotient(number, divisor):
    if divisor & (divisor - 1) == 0:
        return lax.shift_right_logical(number, divisor.bit_length() - 1)
    return lax.div(number, divisor)


def normalized(vectors):
    total = jnp.sum(vectors * vectors, axis=-1, keepdims=True)
    return (vectors * lax.rsqrt(total + 1e-06)).astype(jnp.bfloat16)


def id_rows_of(local_queries, count):
    rows = local_queries * -(-count // 128)
    return -(-rows // 8) * 8


def spread_kernel(queries_ref, candidates_ref, out_ref, digits):
    targets = out_ref.shape[0]
    query_rows = queries_ref.shape[0]
    local_queries, count = candidates_ref.shape
    id_rows = digits.shape[0] // 2
    digits[...] = jnp.full(digits.shape, NOBODY, jnp.float32)
    row = 0
    for q in range(local_queries):
        for start in range(0, count, 128):
            size = min(128, count - start)
            ids = candidates_ref[q : q + 1, start : start + size]
            high = quotient(ids, DIGIT)
            digits[row : row + 1, 0:size] = (ids - high * DIGIT).astype(jnp.float32)
            digits[id_rows + row : id_rows + row + 1, 0:size] = high.astype(jnp.float32)
            row += 1
    queries = queries_ref[...]
    coded = digits[...].astype(jnp.bfloat16)

    def copy(t, carry):
        out_ref[t, 0:query_rows, :] = queries
        out_ref[t, query_rows:, :] = coded
        return carry

    lax.fori_loop(0, targets, copy, 0)


def spread(queries, candidates, targets):
    query_rows, width = queries.shape
    id_rows = id_rows_of(*candidates.shape)
    return pl.pallas_call(
        spread_kernel,
        out_shape=jax.ShapeDtypeStruct((targets, query_rows + 2 * id_rows, width), jnp.bfloat16),
        in_specs=[VMEM, VMEM],
        out_specs=VMEM,
        scratch_shapes=[pltpu.VMEM((2 * id_rows, width), jnp.float32)],
        compiler_params=granted(16),
        name="spread",
    )(pinned(queries), pinned(candidates))


def widen_kernel(half_ref, own_ref, other_ref, table, staged, sems):
    half_rows = own_ref.shape[0]
    half = half_ref[0]
    piece = half_rows // PIECES
    copies = []
    for source, ref in enumerate((own_ref, other_ref)):
        for k in range(PIECES):
            at = pl.ds(k * piece, piece)
            sem = sems.at[source * PIECES + k]
            copies.append(pltpu.make_async_copy(ref.at[at], staged.at[source, at], sem))
            copies[-1].start()
    for source in range(2):
        base = (half if source == 0 else 1 - half) * half_rows
        for k in range(PIECES):
            copies[source * PIECES + k].wait()
            to = pl.ds(pl.multiple_of(base + k * piece, piece), piece)
            table[to, :] = staged[source, pl.ds(k * piece, piece), :].astype(jnp.float32)


def widen(half, own, other):
    half_rows, width = own.shape
    return pl.pallas_call(
        widen_kernel,
        out_shape=pltpu.VMEM((2 * half_rows, width), jnp.float32),
        in_specs=[SMEM, HBM, HBM],
        out_specs=VMEM,
        scratch_shapes=[
            pltpu.VMEM((2, half_rows, width), jnp.bfloat16),
            pltpu.SemaphoreType.DMA((2 * PIECES,)),
        ],
        compiler_params=granted(16),
        cost_estimate=pl.CostEstimate(flops=10**7, bytes_accessed=10**7, transcendentals=0),
        name="widen",
    )(half, pinned(own), pinned(other))


def score_kernel(
    token_count,
    query_rows,
    base_ref,
    codes_hbm,
    lengths_hbm,
    gathered_ref,
    table,
    residuals_ref,
    out_ref,
    codes_ref,
    lengths_ref,
    at_ref,
    residual_rows,
    rows,
    embedded,
    turned,
    so_far,
    largest,
    sems,
):
    passages = lengths_ref.shape[0]
    tokens = codes_ref.shape[0]
    slots = tokens // passages
    targets, sent_rows, width = gathered_ref.shape
    id_rows = (sent_rows - query_rows) // 2
    blocks, _, block = turned.shape
    lengths_copy = pltpu.make_async_copy(lengths_hbm, lengths_ref, sems.at[0])
    codes_copy = pltpu.make_async_copy(codes_hbm, codes_ref, sems.at[1])
    residual_copy = pltpu.make_async_copy(residuals_ref, residual_rows, sems.at[2])
    lengths_copy.start()
    codes_copy.start()
    residual_copy.start()

    words = -(-passages // 32)
    shape = (id_rows, width)

    def collect(t, masks):
        low = gathered_ref[t, query_rows : query_rows + id_rows, :].astype(jnp.float32)
        high = gathered_ref[t, query_rows + id_rows :, :].astype(jnp.float32)
        local = (high * DIGIT + low).astype(jnp.int32) - base_ref[0]
        bits = lax.shift_left(jnp.ones(shape, jnp.int32), local & 31)
        word = lax.shift_right_arithmetic(local, 5)
        return tuple(mask | jnp.where(word == w, bits, 0) for w, mask in enumerate(masks))

    empty = tuple(jnp.zeros(shape, jnp.int32) for _ in range(words))
    masks = lax.fori_loop(0, targets, collect, empty, unroll=min(8, targets))
    joined = []
    for mask in masks:
        folded = mask[0:8]
        for k in range(8, id_rows, 8):
            folded = folded | mask[k : k + 8]
        for shift in (4, 2, 1):
            folded = folded | pltpu.roll(folded, shift, 0)
        for shift in (64, 32, 16, 8, 4, 2, 1):
            folded = folded | pltpu.roll(folded, shift, 1)
        joined.append(folded[0, 0])

    per_device = block // query_rows

    def turn(b, carry):
        vectors = gathered_ref[pl.ds(b * per_device, per_device), 0:query_rows, :]
        ready = normalized(vectors.reshape(block, width).astype(jnp.float32))
        turned[b] = ready.astype(jnp.float32).T.astype(jnp.bfloat16)
        largest[b] = jnp.zeros(largest.shape[1:], jnp.float32)
        return carry

    lax.fori_loop(0, blocks, turn, 0)

    lengths_copy.wait()
    chunks = jnp.int32(0)
    for w in range(words):

        def listing(k, listed):
            p = w * 32 + k
            for j in range(slots // CHUNK):
                at_ref[listed + j] = p * slots + j * CHUNK
            wanted = lax.shift_right_logical(joined[w], k) & 1
            return listed + wanted * quotient(lengths_ref[p] + CHUNK - 1, CHUNK)

        chunks = lax.fori_loop(0, min(32, passages - w * 32), listing, chunks, unroll=4)
    for k in range(GROUP):
        at_ref[chunks + k] = tokens
    groups = quotient(chunks + GROUP - 1, GROUP)
    codes_copy.wait()
    residual_copy.wait()

    slot_numbers = lax.broadcasted_iota(jnp.int32, (CHUNK, width), 0)
    single = table.reshape(table.shape[0], 1, width)

    def fetch(g, k):
        at = jnp.minimum(at_ref[g * GROUP + k], tokens - CHUNK)
        for j in range(CHUNK):
            rows[pl.ds(k * CHUNK + j, 1), :] = single[codes_ref[at + j]]

    def finish(g, k):
        at = jnp.minimum(at_ref[g * GROUP + k], tokens - CHUNK)
        p = quotient(at, slots)
        live = lengths_ref[p] - (at - p * slots)
        near = residual_rows[pl.ds(pl.multiple_of(at, CHUNK), CHUNK), :]
        vectors = rows[pl.ds(k * CHUNK, CHUNK), :] + near.astype(jnp.float32)
        vectors = jnp.where(slot_numbers < live, vectors, vectors[0:1, :])
        return normalized(vectors)

    def score(g, b):
        similar = jnp.dot(embedded[...], turned[b], preferred_element_type=jnp.float32)
        parts = jnp.max(similar.reshape(GROUP, CHUNK // 8, 8, block), axis=1)
        best = so_far[b]
        for k in range(GROUP):
            start = at_ref[g * GROUP + k]
            p = quotient(start, slots)
            best = jnp.where(start == p * slots, parts[k], jnp.maximum(best, parts[k]))
            at = pl.multiple_of(p * 8, 8)
            for lane in range(block // 128):
                largest[b, lane, pl.ds(at, 8), :] = best[:, lane * 128 : (lane + 1) * 128]
        so_far[b] = best

    def step(i, carry):
        scored = jnp.maximum(i - 2, 0)
        if blocks == 1:
            score(scored, 0)
        else:

            def score_block(b, inner):
                score(scored, b)
                return inner

            lax.fori_loop(0, blocks, score_block, 0)
        fetched = jnp.minimum(i, groups - 1)
        finished = jnp.maximum(jnp.minimum(i - 1, groups - 1), 0)
        done = []
        for k in range(GROUP):
            done.append(finish(finished, k))
            fetch(fetched, k)
        for k in range(GROUP):
            embedded[pl.ds(k * CHUNK, CHUNK), :] = done[k]
        return carry

    lax.fori_loop(0, jnp.where(groups > 0, groups + 2, 0), step, 0)

    per_block = block // token_count
    owner = lax.broadcasted_iota(jnp.int32, (per_block, block), 0)
    token_of = quotient(lax.broadcasted_iota(jnp.int32, (per_block, block), 1), token_count)
    summing = (owner == token_of).astype(jnp.bfloat16)

    def total(b, carry):
        kept = []
        for lane in range(block // 128):
            best = largest[b, lane, pl.ds(0, passages, stride=8), :]
            for k in range(1, 8):
                best = jnp.maximum(best, largest[b, lane, pl.ds(k, passages, stride=8), :])
            kept.append(best)
        left = jnp.concatenate(kept, axis=1)
        sums = jnp.zeros((per_block, passages), jnp.float32)
        for _ in range(3):
            part = left.astype(jnp.bfloat16)
            left = left - part.astype(jnp.float32)
            sums = sums + lax.dot_general(
                summing, part, (((1,), (1,)), ((), ())), preferred_element_type=jnp.float32
            )
        out_ref[pl.ds(pl.multiple_of(b * per_block, per_block), per_block), :] = sums
        return carry

    lax.fori_loop(0, blocks, total, 0)


def score_all(base, token_codes, lengths, gathered, table, residuals, query_rows, token_count):
    passages, slots, width = residuals.shape
    targets = gathered.shape[0]
    tokens = passages * slots
    block = min(QUERY_BLOCK, targets * query_rows)
    blocks = targets * query_rows // block
    return pl.pallas_call(
        functools.partial(score_kernel, token_count, query_rows),
        out_shape=jax.ShapeDtypeStruct(
            (targets * query_rows // token_count, passages), jnp.float32
        ),
        in_specs=[SMEM, HBM, HBM, VMEM, VMEM, HBM],
        out_specs=VMEM,
        scratch_shapes=[
            pltpu.SMEM((tokens,), jnp.int32),
            pltpu.SMEM((passages,), jnp.int32),
            pltpu.SMEM((tokens // CHUNK + slots // CHUNK + GROUP,), jnp.int32),
            pltpu.VMEM((tokens, width), jnp.bfloat16),
            pltpu.VMEM((GROUP * CHUNK, width), jnp.float32),
            pltpu.VMEM((GROUP * CHUNK, width), jnp.bfloat16),
            pltpu.VMEM((blocks, width, block), jnp.bfloat16),
            pltpu.VMEM((blocks, 8, block), jnp.float32),
            pltpu.VMEM((blocks, block // 128, (passages + 1) * 8, 128), jnp.float32),
            pltpu.SemaphoreType.DMA((3,)),
        ],
        compiler_params=granted(40),
        name="score",
    )(
        base,
        pinned(token_codes.reshape(tokens)),
        pinned(lengths),
        gathered,
        pinned(table, pltpu.VMEM),
        pinned(residuals.reshape(tokens, width)),
    )


def pick_kernel(passages, candidates_ref, returned_ref, out_ref):
    local_queries, count = candidates_ref.shape
    targets = returned_ref.shape[0]
    passage_numbers = lax.broadcasted_iota(jnp.int32, (passages, count), 0)
    target_numbers = lax.broadcasted_iota(jnp.int32, (targets, count), 0)
    for q in range(local_queries):
        wanted = candidates_ref[q : q + 1, :]
        target = quotient(wanted, passages)
        hits = (passage_numbers == wanted - target * passages).astype(jnp.bfloat16)
        left = returned_ref[:, q * passages : (q + 1) * passages]
        picked = jnp.zeros((targets, count), jnp.float32)
        for _ in range(3):
            part = left.astype(jnp.bfloat16)
            left = left - part.astype(jnp.float32)
            picked = picked + jnp.dot(part, hits, preferred_element_type=jnp.float32)
        kept = jnp.where(target_numbers == target, picked, 0.0)
        out_ref[q : q + 1, :] = jnp.sum(kept, axis=0, keepdims=True)


def pick(candidates, returned, passages):
    return pl.pallas_call(
        functools.partial(pick_kernel, passages),
        out_shape=jax.ShapeDtypeStruct(candidates.shape, jnp.float32),
        in_specs=[VMEM, VMEM],
        out_specs=VMEM,
        compiler_params=granted(8),
        name="pick",
    )(candidates, pinned(returned, pltpu.VMEM))


def body(queries, candidates, token_codes, residuals, lengths, centroids):
    local_queries, token_count, width = queries.shape
    targets = lax.axis_size("shard") * lax.axis_size("sub")
    passages = token_codes.shape[0]
    query_rows = local_queries * token_count
    half = lax.axis_index("sub").astype(jnp.int32)
    me = lax.axis_index("shard").astype(jnp.int32) * lax.axis_size("sub") + half
    other = lax.ppermute(centroids, "sub", [(0, 1), (1, 0)])
    sent = spread(queries.reshape(query_rows, width), candidates, targets)
    gathered = lax.all_to_all(sent, ("shard", "sub"), split_axis=0, concat_axis=0, tiled=True)
    table = widen(half.reshape(1), centroids, other)
    base = (me * passages).reshape(1)
    scores = score_all(
        base, token_codes, lengths, gathered, table, residuals, query_rows, token_count
    )
    returned = lax.all_to_all(
        scores.reshape(targets, local_queries * passages),
        ("shard", "sub"),
        split_axis=0,
        concat_axis=0,
        tiled=True,
    )
    return pick(candidates, returned, passages)


def solution(mesh):
    placed = (
        P(("groups", "shard", "sub"), None, None),
        P(("groups", "shard", "sub"), None),
        P(("groups", "shard", "sub"), None),
        P(("groups", "shard", "sub"), None, None),
        P(("groups", "shard", "sub")),
        P(("groups", "shard", "sub"), None),
    )
    return jax.shard_map(
        body,
        mesh=mesh,
        in_specs=placed,
        out_specs=P(("groups", "shard", "sub"), None),
        check_vma=False,
    )
```

time: 37.8 us -> 40 us (1.058)
  local copies, waits for them, and re-layouts: 2.7 us -> 7.95 us
  Pallas kernels: 14.5 us -> 11.7 us
  blocking collectives: 13.2 us -> 10.5 us
  waiting for transfers between devices: 0.01 us -> 2.11 us
    unnamed x4 -> x8, local copies, waits for them, and re-layouts: 1.34 us -> 7.95 us
    pallas_call x2 -> x3, Pallas kernels: 13.8 us -> 11 us  [the longest x1 7.26 us: score_all(): pl.pallas_call(functools.partial(score_kernel, token_count, query_rows),...]
    all_to_all x1, blocking collectives: 13.2 us -> 10.5 us  [body(): lax.all_to_all(scores.reshape(targets, local_queries * passages), ('shard...]
    all_to_all x1, waiting for transfers between devices: 0.01 us -> 2.11 us  [body(): lax.all_to_all(sent, ('shard', 'sub'), split_axis=0, concat_axis=0, tiled...]
    broadcast_in_dim x1 -> x0, local copies, waits for them, and re-layouts: 1.37 us -> none  [body(): sent = jnp.broadcast_to(own_rows, (targets,) + own_rows.shape[1:])]
  transfers between devices with their start and end apart: 2 -> 2, of which waited for: 0 -> 1; matrix products, arithmetic and copies ran while one was open for 4% -> 0% of each run, Pallas kernels for 26% -> 9%
where the time goes in v7:
time: 40 us; the launch traced here: 39.7 us
  Pallas kernels  11.7 us (29%)
  blocking collectives  10.5 us (26%)
  local copies, waits for them, and re-layouts  7.95 us (20%)
  starting transfers between devices  7.47 us (19%)
  waiting for transfers between devices  2.11 us (5%)
    all_to_all x1, blocking collectives, body(): lax.all_to_all(scores.reshape(targets, local_queries * passages), ('shard...  10.5 us
    unnamed x8, local copies, waits for them, and re-layouts  7.95 us
    pallas_call x1, Pallas kernels, score_all(): pl.pallas_call(functools.partial(score_kernel, token_count, query_rows),...  7.26 us
    all_to_all x1, starting transfers between devices, body(): lax.all_to_all(sent, ('shard', 'sub'), split_axis=0, concat_axis=0, tiled...  7.02 us
    pallas_call x1, Pallas kernels, widen(): pl.pallas_call(widen_kernel, out_shape=pltpu.VMEM((2 * half_rows, width),...  2.28 us
    all_to_all x1, waiting for transfers between devices, body(): lax.all_to_all(sent, ('shard', 'sub'), split_axis=0, concat_axis=0, tiled...  2.11 us
    pallas_call x1, Pallas kernels, spread(): pl.pallas_call(spread_kernel, out_shape=jax.ShapeDtypeStruct((targets, qu...  1.47 us
  transfers between devices with their start and end apart: 2, of which 1 were waited for; matrix products, arithmetic and copies ran while one was open for 0% of the time, Pallas kernels for 9%

profile of v7, /device:TPU:0, one launch (start us, length us, event | category | flops | bytes accessed | tf_op | source)
XLA Modules:
  0.0 39.7 jit_solution(3806974758144464988)
XLA Ops:
  0.0 0.5 %collective-permute-start = (bf16[8192,128]{1,0:T(8,128)(2,1)}, bf16[8192,128]{1,0:T(8,128)(2,1)S(1)}, u32[]{:S(2)}, u32[]{:S(2)}) collective-permute-start(bf16[8192,128]{1,0:T(8,128)(2,1)} %own_ref.1), channel_id=1, source_target_pairs={{0,1},{1,0},{2,3},{3,2},{4,5},{5,4},{6,7},{7,6},{8,9},{9,8},{10,11... | collective-permute-start | bytes 6291464 | tf_op jit(solution)/shard_map/ppermute | solution.py:361
  0.5 1.5 %spread.1 = bf16[16,48,128]{2,1,0:T(8,128)(2,1)} custom-call(bf16[32,128]{1,0:T(8,128)(2,1)} %bitcast.13, s32[1,62]{1,0:T(1,128)} %candidates_ref.3), custom_call_target="tpu_custom_call" | custom-call | tf_op jit(solution)/shard_map/spread/pallas_call | solution.py:74
  1.9 7.0 %all-to-all-start = ((bf16[16,48,128]{2,1,0:T(8,128)(2,1)}), bf16[16,48,128]{2,1,0:T(8,128)(2,1)S(1)}, u32[]{:S(2)}, u32[]{:S(2)}) async-start(bf16[16,48,128]{2,1,0:T(8,128)(2,1)} %spread.1), calls=%async_computation | async-start | bytes 393216 | tf_op jit(solution)/shard_map/all_to_all | solution.py:363
  9.0 0.0 collective-permute-done.other_ref
  9.0 0.0 copy-start.3
  9.0 1.3 %copy-done.3 = bf16[8192,128]{1,0:T(8,128)(2,1)} copy-done((bf16[8192,128]{1,0:T(8,128)(2,1)}, bf16[8192,128]{1,0:T(8,128)(2,1)S(1)}, u32[]{:S(2)}) %copy-start.3) | copy-done | bytes 2097176
  10.3 2.3 %widen.1.table = f32[16384,128]{1,0:T(8,128)S(1)} custom-call(s32[1]{0:T(128)} %bitcast.3.half_ref, bf16[8192,128]{1,0:T(8,128)(2,1)} %own_ref.1, bf16[8192,128]{1,0:T(8,128)(2,1)} %copy-done.3), custom_call_target="tpu_custom_call" | custom-call | flops 10000000 | bytes 10000000 | tf_op jit(solution)/shard_map/widen/pallas_call | solution.py:106
  12.6 0.0 copy-start
  12.6 3.2 %copy-done = f32[16384,128]{1,0:T(8,128)} copy-done((f32[16384,128]{1,0:T(8,128)}, f32[16384,128]{1,0:T(8,128)S(1)}, u32[]{:S(2)}) %copy-start) | copy-done | bytes 8388632
  15.8 2.1 %all-to-all-done.gathered_ref = bf16[16,48,128]{2,1,0:T(8,128)(2,1)S(1)} async-done(((bf16[16,48,128]{2,1,0:T(8,128)(2,1)}), bf16[16,48,128]{2,1,0:T(8,128)(2,1)S(1)}, u32[]{:S(2)}, u32[]{:S(2)}) %all-to-all-start) | async-done | bytes 196640 | tf_op jit(solution)/shard_map/all_to_all | solution.py:363
  17.9 0.0 copy-start.1
  17.9 3.4 %copy-done.1 = f32[16384,128]{1,0:T(8,128)S(1)} copy-done((f32[16384,128]{1,0:T(8,128)S(1)}, f32[16384,128]{1,0:T(8,128)}, u32[]{:S(2)}) %copy-start.1) | copy-done | bytes 8388632
  21.3 0.0 copy-start.2
  21.3 7.3 %score.1 = f32[16,64]{1,0:T(8,128)S(1)} custom-call(s32[1]{0:T(128)} %bitcast.base_ref, s32[8192]{0:T(1024)} %bitcast.12, s32[64]{0:T(128)} %lengths_hbm.1, bf16[16,48,128]{2,1,0:T(8,128)(2,1)S(1)} %all-to-all-done.gathered_ref, f32[16384,128]{1,0:T(8,128)S(1)} %copy-done.1, bf16[8192,128]{1,0:T(8,128)(2,1)} %bitcast.11), custom_call_target="tpu_custom_call" | custom-call | tf_op jit(solution)/shard_map/score/pallas_call | solution.py:293
  28.6 10.5 %all_to_all.16 = f32[16,1,64]{2,1,0:T(1,128)S(1)} all-to-all(f32[16,1,64]{2,1,0:T(1,128)S(1)} %bitcast.9), channel_id=1, replica_groups=mesh['groups'=2,'shard'=8,'sub'=2] {'shard','sub'}, dimensions={0} | all-to-all | bytes 8192 | tf_op jit(solution)/shard_map/all_to_all | solution.py:369
  39.1 0.0 copy-done.2
  39.1 0.7 %pick.1 = f32[1,62]{1,0:T(1,128)} custom-call(s32[1,62]{1,0:T(1,128)S(1)} %copy-done.2, f32[16,64]{1,0:T(8,128)S(1)} %bitcast.10), custom_call_target="tpu_custom_call" | custom-call | tf_op jit(solution)/shard_map/pick/pallas_call | solution.py:344
Async XLA Ops:
  0.0 9.0 %collective-permute-start = (bf16[8192,128]{1,0:T(8,128)(2,1)}, bf16[8192,128]{1,0:T(8,128)(2,1)S(1)}, u32[]{:S(2)}, u32[]{:S(2)}) collective-permute-start(bf16[8192,128]{1,0:T(8,128)(2,1)} %own_ref.1), channel_id=1, source_target_pairs={{0,1},{1,0},{2,3},{3,2},{4,5},{5,4},{6,7},{7,6},{8,9},{9,8},{10,11... | collective-permute-start | bytes 6291464 | tf_op jit(solution)/shard_map/ppermute | solution.py:361
  1.9 16.0 %all-to-all-start = ((bf16[16,48,128]{2,1,0:T(8,128)(2,1)}), bf16[16,48,128]{2,1,0:T(8,128)(2,1)S(1)}, u32[]{:S(2)}, u32[]{:S(2)}) async-start(bf16[16,48,128]{2,1,0:T(8,128)(2,1)} %spread.1), calls=%async_computation | async-start | bytes 393216 | tf_op jit(solution)/shard_map/all_to_all | solution.py:363
  9.0 1.4 %copy-start.3 = (bf16[8192,128]{1,0:T(8,128)(2,1)}, bf16[8192,128]{1,0:T(8,128)(2,1)S(1)}, u32[]{:S(2)}) copy-start(bf16[8192,128]{1,0:T(8,128)(2,1)S(1)} %collective-permute-done.other_ref) | copy-start | bytes 6291460
  12.6 3.2 %copy-start = (f32[16384,128]{1,0:T(8,128)}, f32[16384,128]{1,0:T(8,128)S(1)}, u32[]{:S(2)}) copy-start(f32[16384,128]{1,0:T(8,128)S(1)} %widen.1.table) | copy-start | bytes 25165828
  17.9 3.4 %copy-start.1 = (f32[16384,128]{1,0:T(8,128)S(1)}, f32[16384,128]{1,0:T(8,128)}, u32[]{:S(2)}) copy-start(f32[16384,128]{1,0:T(8,128)} %copy-done) | copy-start | bytes 25165828
  21.3 17.8 %copy-start.2 = (s32[1,62]{1,0:T(1,128)S(1)}, s32[1,62]{1,0:T(1,128)}, u32[]{:S(2)}) copy-start(s32[1,62]{1,0:T(1,128)} %candidates_ref.3) | copy-start | bytes 748

commit v8 on v6

--- a/solution.py
+++ b/solution.py
@@ -28,43 +28,74 @@
     return lax.div(number, divisor)
 
 
+def pinned(array, space=pltpu.HBM):
+    return pltpu.with_memory_space_constraint(array, space)
+
+
+def granted(mebibytes):
+    return pltpu.CompilerParams(vmem_limit_bytes=mebibytes * 1024 * 1024)
+
+
+def widen_kernel(half_ref, own_hbm, other_ref, residuals_hbm, table, residuals, staged, sems):
+    half_rows = own_hbm.shape[0]
+    half = half_ref[0]
+    piece = half_rows // PIECES
+    copies = []
+    for k in range(PIECES):
+        at = pl.ds(k * piece, piece)
+        copies.append(pltpu.make_async_copy(own_hbm.at[at], staged.at[at], sems.at[k]))
+        copies[-1].start()
+    residual_copy = pltpu.make_async_copy(residuals_hbm, residuals, sems.at[PIECES])
+    residual_copy.start()
+    for source, ref in enumerate((other_ref, staged)):
+        base = (1 - half if source == 0 else half) * half_rows
+        for k in range(PIECES):
+            if source == 1:
+                copies[k].wait()
+            to = pl.ds(pl.multiple_of(base + k * piece, piece), piece)
+            table[to, :] = ref[pl.ds(k * piece, piece), :].astype(jnp.float32)
+    residual_copy.wait()
+
+
+def widen(half, own, other, residuals):
+    half_rows, width = own.shape
+    return pl.pallas_call(
+        widen_kernel,
+        out_shape=(
+            pltpu.VMEM((2 * half_rows, width), jnp.float32),
+            pltpu.VMEM(residuals.shape, jnp.bfloat16),
+        ),
+        in_specs=[SMEM, HBM, VMEM, HBM],
+        out_specs=(VMEM, VMEM),
+        scratch_shapes=[
+            pltpu.VMEM((half_rows, width), jnp.bfloat16),
+            pltpu.SemaphoreType.DMA((PIECES + 1,)),
+        ],
+        compiler_params=granted(4),
+        cost_estimate=pl.CostEstimate(flops=10**7, bytes_accessed=10**7, transcendentals=0),
+        name="widen",
+    )(half, pinned(own), pinned(other, pltpu.VMEM), pinned(residuals))
+
+
 def decode_kernel(
-    half_ref,
     codes_hbm,
     lengths_hbm,
-    own_ref,
-    other_ref,
-    residuals_ref,
+    table,
+    residuals,
     embedded,
     at_ref,
     codes_ref,
     lengths_ref,
-    staged,
-    table,
-    residual_rows,
     rows,
     sems,
 ):
     passages = lengths_ref.shape[0]
-    tokens = codes_ref.shape[0]
+    tokens, width = residuals.shape
     slots = tokens // passages
-    half_rows, width = own_ref.shape
-    half = half_ref[0]
     lengths_copy = pltpu.make_async_copy(lengths_hbm, lengths_ref, sems.at[0])
     codes_copy = pltpu.make_async_copy(codes_hbm, codes_ref, sems.at[1])
-    residual_copy = pltpu.make_async_copy(residuals_ref, residual_rows, sems.at[2])
     lengths_copy.start()
     codes_copy.start()
-    piece = half_rows // PIECES
-    copies = []
-    for source, ref in enumerate((own_ref, other_ref)):
-        for k in range(PIECES):
-            at = pl.ds(k * piece, piece)
-            sem = sems.at[3 + source * PIECES + k]
-            copies.append(pltpu.make_async_copy(ref.at[at], staged.at[source, at], sem))
-            copies[-1].start()
-    residual_copy.start()
-
     lengths_copy.wait()
 
     def listing(p, chunks):
@@ -77,29 +108,23 @@
         at_ref[chunks + k] = tokens
     groups = quotient(chunks + GROUP - 1, GROUP)
     at_ref[at_ref.shape[0] - 1] = chunks
-
-    for source in range(2):
-        base = (half if source == 0 else 1 - half) * half_rows
-        for k in range(PIECES):
-            copies[source * PIECES + k].wait()
-            to = pl.ds(pl.multiple_of(base + k * piece, piece), piece)
-            table[to, :] = staged[source, pl.ds(k * piece, piece), :].astype(jnp.float32)
     codes_copy.wait()
-    residual_copy.wait()
 
     slot_numbers = lax.broadcasted_iota(jnp.int32, (CHUNK, width), 0)
-    single = table.reshape(2 * half_rows, 1, width)
+    table_single = table.reshape(table.shape[0], 1, width)
+    rows_single = rows.reshape(rows.shape[0], 1, width)
 
     def fetch(g, k):
         at = jnp.minimum(at_ref[g * GROUP + k], tokens - CHUNK)
+        codes = codes_ref.at[pl.ds(at, CHUNK)]
         for j in range(CHUNK):
-            rows[pl.ds(k * CHUNK + j, 1), :] = single[codes_ref[at + j]]
+            rows_single[k * CHUNK + j] = table_single[codes[j]]
 
     def finish(g, k):
         at = jnp.minimum(at_ref[g * GROUP + k], tokens - CHUNK)
         p = quotient(at, slots)
         live = lengths_ref[p] - (at - p * slots)
-        near = residual_rows[pl.ds(pl.multiple_of(at, CHUNK), CHUNK), :]
+        near = residuals[pl.ds(pl.multiple_of(at, CHUNK), CHUNK), :]
         vectors = rows[pl.ds(k * CHUNK, CHUNK), :] + near.astype(jnp.float32)
         vectors = jnp.where(slot_numbers < live, vectors, vectors[0:1, :])
         return normalized(vectors)
@@ -124,41 +149,32 @@
     keep(groups - 1, [finish(groups - 1, k) for k in range(GROUP)])
 
 
-def pinned(array):
-    return pltpu.with_memory_space_constraint(array, pltpu.HBM)
-
-
-def decode_all(half, token_codes, lengths, own, other, residuals):
-    passages, slots, width = residuals.shape
-    half_rows = own.shape[0]
-    most = passages * (slots // CHUNK) + 2 * SCORE_GROUP
+def decode_all(token_codes, lengths, table, residuals):
+    passages, slots = token_codes.shape
+    tokens, width = residuals.shape
+    most = tokens // CHUNK + 2 * SCORE_GROUP
     return pl.pallas_call(
         decode_kernel,
         out_shape=(
             jax.ShapeDtypeStruct((most * CHUNK, width), jnp.bfloat16),
             jax.ShapeDtypeStruct((most + 1,), jnp.int32),
         ),
-        in_specs=[SMEM, HBM, HBM, HBM, HBM, HBM],
+        in_specs=[HBM, HBM, VMEM, VMEM],
         out_specs=(VMEM, SMEM),
         scratch_shapes=[
-            pltpu.SMEM((passages * slots,), jnp.int32),
+            pltpu.SMEM((tokens,), jnp.int32),
             pltpu.SMEM((passages,), jnp.int32),
-            pltpu.VMEM((2, half_rows, width), jnp.bfloat16),
-            pltpu.VMEM((2 * half_rows, width), jnp.float32),
-            pltpu.VMEM((passages * slots, width), jnp.bfloat16),
             pltpu.VMEM((GROUP * CHUNK, width), jnp.float32),
-            pltpu.SemaphoreType.DMA((3 + 2 * PIECES,)),
+            pltpu.SemaphoreType.DMA((2,)),
         ],
-        compiler_params=pltpu.CompilerParams(vmem_limit_bytes=24 * 1024 * 1024),
+        compiler_params=granted(4),
         cost_estimate=pl.CostEstimate(flops=10**7, bytes_accessed=40 * 10**6, transcendentals=0),
         name="decode",
     )(
-        half,
-        pinned(token_codes.reshape(passages * slots)),
+        pinned(token_codes.reshape(tokens)),
         pinned(lengths),
-        pinned(own),
-        pinned(other),
-        pinned(residuals.reshape(passages * slots, width)),
+        pinned(table, pltpu.VMEM),
+        pinned(residuals, pltpu.VMEM),
     )
 
 
@@ -216,6 +232,7 @@
 def score_all(starts, query_rows, embedded, passages, slots, token_count):
     query_tokens, width = query_rows.shape
     block = min(QUERY_BLOCK, query_tokens)
+    blocks = query_tokens // block
     return pl.pallas_call(
         functools.partial(score_kernel, token_count, slots),
         out_shape=jax.ShapeDtypeStruct((query_tokens // token_count, passages), jnp.float32),
@@ -225,7 +242,7 @@
             pltpu.VMEM((width, block), jnp.bfloat16),
             pltpu.VMEM((block // 128, (passages + 1) * 8, 128), jnp.float32),
         ],
-        compiler_params=pltpu.CompilerParams(vmem_limit_bytes=32 * 1024 * 1024),
+        compiler_params=granted(8 + 2 * blocks),
         name="score",
     )(starts, query_rows, embedded)
 
@@ -255,7 +272,7 @@
         out_shape=jax.ShapeDtypeStruct(candidates.shape, jnp.float32),
         in_specs=[VMEM, VMEM],
         out_specs=VMEM,
-        compiler_params=pltpu.CompilerParams(vmem_limit_bytes=4 * 1024 * 1024),
+        compiler_params=granted(8),
         name="pick",
     )(candidates, pltpu.with_memory_space_constraint(returned, pltpu.VMEM))
 
@@ -270,7 +287,9 @@
     sent = jnp.broadcast_to(own_rows, (targets,) + own_rows.shape[1:])
     gathered = lax.all_to_all(sent, ("shard", "sub"), split_axis=0, concat_axis=0, tiled=True)
     query_rows = gathered.reshape(targets * local_queries * token_count, width)
-    embedded, starts = decode_all(half.reshape(1), token_codes, lengths, centroids, other, residuals)
+    flat = residuals.reshape(passages * slots, width)
+    table, near = widen(half.reshape(1), centroids, other, flat)
+    embedded, starts = decode_all(token_codes, lengths, table, near)
     scores = score_all(starts, query_rows, embedded, passages, slots, token_count)
     returned = lax.all_to_all(
         scores.reshape(targets, local_queries * passages),

time: 37.8 us -> 36.4 us (0.963); the launches traced: 37.9 us -> 36 us
  local copies, waits for them, and re-layouts: 2.7 us -> 1.36 us
    pallas_call x0 -> x1, Pallas kernels: none -> 2.29 us  [widen(): pl.pallas_call(widen_kernel, out_shape=(pltpu.VMEM((2 * half_rows, width)...]
    pallas_call x1, Pallas kernels: 9.93 us -> 7.71 us  [decode_all(): pl.pallas_call(decode_kernel, out_shape=(jax.ShapeDtypeStruct((most * CHU...]
    unnamed x4 -> x2, local copies, waits for them, and re-layouts: 1.34 us -> 0.01 us
  transfers between devices with their start and end apart: 2 -> 2, of which waited for: 0 -> 0; matrix products, arithmetic and copies ran while one was open for 4% -> 4% of each run, Pallas kernels for 26% -> 28%
where the time goes in v8:
time: 36.4 us; the launch traced here: 36 us
  Pallas kernels  14.3 us (39%)
  blocking collectives  12.9 us (35%)
  starting transfers between devices  7.47 us (21%)
  local copies, waits for them, and re-layouts  1.36 us (4%)
    all_to_all x1, blocking collectives, body(): lax.all_to_all(scores.reshape(targets, local_queries * passages), ('shard...  12.9 us
    pallas_call x1, Pallas kernels, decode_all(): pl.pallas_call(decode_kernel, out_shape=(jax.ShapeDtypeStruct((most * CHU...  7.71 us
    all_to_all x1, starting transfers between devices, body(): lax.all_to_all(sent, ('shard', 'sub'), split_axis=0, concat_axis=0, tiled...  7.02 us
    pallas_call x1, Pallas kernels, score_all(): pl.pallas_call(functools.partial(score_kernel, token_count, slots), out_s...  3.6 us
    pallas_call x1, Pallas kernels, widen(): pl.pallas_call(widen_kernel, out_shape=(pltpu.VMEM((2 * half_rows, width)...  2.29 us
    broadcast_in_dim x1, local copies, waits for them, and re-layouts, body(): sent = jnp.broadcast_to(own_rows, (targets,) + own_rows.shape[1:])  1.36 us
  transfers between devices with their start and end apart: 2, of which 0 were waited for; matrix products, arithmetic and copies ran while one was open for 4% of the time, Pallas kernels for 28%

profile of v8, /device:TPU:0, one launch (start us, length us, event | category | flops | bytes accessed | tf_op | source)
XLA Modules:
  0.0 36.0 jit_solution(7102120076956689514)
XLA Ops:
  0.0 0.5 %collective-permute-start = (bf16[8192,128]{1,0:T(8,128)(2,1)}, bf16[8192,128]{1,0:T(8,128)(2,1)S(1)}, u32[]{:S(2)}, u32[]{:S(2)}) collective-permute-start(bf16[8192,128]{1,0:T(8,128)(2,1)} %own_hbm.1), channel_id=1, source_target_pairs={{0,1},{1,0},{2,3},{3,2},{4,5},{5,4},{6,7},{7,6},{8,9},{9,8},{10,11... | collective-permute-start | bytes 6291464 | tf_op jit(solution)/shard_map/ppermute | solution.py:285
  0.5 1.4 %broadcast_in_dim.8 = bf16[16,32,128]{2,1,0:T(8,128)(2,1)} broadcast(bf16[32,128]{1,0:T(8,128)(2,1)} %bitcast.14), dimensions={1,2} | broadcast | bytes 139264 | tf_op jit(solution)/shard_map/broadcast_in_dim | solution.py:287
  1.8 7.0 %all-to-all-start = ((bf16[16,32,128]{2,1,0:T(8,128)(2,1)}), bf16[16,32,128]{2,1,0:T(8,128)(2,1)S(1)}, u32[]{:S(2)}, u32[]{:S(2)}) async-start(bf16[16,32,128]{2,1,0:T(8,128)(2,1)} %broadcast_in_dim.8), calls=%async_computation | async-start | bytes 262144 | tf_op jit(solution)/shard_map/all_to_all | solution.py:288
  8.8 0.0 collective-permute-done.other_ref
  8.9 2.3 %widen.1 = (f32[16384,128]{1,0:T(8,128)S(1)}, bf16[8192,128]{1,0:T(8,128)(2,1)S(1)}) custom-call(s32[1]{0:T(128)} %bitcast.1.half_ref, bf16[8192,128]{1,0:T(8,128)(2,1)} %own_hbm.1, bf16[8192,128]{1,0:T(8,128)(2,1)S(1)} %collective-permute-done.other_ref, bf16[8192,128]{1,0:T(8,128)(2,1)} %bitcast.12), custom_call_target="tpu_custom_call" | custom-call | flops 10000000 | bytes 10000000 | tf_op jit(solution)/shard_map/widen/pallas_call | solution.py:62
  11.2 7.7 %decode.1 = (bf16[9216,128]{1,0:T(8,128)(2,1)S(1)}, s32[577]{0:T(1024)S(1)}) custom-call(s32[8192]{0:T(1024)} %bitcast.13, s32[64]{0:T(128)} %lengths_hbm.1, f32[16384,128]{1,0:T(8,128)S(1)} %get-tuple-element.9.table, bf16[8192,128]{1,0:T(8,128)(2,1)S(1)} %get-tuple-element.10.residuals), custom_call_target="tpu_custom_call" | custom-call | flops 10000000 | bytes 40000000 | tf_op jit(solution)/shard_map/decode/pallas_call | solution.py:156
  18.9 0.0 copy-start
  18.9 0.0 all-to-all-done
  18.9 3.6 %score.1 = f32[16,64]{1,0:T(8,128)S(1)} custom-call(s32[577]{0:T(1024)S(1)} %get-tuple-element.11.at_ref, bf16[512,128]{1,0:T(8,128)(2,1)S(1)} %bitcast.9, bf16[9216,128]{1,0:T(8,128)(2,1)S(1)} %get-tuple-element.12.embedded), custom_call_target="tpu_custom_call" | custom-call | tf_op jit(solution)/shard_map/score/pallas_call | solution.py:236
  22.5 12.9 %all_to_all.16 = f32[16,1,64]{2,1,0:T(1,128)S(1)} all-to-all(f32[16,1,64]{2,1,0:T(1,128)S(1)} %bitcast.10), channel_id=1, replica_groups=mesh['groups'=2,'shard'=8,'sub'=2] {'shard','sub'}, dimensions={0} | all-to-all | bytes 8192 | tf_op jit(solution)/shard_map/all_to_all | solution.py:294
  35.4 0.0 copy-done
  35.4 0.7 %pick.1 = f32[1,62]{1,0:T(1,128)} custom-call(s32[1,62]{1,0:T(1,128)S(1)} %copy-done, f32[16,64]{1,0:T(8,128)S(1)} %bitcast.11), custom_call_target="tpu_custom_call" | custom-call | tf_op jit(solution)/shard_map/pick/pallas_call | solution.py:270
Async XLA Ops:
  0.0 8.8 %collective-permute-start = (bf16[8192,128]{1,0:T(8,128)(2,1)}, bf16[8192,128]{1,0:T(8,128)(2,1)S(1)}, u32[]{:S(2)}, u32[]{:S(2)}) collective-permute-start(bf16[8192,128]{1,0:T(8,128)(2,1)} %own_hbm.1), channel_id=1, source_target_pairs={{0,1},{1,0},{2,3},{3,2},{4,5},{5,4},{6,7},{7,6},{8,9},{9,8},{10,11... | collective-permute-start | bytes 6291464 | tf_op jit(solution)/shard_map/ppermute | solution.py:285
  1.8 17.1 %all-to-all-start = ((bf16[16,32,128]{2,1,0:T(8,128)(2,1)}), bf16[16,32,128]{2,1,0:T(8,128)(2,1)S(1)}, u32[]{:S(2)}, u32[]{:S(2)}) async-start(bf16[16,32,128]{2,1,0:T(8,128)(2,1)} %broadcast_in_dim.8), calls=%async_computation | async-start | bytes 262144 | tf_op jit(solution)/shard_map/all_to_all | solution.py:288
  18.9 16.5 %copy-start = (s32[1,62]{1,0:T(1,128)S(1)}, s32[1,62]{1,0:T(1,128)}, u32[]{:S(2)}) copy-start(s32[1,62]{1,0:T(1,128)} %candidates_ref.1) | copy-start | bytes 748

commit v9 on v7

--- a/solution.py
+++ b/solution.py
@@ -42,8 +42,7 @@
     return -(-rows // 8) * 8
 
 
-def spread_kernel(queries_ref, candidates_ref, out_ref, digits):
-    targets = out_ref.shape[0]
+def pack_kernel(queries_ref, candidates_ref, out_ref, digits):
     query_rows = queries_ref.shape[0]
     local_queries, count = candidates_ref.shape
     id_rows = digits.shape[0] // 2
@@ -57,83 +56,98 @@
             digits[row : row + 1, 0:size] = (ids - high * DIGIT).astype(jnp.float32)
             digits[id_rows + row : id_rows + row + 1, 0:size] = high.astype(jnp.float32)
             row += 1
-    queries = queries_ref[...]
-    coded = digits[...].astype(jnp.bfloat16)
-
-    def copy(t, carry):
-        out_ref[t, 0:query_rows, :] = queries
-        out_ref[t, query_rows:, :] = coded
-        return carry
-
-    lax.fori_loop(0, targets, copy, 0)
-
-
-def spread(queries, candidates, targets):
+    out_ref[0:query_rows, :] = queries_ref[...]
+    out_ref[query_rows:, :] = digits[...].astype(jnp.bfloat16)
+
+
+def pack(queries, candidates):
     query_rows, width = queries.shape
     id_rows = id_rows_of(*candidates.shape)
     return pl.pallas_call(
-        spread_kernel,
-        out_shape=jax.ShapeDtypeStruct((targets, query_rows + 2 * id_rows, width), jnp.bfloat16),
+        pack_kernel,
+        out_shape=pltpu.VMEM((query_rows + 2 * id_rows, width), jnp.bfloat16),
         in_specs=[VMEM, VMEM],
         out_specs=VMEM,
         scratch_shapes=[pltpu.VMEM((2 * id_rows, width), jnp.float32)],
-        compiler_params=granted(16),
-        name="spread",
+        compiler_params=granted(4),
+        name="pack",
     )(pinned(queries), pinned(candidates))
 
 
-def widen_kernel(half_ref, own_ref, other_ref, table, staged, sems):
-    half_rows = own_ref.shape[0]
-    half = half_ref[0]
+def widen_own_kernel(half_ref, own_hbm, residuals_hbm, table, residuals, staged, sems):
+    half_rows = own_hbm.shape[0]
+    base = half_ref[0] * half_rows
     piece = half_rows // PIECES
     copies = []
-    for source, ref in enumerate((own_ref, other_ref)):
-        for k in range(PIECES):
-            at = pl.ds(k * piece, piece)
-            sem = sems.at[source * PIECES + k]
-            copies.append(pltpu.make_async_copy(ref.at[at], staged.at[source, at], sem))
-            copies[-1].start()
-    for source in range(2):
-        base = (half if source == 0 else 1 - half) * half_rows
-        for k in range(PIECES):
-            copies[source * PIECES + k].wait()
-            to = pl.ds(pl.multiple_of(base + k * piece, piece), piece)
-            table[to, :] = staged[source, pl.ds(k * piece, piece), :].astype(jnp.float32)
-
-
-def widen(half, own, other):
+    for k in range(PIECES):
+        at = pl.ds(k * piece, piece)
+        copies.append(pltpu.make_async_copy(own_hbm.at[at], staged.at[at], sems.at[k]))
+        copies[-1].start()
+    residual_copy = pltpu.make_async_copy(residuals_hbm, residuals, sems.at[PIECES])
+    residual_copy.start()
+    for k in range(PIECES):
+        copies[k].wait()
+        to = pl.ds(pl.multiple_of(base + k * piece, piece), piece)
+        table[to, :] = staged[pl.ds(k * piece, piece), :].astype(jnp.float32)
+    residual_copy.wait()
+
+
+def widen_own(half, own, residuals):
     half_rows, width = own.shape
     return pl.pallas_call(
-        widen_kernel,
-        out_shape=pltpu.VMEM((2 * half_rows, width), jnp.float32),
+        widen_own_kernel,
+        out_shape=(
+            pltpu.VMEM((2 * half_rows, width), jnp.float32),
+            pltpu.VMEM(residuals.shape, jnp.bfloat16),
+        ),
         in_specs=[SMEM, HBM, HBM],
+        out_specs=(VMEM, VMEM),
+        scratch_shapes=[
+            pltpu.VMEM((half_rows, width), jnp.bfloat16),
+            pltpu.SemaphoreType.DMA((PIECES + 1,)),
+        ],
+        compiler_params=granted(4),
+        cost_estimate=pl.CostEstimate(flops=10**7, bytes_accessed=5 * 10**6, transcendentals=0),
+        name="widen_own",
+    )(half, pinned(own), pinned(residuals))
+
+
+def widen_other_kernel(half_ref, other_ref, partial_ref, table):
+    half_rows = other_ref.shape[0]
+    base = (1 - half_ref[0]) * half_rows
+    piece = half_rows // PIECES
+    for k in range(PIECES):
+        to = pl.ds(pl.multiple_of(base + k * piece, piece), piece)
+        table[to, :] = other_ref[pl.ds(k * piece, piece), :].astype(jnp.float32)
+
+
+def widen_other(half, other, partial):
+    return pl.pallas_call(
+        widen_other_kernel,
+        out_shape=pltpu.VMEM(partial.shape, jnp.float32),
+        in_specs=[SMEM, VMEM, VMEM],
         out_specs=VMEM,
-        scratch_shapes=[
-            pltpu.VMEM((2, half_rows, width), jnp.bfloat16),
-            pltpu.SemaphoreType.DMA((2 * PIECES,)),
-        ],
-        compiler_params=granted(16),
-        cost_estimate=pl.CostEstimate(flops=10**7, bytes_accessed=10**7, transcendentals=0),
-        name="widen",
-    )(half, pinned(own), pinned(other))
+        input_output_aliases={2: 0},
+        compiler_params=granted(4),
+        cost_estimate=pl.CostEstimate(flops=10**7, bytes_accessed=3 * 10**6, transcendentals=0),
+        name="widen_other",
+    )(half, pinned(other, pltpu.VMEM), pinned(partial, pltpu.VMEM))
 
 
 def score_kernel(
     token_count,
     query_rows,
-    base_ref,
+    me_ref,
     codes_hbm,
     lengths_hbm,
     gathered_ref,
     table,
-    residuals_ref,
+    residuals,
     out_ref,
     codes_ref,
     lengths_ref,
     at_ref,
-    residual_rows,
     rows,
-    embedded,
     turned,
     so_far,
     largest,
@@ -147,10 +161,9 @@
     blocks, _, block = turned.shape
     lengths_copy = pltpu.make_async_copy(lengths_hbm, lengths_ref, sems.at[0])
     codes_copy = pltpu.make_async_copy(codes_hbm, codes_ref, sems.at[1])
-    residual_copy = pltpu.make_async_copy(residuals_ref, residual_rows, sems.at[2])
     lengths_copy.start()
     codes_copy.start()
-    residual_copy.start()
+    base = me_ref[0] * passages
 
     words = -(-passages // 32)
     shape = (id_rows, width)
@@ -158,7 +171,7 @@
     def collect(t, masks):
         low = gathered_ref[t, query_rows : query_rows + id_rows, :].astype(jnp.float32)
         high = gathered_ref[t, query_rows + id_rows :, :].astype(jnp.float32)
-        local = (high * DIGIT + low).astype(jnp.int32) - base_ref[0]
+        local = (high * DIGIT + low).astype(jnp.int32) - base
         bits = lax.shift_left(jnp.ones(shape, jnp.int32), local & 31)
         word = lax.shift_right_arithmetic(local, 5)
         return tuple(mask | jnp.where(word == w, bits, 0) for w, mask in enumerate(masks))
@@ -203,27 +216,28 @@
         at_ref[chunks + k] = tokens
     groups = quotient(chunks + GROUP - 1, GROUP)
     codes_copy.wait()
-    residual_copy.wait()
 
     slot_numbers = lax.broadcasted_iota(jnp.int32, (CHUNK, width), 0)
-    single = table.reshape(table.shape[0], 1, width)
+    table_single = table.reshape(table.shape[0], 1, width)
+    rows_single = rows.reshape(rows.shape[0], 1, width)
 
     def fetch(g, k):
         at = jnp.minimum(at_ref[g * GROUP + k], tokens - CHUNK)
+        codes = codes_ref.at[pl.ds(at, CHUNK)]
         for j in range(CHUNK):
-            rows[pl.ds(k * CHUNK + j, 1), :] = single[codes_ref[at + j]]
+            rows_single[k * CHUNK + j] = table_single[codes[j]]
 
     def finish(g, k):
         at = jnp.minimum(at_ref[g * GROUP + k], tokens - CHUNK)
         p = quotient(at, slots)
         live = lengths_ref[p] - (at - p * slots)
-        near = residual_rows[pl.ds(pl.multiple_of(at, CHUNK), CHUNK), :]
+        near = residuals[pl.ds(pl.multiple_of(at, CHUNK), CHUNK), :]
         vectors = rows[pl.ds(k * CHUNK, CHUNK), :] + near.astype(jnp.float32)
         vectors = jnp.where(slot_numbers < live, vectors, vectors[0:1, :])
         return normalized(vectors)
 
-    def score(g, b):
-        similar = jnp.dot(embedded[...], turned[b], preferred_element_type=jnp.float32)
+    def score(g, b, embedded):
+        similar = jnp.dot(embedded, turned[b], preferred_element_type=jnp.float32)
         parts = jnp.max(similar.reshape(GROUP, CHUNK // 8, 8, block), axis=1)
         best = so_far[b]
         for k in range(GROUP):
@@ -236,32 +250,36 @@
         so_far[b] = best
 
     def step(i, carry):
-        scored = jnp.maximum(i - 2, 0)
-        if blocks == 1:
-            score(scored, 0)
-        else:
-
-            def score_block(b, inner):
-                score(scored, b)
-                return inner
-
-            lax.fori_loop(0, blocks, score_block, 0)
         fetched = jnp.minimum(i, groups - 1)
-        finished = jnp.maximum(jnp.minimum(i - 1, groups - 1), 0)
+        finished = jnp.maximum(i - 1, 0)
         done = []
         for k in range(GROUP):
             done.append(finish(finished, k))
             fetch(fetched, k)
-        for k in range(GROUP):
-            embedded[pl.ds(k * CHUNK, CHUNK), :] = done[k]
+        embedded = jnp.concatenate(done, axis=0)
+        if blocks == 1:
+            score(finished, 0, embedded)
+        else:
+
+            def score_block(b, inner):
+                score(finished, b, embedded)
+                return inner
+
+            lax.fori_loop(0, blocks, score_block, 0)
         return carry
 
-    lax.fori_loop(0, jnp.where(groups > 0, groups + 2, 0), step, 0)
+    lax.fori_loop(0, jnp.where(groups > 0, groups + 1, 0), step, 0)
 
     per_block = block // token_count
+    local_queries = query_rows // token_count
     owner = lax.broadcasted_iota(jnp.int32, (per_block, block), 0)
     token_of = quotient(lax.broadcasted_iota(jnp.int32, (per_block, block), 1), token_count)
-    summing = (owner == token_of).astype(jnp.bfloat16)
+    block_targets = per_block // local_queries
+    near_me = me_ref[0] & (block_targets - 1)
+    far_me = quotient(me_ref[0], block_targets)
+    owner_target = quotient(owner, local_queries)
+    relative = (owner_target ^ near_me) * local_queries + owner - owner_target * local_queries
+    summing = (relative == token_of).astype(jnp.bfloat16)
 
     def total(b, carry):
         kept = []
@@ -278,14 +296,16 @@
             sums = sums + lax.dot_general(
                 summing, part, (((1,), (1,)), ((), ())), preferred_element_type=jnp.float32
             )
-        out_ref[pl.ds(pl.multiple_of(b * per_block, per_block), per_block), :] = sums
+        to = pl.multiple_of((b ^ far_me) * per_block, per_block)
+        out_ref[pl.ds(to, per_block), :] = sums
         return carry
 
     lax.fori_loop(0, blocks, total, 0)
 
 
-def score_all(base, token_codes, lengths, gathered, table, residuals, query_rows, token_count):
-    passages, slots, width = residuals.shape
+def score_all(me, token_codes, lengths, gathered, table, residuals, query_rows, token_count):
+    passages, slots = token_codes.shape
+    width = residuals.shape[1]
     targets = gathered.shape[0]
     tokens = passages * slots
     block = min(QUERY_BLOCK, targets * query_rows)
@@ -295,29 +315,27 @@
         out_shape=jax.ShapeDtypeStruct(
             (targets * query_rows // token_count, passages), jnp.float32
         ),
-        in_specs=[SMEM, HBM, HBM, VMEM, VMEM, HBM],
+        in_specs=[SMEM, HBM, HBM, VMEM, VMEM, VMEM],
         out_specs=VMEM,
         scratch_shapes=[
             pltpu.SMEM((tokens,), jnp.int32),
             pltpu.SMEM((passages,), jnp.int32),
             pltpu.SMEM((tokens // CHUNK + slots // CHUNK + GROUP,), jnp.int32),
-            pltpu.VMEM((tokens, width), jnp.bfloat16),
             pltpu.VMEM((GROUP * CHUNK, width), jnp.float32),
-            pltpu.VMEM((GROUP * CHUNK, width), jnp.bfloat16),
             pltpu.VMEM((blocks, width, block), jnp.bfloat16),
             pltpu.VMEM((blocks, 8, block), jnp.float32),
             pltpu.VMEM((blocks, block // 128, (passages + 1) * 8, 128), jnp.float32),
-            pltpu.SemaphoreType.DMA((3,)),
+            pltpu.SemaphoreType.DMA((2,)),
         ],
-        compiler_params=granted(40),
+        compiler_params=granted(8 + 2 * blocks),
         name="score",
     )(
-        base,
+        me,
         pinned(token_codes.reshape(tokens)),
         pinned(lengths),
         gathered,
         pinned(table, pltpu.VMEM),
-        pinned(residuals.reshape(tokens, width)),
+        pinned(residuals, pltpu.VMEM),
     )
 
 
@@ -351,20 +369,33 @@
     )(candidates, pinned(returned, pltpu.VMEM))
 
 
+def gather_relative(own, targets):
+    bits = targets.bit_length() - 1
+    held = own[None, None]
+    for first in range(bits - 1, -1, -1):
+        pairs = [(device, device ^ (1 << first)) for device in range(targets)]
+        received = lax.ppermute(held, ("shard", "sub"), pairs)
+        held = jnp.concatenate([held, received], axis=1)
+        if first > 0:
+            held = held.reshape((-1, 1) + own.shape)
+    return held.reshape((targets,) + own.shape)
+
+
 def body(queries, candidates, token_codes, residuals, lengths, centroids):
     local_queries, token_count, width = queries.shape
     targets = lax.axis_size("shard") * lax.axis_size("sub")
-    passages = token_codes.shape[0]
+    passages, slots = token_codes.shape
     query_rows = local_queries * token_count
     half = lax.axis_index("sub").astype(jnp.int32)
     me = lax.axis_index("shard").astype(jnp.int32) * lax.axis_size("sub") + half
+    half = half.reshape(1)
     other = lax.ppermute(centroids, "sub", [(0, 1), (1, 0)])
-    sent = spread(queries.reshape(query_rows, width), candidates, targets)
-    gathered = lax.all_to_all(sent, ("shard", "sub"), split_axis=0, concat_axis=0, tiled=True)
-    table = widen(half.reshape(1), centroids, other)
-    base = (me * passages).reshape(1)
+    sent = pack(queries.reshape(query_rows, width), candidates)
+    gathered = gather_relative(sent, targets)
+    partial, near = widen_own(half, centroids, residuals.reshape(passages * slots, width))
+    table = widen_other(half, other, partial)
     scores = score_all(
-        base, token_codes, lengths, gathered, table, residuals, query_rows, token_count
+        me.reshape(1), token_codes, lengths, gathered, table, near, query_rows, token_count
     )
     returned = lax.all_to_all(
         scores.reshape(targets, local_queries * passages),

time: 40 us -> 38.9 us (0.972); the launches traced: 39.7 us -> 39.2 us
  local copies, waits for them, and re-layouts: 7.95 us -> 0.04 us
  waiting for transfers between devices: 2.11 us -> 5.86 us
  blocking collectives: 10.5 us -> 12.6 us
  Pallas kernels: 11.7 us -> 12.7 us
  starting transfers between devices: 7.47 us -> 7.91 us
    unnamed x8 -> x2, local copies, waits for them, and re-layouts: 7.95 us -> 0.01 us
    ppermute x0 -> x4, starting transfers between devices: none -> 7.46 us  [gather_relative(): received = lax.ppermute(held, ('shard', 'sub'), pairs)]
    all_to_all x1 -> x0, starting transfers between devices: 7.02 us -> none  [body(): lax.all_to_all(sent, ('shard', 'sub'), split_axis=0, concat_axis=0, tiled...]
    ppermute x0 -> x4, waiting for transfers between devices: none -> 5.86 us  [gather_relative(): received = lax.ppermute(held, ('shard', 'sub'), pairs)]
    all_to_all x1 -> x0, waiting for transfers between devices: 2.11 us -> none  [body(): lax.all_to_all(sent, ('shard', 'sub'), split_axis=0, concat_axis=0, tiled...]
    all_to_all x1, blocking collectives: 10.5 us -> 12.6 us  [body(): lax.all_to_all(scores.reshape(targets, local_queries * passages), ('shard...]
    pallas_call x1, Pallas kernels: 7.26 us -> 8.72 us  [score_all(): pl.pallas_call(functools.partial(score_kernel, token_count, query_rows),...]
    pallas_call x2 -> x3, Pallas kernels: 3.75 us -> 3.27 us  [the longest x1 2.29 us: widen_own(): pl.pallas_call(widen_own_kernel, out_shape=(pltpu.VMEM((2 * half_rows, wi...]
  transfers between devices with their start and end apart: 2 -> 5, of which waited for: 1 -> 3; matrix products, arithmetic and copies ran while one was open for 0% -> 0% of each run, Pallas kernels for 9% -> 8%
where the time goes in v9:
time: 38.9 us; the launch traced here: 39.2 us
  Pallas kernels  12.7 us (33%)
  blocking collectives  12.6 us (32%)
  starting transfers between devices  7.91 us (20%)
  waiting for transfers between devices  5.86 us (15%)
    all_to_all x1, blocking collectives, body(): lax.all_to_all(scores.reshape(targets, local_queries * passages), ('shard...  12.6 us
    pallas_call x1, Pallas kernels, score_all(): pl.pallas_call(functools.partial(score_kernel, token_count, query_rows),...  8.72 us
    ppermute x4, starting transfers between devices, gather_relative(): received = lax.ppermute(held, ('shard', 'sub'), pairs)  7.46 us
    ppermute x4, waiting for transfers between devices, gather_relative(): received = lax.ppermute(held, ('shard', 'sub'), pairs)  5.86 us
    pallas_call x1, Pallas kernels, widen_own(): pl.pallas_call(widen_own_kernel, out_shape=(pltpu.VMEM((2 * half_rows, wi...  2.29 us
  transfers between devices with their start and end apart: 5, of which 3 were waited for; matrix products, arithmetic and copies ran while one was open for 0% of the time, Pallas kernels for 8%

profile of v9, /device:TPU:0, one launch (start us, length us, event | category | flops | bytes accessed | tf_op | source)
XLA Modules:
  0.0 39.2 jit_solution(13093699217835636286)
XLA Ops:
  0.0 0.5 %collective-permute-start.4 = (bf16[8192,128]{1,0:T(8,128)(2,1)}, bf16[8192,128]{1,0:T(8,128)(2,1)S(1)}, u32[]{:S(2)}, u32[]{:S(2)}) collective-permute-start(bf16[8192,128]{1,0:T(8,128)(2,1)} %own_hbm.1), channel_id=1, source_target_pairs={{0,1},{1,0},{2,3},{3,2},{4,5},{5,4},{6,7},{7,6},{8,9},{9,8},{10,11... | collective-permute-start | bytes 6291464 | tf_op jit(solution)/shard_map/ppermute | solution.py:392
  0.5 0.7 %pack.1 = bf16[48,128]{1,0:T(8,128)(2,1)S(1)} custom-call(bf16[32,128]{1,0:T(8,128)(2,1)} %bitcast.26, s32[1,62]{1,0:T(1,128)} %candidates_ref.3), custom_call_target="tpu_custom_call" | custom-call | tf_op jit(solution)/shard_map/pack/pallas_call | solution.py:66
  1.2 3.6 %collective-permute-start = (bf16[1,1,48,128]{3,2,1,0:T(8,128)(2,1)S(1)}, bf16[1,1,48,128]{3,2,1,0:T(8,128)(2,1)S(1)}, u32[]{:S(2)}, u32[]{:S(2)}) collective-permute-start(bf16[1,1,48,128]{3,2,1,0:T(8,128)(2,1)S(1)} %bitcast.16), channel_id=1, source_target_pairs={{0,8},{1,9},{2,10},{3,11},{4,12},{5,13},{6,14},{7,15},{8,0},{9,1},... | collective-permute-start | bytes 36872 | tf_op jit(solution)/shard_map/ppermute | solution.py:377
  4.8 1.7 %collective-permute-done = bf16[1,1,48,128]{3,2,1,0:T(8,128)(2,1)S(1)} collective-permute-done((bf16[1,1,48,128]{3,2,1,0:T(8,128)(2,1)S(1)}, bf16[1,1,48,128]{3,2,1,0:T(8,128)(2,1)S(1)}, u32[]{:S(2)}, u32[]{:S(2)}) %collective-permute-start) | collective-permute-done | bytes 12320 | tf_op jit(solution)/shard_map/ppermute | solution.py:377
  6.4 1.9 %collective-permute-start.1 = (bf16[2,1,48,128]{3,2,0,1:T(8,128)(2,1)S(1)}, bf16[2,1,48,128]{3,2,0,1:T(8,128)(2,1)S(1)}, u32[]{:S(2)}, u32[]{:S(2)}) collective-permute-start(bf16[2,1,48,128]{3,2,0,1:T(8,128)(2,1)S(1)} %maximum_bitcast_fusion), channel_id=1, source_target_pairs={{0,4},{1,5},{2,6},{3,7},{4,0},{5,1},{6,2},{7,3},{8,12},{9,13},{10,... | collective-permute-start | bytes 73736 | tf_op jit(solution)/shard_map/ppermute | solution.py:377
  8.3 1.9 %collective-permute-done.1 = bf16[2,1,48,128]{3,2,0,1:T(8,128)(2,1)S(1)} collective-permute-done((bf16[2,1,48,128]{3,2,0,1:T(8,128)(2,1)S(1)}, bf16[2,1,48,128]{3,2,0,1:T(8,128)(2,1)S(1)}, u32[]{:S(2)}, u32[]{:S(2)}) %collective-permute-start.1) | collective-permute-done | bytes 24608 | tf_op jit(solution)/shard_map/ppermute | solution.py:377
  10.3 1.9 %collective-permute-start.2 = (bf16[4,1,48,128]{3,2,0,1:T(8,128)(2,1)S(1)}, bf16[4,1,48,128]{3,2,0,1:T(8,128)(2,1)S(1)}, u32[]{:S(2)}, u32[]{:S(2)}) collective-permute-start(bf16[4,1,48,128]{3,2,0,1:T(8,128)(2,1)S(1)} %bitcast.23), channel_id=1, source_target_pairs={{0,2},{1,3},{2,0},{3,1},{4,6},{5,7},{6,4},{7,5},{8,10},{9,11},{10,... | collective-permute-start | bytes 147464 | tf_op jit(solution)/shard_map/ppermute | solution.py:377
  12.2 2.3 %collective-permute-done.2 = bf16[4,1,48,128]{3,2,0,1:T(8,128)(2,1)S(1)} collective-permute-done((bf16[4,1,48,128]{3,2,0,1:T(8,128)(2,1)S(1)}, bf16[4,1,48,128]{3,2,0,1:T(8,128)(2,1)S(1)}, u32[]{:S(2)}, u32[]{:S(2)}) %collective-permute-start.2) | collective-permute-done | bytes 49184 | tf_op jit(solution)/shard_map/ppermute | solution.py:377
  14.5 0.1 collective-permute-start.3
  14.5 2.3 %widen_own.1 = (f32[16384,128]{1,0:T(8,128)S(1)}, bf16[8192,128]{1,0:T(8,128)(2,1)S(1)}) custom-call(s32[1]{0:T(128)} %bitcast.8.half_ref, bf16[8192,128]{1,0:T(8,128)(2,1)} %own_hbm.1, bf16[8192,128]{1,0:T(8,128)(2,1)} %bitcast.20), custom_call_target="tpu_custom_call" | custom-call | flops 10000000 | bytes 5000000 | tf_op jit(solution)/shard_map/widen_own/pallas_call | solution.py:97
  16.8 0.0 collective-permute-done.3
  16.9 0.0 collective-permute-done.4.other_ref
  16.9 0.3 widen_other.1.table
  17.2 0.0 copy-start
  17.2 8.7 %score.1 = f32[16,64]{1,0:T(8,128)S(1)} custom-call(s32[1]{0:T(128)} %bitcast.me_ref, s32[8192]{0:T(1024)} %bitcast.25, s32[64]{0:T(128)} %lengths_hbm.1, bf16[16,48,128]{2,1,0:T(8,128)(2,1)S(1)} %bitcast.15, f32[16384,128]{1,0:T(8,128)S(1)} %widen_other.1.table, bf16[8192,128]{1,0:T(8,128)(2,1)S(1)} %get-tuple-element.8.residuals), custom_call_target="tpu_custom_call" | custom-call | tf_op jit(solution)/shard_map/score/pallas_call | solution.py:313
  25.9 12.6 %all_to_all.11 = f32[16,1,64]{2,1,0:T(1,128)S(1)} all-to-all(f32[16,1,64]{2,1,0:T(1,128)S(1)} %bitcast.18), channel_id=1, replica_groups=mesh['groups'=2,'shard'=8,'sub'=2] {'shard','sub'}, dimensions={0} | all-to-all | bytes 8192 | tf_op jit(solution)/shard_map/all_to_all | solution.py:400
  38.5 0.0 copy-done
  38.5 0.7 %pick.1 = f32[1,62]{1,0:T(1,128)} custom-call(s32[1,62]{1,0:T(1,128)S(1)} %copy-done, f32[16,64]{1,0:T(8,128)S(1)} %bitcast.19), custom_call_target="tpu_custom_call" | custom-call | tf_op jit(solution)/shard_map/pick/pallas_call | solution.py:362
  (7 shorter events, 0.1 us)
Async XLA Ops:
  0.0 16.9 %collective-permute-start.4 = (bf16[8192,128]{1,0:T(8,128)(2,1)}, bf16[8192,128]{1,0:T(8,128)(2,1)S(1)}, u32[]{:S(2)}, u32[]{:S(2)}) collective-permute-start(bf16[8192,128]{1,0:T(8,128)(2,1)} %own_hbm.1), channel_id=1, source_target_pairs={{0,1},{1,0},{2,3},{3,2},{4,5},{5,4},{6,7},{7,6},{8,9},{9,8},{10,11... | collective-permute-start | bytes 6291464 | tf_op jit(solution)/shard_map/ppermute | solution.py:392
  1.2 5.3 %collective-permute-start = (bf16[1,1,48,128]{3,2,1,0:T(8,128)(2,1)S(1)}, bf16[1,1,48,128]{3,2,1,0:T(8,128)(2,1)S(1)}, u32[]{:S(2)}, u32[]{:S(2)}) collective-permute-start(bf16[1,1,48,128]{3,2,1,0:T(8,128)(2,1)S(1)} %bitcast.16), channel_id=1, source_target_pairs={{0,8},{1,9},{2,10},{3,11},{4,12},{5,13},{6,14},{7,15},{8,0},{9,1},... | collective-permute-start | bytes 36872 | tf_op jit(solution)/shard_map/ppermute | solution.py:377
  6.4 3.8 %collective-permute-start.1 = (bf16[2,1,48,128]{3,2,0,1:T(8,128)(2,1)S(1)}, bf16[2,1,48,128]{3,2,0,1:T(8,128)(2,1)S(1)}, u32[]{:S(2)}, u32[]{:S(2)}) collective-permute-start(bf16[2,1,48,128]{3,2,0,1:T(8,128)(2,1)S(1)} %maximum_bitcast_fusion), channel_id=1, source_target_pairs={{0,4},{1,5},{2,6},{3,7},{4,0},{5,1},{6,2},{7,3},{8,12},{9,13},{10,... | collective-permute-start | bytes 73736 | tf_op jit(solution)/shard_map/ppermute | solution.py:377
  10.3 4.2 %collective-permute-start.2 = (bf16[4,1,48,128]{3,2,0,1:T(8,128)(2,1)S(1)}, bf16[4,1,48,128]{3,2,0,1:T(8,128)(2,1)S(1)}, u32[]{:S(2)}, u32[]{:S(2)}) collective-permute-start(bf16[4,1,48,128]{3,2,0,1:T(8,128)(2,1)S(1)} %bitcast.23), channel_id=1, source_target_pairs={{0,2},{1,3},{2,0},{3,1},{4,6},{5,7},{6,4},{7,5},{8,10},{9,11},{10,... | collective-permute-start | bytes 147464 | tf_op jit(solution)/shard_map/ppermute | solution.py:377
  14.5 2.4 %collective-permute-start.3 = (bf16[8,1,48,128]{3,2,0,1:T(8,128)(2,1)S(1)}, bf16[8,1,48,128]{3,2,0,1:T(8,128)(2,1)S(1)}, u32[]{:S(2)}, u32[]{:S(2)}) collective-permute-start(bf16[8,1,48,128]{3,2,0,1:T(8,128)(2,1)S(1)} %bitcast.21), channel_id=1, source_target_pairs={{0,1},{1,0},{2,3},{3,2},{4,5},{5,4},{6,7},{7,6},{8,9},{9,8},{10,11... | collective-permute-start | bytes 294920 | tf_op jit(solution)/shard_map/ppermute | solution.py:377
  17.2 21.3 %copy-start = (s32[1,62]{1,0:T(1,128)S(1)}, s32[1,62]{1,0:T(1,128)}, u32[]{:S(2)}) copy-start(s32[1,62]{1,0:T(1,128)} %candidates_ref.3) | copy-start | bytes 748

commit v10 on v8

--- a/solution.py
+++ b/solution.py
@@ -86,6 +86,7 @@
     at_ref,
     codes_ref,
     lengths_ref,
+    live_ref,
     rows,
     sems,
 ):
@@ -101,11 +102,13 @@
     def listing(p, chunks):
         for k in range(slots // CHUNK):
             at_ref[chunks + k] = p * slots + k * CHUNK
+            live_ref[chunks + k] = lengths_ref[p] - k * CHUNK
         return chunks + quotient(lengths_ref[p] + CHUNK - 1, CHUNK)
 
     chunks = lax.fori_loop(0, passages, listing, 0, unroll=4)
     for k in range(SCORE_GROUP):
         at_ref[chunks + k] = tokens
+        live_ref[chunks + k] = 0
     groups = quotient(chunks + GROUP - 1, GROUP)
     at_ref[at_ref.shape[0] - 1] = chunks
     codes_copy.wait()
@@ -117,16 +120,15 @@
     def fetch(g, k):
         at = jnp.minimum(at_ref[g * GROUP + k], tokens - CHUNK)
         codes = codes_ref.at[pl.ds(at, CHUNK)]
+        fetched = [table_single[codes[j]] for j in range(CHUNK)]
         for j in range(CHUNK):
-            rows_single[k * CHUNK + j] = table_single[codes[j]]
+            rows_single[k * CHUNK + j] = fetched[j]
 
     def finish(g, k):
         at = jnp.minimum(at_ref[g * GROUP + k], tokens - CHUNK)
-        p = quotient(at, slots)
-        live = lengths_ref[p] - (at - p * slots)
         near = residuals[pl.ds(pl.multiple_of(at, CHUNK), CHUNK), :]
         vectors = rows[pl.ds(k * CHUNK, CHUNK), :] + near.astype(jnp.float32)
-        vectors = jnp.where(slot_numbers < live, vectors, vectors[0:1, :])
+        vectors = jnp.where(slot_numbers < live_ref[g * GROUP + k], vectors, vectors[0:1, :])
         return normalized(vectors)
 
     def keep(g, done):
@@ -164,6 +166,7 @@
         scratch_shapes=[
             pltpu.SMEM((tokens,), jnp.int32),
             pltpu.SMEM((passages,), jnp.int32),
+            pltpu.SMEM((most,), jnp.int32),
             pltpu.VMEM((GROUP * CHUNK, width), jnp.float32),
             pltpu.SemaphoreType.DMA((2,)),
         ],

time: 36.4 us -> 37.6 us (1.033)
  Pallas kernels: 14.3 us -> 15.4 us
    pallas_call x1, Pallas kernels: 7.71 us -> 8.54 us  [decode_all(): pl.pallas_call(decode_kernel, out_shape=(jax.ShapeDtypeStruct((most * CHU...]
  transfers between devices with their start and end apart: 2 -> 2, of which waited for: 0 -> 0; matrix products, arithmetic and copies ran while one was open for 4% -> 4% of each run, Pallas kernels for 28% -> 29%
where the time goes in v10:
time: 37.6 us; the launch traced here: 37.2 us
  Pallas kernels  15.4 us (41%)
  blocking collectives  12.9 us (34%)
  starting transfers between devices  7.47 us (20%)
  local copies, waits for them, and re-layouts  1.36 us (4%)
    all_to_all x1, blocking collectives, body(): lax.all_to_all(scores.reshape(targets, local_queries * passages), ('shard...  12.9 us
    pallas_call x1, Pallas kernels, decode_all(): pl.pallas_call(decode_kernel, out_shape=(jax.ShapeDtypeStruct((most * CHU...  8.54 us
    all_to_all x1, starting transfers between devices, body(): lax.all_to_all(sent, ('shard', 'sub'), split_axis=0, concat_axis=0, tiled...  7.02 us
    pallas_call x1, Pallas kernels, score_all(): pl.pallas_call(functools.partial(score_kernel, token_count, slots), out_s...  3.88 us
    pallas_call x1, Pallas kernels, widen(): pl.pallas_call(widen_kernel, out_shape=(pltpu.VMEM((2 * half_rows, width)...  2.29 us
    broadcast_in_dim x1, local copies, waits for them, and re-layouts, body(): sent = jnp.broadcast_to(own_rows, (targets,) + own_rows.shape[1:])  1.36 us
  transfers between devices with their start and end apart: 2, of which 0 were waited for; matrix products, arithmetic and copies ran while one was open for 4% of the time, Pallas kernels for 29%

profile of v10, /device:TPU:0, one launch (start us, length us, event | category | flops | bytes accessed | tf_op | source)
XLA Modules:
  0.0 37.2 jit_solution(4581788165415786219)
XLA Ops:
  0.0 0.5 %collective-permute-start = (bf16[8192,128]{1,0:T(8,128)(2,1)}, bf16[8192,128]{1,0:T(8,128)(2,1)S(1)}, u32[]{:S(2)}, u32[]{:S(2)}) collective-permute-start(bf16[8192,128]{1,0:T(8,128)(2,1)} %own_hbm.1), channel_id=1, source_target_pairs={{0,1},{1,0},{2,3},{3,2},{4,5},{5,4},{6,7},{7,6},{8,9},{9,8},{10,11... | collective-permute-start | bytes 6291464 | tf_op jit(solution)/shard_map/ppermute | solution.py:288
  0.5 1.4 %broadcast_in_dim.8 = bf16[16,32,128]{2,1,0:T(8,128)(2,1)} broadcast(bf16[32,128]{1,0:T(8,128)(2,1)} %bitcast.14), dimensions={1,2} | broadcast | bytes 139264 | tf_op jit(solution)/shard_map/broadcast_in_dim | solution.py:290
  1.8 7.0 %all-to-all-start = ((bf16[16,32,128]{2,1,0:T(8,128)(2,1)}), bf16[16,32,128]{2,1,0:T(8,128)(2,1)S(1)}, u32[]{:S(2)}, u32[]{:S(2)}) async-start(bf16[16,32,128]{2,1,0:T(8,128)(2,1)} %broadcast_in_dim.8), calls=%async_computation | async-start | bytes 262144 | tf_op jit(solution)/shard_map/all_to_all | solution.py:291
  8.8 0.0 collective-permute-done.other_ref
  8.9 2.3 %widen.1 = (f32[16384,128]{1,0:T(8,128)S(1)}, bf16[8192,128]{1,0:T(8,128)(2,1)S(1)}) custom-call(s32[1]{0:T(128)} %bitcast.1.half_ref, bf16[8192,128]{1,0:T(8,128)(2,1)} %own_hbm.1, bf16[8192,128]{1,0:T(8,128)(2,1)S(1)} %collective-permute-done.other_ref, bf16[8192,128]{1,0:T(8,128)(2,1)} %bitcast.12), custom_call_target="tpu_custom_call" | custom-call | flops 10000000 | bytes 10000000 | tf_op jit(solution)/shard_map/widen/pallas_call | solution.py:62
  11.2 8.5 %decode.1 = (bf16[9216,128]{1,0:T(8,128)(2,1)S(1)}, s32[577]{0:T(1024)S(1)}) custom-call(s32[8192]{0:T(1024)} %bitcast.13, s32[64]{0:T(128)} %lengths_hbm.1, f32[16384,128]{1,0:T(8,128)S(1)} %get-tuple-element.9.table, bf16[8192,128]{1,0:T(8,128)(2,1)S(1)} %get-tuple-element.10.residuals), custom_call_target="tpu_custom_call" | custom-call | flops 10000000 | bytes 40000000 | tf_op jit(solution)/shard_map/decode/pallas_call | solution.py:158
  19.7 0.0 copy-start
  19.7 0.0 all-to-all-done
  19.7 3.9 %score.1 = f32[16,64]{1,0:T(8,128)S(1)} custom-call(s32[577]{0:T(1024)S(1)} %get-tuple-element.11.at_ref, bf16[512,128]{1,0:T(8,128)(2,1)S(1)} %bitcast.9, bf16[9216,128]{1,0:T(8,128)(2,1)S(1)} %get-tuple-element.12.embedded), custom_call_target="tpu_custom_call" | custom-call | tf_op jit(solution)/shard_map/score/pallas_call | solution.py:239
  23.6 12.9 %all_to_all.16 = f32[16,1,64]{2,1,0:T(1,128)S(1)} all-to-all(f32[16,1,64]{2,1,0:T(1,128)S(1)} %bitcast.10), channel_id=1, replica_groups=mesh['groups'=2,'shard'=8,'sub'=2] {'shard','sub'}, dimensions={0} | all-to-all | bytes 8192 | tf_op jit(solution)/shard_map/all_to_all | solution.py:297
  36.5 0.0 copy-done
  36.5 0.7 %pick.1 = f32[1,62]{1,0:T(1,128)} custom-call(s32[1,62]{1,0:T(1,128)S(1)} %copy-done, f32[16,64]{1,0:T(8,128)S(1)} %bitcast.11), custom_call_target="tpu_custom_call" | custom-call | tf_op jit(solution)/shard_map/pick/pallas_call | solution.py:273
Async XLA Ops:
  0.0 8.8 %collective-permute-start = (bf16[8192,128]{1,0:T(8,128)(2,1)}, bf16[8192,128]{1,0:T(8,128)(2,1)S(1)}, u32[]{:S(2)}, u32[]{:S(2)}) collective-permute-start(bf16[8192,128]{1,0:T(8,128)(2,1)} %own_hbm.1), channel_id=1, source_target_pairs={{0,1},{1,0},{2,3},{3,2},{4,5},{5,4},{6,7},{7,6},{8,9},{9,8},{10,11... | collective-permute-start | bytes 6291464 | tf_op jit(solution)/shard_map/ppermute | solution.py:288
  1.8 17.9 %all-to-all-start = ((bf16[16,32,128]{2,1,0:T(8,128)(2,1)}), bf16[16,32,128]{2,1,0:T(8,128)(2,1)S(1)}, u32[]{:S(2)}, u32[]{:S(2)}) async-start(bf16[16,32,128]{2,1,0:T(8,128)(2,1)} %broadcast_in_dim.8), calls=%async_computation | async-start | bytes 262144 | tf_op jit(solution)/shard_map/all_to_all | solution.py:291
  19.7 16.8 %copy-start = (s32[1,62]{1,0:T(1,128)S(1)}, s32[1,62]{1,0:T(1,128)}, u32[]{:S(2)}) copy-start(s32[1,62]{1,0:T(1,128)} %candidates_ref.1) | copy-start | bytes 748

commit v11 on v8

--- a/solution.py
+++ b/solution.py
@@ -36,154 +36,217 @@
     return pltpu.CompilerParams(vmem_limit_bytes=mebibytes * 1024 * 1024)
 
 
-def widen_kernel(half_ref, own_hbm, other_ref, residuals_hbm, table, residuals, staged, sems):
+def spread_kernel(queries_ref, out_ref):
+    queries = queries_ref[...]
+
+    def copy(t, carry):
+        out_ref[t] = queries
+        return carry
+
+    lax.fori_loop(0, out_ref.shape[0], copy, 0, unroll=8)
+
+
+def spread(queries, targets):
+    return pl.pallas_call(
+        spread_kernel,
+        out_shape=pltpu.VMEM((targets,) + queries.shape, jnp.bfloat16),
+        in_specs=[VMEM],
+        out_specs=VMEM,
+        compiler_params=granted(4),
+        name="spread",
+    )(pinned(queries))
+
+
+def widen_kernel(
+    slots,
+    half_ref,
+    lengths_hbm,
+    own_hbm,
+    other_ref,
+    table,
+    starts_hbm,
+    lives_hbm,
+    lengths_ref,
+    starts_ref,
+    lives_ref,
+    staged,
+    sems,
+):
+    passages = lengths_ref.shape[0]
     half_rows = own_hbm.shape[0]
     half = half_ref[0]
+    lengths_copy = pltpu.make_async_copy(lengths_hbm, lengths_ref, sems.at[0])
+    lengths_copy.start()
     piece = half_rows // PIECES
     copies = []
     for k in range(PIECES):
         at = pl.ds(k * piece, piece)
-        copies.append(pltpu.make_async_copy(own_hbm.at[at], staged.at[at], sems.at[k]))
+        copies.append(pltpu.make_async_copy(own_hbm.at[at], staged.at[at], sems.at[3 + k]))
         copies[-1].start()
-    residual_copy = pltpu.make_async_copy(residuals_hbm, residuals, sems.at[PIECES])
-    residual_copy.start()
-    for source, ref in enumerate((other_ref, staged)):
-        base = (1 - half if source == 0 else half) * half_rows
-        for k in range(PIECES):
-            if source == 1:
-                copies[k].wait()
-            to = pl.ds(pl.multiple_of(base + k * piece, piece), piece)
-            table[to, :] = ref[pl.ds(k * piece, piece), :].astype(jnp.float32)
-    residual_copy.wait()
-
-
-def widen(half, own, other, residuals):
+
+    def widened(ref, base, k):
+        to = pl.ds(pl.multiple_of(base + k * piece, piece), piece)
+        table[to, :] = ref[pl.ds(k * piece, piece), :].astype(jnp.float32)
+
+    for k in range(PIECES):
+        widened(other_ref, (1 - half) * half_rows, k)
+    lengths_copy.wait()
+
+    def listing(p, chunks):
+        length = lengths_ref[p]
+        for k in range(slots // CHUNK):
+            starts_ref[chunks + k] = p * slots + k * CHUNK
+            lives_ref[chunks + k] = length - k * CHUNK
+        return chunks + quotient(length + CHUNK - 1, CHUNK)
+
+    chunks = lax.fori_loop(0, passages, listing, 0, unroll=4)
+    for k in range(SCORE_GROUP):
+        starts_ref[chunks + k] = passages * slots
+        lives_ref[chunks + k] = 0
+    starts_ref[starts_ref.shape[0] - 1] = chunks
+    starts_copy = pltpu.make_async_copy(starts_ref, starts_hbm, sems.at[1])
+    lives_copy = pltpu.make_async_copy(lives_ref, lives_hbm, sems.at[2])
+    starts_copy.start()
+    lives_copy.start()
+    for k in range(PIECES):
+        copies[k].wait()
+        widened(staged, half * half_rows, k)
+    starts_copy.wait()
+    lives_copy.wait()
+
+
+def widen(half, lengths, own, other, slots):
     half_rows, width = own.shape
-    return pl.pallas_call(
-        widen_kernel,
-        out_shape=(
-            pltpu.VMEM((2 * half_rows, width), jnp.float32),
-            pltpu.VMEM(residuals.shape, jnp.bfloat16),
-        ),
-        in_specs=[SMEM, HBM, VMEM, HBM],
-        out_specs=(VMEM, VMEM),
+    most = lengths.shape[0] * (slots // CHUNK) + SCORE_GROUP + slots // CHUNK
+    most = -(-most // 128) * 128
+    listed = pltpu.HBM((most,), jnp.int32)
+    return pl.pallas_call(
+        functools.partial(widen_kernel, slots),
+        out_shape=(pltpu.VMEM((2 * half_rows, width), jnp.float32), listed, listed),
+        in_specs=[SMEM, HBM, HBM, VMEM],
+        out_specs=(VMEM, HBM, HBM),
         scratch_shapes=[
+            pltpu.SMEM(lengths.shape, jnp.int32),
+            pltpu.SMEM((most,), jnp.int32),
+            pltpu.SMEM((most,), jnp.int32),
             pltpu.VMEM((half_rows, width), jnp.bfloat16),
-            pltpu.SemaphoreType.DMA((PIECES + 1,)),
+            pltpu.SemaphoreType.DMA((3 + PIECES,)),
         ],
         compiler_params=granted(4),
         cost_estimate=pl.CostEstimate(flops=10**7, bytes_accessed=10**7, transcendentals=0),
         name="widen",
-    )(half, pinned(own), pinned(other, pltpu.VMEM), pinned(residuals))
+    )(half, pinned(lengths), pinned(own), pinned(other, pltpu.VMEM))
 
 
 def decode_kernel(
     codes_hbm,
-    lengths_hbm,
+    starts_hbm,
+    lives_hbm,
+    residuals_hbm,
     table,
+    embedded,
+    codes_ref,
+    starts_ref,
+    lives_ref,
     residuals,
-    embedded,
-    at_ref,
-    codes_ref,
-    lengths_ref,
     rows,
     sems,
 ):
-    passages = lengths_ref.shape[0]
     tokens, width = residuals.shape
-    slots = tokens // passages
-    lengths_copy = pltpu.make_async_copy(lengths_hbm, lengths_ref, sems.at[0])
-    codes_copy = pltpu.make_async_copy(codes_hbm, codes_ref, sems.at[1])
-    lengths_copy.start()
-    codes_copy.start()
-    lengths_copy.wait()
-
-    def listing(p, chunks):
-        for k in range(slots // CHUNK):
-            at_ref[chunks + k] = p * slots + k * CHUNK
-        return chunks + quotient(lengths_ref[p] + CHUNK - 1, CHUNK)
-
-    chunks = lax.fori_loop(0, passages, listing, 0, unroll=4)
-    for k in range(SCORE_GROUP):
-        at_ref[chunks + k] = tokens
-    groups = quotient(chunks + GROUP - 1, GROUP)
-    at_ref[at_ref.shape[0] - 1] = chunks
-    codes_copy.wait()
+    moves = []
+    pairs = ((starts_hbm, starts_ref), (lives_hbm, lives_ref), (codes_hbm, codes_ref))
+    for k, (source, to) in enumerate(pairs):
+        moves.append(pltpu.make_async_copy(source, to, sems.at[k]))
+        moves[-1].start()
+    piece = tokens // PIECES
+    copies = []
+    for k in range(PIECES):
+        at = pl.ds(k * piece, piece)
+        copies.append(
+            pltpu.make_async_copy(residuals_hbm.at[at], residuals.at[at], sems.at[3 + k])
+        )
+        copies[-1].start()
 
     slot_numbers = lax.broadcasted_iota(jnp.int32, (CHUNK, width), 0)
     table_single = table.reshape(table.shape[0], 1, width)
     rows_single = rows.reshape(rows.shape[0], 1, width)
 
-    def fetch(g, k):
-        at = jnp.minimum(at_ref[g * GROUP + k], tokens - CHUNK)
-        codes = codes_ref.at[pl.ds(at, CHUNK)]
-        for j in range(CHUNK):
-            rows_single[k * CHUNK + j] = table_single[codes[j]]
-
-    def finish(g, k):
-        at = jnp.minimum(at_ref[g * GROUP + k], tokens - CHUNK)
-        p = quotient(at, slots)
-        live = lengths_ref[p] - (at - p * slots)
-        near = residuals[pl.ds(pl.multiple_of(at, CHUNK), CHUNK), :]
-        vectors = rows[pl.ds(k * CHUNK, CHUNK), :] + near.astype(jnp.float32)
-        vectors = jnp.where(slot_numbers < live, vectors, vectors[0:1, :])
-        return normalized(vectors)
+    def fetch(g):
+        for k in range(GROUP):
+            at = jnp.minimum(starts_ref[g * GROUP + k], tokens - CHUNK)
+            codes = codes_ref.at[pl.ds(at, CHUNK)]
+            fetched = [table_single[codes[j]] for j in range(CHUNK)]
+            for j in range(CHUNK):
+                rows_single[k * CHUNK + j] = fetched[j]
+
+    def finish(g):
+        summed = []
+        for k in range(GROUP):
+            at = jnp.minimum(starts_ref[g * GROUP + k], tokens - CHUNK)
+            near = residuals[pl.ds(pl.multiple_of(at, CHUNK), CHUNK), :]
+            vectors = rows[pl.ds(k * CHUNK, CHUNK), :] + near.astype(jnp.float32)
+            live = slot_numbers < lives_ref[g * GROUP + k]
+            summed.append(jnp.where(live, vectors, vectors[0:1, :]))
+        return normalized(jnp.concatenate(summed, axis=0))
 
     def keep(g, done):
-        for k in range(GROUP):
-            start = pl.multiple_of((g * GROUP + k) * CHUNK, CHUNK)
-            embedded[pl.ds(start, CHUNK), :] = done[k]
-
-    for k in range(GROUP):
-        fetch(0, k)
+        size = GROUP * CHUNK
+        embedded[pl.ds(pl.multiple_of(g * size, size), size), :] = done
+
+    for move in moves:
+        move.wait()
+    groups = quotient(starts_ref[starts_ref.shape[0] - 1] + GROUP - 1, GROUP)
+    fetch(0)
+    for copy in copies:
+        copy.wait()
 
     def decode(g, carry):
-        done = []
-        for k in range(GROUP):
-            done.append(finish(g - 1, k))
-            fetch(g, k)
+        done = finish(g - 1)
+        fetch(g)
         keep(g - 1, done)
         return carry
 
     lax.fori_loop(1, groups, decode, 0)
-    keep(groups - 1, [finish(groups - 1, k) for k in range(GROUP)])
-
-
-def decode_all(token_codes, lengths, table, residuals):
-    passages, slots = token_codes.shape
+    keep(groups - 1, finish(groups - 1))
+
+
+def decode_all(token_codes, starts, lives, residuals, table):
     tokens, width = residuals.shape
-    most = tokens // CHUNK + 2 * SCORE_GROUP
+    rounding = SCORE_GROUP * CHUNK
     return pl.pallas_call(
         decode_kernel,
-        out_shape=(
-            jax.ShapeDtypeStruct((most * CHUNK, width), jnp.bfloat16),
-            jax.ShapeDtypeStruct((most + 1,), jnp.int32),
-        ),
-        in_specs=[HBM, HBM, VMEM, VMEM],
-        out_specs=(VMEM, SMEM),
+        out_shape=jax.ShapeDtypeStruct((-(-tokens // rounding) * rounding, width), jnp.bfloat16),
+        in_specs=[HBM, HBM, HBM, HBM, VMEM],
+        out_specs=VMEM,
         scratch_shapes=[
             pltpu.SMEM((tokens,), jnp.int32),
-            pltpu.SMEM((passages,), jnp.int32),
+            pltpu.SMEM(starts.shape, jnp.int32),
+            pltpu.SMEM(lives.shape, jnp.int32),
+            pltpu.VMEM((tokens, width), jnp.bfloat16),
             pltpu.VMEM((GROUP * CHUNK, width), jnp.float32),
-            pltpu.SemaphoreType.DMA((2,)),
+            pltpu.SemaphoreType.DMA((3 + PIECES,)),
         ],
-        compiler_params=granted(4),
+        compiler_params=granted(6),
         cost_estimate=pl.CostEstimate(flops=10**7, bytes_accessed=40 * 10**6, transcendentals=0),
         name="decode",
     )(
         pinned(token_codes.reshape(tokens)),
-        pinned(lengths),
+        pinned(starts),
+        pinned(lives),
+        pinned(residuals),
         pinned(table, pltpu.VMEM),
-        pinned(residuals, pltpu.VMEM),
     )
 
 
-def score_kernel(token_count, slots, at_ref, queries_ref, embedded, out_ref, turned, largest):
+def score_kernel(
+    token_count, slots, starts_hbm, queries_ref, embedded, out_ref, at_ref, turned, largest, sem
+):
+    starts_copy = pltpu.make_async_copy(starts_hbm, at_ref, sem)
+    starts_copy.start()
     passages = out_ref.shape[1]
     query_tokens = queries_ref.shape[0]
     block = min(QUERY_BLOCK, query_tokens)
     blocks = query_tokens // block
-    groups = quotient(at_ref[at_ref.shape[0] - 1] + SCORE_GROUP - 1, SCORE_GROUP)
     per_block = block // token_count
     owner = lax.broadcasted_iota(jnp.int32, (per_block, block), 0)
     token_of = lax.broadcasted_iota(jnp.int32, (per_block, block), 1) // token_count
@@ -208,6 +271,11 @@
                     largest[lane, pl.ds(at, 8), :] = so_far[:, lane * 128 : (lane + 1) * 128]
             return so_far
 
+        @pl.when(b == 0)
+        def arrived():
+            starts_copy.wait()
+
+        groups = quotient(at_ref[at_ref.shape[0] - 1] + SCORE_GROUP - 1, SCORE_GROUP)
         lax.fori_loop(0, groups, score, jnp.zeros((8, block), jnp.float32))
         kept = []
         for lane in range(block // 128):
@@ -236,15 +304,17 @@
     return pl.pallas_call(
         functools.partial(score_kernel, token_count, slots),
         out_shape=jax.ShapeDtypeStruct((query_tokens // token_count, passages), jnp.float32),
-        in_specs=[SMEM, VMEM, VMEM],
+        in_specs=[HBM, VMEM, VMEM],
         out_specs=VMEM,
         scratch_shapes=[
+            pltpu.SMEM(starts.shape, jnp.int32),
             pltpu.VMEM((width, block), jnp.bfloat16),
             pltpu.VMEM((block // 128, (passages + 1) * 8, 128), jnp.float32),
+            pltpu.SemaphoreType.DMA,
         ],
         compiler_params=granted(8 + 2 * blocks),
         name="score",
-    )(starts, query_rows, embedded)
+    )(pinned(starts), query_rows, embedded)
 
 
 def pick_kernel(passages, candidates_ref, returned_ref, out_ref):
@@ -283,13 +353,12 @@
     passages, slots = token_codes.shape
     half = lax.axis_index("sub").astype(jnp.int32)
     other = lax.ppermute(centroids, "sub", [(0, 1), (1, 0)])
-    own_rows = queries.reshape(1, local_queries * token_count, width)
-    sent = jnp.broadcast_to(own_rows, (targets,) + own_rows.shape[1:])
+    sent = spread(queries.reshape(local_queries * token_count, width), targets)
     gathered = lax.all_to_all(sent, ("shard", "sub"), split_axis=0, concat_axis=0, tiled=True)
     query_rows = gathered.reshape(targets * local_queries * token_count, width)
     flat = residuals.reshape(passages * slots, width)
-    table, near = widen(half.reshape(1), centroids, other, flat)
-    embedded, starts = decode_all(token_codes, lengths, table, near)
+    table, starts, lives = widen(half.reshape(1), lengths, centroids, other, slots)
+    embedded = decode_all(token_codes, starts, lives, flat, table)
     scores = score_all(starts, query_rows, embedded, passages, slots, token_count)
     returned = lax.all_to_all(
         scores.reshape(targets, local_queries * passages),

time: 36.4 us -> 36.1 us (level)
  Pallas kernels: 14.3 us -> 15.9 us
  local copies, waits for them, and re-layouts: 1.36 us -> 0.01 us
  blocking collectives: 12.9 us -> 12 us
    pallas_call x2 -> x3, Pallas kernels: 10 us -> 11.4 us  [the longest x1 7.72 us: decode_all(): pl.pallas_call(decode_kernel, out_shape=jax.ShapeDtypeStruct((-(-tokens /...]
    broadcast_in_dim x1 -> x0, local copies, waits for them, and re-layouts: 1.36 us -> none  [body(): sent = jnp.broadcast_to(own_rows, (targets,) + own_rows.shape[1:])]
    all_to_all x1, blocking collectives: 12.9 us -> 12 us  [body(): lax.all_to_all(scores.reshape(targets, local_queries * passages), ('shard...]
  transfers between devices with their start and end apart: 2 -> 2, of which waited for: 0 -> 0; matrix products, arithmetic and copies ran while one was open for 4% -> 0% of each run, Pallas kernels for 28% -> 32%
where the time goes in v11:
time: 36.1 us; the launch traced here: 35.5 us
  Pallas kernels  15.9 us (44%)
  blocking collectives  12 us (33%)
  starting transfers between devices  7.47 us (21%)
    all_to_all x1, blocking collectives, body(): lax.all_to_all(scores.reshape(targets, local_queries * passages), ('shard...  12 us
    pallas_call x1, Pallas kernels, decode_all(): pl.pallas_call(decode_kernel, out_shape=jax.ShapeDtypeStruct((-(-tokens /...  7.72 us
    all_to_all x1, starting transfers between devices, body(): lax.all_to_all(sent, ('shard', 'sub'), split_axis=0, concat_axis=0, tiled...  7.02 us
    pallas_call x1, Pallas kernels, score_all(): pl.pallas_call(functools.partial(score_kernel, token_count, slots), out_s...  3.87 us
    pallas_call x1, Pallas kernels, widen(): pl.pallas_call(functools.partial(widen_kernel, slots), out_shape=(pltpu.V...  2.33 us
    pallas_call x1, Pallas kernels, spread(): pl.pallas_call(spread_kernel, out_shape=pltpu.VMEM((targets,) + queries.s...  1.37 us
  transfers between devices with their start and end apart: 2, of which 0 were waited for; matrix products, arithmetic and copies ran while one was open for 0% of the time, Pallas kernels for 32%

profile of v11, /device:TPU:0, one launch (start us, length us, event | category | flops | bytes accessed | tf_op | source)
XLA Modules:
  0.0 35.5 jit_solution(6040141315745989160)
XLA Ops:
  0.0 0.5 %collective-permute-start = (bf16[8192,128]{1,0:T(8,128)(2,1)}, bf16[8192,128]{1,0:T(8,128)(2,1)S(1)}, u32[]{:S(2)}, u32[]{:S(2)}) collective-permute-start(bf16[8192,128]{1,0:T(8,128)(2,1)} %own_hbm.1), channel_id=1, source_target_pairs={{0,1},{1,0},{2,3},{3,2},{4,5},{5,4},{6,7},{7,6},{8,9},{9,8},{10,11... | collective-permute-start | bytes 6291464 | tf_op jit(solution)/shard_map/ppermute | solution.py:355
  0.5 1.4 %spread.1 = bf16[16,32,128]{2,1,0:T(8,128)(2,1)} custom-call(bf16[32,128]{1,0:T(8,128)(2,1)} %bitcast.14), custom_call_target="tpu_custom_call" | custom-call | tf_op jit(solution)/shard_map/spread/pallas_call | solution.py:50
  1.8 7.0 %all-to-all-start = ((bf16[16,32,128]{2,1,0:T(8,128)(2,1)}), bf16[16,32,128]{2,1,0:T(8,128)(2,1)S(1)}, u32[]{:S(2)}, u32[]{:S(2)}) async-start(bf16[16,32,128]{2,1,0:T(8,128)(2,1)} %spread.1), calls=%async_computation | async-start | bytes 262144 | tf_op jit(solution)/shard_map/all_to_all | solution.py:357
  8.8 0.0 collective-permute-done.other_ref
  8.9 2.3 %widen.1 = (f32[16384,128]{1,0:T(8,128)S(1)}, s32[640]{0:T(1024)}, s32[640]{0:T(1024)}) custom-call(s32[1]{0:T(128)} %bitcast.half_ref, s32[64]{0:T(128)} %lengths_hbm.1, bf16[8192,128]{1,0:T(8,128)(2,1)} %own_hbm.1, bf16[8192,128]{1,0:T(8,128)(2,1)S(1)} %collective-permute-done.other_ref), custom_call_target="tpu_custom_call" | custom-call | flops 10000000 | bytes 10000000 | tf_op jit(solution)/shard_map/widen/pallas_call | solution.py:123
  11.2 7.7 %decode.1.embedded = bf16[8192,128]{1,0:T(8,128)(2,1)S(1)} custom-call(s32[8192]{0:T(1024)} %bitcast.13, s32[640]{0:T(1024)} %get-tuple-element.8.starts_hbm, s32[640]{0:T(1024)} %get-tuple-element.9.lives_hbm, bf16[8192,128]{1,0:T(8,128)(2,1)} %bitcast.12, f32[16384,128]{1,0:T(8,128)S(1)} %get-tuple-element.10.table), custom_call_target="tpu_custom_call" | custom-call | flops 10000000 | bytes 40000000 | tf_op jit(solution)/shard_map/decode/pallas_call | solution.py:216
  18.9 0.0 copy-start
  18.9 0.0 all-to-all-done
  18.9 3.9 %score.1 = f32[16,64]{1,0:T(8,128)S(1)} custom-call(s32[640]{0:T(1024)} %get-tuple-element.8.starts_hbm, bf16[512,128]{1,0:T(8,128)(2,1)S(1)} %bitcast.9, bf16[8192,128]{1,0:T(8,128)(2,1)S(1)} %decode.1.embedded), custom_call_target="tpu_custom_call" | custom-call | tf_op jit(solution)/shard_map/score/pallas_call | solution.py:304
  22.8 12.0 %all_to_all.16 = f32[16,1,64]{2,1,0:T(1,128)S(1)} all-to-all(f32[16,1,64]{2,1,0:T(1,128)S(1)} %bitcast.10), channel_id=1, replica_groups=mesh['groups'=2,'shard'=8,'sub'=2] {'shard','sub'}, dimensions={0} | all-to-all | bytes 8192 | tf_op jit(solution)/shard_map/all_to_all | solution.py:363
  34.8 0.0 copy-done
  34.8 0.7 %pick.1 = f32[1,62]{1,0:T(1,128)} custom-call(s32[1,62]{1,0:T(1,128)S(1)} %copy-done, f32[16,64]{1,0:T(8,128)S(1)} %bitcast.11), custom_call_target="tpu_custom_call" | custom-call | tf_op jit(solution)/shard_map/pick/pallas_call | solution.py:340
Async XLA Ops:
  0.0 8.9 %collective-permute-start = (bf16[8192,128]{1,0:T(8,128)(2,1)}, bf16[8192,128]{1,0:T(8,128)(2,1)S(1)}, u32[]{:S(2)}, u32[]{:S(2)}) collective-permute-start(bf16[8192,128]{1,0:T(8,128)(2,1)} %own_hbm.1), channel_id=1, source_target_pairs={{0,1},{1,0},{2,3},{3,2},{4,5},{5,4},{6,7},{7,6},{8,9},{9,8},{10,11... | collective-permute-start | bytes 6291464 | tf_op jit(solution)/shard_map/ppermute | solution.py:355
  1.8 17.1 %all-to-all-start = ((bf16[16,32,128]{2,1,0:T(8,128)(2,1)}), bf16[16,32,128]{2,1,0:T(8,128)(2,1)S(1)}, u32[]{:S(2)}, u32[]{:S(2)}) async-start(bf16[16,32,128]{2,1,0:T(8,128)(2,1)} %spread.1), calls=%async_computation | async-start | bytes 262144 | tf_op jit(solution)/shard_map/all_to_all | solution.py:357
  18.9 15.9 %copy-start = (s32[1,62]{1,0:T(1,128)S(1)}, s32[1,62]{1,0:T(1,128)}, u32[]{:S(2)}) copy-start(s32[1,62]{1,0:T(1,128)} %candidates_ref.1) | copy-start | bytes 748

commit v12 on v8

--- a/solution.py
+++ b/solution.py
@@ -36,7 +36,28 @@
     return pltpu.CompilerParams(vmem_limit_bytes=mebibytes * 1024 * 1024)
 
 
-def widen_kernel(half_ref, own_hbm, other_ref, residuals_hbm, table, residuals, staged, sems):
+def spread_kernel(queries_hbm, out_hbm, sems):
+    copies = []
+    for k in range(sems.shape[0]):
+        copies.append(pltpu.make_async_copy(queries_hbm, out_hbm.at[k], sems.at[k]))
+        copies[-1].start()
+    for copy in copies:
+        copy.wait()
+
+
+def spread(queries, targets):
+    return pl.pallas_call(
+        spread_kernel,
+        out_shape=pltpu.HBM((targets,) + queries.shape, jnp.bfloat16),
+        in_specs=[HBM],
+        out_specs=HBM,
+        scratch_shapes=[pltpu.SemaphoreType.DMA((targets,))],
+        compiler_params=granted(4),
+        name="spread",
+    )(pinned(queries))
+
+
+def widen_kernel(half_ref, own_hbm, other_ref, table, staged, sems):
     half_rows = own_hbm.shape[0]
     half = half_ref[0]
     piece = half_rows // PIECES
@@ -45,145 +66,151 @@
         at = pl.ds(k * piece, piece)
         copies.append(pltpu.make_async_copy(own_hbm.at[at], staged.at[at], sems.at[k]))
         copies[-1].start()
-    residual_copy = pltpu.make_async_copy(residuals_hbm, residuals, sems.at[PIECES])
-    residual_copy.start()
-    for source, ref in enumerate((other_ref, staged)):
-        base = (1 - half if source == 0 else half) * half_rows
-        for k in range(PIECES):
-            if source == 1:
-                copies[k].wait()
-            to = pl.ds(pl.multiple_of(base + k * piece, piece), piece)
-            table[to, :] = ref[pl.ds(k * piece, piece), :].astype(jnp.float32)
-    residual_copy.wait()
-
-
-def widen(half, own, other, residuals):
+
+    def widened(ref, base, k):
+        to = pl.ds(pl.multiple_of(base + k * piece, piece), piece)
+        table[to, :] = ref[pl.ds(k * piece, piece), :].astype(jnp.float32)
+
+    for k in range(PIECES):
+        widened(other_ref, (1 - half) * half_rows, k)
+    for k in range(PIECES):
+        copies[k].wait()
+        widened(staged, half * half_rows, k)
+
+
+def widen(half, own, other):
     half_rows, width = own.shape
     return pl.pallas_call(
         widen_kernel,
-        out_shape=(
-            pltpu.VMEM((2 * half_rows, width), jnp.float32),
-            pltpu.VMEM(residuals.shape, jnp.bfloat16),
-        ),
-        in_specs=[SMEM, HBM, VMEM, HBM],
-        out_specs=(VMEM, VMEM),
+        out_shape=pltpu.VMEM((2 * half_rows, width), jnp.float32),
+        in_specs=[SMEM, HBM, VMEM],
+        out_specs=VMEM,
         scratch_shapes=[
             pltpu.VMEM((half_rows, width), jnp.bfloat16),
-            pltpu.SemaphoreType.DMA((PIECES + 1,)),
+            pltpu.SemaphoreType.DMA((PIECES,)),
         ],
         compiler_params=granted(4),
         cost_estimate=pl.CostEstimate(flops=10**7, bytes_accessed=10**7, transcendentals=0),
         name="widen",
-    )(half, pinned(own), pinned(other, pltpu.VMEM), pinned(residuals))
+    )(half, pinned(own), pinned(other, pltpu.VMEM))
 
 
 def decode_kernel(
     codes_hbm,
     lengths_hbm,
+    residuals_hbm,
     table,
-    residuals,
     embedded,
-    at_ref,
+    starts_hbm,
     codes_ref,
     lengths_ref,
-    rows,
+    starts_ref,
+    residuals,
     sems,
 ):
+    tokens, width = residuals.shape
     passages = lengths_ref.shape[0]
-    tokens, width = residuals.shape
     slots = tokens // passages
     lengths_copy = pltpu.make_async_copy(lengths_hbm, lengths_ref, sems.at[0])
     codes_copy = pltpu.make_async_copy(codes_hbm, codes_ref, sems.at[1])
     lengths_copy.start()
     codes_copy.start()
+    piece = tokens // PIECES
+    copies = []
+    for k in range(PIECES):
+        at = pl.ds(k * piece, piece)
+        copies.append(
+            pltpu.make_async_copy(residuals_hbm.at[at], residuals.at[at], sems.at[3 + k])
+        )
+        copies[-1].start()
     lengths_copy.wait()
 
     def listing(p, chunks):
         for k in range(slots // CHUNK):
-            at_ref[chunks + k] = p * slots + k * CHUNK
+            starts_ref[chunks + k] = p * slots + k * CHUNK
         return chunks + quotient(lengths_ref[p] + CHUNK - 1, CHUNK)
 
     chunks = lax.fori_loop(0, passages, listing, 0, unroll=4)
     for k in range(SCORE_GROUP):
-        at_ref[chunks + k] = tokens
-    groups = quotient(chunks + GROUP - 1, GROUP)
-    at_ref[at_ref.shape[0] - 1] = chunks
+        starts_ref[chunks + k] = tokens
+    starts_ref[starts_ref.shape[0] - 1] = chunks
+    starts_copy = pltpu.make_async_copy(starts_ref, starts_hbm, sems.at[2])
+    starts_copy.start()
+
+    slot_numbers = lax.broadcasted_iota(jnp.int32, (CHUNK, width), 0)
+    sublanes = lax.broadcasted_iota(jnp.int32, (8, width), 0)
+
+    def fetched(codes, first):
+        tile = table[pl.ds(codes[first], 8, stride=0), :]
+        for j in range(1, 8):
+            tile = jnp.where(sublanes == j, table[pl.ds(codes[first + j], 8, stride=0), :], tile)
+        return tile
+
     codes_copy.wait()
-
-    slot_numbers = lax.broadcasted_iota(jnp.int32, (CHUNK, width), 0)
-    table_single = table.reshape(table.shape[0], 1, width)
-    rows_single = rows.reshape(rows.shape[0], 1, width)
-
-    def fetch(g, k):
-        at = jnp.minimum(at_ref[g * GROUP + k], tokens - CHUNK)
-        codes = codes_ref.at[pl.ds(at, CHUNK)]
-        for j in range(CHUNK):
-            rows_single[k * CHUNK + j] = table_single[codes[j]]
-
-    def finish(g, k):
-        at = jnp.minimum(at_ref[g * GROUP + k], tokens - CHUNK)
-        p = quotient(at, slots)
-        live = lengths_ref[p] - (at - p * slots)
-        near = residuals[pl.ds(pl.multiple_of(at, CHUNK), CHUNK), :]
-        vectors = rows[pl.ds(k * CHUNK, CHUNK), :] + near.astype(jnp.float32)
-        vectors = jnp.where(slot_numbers < live, vectors, vectors[0:1, :])
-        return normalized(vectors)
-
-    def keep(g, done):
+    for copy in copies:
+        copy.wait()
+
+    def decode(g, carry):
+        summed = []
         for k in range(GROUP):
-            start = pl.multiple_of((g * GROUP + k) * CHUNK, CHUNK)
-            embedded[pl.ds(start, CHUNK), :] = done[k]
-
-    for k in range(GROUP):
-        fetch(0, k)
-
-    def decode(g, carry):
-        done = []
-        for k in range(GROUP):
-            done.append(finish(g - 1, k))
-            fetch(g, k)
-        keep(g - 1, done)
+            at = jnp.minimum(starts_ref[g * GROUP + k], tokens - CHUNK)
+            codes = codes_ref.at[pl.ds(at, CHUNK)]
+            rows = jnp.concatenate([fetched(codes, j) for j in range(0, CHUNK, 8)], axis=0)
+            near = residuals[pl.ds(pl.multiple_of(at, CHUNK), CHUNK), :]
+            vectors = rows + near.astype(jnp.float32)
+            p = quotient(at, slots)
+            live = slot_numbers < lengths_ref[p] - (at - p * slots)
+            summed.append(jnp.where(live, vectors, vectors[0:1, :]))
+        size = GROUP * CHUNK
+        done = normalized(jnp.concatenate(summed, axis=0))
+        embedded[pl.ds(pl.multiple_of(g * size, size), size), :] = done
         return carry
 
-    lax.fori_loop(1, groups, decode, 0)
-    keep(groups - 1, [finish(groups - 1, k) for k in range(GROUP)])
-
-
-def decode_all(token_codes, lengths, table, residuals):
+    lax.fori_loop(0, quotient(chunks + GROUP - 1, GROUP), decode, 0)
+    starts_copy.wait()
+
+
+def decode_all(token_codes, lengths, residuals, table):
+    tokens, width = residuals.shape
+    rounding = SCORE_GROUP * CHUNK
     passages, slots = token_codes.shape
-    tokens, width = residuals.shape
-    most = tokens // CHUNK + 2 * SCORE_GROUP
+    most = tokens // CHUNK + SCORE_GROUP + slots // CHUNK
+    most = -(-most // 128) * 128
     return pl.pallas_call(
         decode_kernel,
         out_shape=(
-            jax.ShapeDtypeStruct((most * CHUNK, width), jnp.bfloat16),
-            jax.ShapeDtypeStruct((most + 1,), jnp.int32),
+            jax.ShapeDtypeStruct((-(-tokens // rounding) * rounding, width), jnp.bfloat16),
+            pltpu.HBM((most,), jnp.int32),
         ),
-        in_specs=[HBM, HBM, VMEM, VMEM],
-        out_specs=(VMEM, SMEM),
+        in_specs=[HBM, HBM, HBM, VMEM],
+        out_specs=(VMEM, HBM),
         scratch_shapes=[
             pltpu.SMEM((tokens,), jnp.int32),
             pltpu.SMEM((passages,), jnp.int32),
-            pltpu.VMEM((GROUP * CHUNK, width), jnp.float32),
-            pltpu.SemaphoreType.DMA((2,)),
+            pltpu.SMEM((most,), jnp.int32),
+            pltpu.VMEM((tokens, width), jnp.bfloat16),
+            pltpu.SemaphoreType.DMA((3 + PIECES,)),
         ],
-        compiler_params=granted(4),
+        compiler_params=granted(6),
         cost_estimate=pl.CostEstimate(flops=10**7, bytes_accessed=40 * 10**6, transcendentals=0),
         name="decode",
     )(
         pinned(token_codes.reshape(tokens)),
         pinned(lengths),
+        pinned(residuals),
         pinned(table, pltpu.VMEM),
-        pinned(residuals, pltpu.VMEM),
     )
 
 
-def score_kernel(token_count, slots, at_ref, queries_ref, embedded, out_ref, turned, largest):
+def score_kernel(
+    token_count, slots, starts_hbm, queries_ref, embedded, out_ref, at_ref, turned, largest, sem
+):
+    starts_copy = pltpu.make_async_copy(starts_hbm, at_ref, sem)
+    starts_copy.start()
     passages = out_ref.shape[1]
     query_tokens = queries_ref.shape[0]
     block = min(QUERY_BLOCK, query_tokens)
     blocks = query_tokens // block
-    groups = quotient(at_ref[at_ref.shape[0] - 1] + SCORE_GROUP - 1, SCORE_GROUP)
     per_block = block // token_count
     owner = lax.broadcasted_iota(jnp.int32, (per_block, block), 0)
     token_of = lax.broadcasted_iota(jnp.int32, (per_block, block), 1) // token_count
@@ -208,6 +235,11 @@
                     largest[lane, pl.ds(at, 8), :] = so_far[:, lane * 128 : (lane + 1) * 128]
             return so_far
 
+        @pl.when(b == 0)
+        def arrived():
+            starts_copy.wait()
+
+        groups = quotient(at_ref[at_ref.shape[0] - 1] + SCORE_GROUP - 1, SCORE_GROUP)
         lax.fori_loop(0, groups, score, jnp.zeros((8, block), jnp.float32))
         kept = []
         for lane in range(block // 128):
@@ -236,15 +268,17 @@
     return pl.pallas_call(
         functools.partial(score_kernel, token_count, slots),
         out_shape=jax.ShapeDtypeStruct((query_tokens // token_count, passages), jnp.float32),
-        in_specs=[SMEM, VMEM, VMEM],
+        in_specs=[HBM, VMEM, VMEM],
         out_specs=VMEM,
         scratch_shapes=[
+            pltpu.SMEM(starts.shape, jnp.int32),
             pltpu.VMEM((width, block), jnp.bfloat16),
             pltpu.VMEM((block // 128, (passages + 1) * 8, 128), jnp.float32),
+            pltpu.SemaphoreType.DMA,
         ],
         compiler_params=granted(8 + 2 * blocks),
         name="score",
-    )(starts, query_rows, embedded)
+    )(pinned(starts), query_rows, embedded)
 
 
 def pick_kernel(passages, candidates_ref, returned_ref, out_ref):
@@ -283,13 +317,12 @@
     passages, slots = token_codes.shape
     half = lax.axis_index("sub").astype(jnp.int32)
     other = lax.ppermute(centroids, "sub", [(0, 1), (1, 0)])
-    own_rows = queries.reshape(1, local_queries * token_count, width)
-    sent = jnp.broadcast_to(own_rows, (targets,) + own_rows.shape[1:])
+    sent = spread(queries.reshape(local_queries * token_count, width), targets)
     gathered = lax.all_to_all(sent, ("shard", "sub"), split_axis=0, concat_axis=0, tiled=True)
     query_rows = gathered.reshape(targets * local_queries * token_count, width)
     flat = residuals.reshape(passages * slots, width)
-    table, near = widen(half.reshape(1), centroids, other, flat)
-    embedded, starts = decode_all(token_codes, lengths, table, near)
+    table = widen(half.reshape(1), centroids, other)
+    embedded, starts = decode_all(token_codes, lengths, flat, table)
     scores = score_all(starts, query_rows, embedded, passages, slots, token_count)
     returned = lax.all_to_all(
         scores.reshape(targets, local_queries * passages),

time: 36.4 us -> 40.4 us (1.11)
  Pallas kernels: 14.3 us -> 19.2 us
  local copies, waits for them, and re-layouts: 1.36 us -> 0.01 us
    pallas_call x2 -> x3, Pallas kernels: 10 us -> 14.7 us  [the longest x1 7.85 us: decode_all(): pl.pallas_call(decode_kernel, out_shape=(jax.ShapeDtypeStruct((-(-tokens...]
    broadcast_in_dim x1 -> x0, local copies, waits for them, and re-layouts: 1.36 us -> none  [body(): sent = jnp.broadcast_to(own_rows, (targets,) + own_rows.shape[1:])]
  transfers between devices with their start and end apart: 2 -> 2, of which waited for: 0 -> 0; matrix products, arithmetic and copies ran while one was open for 4% -> 0% of each run, Pallas kernels for 28% -> 37%
where the time goes in v12:
time: 40.4 us; the launch traced here: 40 us
  Pallas kernels  19.2 us (48%)
  blocking collectives  13.2 us (33%)
  starting transfers between devices  7.48 us (19%)
    all_to_all x1, blocking collectives, body(): lax.all_to_all(scores.reshape(targets, local_queries * passages), ('shard...  13.2 us
    pallas_call x1, Pallas kernels, decode_all(): pl.pallas_call(decode_kernel, out_shape=(jax.ShapeDtypeStruct((-(-tokens...  7.85 us
    all_to_all x1, starting transfers between devices, body(): lax.all_to_all(sent, ('shard', 'sub'), split_axis=0, concat_axis=0, tiled...  7.03 us
    pallas_call x1, Pallas kernels, spread(): pl.pallas_call(spread_kernel, out_shape=pltpu.HBM((targets,) + queries.sh...  5.22 us
    pallas_call x1, Pallas kernels, score_all(): pl.pallas_call(functools.partial(score_kernel, token_count, slots), out_s...  3.88 us
    pallas_call x1, Pallas kernels, widen(): pl.pallas_call(widen_kernel, out_shape=pltpu.VMEM((2 * half_rows, width),...  1.62 us
  transfers between devices with their start and end apart: 2, of which 0 were waited for; matrix products, arithmetic and copies ran while one was open for 0% of the time, Pallas kernels for 37%

profile of v12, /device:TPU:0, one launch (start us, length us, event | category | flops | bytes accessed | tf_op | source)
XLA Modules:
  0.0 40.0 jit_solution(18205000705745557353)
XLA Ops:
  0.0 0.5 %collective-permute-start = (bf16[8192,128]{1,0:T(8,128)(2,1)}, bf16[8192,128]{1,0:T(8,128)(2,1)S(1)}, u32[]{:S(2)}, u32[]{:S(2)}) collective-permute-start(bf16[8192,128]{1,0:T(8,128)(2,1)} %own_hbm.1), channel_id=1, source_target_pairs={{0,1},{1,0},{2,3},{3,2},{4,5},{5,4},{6,7},{7,6},{8,9},{9,8},{10,11... | collective-permute-start | bytes 6291464 | tf_op jit(solution)/shard_map/ppermute | solution.py:319
  0.5 5.2 %spread.1 = bf16[16,32,128]{2,1,0:T(8,128)(2,1)} custom-call(bf16[32,128]{1,0:T(8,128)(2,1)} %bitcast.14), custom_call_target="tpu_custom_call" | custom-call | tf_op jit(solution)/shard_map/spread/pallas_call | solution.py:49
  5.7 7.0 %all-to-all-start = ((bf16[16,32,128]{2,1,0:T(8,128)(2,1)}), bf16[16,32,128]{2,1,0:T(8,128)(2,1)S(1)}, u32[]{:S(2)}, u32[]{:S(2)}) async-start(bf16[16,32,128]{2,1,0:T(8,128)(2,1)} %spread.1), calls=%async_computation | async-start | bytes 262144 | tf_op jit(solution)/shard_map/all_to_all | solution.py:321
  12.7 0.0 collective-permute-done.other_ref
  12.7 1.6 %widen.1.table = f32[16384,128]{1,0:T(8,128)S(1)} custom-call(s32[1]{0:T(128)} %bitcast.2.half_ref, bf16[8192,128]{1,0:T(8,128)(2,1)} %own_hbm.1, bf16[8192,128]{1,0:T(8,128)(2,1)S(1)} %collective-permute-done.other_ref), custom_call_target="tpu_custom_call" | custom-call | flops 10000000 | bytes 10000000 | tf_op jit(solution)/shard_map/widen/pallas_call | solution.py:83
  14.4 7.9 %decode.1 = (bf16[8192,128]{1,0:T(8,128)(2,1)S(1)}, s32[640]{0:T(1024)}) custom-call(s32[8192]{0:T(1024)} %bitcast.13, s32[64]{0:T(128)} %lengths_hbm.1, bf16[8192,128]{1,0:T(8,128)(2,1)} %bitcast.12, f32[16384,128]{1,0:T(8,128)S(1)} %widen.1.table), custom_call_target="tpu_custom_call" | custom-call | flops 10000000 | bytes 40000000 | tf_op jit(solution)/shard_map/decode/pallas_call | solution.py:179
  22.2 0.0 copy-start
  22.2 0.0 all-to-all-done
  22.2 3.9 %score.1 = f32[16,64]{1,0:T(8,128)S(1)} custom-call(s32[640]{0:T(1024)} %get-tuple-element.7.starts_hbm, bf16[512,128]{1,0:T(8,128)(2,1)S(1)} %bitcast.9, bf16[8192,128]{1,0:T(8,128)(2,1)S(1)} %get-tuple-element.8.embedded), custom_call_target="tpu_custom_call" | custom-call | tf_op jit(solution)/shard_map/score/pallas_call | solution.py:268
  26.1 13.2 %all_to_all.16 = f32[16,1,64]{2,1,0:T(1,128)S(1)} all-to-all(f32[16,1,64]{2,1,0:T(1,128)S(1)} %bitcast.10), channel_id=1, replica_groups=mesh['groups'=2,'shard'=8,'sub'=2] {'shard','sub'}, dimensions={0} | all-to-all | bytes 8192 | tf_op jit(solution)/shard_map/all_to_all | solution.py:327
  39.4 0.0 copy-done
  39.4 0.7 %pick.1 = f32[1,62]{1,0:T(1,128)} custom-call(s32[1,62]{1,0:T(1,128)S(1)} %copy-done, f32[16,64]{1,0:T(8,128)S(1)} %bitcast.11), custom_call_target="tpu_custom_call" | custom-call | tf_op jit(solution)/shard_map/pick/pallas_call | solution.py:304
Async XLA Ops:
  0.0 12.7 %collective-permute-start = (bf16[8192,128]{1,0:T(8,128)(2,1)}, bf16[8192,128]{1,0:T(8,128)(2,1)S(1)}, u32[]{:S(2)}, u32[]{:S(2)}) collective-permute-start(bf16[8192,128]{1,0:T(8,128)(2,1)} %own_hbm.1), channel_id=1, source_target_pairs={{0,1},{1,0},{2,3},{3,2},{4,5},{5,4},{6,7},{7,6},{8,9},{9,8},{10,11... | collective-permute-start | bytes 6291464 | tf_op jit(solution)/shard_map/ppermute | solution.py:319
  5.7 16.6 %all-to-all-start = ((bf16[16,32,128]{2,1,0:T(8,128)(2,1)}), bf16[16,32,128]{2,1,0:T(8,128)(2,1)S(1)}, u32[]{:S(2)}, u32[]{:S(2)}) async-start(bf16[16,32,128]{2,1,0:T(8,128)(2,1)} %spread.1), calls=%async_computation | async-start | bytes 262144 | tf_op jit(solution)/shard_map/all_to_all | solution.py:321
  22.2 17.1 %copy-start = (s32[1,62]{1,0:T(1,128)S(1)}, s32[1,62]{1,0:T(1,128)}, u32[]{:S(2)}) copy-start(s32[1,62]{1,0:T(1,128)} %candidates_ref.1) | copy-start | bytes 748

commit v13 on v7

--- a/solution.py
+++ b/solution.py
@@ -42,7 +42,8 @@
     return -(-rows // 8) * 8
 
 
-def spread_kernel(queries_ref, candidates_ref, out_ref, digits):
+def spread_kernel(me_ref, queries_ref, candidates_ref, out_ref, digits):
+    del me_ref
     targets = out_ref.shape[0]
     query_rows = queries_ref.shape[0]
     local_queries, count = candidates_ref.shape
@@ -65,92 +66,73 @@
         out_ref[t, query_rows:, :] = coded
         return carry
 
-    lax.fori_loop(0, targets, copy, 0)
-
-
-def spread(queries, candidates, targets):
+    lax.fori_loop(0, targets, copy, 0, unroll=8)
+
+
+def spread(me, queries, candidates, targets):
     query_rows, width = queries.shape
     id_rows = id_rows_of(*candidates.shape)
     return pl.pallas_call(
         spread_kernel,
-        out_shape=jax.ShapeDtypeStruct((targets, query_rows + 2 * id_rows, width), jnp.bfloat16),
-        in_specs=[VMEM, VMEM],
+        out_shape=pltpu.VMEM((targets, query_rows + 2 * id_rows, width), jnp.bfloat16),
+        in_specs=[SMEM, VMEM, VMEM],
         out_specs=VMEM,
         scratch_shapes=[pltpu.VMEM((2 * id_rows, width), jnp.float32)],
         compiler_params=granted(16),
         name="spread",
-    )(pinned(queries), pinned(candidates))
-
-
-def widen_kernel(half_ref, own_ref, other_ref, table, staged, sems):
-    half_rows = own_ref.shape[0]
-    half = half_ref[0]
-    piece = half_rows // PIECES
-    copies = []
-    for source, ref in enumerate((own_ref, other_ref)):
-        for k in range(PIECES):
-            at = pl.ds(k * piece, piece)
-            sem = sems.at[source * PIECES + k]
-            copies.append(pltpu.make_async_copy(ref.at[at], staged.at[source, at], sem))
-            copies[-1].start()
-    for source in range(2):
-        base = (half if source == 0 else 1 - half) * half_rows
-        for k in range(PIECES):
-            copies[source * PIECES + k].wait()
-            to = pl.ds(pl.multiple_of(base + k * piece, piece), piece)
-            table[to, :] = staged[source, pl.ds(k * piece, piece), :].astype(jnp.float32)
-
-
-def widen(half, own, other):
-    half_rows, width = own.shape
-    return pl.pallas_call(
-        widen_kernel,
-        out_shape=pltpu.VMEM((2 * half_rows, width), jnp.float32),
-        in_specs=[SMEM, HBM, HBM],
-        out_specs=VMEM,
-        scratch_shapes=[
-            pltpu.VMEM((2, half_rows, width), jnp.bfloat16),
-            pltpu.SemaphoreType.DMA((2 * PIECES,)),
-        ],
-        compiler_params=granted(16),
-        cost_estimate=pl.CostEstimate(flops=10**7, bytes_accessed=10**7, transcendentals=0),
-        name="widen",
-    )(half, pinned(own), pinned(other))
+    )(me, pinned(queries), pinned(candidates))
 
 
 def score_kernel(
     token_count,
     query_rows,
-    base_ref,
+    me_ref,
+    half_ref,
     codes_hbm,
     lengths_hbm,
+    own_hbm,
+    residuals_hbm,
+    other_ref,
     gathered_ref,
-    table,
-    residuals_ref,
     out_ref,
     codes_ref,
     lengths_ref,
-    at_ref,
-    residual_rows,
+    list_ref,
+    table,
+    staged,
+    residuals,
     rows,
-    embedded,
     turned,
     so_far,
     largest,
     sems,
 ):
-    passages = lengths_ref.shape[0]
-    tokens = codes_ref.shape[0]
-    slots = tokens // passages
-    targets, sent_rows, width = gathered_ref.shape
+    passages, slots = codes_ref.shape
+    half_rows, width = own_hbm.shape
+    tokens = passages * slots
+    per_passage = slots // CHUNK
+    targets, sent_rows, _ = gathered_ref.shape
     id_rows = (sent_rows - query_rows) // 2
     blocks, _, block = turned.shape
+    base = me_ref[0] * passages
+    half = half_ref[0]
     lengths_copy = pltpu.make_async_copy(lengths_hbm, lengths_ref, sems.at[0])
     codes_copy = pltpu.make_async_copy(codes_hbm, codes_ref, sems.at[1])
-    residual_copy = pltpu.make_async_copy(residuals_ref, residual_rows, sems.at[2])
     lengths_copy.start()
     codes_copy.start()
-    residual_copy.start()
+
+    def pieces(source, to, first):
+        size = source.shape[0] // PIECES
+        copies = []
+        for k in range(PIECES):
+            at = pl.ds(k * size, size)
+            sem = sems.at[first + k]
+            copies.append(pltpu.make_async_copy(source.at[at], to.at[at], sem))
+            copies[-1].start()
+        return copies
+
+    own_copies = pieces(own_hbm, staged, 2)
+    residual_copies = pieces(residuals_hbm, residuals, 2 + PIECES)
 
     words = -(-passages // 32)
     shape = (id_rows, width)
@@ -158,13 +140,13 @@
     def collect(t, masks):
         low = gathered_ref[t, query_rows : query_rows + id_rows, :].astype(jnp.float32)
         high = gathered_ref[t, query_rows + id_rows :, :].astype(jnp.float32)
-        local = (high * DIGIT + low).astype(jnp.int32) - base_ref[0]
+        local = (high * DIGIT + low).astype(jnp.int32) - base
         bits = lax.shift_left(jnp.ones(shape, jnp.int32), local & 31)
         word = lax.shift_right_arithmetic(local, 5)
         return tuple(mask | jnp.where(word == w, bits, 0) for w, mask in enumerate(masks))
 
     empty = tuple(jnp.zeros(shape, jnp.int32) for _ in range(words))
-    masks = lax.fori_loop(0, targets, collect, empty, unroll=min(8, targets))
+    masks = lax.fori_loop(0, targets, collect, empty, unroll=min(16, targets))
     joined = []
     for mask in masks:
         folded = mask[0:8]
@@ -187,76 +169,93 @@
 
     lax.fori_loop(0, blocks, turn, 0)
 
+    piece = half_rows // PIECES
+
+    def widened(ref, start, k):
+        to = pl.ds(pl.multiple_of(start + k * piece, piece), piece)
+        table[to, :] = ref[pl.ds(k * piece, piece), :].astype(jnp.float32)
+
+    for k in range(PIECES):
+        widened(other_ref, (1 - half) * half_rows, k)
+
     lengths_copy.wait()
     chunks = jnp.int32(0)
     for w in range(words):
 
         def listing(k, listed):
             p = w * 32 + k
-            for j in range(slots // CHUNK):
-                at_ref[listed + j] = p * slots + j * CHUNK
+            for j in range(per_passage):
+                list_ref[listed + j] = p * per_passage + j
             wanted = lax.shift_right_logical(joined[w], k) & 1
             return listed + wanted * quotient(lengths_ref[p] + CHUNK - 1, CHUNK)
 
         chunks = lax.fori_loop(0, min(32, passages - w * 32), listing, chunks, unroll=4)
     for k in range(GROUP):
-        at_ref[chunks + k] = tokens
+        list_ref[chunks + k] = passages * per_passage
     groups = quotient(chunks + GROUP - 1, GROUP)
+
+    for k in range(PIECES):
+        own_copies[k].wait()
+        widened(staged, half * half_rows, k)
     codes_copy.wait()
-    residual_copy.wait()
+    for copy in residual_copies:
+        copy.wait()
 
     slot_numbers = lax.broadcasted_iota(jnp.int32, (CHUNK, width), 0)
-    single = table.reshape(table.shape[0], 1, width)
+    table_single = table.reshape(2 * half_rows, 1, width)
+    rows_single = rows.reshape(rows.shape[0], 1, width)
+    codes_chunks = codes_ref.reshape(passages * per_passage, CHUNK)
+
+    def chunk_at(g, k):
+        return jnp.minimum(list_ref[g * GROUP + k], passages * per_passage - 1)
 
     def fetch(g, k):
-        at = jnp.minimum(at_ref[g * GROUP + k], tokens - CHUNK)
+        chunk = chunk_at(g, k)
         for j in range(CHUNK):
-            rows[pl.ds(k * CHUNK + j, 1), :] = single[codes_ref[at + j]]
+            rows_single[k * CHUNK + j] = table_single[codes_chunks[chunk, j]]
 
     def finish(g, k):
-        at = jnp.minimum(at_ref[g * GROUP + k], tokens - CHUNK)
-        p = quotient(at, slots)
-        live = lengths_ref[p] - (at - p * slots)
-        near = residual_rows[pl.ds(pl.multiple_of(at, CHUNK), CHUNK), :]
+        chunk = chunk_at(g, k)
+        p = quotient(chunk, per_passage)
+        live = lengths_ref[p] - (chunk - p * per_passage) * CHUNK
+        near = residuals[pl.ds(pl.multiple_of(chunk * CHUNK, CHUNK), CHUNK), :]
         vectors = rows[pl.ds(k * CHUNK, CHUNK), :] + near.astype(jnp.float32)
-        vectors = jnp.where(slot_numbers < live, vectors, vectors[0:1, :])
-        return normalized(vectors)
-
-    def score(g, b):
-        similar = jnp.dot(embedded[...], turned[b], preferred_element_type=jnp.float32)
+        return jnp.where(slot_numbers < live, vectors, vectors[0:1, :])
+
+    def score(g, b, embedded):
+        similar = jnp.dot(embedded, turned[b], preferred_element_type=jnp.float32)
         parts = jnp.max(similar.reshape(GROUP, CHUNK // 8, 8, block), axis=1)
         best = so_far[b]
         for k in range(GROUP):
-            start = at_ref[g * GROUP + k]
-            p = quotient(start, slots)
-            best = jnp.where(start == p * slots, parts[k], jnp.maximum(best, parts[k]))
+            chunk = list_ref[g * GROUP + k]
+            p = quotient(chunk, per_passage)
+            fresh = chunk == p * per_passage
+            best = jnp.where(fresh, parts[k], jnp.maximum(best, parts[k]))
             at = pl.multiple_of(p * 8, 8)
             for lane in range(block // 128):
                 largest[b, lane, pl.ds(at, 8), :] = best[:, lane * 128 : (lane + 1) * 128]
         so_far[b] = best
 
     def step(i, carry):
-        scored = jnp.maximum(i - 2, 0)
+        fetched = jnp.minimum(i, groups - 1)
+        finished = jnp.maximum(i - 1, 0)
+        summed = []
+        for k in range(GROUP):
+            summed.append(finish(finished, k))
+            fetch(fetched, k)
+        embedded = normalized(jnp.concatenate(summed, axis=0))
         if blocks == 1:
-            score(scored, 0)
+            score(finished, 0, embedded)
         else:
 
             def score_block(b, inner):
-                score(scored, b)
+                score(finished, b, embedded)
                 return inner
 
             lax.fori_loop(0, blocks, score_block, 0)
-        fetched = jnp.minimum(i, groups - 1)
-        finished = jnp.maximum(jnp.minimum(i - 1, groups - 1), 0)
-        done = []
-        for k in range(GROUP):
-            done.append(finish(finished, k))
-            fetch(fetched, k)
-        for k in range(GROUP):
-            embedded[pl.ds(k * CHUNK, CHUNK), :] = done[k]
         return carry
 
-    lax.fori_loop(0, jnp.where(groups > 0, groups + 2, 0), step, 0)
+    lax.fori_loop(0, jnp.where(groups > 0, groups + 1, 0), step, 0)
 
     per_block = block // token_count
     owner = lax.broadcasted_iota(jnp.int32, (per_block, block), 0)
@@ -284,40 +283,46 @@
     lax.fori_loop(0, blocks, total, 0)
 
 
-def score_all(base, token_codes, lengths, gathered, table, residuals, query_rows, token_count):
-    passages, slots, width = residuals.shape
+def score_all(
+    me, half, token_codes, lengths, own, residuals, other, gathered, query_rows, token_count
+):
+    passages, slots = token_codes.shape
+    half_rows, width = own.shape
     targets = gathered.shape[0]
-    tokens = passages * slots
     block = min(QUERY_BLOCK, targets * query_rows)
     blocks = targets * query_rows // block
+    most = passages * (slots // CHUNK) + slots // CHUNK + GROUP
     return pl.pallas_call(
         functools.partial(score_kernel, token_count, query_rows),
         out_shape=jax.ShapeDtypeStruct(
             (targets * query_rows // token_count, passages), jnp.float32
         ),
-        in_specs=[SMEM, HBM, HBM, VMEM, VMEM, HBM],
+        in_specs=[SMEM, SMEM, HBM, HBM, HBM, HBM, VMEM, VMEM],
         out_specs=VMEM,
         scratch_shapes=[
-            pltpu.SMEM((tokens,), jnp.int32),
+            pltpu.SMEM((passages, slots), jnp.int32),
             pltpu.SMEM((passages,), jnp.int32),
-            pltpu.SMEM((tokens // CHUNK + slots // CHUNK + GROUP,), jnp.int32),
-            pltpu.VMEM((tokens, width), jnp.bfloat16),
+            pltpu.SMEM((most,), jnp.int32),
+            pltpu.VMEM((2 * half_rows, width), jnp.float32),
+            pltpu.VMEM((half_rows, width), jnp.bfloat16),
+            pltpu.VMEM((passages * slots, width), jnp.bfloat16),
             pltpu.VMEM((GROUP * CHUNK, width), jnp.float32),
-            pltpu.VMEM((GROUP * CHUNK, width), jnp.bfloat16),
             pltpu.VMEM((blocks, width, block), jnp.bfloat16),
             pltpu.VMEM((blocks, 8, block), jnp.float32),
             pltpu.VMEM((blocks, block // 128, (passages + 1) * 8, 128), jnp.float32),
-            pltpu.SemaphoreType.DMA((3,)),
+            pltpu.SemaphoreType.DMA((2 + 2 * PIECES,)),
         ],
-        compiler_params=granted(40),
+        compiler_params=granted(20 + 2 * blocks),
         name="score",
     )(
-        base,
-        pinned(token_codes.reshape(tokens)),
+        me,
+        half,
+        pinned(token_codes),
         pinned(lengths),
-        gathered,
-        pinned(table, pltpu.VMEM),
-        pinned(residuals.reshape(tokens, width)),
+        pinned(own),
+        pinned(residuals.reshape(passages * slots, width)),
+        pinned(other, pltpu.VMEM),
+        pinned(gathered, pltpu.VMEM),
     )
 
 
@@ -358,13 +363,13 @@
     query_rows = local_queries * token_count
     half = lax.axis_index("sub").astype(jnp.int32)
     me = lax.axis_index("shard").astype(jnp.int32) * lax.axis_size("sub") + half
+    half = half.reshape(1)
+    me = me.reshape(1)
     other = lax.ppermute(centroids, "sub", [(0, 1), (1, 0)])
-    sent = spread(queries.reshape(query_rows, width), candidates, targets)
+    sent = spread(me, queries.reshape(query_rows, width), candidates, targets)
     gathered = lax.all_to_all(sent, ("shard", "sub"), split_axis=0, concat_axis=0, tiled=True)
-    table = widen(half.reshape(1), centroids, other)
-    base = (me * passages).reshape(1)
     scores = score_all(
-        base, token_codes, lengths, gathered, table, residuals, query_rows, token_count
+        me, half, token_codes, lengths, centroids, residuals, other, gathered, query_rows, token_count
     )
     returned = lax.all_to_all(
         scores.reshape(targets, local_queries * passages),

time: 40 us -> 38.1 us (0.953)
  blocking collectives: 10.5 us -> 25.2 us
  local copies, waits for them, and re-layouts: 7.95 us -> 0.01 us
  starting transfers between devices: 7.47 us -> 0.45 us
  waiting for transfers between devices: 2.11 us -> 0.01 us
  Pallas kernels: 11.7 us -> 12.1 us
    all_to_all x0 -> x1, blocking collectives: none -> 15.8 us  [body(): lax.all_to_all(sent, ('shard', 'sub'), split_axis=0, concat_axis=0, tiled...]
    unnamed x8 -> x2, local copies, waits for them, and re-layouts: 7.95 us -> 0.01 us
    all_to_all x1 -> x0, starting transfers between devices: 7.02 us -> none  [body(): lax.all_to_all(sent, ('shard', 'sub'), split_axis=0, concat_axis=0, tiled...]
    pallas_call x1, Pallas kernels: 7.26 us -> 10.8 us  [score_all(): pl.pallas_call(functools.partial(score_kernel, token_count, query_rows),...]
    pallas_call x2 -> x1, Pallas kernels: 3.75 us -> 0.73 us  [spread(): pl.pallas_call(spread_kernel, out_shape=pltpu.VMEM((targets, query_rows +...]
    all_to_all x1 -> x0, waiting for transfers between devices: 2.11 us -> none  [body(): lax.all_to_all(sent, ('shard', 'sub'), split_axis=0, concat_axis=0, tiled...]
    all_to_all x1, blocking collectives: 10.5 us -> 9.41 us  [body(): lax.all_to_all(scores.reshape(targets, local_queries * passages), ('shard...]
  transfers between devices with their start and end apart: 2 -> 1, of which waited for: 1 -> 0; matrix products, arithmetic and copies ran while one was open for 0% -> 0% of each run, Pallas kernels for 9% -> 2%
where the time goes in v13:
time: 38.1 us; the launch traced here: 37.8 us
  blocking collectives  25.2 us (66%)
  Pallas kernels  12.1 us (32%)
  starting transfers between devices  0.45 us (1%)
    all_to_all x1, blocking collectives, body(): lax.all_to_all(sent, ('shard', 'sub'), split_axis=0, concat_axis=0, tiled...  15.8 us
    pallas_call x1, Pallas kernels, score_all(): pl.pallas_call(functools.partial(score_kernel, token_count, query_rows),...  10.8 us
    all_to_all x1, blocking collectives, body(): lax.all_to_all(scores.reshape(targets, local_queries * passages), ('shard...  9.41 us
  transfers between devices with their start and end apart: 1, of which 0 were waited for; matrix products, arithmetic and copies ran while one was open for 0% of the time, Pallas kernels for 2%

profile of v13, /device:TPU:0, one launch (start us, length us, event | category | flops | bytes accessed | tf_op | source)
XLA Modules:
  0.0 37.8 jit_solution(16039373383709662653)
XLA Ops:
  0.0 0.5 %collective-permute-start = (bf16[8192,128]{1,0:T(8,128)(2,1)}, bf16[8192,128]{1,0:T(8,128)(2,1)S(1)}, u32[]{:S(2)}, u32[]{:S(2)}) collective-permute-start(bf16[8192,128]{1,0:T(8,128)(2,1)} %own_hbm.1), channel_id=1, source_target_pairs={{0,1},{1,0},{2,3},{3,2},{4,5},{5,4},{6,7},{7,6},{8,9},{9,8},{10,11... | collective-permute-start | bytes 6291464 | tf_op jit(solution)/shard_map/ppermute | solution.py:368
  0.5 0.7 %spread.1 = bf16[16,48,128]{2,1,0:T(8,128)(2,1)S(1)} custom-call(s32[1]{0:T(128)} %bitcast.me_ref, bf16[32,128]{1,0:T(8,128)(2,1)} %bitcast.11, s32[1,62]{1,0:T(1,128)} %candidates_ref.3), custom_call_target="tpu_custom_call" | custom-call | tf_op jit(solution)/shard_map/spread/pallas_call | solution.py:75
  1.2 15.8 %all_to_all.16.gathered_ref = bf16[16,48,128]{2,1,0:T(8,128)(2,1)S(1)} all-to-all(bf16[16,48,128]{2,1,0:T(8,128)(2,1)S(1)} %spread.1), channel_id=1, replica_groups=mesh['groups'=2,'shard'=8,'sub'=2] {'shard','sub'}, dimensions={0} | all-to-all | bytes 393216 | tf_op jit(solution)/shard_map/all_to_all | solution.py:370
  17.0 0.0 collective-permute-done.other_ref
  17.0 0.0 copy-start
  17.0 10.8 %score.1 = f32[16,64]{1,0:T(8,128)S(1)} custom-call(s32[1]{0:T(128)} %bitcast.me_ref, s32[1]{0:T(128)} %bitcast.1.half_ref, s32[64,128]{1,0:T(8,128)} %codes_hbm.1, s32[64]{0:T(128)} %lengths_hbm.1, bf16[8192,128]{1,0:T(8,128)(2,1)} %own_hbm.1, bf16[8192,128]{1,0:T(8,128)(2,1)} %bitcast.10, bf16[8192,128]{1,0:T(8,128)(2,1)S(1)} %collective-permute-done.other_ref, ...), custom_call_target="tpu_custom_call" | custom-call | tf_op jit(solution)/shard_map/score/pallas_call | solution.py:295
  27.8 9.4 %all_to_all.17 = f32[16,1,64]{2,1,0:T(1,128)S(1)} all-to-all(f32[16,1,64]{2,1,0:T(1,128)S(1)} %bitcast.8), channel_id=1, replica_groups=mesh['groups'=2,'shard'=8,'sub'=2] {'shard','sub'}, dimensions={0} | all-to-all | bytes 8192 | tf_op jit(solution)/shard_map/all_to_all | solution.py:374
  37.2 0.0 copy-done
  37.2 0.7 %pick.1 = f32[1,62]{1,0:T(1,128)} custom-call(s32[1,62]{1,0:T(1,128)S(1)} %copy-done, f32[16,64]{1,0:T(8,128)S(1)} %bitcast.9), custom_call_target="tpu_custom_call" | custom-call | tf_op jit(solution)/shard_map/pick/pallas_call | solution.py:349
Async XLA Ops:
  0.0 17.0 %collective-permute-start = (bf16[8192,128]{1,0:T(8,128)(2,1)}, bf16[8192,128]{1,0:T(8,128)(2,1)S(1)}, u32[]{:S(2)}, u32[]{:S(2)}) collective-permute-start(bf16[8192,128]{1,0:T(8,128)(2,1)} %own_hbm.1), channel_id=1, source_target_pairs={{0,1},{1,0},{2,3},{3,2},{4,5},{5,4},{6,7},{7,6},{8,9},{9,8},{10,11... | collective-permute-start | bytes 6291464 | tf_op jit(solution)/shard_map/ppermute | solution.py:368
  17.0 20.2 %copy-start = (s32[1,62]{1,0:T(1,128)S(1)}, s32[1,62]{1,0:T(1,128)}, u32[]{:S(2)}) copy-start(s32[1,62]{1,0:T(1,128)} %candidates_ref.3) | copy-start | bytes 748

commit v14 on v12

--- a/solution.py
+++ b/solution.py
@@ -9,7 +9,8 @@
 
 CHUNK = 16
 GROUP = 16
-SCORE_GROUP = 32
+SCORE_GROUP = 64
+SCORE_PARTS = 2
 PIECES = 4
 QUERY_BLOCK = 512
 SMEM = pl.BlockSpec(memory_space=pltpu.SMEM)
@@ -36,31 +37,35 @@
     return pltpu.CompilerParams(vmem_limit_bytes=mebibytes * 1024 * 1024)
 
 
-def spread_kernel(queries_hbm, out_hbm, sems):
-    copies = []
-    for k in range(sems.shape[0]):
-        copies.append(pltpu.make_async_copy(queries_hbm, out_hbm.at[k], sems.at[k]))
-        copies[-1].start()
-    for copy in copies:
-        copy.wait()
+def spread_kernel(queries_ref, out_ref):
+    queries = queries_ref[...]
+
+    def copy(t, carry):
+        out_ref[t] = queries
+        return carry
+
+    lax.fori_loop(0, out_ref.shape[0], copy, 0, unroll=8)
 
 
 def spread(queries, targets):
     return pl.pallas_call(
         spread_kernel,
-        out_shape=pltpu.HBM((targets,) + queries.shape, jnp.bfloat16),
-        in_specs=[HBM],
-        out_specs=HBM,
-        scratch_shapes=[pltpu.SemaphoreType.DMA((targets,))],
+        out_shape=pltpu.VMEM((targets,) + queries.shape, jnp.bfloat16),
+        in_specs=[VMEM],
+        out_specs=VMEM,
         compiler_params=granted(4),
         name="spread",
     )(pinned(queries))
 
 
-def widen_kernel(half_ref, own_hbm, other_ref, table, staged, sems):
+def widen_kernel(
+    half_ref, codes_hbm, own_hbm, other_ref, table, paired_hbm, staged, codes, paired, sems
+):
     half_rows = own_hbm.shape[0]
     half = half_ref[0]
     piece = half_rows // PIECES
+    codes_copy = pltpu.make_async_copy(codes_hbm, codes, sems.at[PIECES])
+    codes_copy.start()
     copies = []
     for k in range(PIECES):
         at = pl.ds(k * piece, piece)
@@ -73,26 +78,38 @@
 
     for k in range(PIECES):
         widened(other_ref, (1 - half) * half_rows, k)
+    codes_copy.wait()
+    slots = codes.shape[1]
+    following = pltpu.roll(codes[...], slots - 1, 1)
+    paired[...] = codes[...] | lax.shift_left(following, jnp.full_like(following, 16))
+    paired_copy = pltpu.make_async_copy(paired, paired_hbm, sems.at[PIECES + 1])
+    paired_copy.start()
     for k in range(PIECES):
         copies[k].wait()
         widened(staged, half * half_rows, k)
-
-
-def widen(half, own, other):
+    paired_copy.wait()
+
+
+def widen(half, token_codes, own, other):
     half_rows, width = own.shape
     return pl.pallas_call(
         widen_kernel,
-        out_shape=pltpu.VMEM((2 * half_rows, width), jnp.float32),
-        in_specs=[SMEM, HBM, VMEM],
-        out_specs=VMEM,
+        out_shape=(
+            pltpu.VMEM((2 * half_rows, width), jnp.float32),
+            pltpu.HBM(token_codes.shape, jnp.int32),
+        ),
+        in_specs=[SMEM, HBM, HBM, VMEM],
+        out_specs=(VMEM, HBM),
         scratch_shapes=[
             pltpu.VMEM((half_rows, width), jnp.bfloat16),
-            pltpu.SemaphoreType.DMA((PIECES,)),
+            pltpu.VMEM(token_codes.shape, jnp.int32),
+            pltpu.VMEM(token_codes.shape, jnp.int32),
+            pltpu.SemaphoreType.DMA((PIECES + 2,)),
         ],
         compiler_params=granted(4),
         cost_estimate=pl.CostEstimate(flops=10**7, bytes_accessed=10**7, transcendentals=0),
         name="widen",
-    )(half, pinned(own), pinned(other, pltpu.VMEM))
+    )(half, pinned(token_codes), pinned(own), pinned(other, pltpu.VMEM))
 
 
 def decode_kernel(
@@ -106,6 +123,7 @@
     lengths_ref,
     starts_ref,
     residuals,
+    rows,
     sems,
 ):
     tokens, width = residuals.shape
@@ -138,35 +156,46 @@
     starts_copy.start()
 
     slot_numbers = lax.broadcasted_iota(jnp.int32, (CHUNK, width), 0)
-    sublanes = lax.broadcasted_iota(jnp.int32, (8, width), 0)
-
-    def fetched(codes, first):
-        tile = table[pl.ds(codes[first], 8, stride=0), :]
-        for j in range(1, 8):
-            tile = jnp.where(sublanes == j, table[pl.ds(codes[first + j], 8, stride=0), :], tile)
-        return tile
-
-    codes_copy.wait()
-    for copy in copies:
-        copy.wait()
-
-    def decode(g, carry):
+    table_single = table.reshape(table.shape[0], 1, width)
+    rows_single = rows.reshape(rows.shape[0], 1, width)
+
+    def fetch(g):
+        for k in range(GROUP):
+            at = jnp.minimum(starts_ref[g * GROUP + k], tokens - CHUNK)
+            for j in range(0, CHUNK, 2):
+                pair = codes_ref[at + j]
+                rows_single[k * CHUNK + j] = table_single[pair & 0xFFFF]
+                rows_single[k * CHUNK + j + 1] = table_single[lax.shift_right_logical(pair, 16)]
+
+    def finish(g):
         summed = []
         for k in range(GROUP):
             at = jnp.minimum(starts_ref[g * GROUP + k], tokens - CHUNK)
-            codes = codes_ref.at[pl.ds(at, CHUNK)]
-            rows = jnp.concatenate([fetched(codes, j) for j in range(0, CHUNK, 8)], axis=0)
             near = residuals[pl.ds(pl.multiple_of(at, CHUNK), CHUNK), :]
-            vectors = rows + near.astype(jnp.float32)
+            vectors = rows[pl.ds(k * CHUNK, CHUNK), :] + near.astype(jnp.float32)
             p = quotient(at, slots)
             live = slot_numbers < lengths_ref[p] - (at - p * slots)
             summed.append(jnp.where(live, vectors, vectors[0:1, :]))
+        return normalized(jnp.concatenate(summed, axis=0))
+
+    def keep(g, done):
         size = GROUP * CHUNK
-        done = normalized(jnp.concatenate(summed, axis=0))
         embedded[pl.ds(pl.multiple_of(g * size, size), size), :] = done
+
+    codes_copy.wait()
+    groups = quotient(chunks + GROUP - 1, GROUP)
+    fetch(0)
+    for copy in copies:
+        copy.wait()
+
+    def decode(g, carry):
+        done = finish(g - 1)
+        fetch(g)
+        keep(g - 1, done)
         return carry
 
-    lax.fori_loop(0, quotient(chunks + GROUP - 1, GROUP), decode, 0)
+    lax.fori_loop(1, groups, decode, 0)
+    keep(groups - 1, finish(groups - 1))
     starts_copy.wait()
 
 
@@ -189,6 +218,7 @@
             pltpu.SMEM((passages,), jnp.int32),
             pltpu.SMEM((most,), jnp.int32),
             pltpu.VMEM((tokens, width), jnp.bfloat16),
+            pltpu.VMEM((GROUP * CHUNK, width), jnp.float32),
             pltpu.SemaphoreType.DMA((3 + PIECES,)),
         ],
         compiler_params=granted(6),
@@ -222,17 +252,20 @@
         turned[...] = vectors.astype(jnp.float32).T.astype(jnp.bfloat16)
 
         def score(g, so_far):
-            size = SCORE_GROUP * CHUNK
-            at = pl.ds(pl.multiple_of(g * size, size), size)
-            similar = jnp.dot(embedded[at, :], turned[...], preferred_element_type=jnp.float32)
-            parts = jnp.max(similar.reshape(SCORE_GROUP, CHUNK // 8, 8, block), axis=1)
-            for k in range(SCORE_GROUP):
-                start = at_ref[g * SCORE_GROUP + k]
-                p = quotient(start, slots)
-                so_far = jnp.where(start == p * slots, parts[k], jnp.maximum(so_far, parts[k]))
-                at = pl.multiple_of(p * 8, 8)
-                for lane in range(block // 128):
-                    largest[lane, pl.ds(at, 8), :] = so_far[:, lane * 128 : (lane + 1) * 128]
+            count = SCORE_GROUP // SCORE_PARTS
+            size = count * CHUNK
+            for part in range(SCORE_PARTS):
+                first = g * SCORE_PARTS + part
+                at = pl.ds(pl.multiple_of(first * size, size), size)
+                similar = jnp.dot(embedded[at, :], turned[...], preferred_element_type=jnp.float32)
+                parts = jnp.max(similar.reshape(count, CHUNK // 8, 8, block), axis=1)
+                for k in range(count):
+                    start = at_ref[first * count + k]
+                    p = quotient(start, slots)
+                    so_far = jnp.where(start == p * slots, parts[k], jnp.maximum(so_far, parts[k]))
+                    to = pl.multiple_of(p * 8, 8)
+                    for lane in range(block // 128):
+                        largest[lane, pl.ds(to, 8), :] = so_far[:, lane * 128 : (lane + 1) * 128]
             return so_far
 
         @pl.when(b == 0)
@@ -321,8 +354,8 @@
     gathered = lax.all_to_all(sent, ("shard", "sub"), split_axis=0, concat_axis=0, tiled=True)
     query_rows = gathered.reshape(targets * local_queries * token_count, width)
     flat = residuals.reshape(passages * slots, width)
-    table = widen(half.reshape(1), centroids, other)
-    embedded, starts = decode_all(token_codes, lengths, flat, table)
+    table, paired = widen(half.reshape(1), token_codes, centroids, other)
+    embedded, starts = decode_all(paired, lengths, flat, table)
     scores = score_all(starts, query_rows, embedded, passages, slots, token_count)
     returned = lax.all_to_all(
         scores.reshape(targets, local_queries * passages),

time: 40.4 us -> 35 us (0.87)
  Pallas kernels: 19.2 us -> 14.9 us
  blocking collectives: 13.2 us -> 12.2 us
    pallas_call x2, Pallas kernels: 6.84 us -> 3.02 us  [the longest x1 1.66 us: widen(): pl.pallas_call(widen_kernel, out_shape=(pltpu.VMEM((2 * half_rows, width)...]
    all_to_all x1, blocking collectives: 13.2 us -> 12.2 us  [body(): lax.all_to_all(scores.reshape(targets, local_queries * passages), ('shard...]
    pallas_call x1, Pallas kernels: 3.88 us -> 3.17 us  [score_all(): pl.pallas_call(functools.partial(score_kernel, token_count, slots), out_s...]
  transfers between devices with their start and end apart: 2 -> 2, of which waited for: 0 -> 0; matrix products, arithmetic and copies ran while one was open for 0% -> 0% of each run, Pallas kernels for 37% -> 32%
where the time goes in v14:
time: 35 us; the launch traced here: 34.6 us
  Pallas kernels  14.9 us (43%)
  blocking collectives  12.2 us (35%)
  starting transfers between devices  7.47 us (21%)
    all_to_all x1, blocking collectives, body(): lax.all_to_all(scores.reshape(targets, local_queries * passages), ('shard...  12.2 us
    pallas_call x1, Pallas kernels, decode_all(): pl.pallas_call(decode_kernel, out_shape=(jax.ShapeDtypeStruct((-(-tokens...  8.07 us
    all_to_all x1, starting transfers between devices, body(): lax.all_to_all(sent, ('shard', 'sub'), split_axis=0, concat_axis=0, tiled...  7.02 us
    pallas_call x1, Pallas kernels, score_all(): pl.pallas_call(functools.partial(score_kernel, token_count, slots), out_s...  3.17 us
    pallas_call x1, Pallas kernels, widen(): pl.pallas_call(widen_kernel, out_shape=(pltpu.VMEM((2 * half_rows, width)...  1.66 us
    pallas_call x1, Pallas kernels, spread(): pl.pallas_call(spread_kernel, out_shape=pltpu.VMEM((targets,) + queries.s...  1.36 us
  transfers between devices with their start and end apart: 2, of which 0 were waited for; matrix products, arithmetic and copies ran while one was open for 0% of the time, Pallas kernels for 32%

profile of v14, /device:TPU:0, one launch (start us, length us, event | category | flops | bytes accessed | tf_op | source)
XLA Modules:
  0.0 34.6 jit_solution(5823295386224049239)
XLA Ops:
  0.0 0.5 %collective-permute-start = (bf16[8192,128]{1,0:T(8,128)(2,1)}, bf16[8192,128]{1,0:T(8,128)(2,1)S(1)}, u32[]{:S(2)}, u32[]{:S(2)}) collective-permute-start(bf16[8192,128]{1,0:T(8,128)(2,1)} %own_hbm.1), channel_id=1, source_target_pairs={{0,1},{1,0},{2,3},{3,2},{4,5},{5,4},{6,7},{7,6},{8,9},{9,8},{10,11... | collective-permute-start | bytes 6291464 | tf_op jit(solution)/shard_map/ppermute | solution.py:352
  0.5 1.4 %spread.1 = bf16[16,32,128]{2,1,0:T(8,128)(2,1)} custom-call(bf16[32,128]{1,0:T(8,128)(2,1)} %bitcast.14), custom_call_target="tpu_custom_call" | custom-call | tf_op jit(solution)/shard_map/spread/pallas_call | solution.py:51
  1.8 7.0 %all-to-all-start = ((bf16[16,32,128]{2,1,0:T(8,128)(2,1)}), bf16[16,32,128]{2,1,0:T(8,128)(2,1)S(1)}, u32[]{:S(2)}, u32[]{:S(2)}) async-start(bf16[16,32,128]{2,1,0:T(8,128)(2,1)} %spread.1), calls=%async_computation | async-start | bytes 262144 | tf_op jit(solution)/shard_map/all_to_all | solution.py:354
  8.8 0.0 collective-permute-done.other_ref
  8.9 1.7 %widen.1 = (f32[16384,128]{1,0:T(8,128)S(1)}, s32[64,128]{1,0:T(8,128)}) custom-call(s32[1]{0:T(128)} %bitcast.half_ref, s32[64,128]{1,0:T(8,128)} %codes_hbm.1, bf16[8192,128]{1,0:T(8,128)(2,1)} %own_hbm.1, bf16[8192,128]{1,0:T(8,128)(2,1)S(1)} %collective-permute-done.other_ref), custom_call_target="tpu_custom_call" | custom-call | flops 10000000 | bytes 10000000 | tf_op jit(solution)/shard_map/widen/pallas_call | solution.py:95
  10.5 8.1 %decode.1 = (bf16[8192,128]{1,0:T(8,128)(2,1)S(1)}, s32[640]{0:T(1024)}) custom-call(s32[8192]{0:T(1024)} %bitcast.13, s32[64]{0:T(128)} %lengths_hbm.1, bf16[8192,128]{1,0:T(8,128)(2,1)} %bitcast.12, f32[16384,128]{1,0:T(8,128)S(1)} %get-tuple-element.10.table), custom_call_target="tpu_custom_call" | custom-call | flops 10000000 | bytes 40000000 | tf_op jit(solution)/shard_map/decode/pallas_call | solution.py:208
  18.6 0.0 copy-start
  18.6 0.0 all-to-all-done
  18.6 3.2 %score.1 = f32[16,64]{1,0:T(8,128)S(1)} custom-call(s32[640]{0:T(1024)} %get-tuple-element.11.starts_hbm, bf16[512,128]{1,0:T(8,128)(2,1)S(1)} %bitcast.9, bf16[8192,128]{1,0:T(8,128)(2,1)S(1)} %get-tuple-element.12.embedded), custom_call_target="tpu_custom_call" | custom-call | tf_op jit(solution)/shard_map/score/pallas_call | solution.py:301
  21.8 12.2 %all_to_all.16 = f32[16,1,64]{2,1,0:T(1,128)S(1)} all-to-all(f32[16,1,64]{2,1,0:T(1,128)S(1)} %bitcast.10), channel_id=1, replica_groups=mesh['groups'=2,'shard'=8,'sub'=2] {'shard','sub'}, dimensions={0} | all-to-all | bytes 8192 | tf_op jit(solution)/shard_map/all_to_all | solution.py:360
  34.0 0.0 copy-done
  34.0 0.7 %pick.1 = f32[1,62]{1,0:T(1,128)} custom-call(s32[1,62]{1,0:T(1,128)S(1)} %copy-done, f32[16,64]{1,0:T(8,128)S(1)} %bitcast.11), custom_call_target="tpu_custom_call" | custom-call | tf_op jit(solution)/shard_map/pick/pallas_call | solution.py:337
Async XLA Ops:
  0.0 8.8 %collective-permute-start = (bf16[8192,128]{1,0:T(8,128)(2,1)}, bf16[8192,128]{1,0:T(8,128)(2,1)S(1)}, u32[]{:S(2)}, u32[]{:S(2)}) collective-permute-start(bf16[8192,128]{1,0:T(8,128)(2,1)} %own_hbm.1), channel_id=1, source_target_pairs={{0,1},{1,0},{2,3},{3,2},{4,5},{5,4},{6,7},{7,6},{8,9},{9,8},{10,11... | collective-permute-start | bytes 6291464 | tf_op jit(solution)/shard_map/ppermute | solution.py:352
  1.8 16.8 %all-to-all-start = ((bf16[16,32,128]{2,1,0:T(8,128)(2,1)}), bf16[16,32,128]{2,1,0:T(8,128)(2,1)S(1)}, u32[]{:S(2)}, u32[]{:S(2)}) async-start(bf16[16,32,128]{2,1,0:T(8,128)(2,1)} %spread.1), calls=%async_computation | async-start | bytes 262144 | tf_op jit(solution)/shard_map/all_to_all | solution.py:354
  18.6 15.4 %copy-start = (s32[1,62]{1,0:T(1,128)S(1)}, s32[1,62]{1,0:T(1,128)}, u32[]{:S(2)}) copy-start(s32[1,62]{1,0:T(1,128)} %candidates_ref.1) | copy-start | bytes 748

commit v15 on v14

--- a/solution.py
+++ b/solution.py
@@ -19,7 +19,12 @@
 
 
 def normalized(vectors):
-    total = jnp.sum(vectors * vectors, axis=-1, keepdims=True)
+    squares = vectors * vectors
+    high = squares.astype(jnp.bfloat16)
+    low = (squares - high.astype(jnp.float32)).astype(jnp.bfloat16)
+    ones = jnp.ones((2 * vectors.shape[1], vectors.shape[1]), jnp.bfloat16)
+    split = jnp.concatenate([high, low], axis=1)
+    total = jnp.dot(split, ones, preferred_element_type=jnp.float32)
     return (vectors * lax.rsqrt(total + 1e-06)).astype(jnp.bfloat16)
 
 
@@ -58,14 +63,10 @@
     )(pinned(queries))
 
 
-def widen_kernel(
-    half_ref, codes_hbm, own_hbm, other_ref, table, paired_hbm, staged, codes, paired, sems
-):
+def widen_kernel(half_ref, own_hbm, other_ref, table, staged, sems):
     half_rows = own_hbm.shape[0]
     half = half_ref[0]
     piece = half_rows // PIECES
-    codes_copy = pltpu.make_async_copy(codes_hbm, codes, sems.at[PIECES])
-    codes_copy.start()
     copies = []
     for k in range(PIECES):
         at = pl.ds(k * piece, piece)
@@ -78,38 +79,26 @@
 
     for k in range(PIECES):
         widened(other_ref, (1 - half) * half_rows, k)
-    codes_copy.wait()
-    slots = codes.shape[1]
-    following = pltpu.roll(codes[...], slots - 1, 1)
-    paired[...] = codes[...] | lax.shift_left(following, jnp.full_like(following, 16))
-    paired_copy = pltpu.make_async_copy(paired, paired_hbm, sems.at[PIECES + 1])
-    paired_copy.start()
     for k in range(PIECES):
         copies[k].wait()
         widened(staged, half * half_rows, k)
-    paired_copy.wait()
-
-
-def widen(half, token_codes, own, other):
+
+
+def widen(half, own, other):
     half_rows, width = own.shape
     return pl.pallas_call(
         widen_kernel,
-        out_shape=(
-            pltpu.VMEM((2 * half_rows, width), jnp.float32),
-            pltpu.HBM(token_codes.shape, jnp.int32),
-        ),
-        in_specs=[SMEM, HBM, HBM, VMEM],
-        out_specs=(VMEM, HBM),
+        out_shape=pltpu.VMEM((2 * half_rows, width), jnp.float32),
+        in_specs=[SMEM, HBM, VMEM],
+        out_specs=VMEM,
         scratch_shapes=[
             pltpu.VMEM((half_rows, width), jnp.bfloat16),
-            pltpu.VMEM(token_codes.shape, jnp.int32),
-            pltpu.VMEM(token_codes.shape, jnp.int32),
-            pltpu.SemaphoreType.DMA((PIECES + 2,)),
+            pltpu.SemaphoreType.DMA((PIECES,)),
         ],
         compiler_params=granted(4),
         cost_estimate=pl.CostEstimate(flops=10**7, bytes_accessed=10**7, transcendentals=0),
         name="widen",
-    )(half, pinned(token_codes), pinned(own), pinned(other, pltpu.VMEM))
+    )(half, pinned(own), pinned(other, pltpu.VMEM))
 
 
 def decode_kernel(
@@ -162,10 +151,8 @@
     def fetch(g):
         for k in range(GROUP):
             at = jnp.minimum(starts_ref[g * GROUP + k], tokens - CHUNK)
-            for j in range(0, CHUNK, 2):
-                pair = codes_ref[at + j]
-                rows_single[k * CHUNK + j] = table_single[pair & 0xFFFF]
-                rows_single[k * CHUNK + j + 1] = table_single[lax.shift_right_logical(pair, 16)]
+            for j in range(CHUNK):
+                rows_single[k * CHUNK + j] = table_single[codes_ref[at + j]]
 
     def finish(g):
         summed = []
@@ -354,8 +341,8 @@
     gathered = lax.all_to_all(sent, ("shard", "sub"), split_axis=0, concat_axis=0, tiled=True)
     query_rows = gathered.reshape(targets * local_queries * token_count, width)
     flat = residuals.reshape(passages * slots, width)
-    table, paired = widen(half.reshape(1), token_codes, centroids, other)
-    embedded, starts = decode_all(paired, lengths, flat, table)
+    table = widen(half.reshape(1), centroids, other)
+    embedded, starts = decode_all(token_codes, lengths, flat, table)
     scores = score_all(starts, query_rows, embedded, passages, slots, token_count)
     returned = lax.all_to_all(
         scores.reshape(targets, local_queries * passages),

time: 35 us -> 36.2 us (1.034)
  blocking collectives: 12.2 us -> 13 us
  Pallas kernels: 14.9 us -> 15.3 us
    all_to_all x1, blocking collectives: 12.2 us -> 13 us  [body(): lax.all_to_all(scores.reshape(targets, local_queries * passages), ('shard...]
where the time goes in v15:
time: 36.2 us; the launch traced here: 35.8 us
  Pallas kernels  15.3 us (42%)
  blocking collectives  13 us (36%)
  starting transfers between devices  7.47 us (21%)
    all_to_all x1, blocking collectives, body(): lax.all_to_all(scores.reshape(targets, local_queries * passages), ('shard...  13 us
    pallas_call x1, Pallas kernels, decode_all(): pl.pallas_call(decode_kernel, out_shape=(jax.ShapeDtypeStruct((-(-tokens...  8.42 us
    all_to_all x1, starting transfers between devices, body(): lax.all_to_all(sent, ('shard', 'sub'), split_axis=0, concat_axis=0, tiled...  7.02 us
    pallas_call x1, Pallas kernels, score_all(): pl.pallas_call(functools.partial(score_kernel, token_count, slots), out_s...  3.21 us
    pallas_call x1, Pallas kernels, widen(): pl.pallas_call(widen_kernel, out_shape=pltpu.VMEM((2 * half_rows, width),...  1.62 us
    pallas_call x1, Pallas kernels, spread(): pl.pallas_call(spread_kernel, out_shape=pltpu.VMEM((targets,) + queries.s...  1.37 us
  transfers between devices with their start and end apart: 2, of which 0 were waited for; matrix products, arithmetic and copies ran while one was open for 0% of the time, Pallas kernels for 32%

profile of v15, /device:TPU:0, one launch (start us, length us, event | category | flops | bytes accessed | tf_op | source)
XLA Modules:
  0.0 35.8 jit_solution(7592982796712179282)
XLA Ops:
  0.0 0.5 %collective-permute-start = (bf16[8192,128]{1,0:T(8,128)(2,1)}, bf16[8192,128]{1,0:T(8,128)(2,1)S(1)}, u32[]{:S(2)}, u32[]{:S(2)}) collective-permute-start(bf16[8192,128]{1,0:T(8,128)(2,1)} %own_hbm.1), channel_id=1, source_target_pairs={{0,1},{1,0},{2,3},{3,2},{4,5},{5,4},{6,7},{7,6},{8,9},{9,8},{10,11... | collective-permute-start | bytes 6291464 | tf_op jit(solution)/shard_map/ppermute | solution.py:339
  0.5 1.4 %spread.1 = bf16[16,32,128]{2,1,0:T(8,128)(2,1)} custom-call(bf16[32,128]{1,0:T(8,128)(2,1)} %bitcast.14), custom_call_target="tpu_custom_call" | custom-call | tf_op jit(solution)/shard_map/spread/pallas_call | solution.py:56
  1.8 7.0 %all-to-all-start = ((bf16[16,32,128]{2,1,0:T(8,128)(2,1)}), bf16[16,32,128]{2,1,0:T(8,128)(2,1)S(1)}, u32[]{:S(2)}, u32[]{:S(2)}) async-start(bf16[16,32,128]{2,1,0:T(8,128)(2,1)} %spread.1), calls=%async_computation | async-start | bytes 262144 | tf_op jit(solution)/shard_map/all_to_all | solution.py:341
  8.8 0.0 collective-permute-done.other_ref
  8.9 1.6 %widen.1.table = f32[16384,128]{1,0:T(8,128)S(1)} custom-call(s32[1]{0:T(128)} %bitcast.2.half_ref, bf16[8192,128]{1,0:T(8,128)(2,1)} %own_hbm.1, bf16[8192,128]{1,0:T(8,128)(2,1)S(1)} %collective-permute-done.other_ref), custom_call_target="tpu_custom_call" | custom-call | flops 10000000 | bytes 10000000 | tf_op jit(solution)/shard_map/widen/pallas_call | solution.py:89
  10.5 8.4 %decode.1 = (bf16[8192,128]{1,0:T(8,128)(2,1)S(1)}, s32[640]{0:T(1024)}) custom-call(s32[8192]{0:T(1024)} %bitcast.13, s32[64]{0:T(128)} %lengths_hbm.1, bf16[8192,128]{1,0:T(8,128)(2,1)} %bitcast.12, f32[16384,128]{1,0:T(8,128)S(1)} %widen.1.table), custom_call_target="tpu_custom_call" | custom-call | flops 10000000 | bytes 40000000 | tf_op jit(solution)/shard_map/decode/pallas_call | solution.py:195
  18.9 0.0 copy-start
  18.9 0.0 all-to-all-done
  18.9 3.2 %score.1 = f32[16,64]{1,0:T(8,128)S(1)} custom-call(s32[640]{0:T(1024)} %get-tuple-element.7.starts_hbm, bf16[512,128]{1,0:T(8,128)(2,1)S(1)} %bitcast.9, bf16[8192,128]{1,0:T(8,128)(2,1)S(1)} %get-tuple-element.8.embedded), custom_call_target="tpu_custom_call" | custom-call | tf_op jit(solution)/shard_map/score/pallas_call | solution.py:288
  22.2 13.0 %all_to_all.16 = f32[16,1,64]{2,1,0:T(1,128)S(1)} all-to-all(f32[16,1,64]{2,1,0:T(1,128)S(1)} %bitcast.10), channel_id=1, replica_groups=mesh['groups'=2,'shard'=8,'sub'=2] {'shard','sub'}, dimensions={0} | all-to-all | bytes 8192 | tf_op jit(solution)/shard_map/all_to_all | solution.py:347
  35.1 0.0 copy-done
  35.2 0.7 %pick.1 = f32[1,62]{1,0:T(1,128)} custom-call(s32[1,62]{1,0:T(1,128)S(1)} %copy-done, f32[16,64]{1,0:T(8,128)S(1)} %bitcast.11), custom_call_target="tpu_custom_call" | custom-call | tf_op jit(solution)/shard_map/pick/pallas_call | solution.py:324
Async XLA Ops:
  0.0 8.9 %collective-permute-start = (bf16[8192,128]{1,0:T(8,128)(2,1)}, bf16[8192,128]{1,0:T(8,128)(2,1)S(1)}, u32[]{:S(2)}, u32[]{:S(2)}) collective-permute-start(bf16[8192,128]{1,0:T(8,128)(2,1)} %own_hbm.1), channel_id=1, source_target_pairs={{0,1},{1,0},{2,3},{3,2},{4,5},{5,4},{6,7},{7,6},{8,9},{9,8},{10,11... | collective-permute-start | bytes 6291464 | tf_op jit(solution)/shard_map/ppermute | solution.py:339
  1.8 17.1 %all-to-all-start = ((bf16[16,32,128]{2,1,0:T(8,128)(2,1)}), bf16[16,32,128]{2,1,0:T(8,128)(2,1)S(1)}, u32[]{:S(2)}, u32[]{:S(2)}) async-start(bf16[16,32,128]{2,1,0:T(8,128)(2,1)} %spread.1), calls=%async_computation | async-start | bytes 262144 | tf_op jit(solution)/shard_map/all_to_all | solution.py:341
  18.9 16.2 %copy-start = (s32[1,62]{1,0:T(1,128)S(1)}, s32[1,62]{1,0:T(1,128)}, u32[]{:S(2)}) copy-start(s32[1,62]{1,0:T(1,128)} %candidates_ref.1) | copy-start | bytes 748

commit v16 on v11

v16 whole, which is shorter than its diff:
```python
import functools

import jax
import jax.numpy as jnp
from jax import lax
from jax.experimental import pallas as pl
from jax.experimental.pallas import tpu as pltpu
from jax.sharding import PartitionSpec as P

CHUNK = 16
GROUP = 16
SCORE_GROUP = 64
SCORE_PARTS = 2
STEPS = 3
PIECES = 4
QUERY_BLOCK = 512
SMEM = pl.BlockSpec(memory_space=pltpu.SMEM)
VMEM = pl.BlockSpec(memory_space=pltpu.VMEM)
HBM = pl.BlockSpec(memory_space=pltpu.HBM)


def normalized(vectors):
    total = jnp.sum(vectors * vectors, axis=-1, keepdims=True)
    return (vectors * lax.rsqrt(total + 1e-06)).astype(jnp.bfloat16)


def quotient(number, divisor):
    if divisor & (divisor - 1) == 0:
        return lax.shift_right_logical(number, divisor.bit_length() - 1)
    return lax.div(number, divisor)


def pinned(array, space=pltpu.HBM):
    return pltpu.with_memory_space_constraint(array, space)


def granted(mebibytes):
    return pltpu.CompilerParams(vmem_limit_bytes=mebibytes * 1024 * 1024)


def prepare_kernel(
    half_ref,
    lengths_hbm,
    codes_hbm,
    own_hbm,
    residuals_hbm,
    table,
    residuals,
    codes,
    starts,
    lives,
    nothing,
    lengths_ref,
    starts_ref,
    lives_ref,
    staged,
    sems,
):
    passages = lengths_ref.shape[0]
    slots = codes_hbm.shape[0] // passages
    half_rows = own_hbm.shape[0]
    moves = []

    def move(source, to):
        moves.append(pltpu.make_async_copy(source, to, sems.at[len(moves)]))
        moves[-1].start()
        return moves[-1]

    lengths_copy = move(lengths_hbm, lengths_ref)
    piece = half_rows // PIECES
    copies = []
    for k in range(PIECES):
        at = pl.ds(k * piece, piece)
        copies.append(move(own_hbm.at[at], staged.at[at]))
    codes_copy = move(codes_hbm, codes)
    residual_copy = move(residuals_hbm, residuals)
    nothing[...] = jnp.zeros(nothing.shape, nothing.dtype)
    lengths_copy.wait()

    def listing(p, chunks):
        length = lengths_ref[p]
        for k in range(slots // CHUNK):
            starts_ref[chunks + k] = p * slots + k * CHUNK
            lives_ref[chunks + k] = length - k * CHUNK
        return chunks + quotient(length + CHUNK - 1, CHUNK)

    chunks = lax.fori_loop(0, passages, listing, 0, unroll=4)
    for k in range(SCORE_GROUP):
        starts_ref[chunks + k] = passages * slots
        lives_ref[chunks + k] = 0
    starts_ref[starts_ref.shape[0] - 1] = chunks
    starts_copy = move(starts_ref, starts)
    lives_copy = move(lives_ref, lives)
    for k in range(PIECES):
        copies[k].wait()
        to = pl.ds(pl.multiple_of(half_ref[0] * half_rows + k * piece, piece), piece)
        table[to, :] = staged[pl.ds(k * piece, piece), :].astype(jnp.float32)
    for copy in (codes_copy, starts_copy, lives_copy, residual_copy):
        copy.wait()


def prepare(half, lengths, token_codes, own, residuals):
    half_rows, width = own.shape
    passages = lengths.shape[0]
    slots = token_codes.shape[0] // passages
    most = passages * (slots // CHUNK) + SCORE_GROUP + slots // CHUNK
    most = -(-most // 1024) * 1024
    return pl.pallas_call(
        prepare_kernel,
        out_shape=(
            pltpu.VMEM((2 * half_rows, width), jnp.float32),
            pltpu.VMEM(residuals.shape, jnp.bfloat16),
            pltpu.VMEM(token_codes.shape, jnp.int32),
            pltpu.VMEM((most,), jnp.int32),
            pltpu.VMEM((most,), jnp.int32),
            pltpu.VMEM((16, width), jnp.bfloat16),
        ),
        in_specs=[SMEM, HBM, HBM, HBM, HBM],
        out_specs=(VMEM,) * 6,
        scratch_shapes=[
            pltpu.SMEM(lengths.shape, jnp.int32),
            pltpu.SMEM((most,), jnp.int32),
            pltpu.SMEM((most,), jnp.int32),
            pltpu.VMEM((half_rows, width), jnp.bfloat16),
            pltpu.SemaphoreType.DMA((5 + PIECES,)),
        ],
        compiler_params=granted(4),
        cost_estimate=pl.CostEstimate(flops=10**7, bytes_accessed=8 * 10**6, transcendentals=0),
        name="prepare",
    )(half, pinned(lengths), pinned(token_codes), pinned(own), pinned(residuals))


def decode_kernel(step, *refs):
    if step == 0:
        half_ref, other_ref, codes, starts, lives, residuals, _, _, table, embedded = refs[:10]
    else:
        codes, starts, lives, residuals, table, _, _, embedded = refs[:8]
    nothing, codes_ref, starts_ref, lives_ref, rows, sems = refs[-6:]
    tokens = codes_ref.shape[0]
    width = rows.shape[1]
    moves = []
    pairs = ((starts, starts_ref), (lives, lives_ref), (codes, codes_ref))
    for k, (source, to) in enumerate(pairs):
        moves.append(pltpu.make_async_copy(source, to, sems.at[k]))
        moves[-1].start()
    nothing[...] = jnp.zeros(nothing.shape, nothing.dtype)
    if step == 0:
        half_rows = other_ref.shape[0]
        piece = half_rows // PIECES
        for k in range(PIECES):
            to = pl.ds(pl.multiple_of((1 - half_ref[0]) * half_rows + k * piece, piece), piece)
            table[to, :] = other_ref[pl.ds(k * piece, piece), :].astype(jnp.float32)

    slot_numbers = lax.broadcasted_iota(jnp.int32, (CHUNK, width), 0)
    table_single = table.reshape(table.shape[0], 1, width)
    rows_single = rows.reshape(rows.shape[0], 1, width)

    def fetch(g):
        for k in range(GROUP):
            at = jnp.minimum(starts_ref[g * GROUP + k], tokens - CHUNK)
            for j in range(CHUNK):
                rows_single[k * CHUNK + j] = table_single[codes_ref[at + j]]

    def finish(g):
        summed = []
        for k in range(GROUP):
            at = jnp.minimum(starts_ref[g * GROUP + k], tokens - CHUNK)
            near = residuals[pl.ds(pl.multiple_of(at, CHUNK), CHUNK), :]
            vectors = rows[pl.ds(k * CHUNK, CHUNK), :] + near.astype(jnp.float32)
            live = slot_numbers < lives_ref[g * GROUP + k]
            summed.append(jnp.where(live, vectors, vectors[0:1, :]))
        return normalized(jnp.concatenate(summed, axis=0))

    def keep(g, done):
        size = GROUP * CHUNK
        embedded[pl.ds(pl.multiple_of(g * size, size), size), :] = done

    for move in moves:
        move.wait()
    groups = quotient(starts_ref[starts_ref.shape[0] - 1] + GROUP - 1, GROUP)
    groups = jnp.maximum(groups, STEPS)
    low = quotient(groups * (65536 * step // STEPS + 1), 65536)
    high = quotient(groups * (65536 * (step + 1) // STEPS + 1), 65536)
    fetch(low)

    def decode(g, carry):
        done = finish(g - 1)
        fetch(g)
        keep(g - 1, done)
        return carry

    lax.fori_loop(low + 1, high, decode, 0)
    keep(high - 1, finish(high - 1))


def decode_step(step, half, other, codes, starts, lives, residuals, table, embedded, held):
    tokens, width = residuals.shape
    rounding = SCORE_GROUP * CHUNK
    space = (-(-tokens // rounding) * rounding, width)
    inside = lambda array: pinned(array, pltpu.VMEM)
    shared = [inside(codes), inside(starts), inside(lives), inside(residuals), inside(table)]
    if step == 0:
        operands = [half, inside(other)] + shared + [inside(held)]
        in_specs = [SMEM] + [VMEM] * 7
        out_shape = [pltpu.VMEM(table.shape, table.dtype), pltpu.VMEM(space, jnp.bfloat16)]
        aliases = {6: 0}
    else:
        operands = shared + [inside(embedded), inside(held)]
        in_specs = [VMEM] * 7
        out_shape = [pltpu.VMEM(space, jnp.bfloat16)]
        aliases = {5: 0}
    out_shape.append(pltpu.VMEM((16, width), jnp.bfloat16))
    results = pl.pallas_call(
        functools.partial(decode_kernel, step),
        out_shape=tuple(out_shape),
        in_specs=in_specs,
        out_specs=(VMEM,) * len(out_shape),
        input_output_aliases=aliases,
        scratch_shapes=[
            pltpu.SMEM((tokens,), jnp.int32),
            pltpu.SMEM(starts.shape, jnp.int32),
            pltpu.SMEM(lives.shape, jnp.int32),
            pltpu.VMEM((GROUP * CHUNK, width), jnp.float32),
            pltpu.SemaphoreType.DMA((3,)),
        ],
        compiler_params=granted(4),
        cost_estimate=pl.CostEstimate(flops=10**7, bytes_accessed=10**7, transcendentals=0),
        name="decode",
    )(*operands)
    if step == 0:
        return results
    return (table,) + tuple(results)


def score_kernel(
    token_count,
    local_queries,
    slots,
    me_ref,
    starts,
    queries_ref,
    embedded,
    out_ref,
    at_ref,
    turned,
    largest,
    sem,
):
    starts_copy = pltpu.make_async_copy(starts, at_ref, sem)
    starts_copy.start()
    passages = out_ref.shape[1]
    query_tokens = queries_ref.shape[0]
    block = min(QUERY_BLOCK, query_tokens)
    blocks = query_tokens // block
    per_block = block // token_count
    owner = lax.broadcasted_iota(jnp.int32, (per_block, block), 0)
    token_of = quotient(lax.broadcasted_iota(jnp.int32, (per_block, block), 1), token_count)
    block_targets = per_block // local_queries
    near_me = me_ref[0] & (block_targets - 1)
    far_me = quotient(me_ref[0], block_targets)
    owner_target = quotient(owner, local_queries)
    relative = (owner_target ^ near_me) * local_queries + owner - owner_target * local_queries
    summing = (relative == token_of).astype(jnp.bfloat16)

    def score_block(b, carry):
        at = pl.ds(pl.multiple_of(b * block, block), block)
        vectors = normalized(queries_ref[at, :].astype(jnp.float32))
        turned[...] = vectors.astype(jnp.float32).T.astype(jnp.bfloat16)

        def score(g, so_far):
            count = SCORE_GROUP // SCORE_PARTS
            size = count * CHUNK
            for part in range(SCORE_PARTS):
                first = g * SCORE_PARTS + part
                at = pl.ds(pl.multiple_of(first * size, size), size)
                similar = jnp.dot(embedded[at, :], turned[...], preferred_element_type=jnp.float32)
                parts = jnp.max(similar.reshape(count, CHUNK // 8, 8, block), axis=1)
                for k in range(count):
                    start = at_ref[first * count + k]
                    p = quotient(start, slots)
                    so_far = jnp.where(start == p * slots, parts[k], jnp.maximum(so_far, parts[k]))
                    to = pl.multiple_of(p * 8, 8)
                    for lane in range(block // 128):
                        largest[lane, pl.ds(to, 8), :] = so_far[:, lane * 128 : (lane + 1) * 128]
            return so_far

        @pl.when(b == 0)
        def arrived():
            starts_copy.wait()

        groups = quotient(at_ref[at_ref.shape[0] - 1] + SCORE_GROUP - 1, SCORE_GROUP)
        lax.fori_loop(0, groups, score, jnp.zeros((8, block), jnp.float32))
        kept = []
        for lane in range(block // 128):
            best = largest[lane, pl.ds(0, passages, stride=8), :]
            for k in range(1, 8):
                best = jnp.maximum(best, largest[lane, pl.ds(k, passages, stride=8), :])
            kept.append(best)
        best = jnp.concatenate(kept, axis=1)
        sums = jnp.zeros((per_block, passages), jnp.float32)
        for _ in range(3):
            part = best.astype(jnp.bfloat16)
            best = best - part.astype(jnp.float32)
            sums = sums + lax.dot_general(
                summing, part, (((1,), (1,)), ((), ())), preferred_element_type=jnp.float32
            )
        to = pl.multiple_of((b ^ far_me) * per_block, per_block)
        out_ref[pl.ds(to, per_block), :] = sums
        return carry

    lax.fori_loop(0, blocks, score_block, 0)


def score_all(me, starts, query_rows, embedded, passages, slots, token_count, local_queries):
    query_tokens, width = query_rows.shape
    block = min(QUERY_BLOCK, query_tokens)
    blocks = query_tokens // block
    return pl.pallas_call(
        functools.partial(score_kernel, token_count, local_queries, slots),
        out_shape=jax.ShapeDtypeStruct((query_tokens // token_count, passages), jnp.float32),
        in_specs=[SMEM, VMEM, VMEM, VMEM],
        out_specs=VMEM,
        scratch_shapes=[
            pltpu.SMEM(starts.shape, jnp.int32),
            pltpu.VMEM((width, block), jnp.bfloat16),
            pltpu.VMEM((block // 128, (passages + 1) * 8, 128), jnp.float32),
            pltpu.SemaphoreType.DMA,
        ],
        compiler_params=granted(8 + 2 * blocks),
        name="score",
    )(
        me,
        pinned(starts, pltpu.VMEM),
        pinned(query_rows, pltpu.VMEM),
        pinned(embedded, pltpu.VMEM),
    )


def pick_kernel(passages, candidates_ref, returned_ref, out_ref):
    local_queries, count = candidates_ref.shape
    targets = returned_ref.shape[0]
    passage_numbers = lax.broadcasted_iota(jnp.int32, (passages, count), 0)
    target_numbers = lax.broadcasted_iota(jnp.int32, (targets, count), 0)
    for q in range(local_queries):
        wanted = candidates_ref[q : q + 1, :]
        target = quotient(wanted, passages)
        hits = (passage_numbers == wanted - target * passages).astype(jnp.bfloat16)
        left = returned_ref[:, q * passages : (q + 1) * passages]
        picked = jnp.zeros((targets, count), jnp.float32)
        for _ in range(3):
            part = left.astype(jnp.bfloat16)
            left = left - part.astype(jnp.float32)
            picked = picked + jnp.dot(part, hits, preferred_element_type=jnp.float32)
        kept = jnp.where(target_numbers == target, picked, 0.0)
        out_ref[q : q + 1, :] = jnp.sum(kept, axis=0, keepdims=True)


def pick(candidates, returned, passages):
    return pl.pallas_call(
        functools.partial(pick_kernel, passages),
        out_shape=jax.ShapeDtypeStruct(candidates.shape, jnp.float32),
        in_specs=[VMEM, VMEM],
        out_specs=VMEM,
        compiler_params=granted(8),
        name="pick",
    )(candidates, pltpu.with_memory_space_constraint(returned, pltpu.VMEM))


def body(queries, candidates, token_codes, residuals, lengths, centroids):
    local_queries, token_count, width = queries.shape
    targets = lax.axis_size("shard") * lax.axis_size("sub")
    passages, slots = token_codes.shape
    half = lax.axis_index("sub").astype(jnp.int32)
    me = lax.axis_index("shard").astype(jnp.int32) * lax.axis_size("sub") + half
    half = half.reshape(1)
    near = residuals.reshape(passages * slots, width)
    other = lax.ppermute(centroids, "sub", [(0, 1), (1, 0)])

    held = queries.reshape(1, 1, local_queries * token_count, width)
    bits = targets.bit_length() - 1
    embedded = None
    for turn, first in enumerate(range(bits - 1, -1, -1)):
        pairs = [(device, device ^ (1 << first)) for device in range(targets)]
        received = lax.ppermute(held, ("shard", "sub"), pairs)
        if turn == 0:
            ready = prepare(half, lengths, token_codes.reshape(passages * slots), centroids, near)
            table, near, codes, starts, lives, nothing = ready
        elif turn <= STEPS:
            table, embedded, nothing = decode_step(
                turn - 1, half, other, codes, starts, lives, near, table, embedded, held
            )
        received = received + nothing[0:1, :]
        held = jnp.concatenate([held, received], axis=1)
        if first > 0:
            held = held.reshape((-1, 1) + held.shape[2:])
    query_rows = held.reshape(targets * local_queries * token_count, width)
    scores = score_all(
        me.reshape(1), starts, query_rows, embedded, passages, slots, token_count, local_queries
    )
    returned = lax.all_to_all(
        scores.reshape(targets, local_queries * passages),
        ("shard", "sub"),
        split_axis=0,
        concat_axis=0,
        tiled=True,
    )
    return pick(candidates, returned, passages)


def solution(mesh):
    placed = (
        P(("groups", "shard", "sub"), None, None),
        P(("groups", "shard", "sub"), None),
        P(("groups", "shard", "sub"), None),
        P(("groups", "shard", "sub"), None, None),
        P(("groups", "shard", "sub")),
        P(("groups", "shard", "sub"), None),
    )
    return jax.shard_map(
        body,
        mesh=mesh,
        in_specs=placed,
        out_specs=P(("groups", "shard", "sub"), None),
        check_vma=False,
    )
```

time: 36.1 us -> 47.7 us (1.32)
  local copies, waits for them, and re-layouts: 0.01 us -> 13.2 us
  blocking collectives: 12 us -> 8.98 us
  Pallas kernels: 15.9 us -> 17.2 us
    unnamed x2 -> x14, local copies, waits for them, and re-layouts: 0.01 us -> 13.2 us
    ppermute x0 -> x4, starting transfers between devices: none -> 7.18 us  [body(): received = lax.ppermute(held, ('shard', 'sub'), pairs)]
    all_to_all x1 -> x0, starting transfers between devices: 7.02 us -> none  [body(): lax.all_to_all(sent, ('shard', 'sub'), split_axis=0, concat_axis=0, tiled...]
    all_to_all x1, blocking collectives: 12 us -> 8.98 us  [body(): lax.all_to_all(scores.reshape(targets, local_queries * passages), ('shard...]
    pallas_call x4 -> x5, Pallas kernels: 15.3 us -> 16.6 us  [the longest x3 10.9 us: decode_step(): pl.pallas_call(functools.partial(decode_kernel, step), out_shape=tuple(ou...]
  transfers between devices with their start and end apart: 2 -> 5, of which waited for: 0 -> 0; matrix products, arithmetic and copies ran while one was open for 0% -> 0% of each run, Pallas kernels for 32% -> 29%
where the time goes in v16:
time: 47.7 us; the launch traced here: 47.3 us
  Pallas kernels  17.2 us (36%)
  local copies, waits for them, and re-layouts  13.2 us (28%)
  blocking collectives  8.98 us (19%)
  starting transfers between devices  7.63 us (16%)
    unnamed x14, local copies, waits for them, and re-layouts  13.2 us
    pallas_call x3, Pallas kernels, decode_step(): pl.pallas_call(functools.partial(decode_kernel, step), out_shape=tuple(ou...  10.9 us
    all_to_all x1, blocking collectives, body(): lax.all_to_all(scores.reshape(targets, local_queries * passages), ('shard...  8.98 us
    ppermute x4, starting transfers between devices, body(): received = lax.ppermute(held, ('shard', 'sub'), pairs)  7.18 us
    pallas_call x1, Pallas kernels, score_all(): pl.pallas_call(functools.partial(score_kernel, token_count, local_queries...  3.03 us
    pallas_call x1, Pallas kernels, prepare(): pl.pallas_call(prepare_kernel, out_shape=(pltpu.VMEM((2 * half_rows, widt...  2.59 us
  transfers between devices with their start and end apart: 5, of which 0 were waited for; matrix products, arithmetic and copies ran while one was open for 0% of the time, Pallas kernels for 29%

profile of v16, /device:TPU:0, one launch (start us, length us, event | category | flops | bytes accessed | tf_op | source)
XLA Modules:
  0.0 47.3 jit_solution(2845709938492194420)
XLA Ops:
  0.0 0.5 collective-permute-start.2
  0.5 3.6 %collective-permute-start = (bf16[1,1,32,128]{3,2,1,0:T(8,128)(2,1)}, bf16[1,1,32,128]{3,2,1,0:T(8,128)(2,1)S(1)}, u32[]{:S(2)}, u32[]{:S(2)}) collective-permute-start(bf16[1,1,32,128]{3,2,1,0:T(8,128)(2,1)} %bitcast.33), channel_id=1, source_target_pairs={{0,8},{1,9},{2,10},{3,11},{4,12},{5,13},{6,14},{7,15},{8,0},{9,1},... | collective-permute-start | bytes 24584 | tf_op jit(solution)/shard_map/ppermute | solution.py:384
  4.0 0.0 copy-start.6
  4.0 2.6 %prepare.1 = (f32[16384,128]{1,0:T(8,128)S(1)}, bf16[8192,128]{1,0:T(8,128)(2,1)S(1)}, s32[8192]{0:T(1024)S(1)}, s32[1024]{0:T(1024)S(1)}, s32[1024]{0:T(1024)S(1)}, /*index=5*/bf16[16,128]{1,0:T(8,128)(2,1)S(1)}) custom-call(s32[1]{0:T(128)} %bitcast.1.half_ref.refs_0_, s32[64]{0:T(128)} %lengths_hbm.1, s32[8192]{0:T(1024)} %bitcast.32, ...), custom_call_target="tpu_custom_call" | custom-call | flops 10000000 | bytes 8000000 | tf_op jit(solution)/shard_map/prepare/pallas_call | solution.py:108
  6.6 0.0 copy-start
  6.6 3.2 %copy-done = f32[16384,128]{1,0:T(8,128)} copy-done((f32[16384,128]{1,0:T(8,128)}, f32[16384,128]{1,0:T(8,128)S(1)}, u32[]{:S(2)}) %copy-start) | copy-done | bytes 8388632
  9.9 0.0 collective-permute-done
  9.9 0.0 copy-done.6
  9.9 1.6 %collective-permute-start.1 = (bf16[2,1,32,128]{3,2,1,0:T(8,128)(2,1)S(1)}, bf16[2,1,32,128]{3,2,1,0:T(8,128)(2,1)S(1)}, u32[]{:S(2)}, u32[]{:S(2)}) collective-permute-start(bf16[2,1,32,128]{3,2,1,0:T(8,128)(2,1)S(1)} %maximum_bitcast_fusion.refs_7_), channel_id=1, source_target_pairs={{0,4},{1,5},{2,6},{3,7},{4,0},{5,1},{6,2},{7,3},{8,12},{9,13},{10,... | collective-permute-start | bytes 49160 | tf_op jit(solution)/shard_map/ppermute | solution.py:384
  11.5 0.0 collective-permute-done.2.refs_1_
  11.5 0.0 copy-start.1
  11.5 3.4 %copy-done.1 = f32[16384,128]{1,0:T(8,128)S(1)} copy-done((f32[16384,128]{1,0:T(8,128)S(1)}, f32[16384,128]{1,0:T(8,128)}, u32[]{:S(2)}) %copy-start.1) | copy-done | bytes 8388632
  14.9 4.5 %decode.3 = (f32[16384,128]{1,0:T(8,128)S(1)}, bf16[8192,128]{1,0:T(8,128)(2,1)S(1)}, bf16[16,128]{1,0:T(8,128)(2,1)S(1)}) custom-call(s32[1]{0:T(128)} %bitcast.1.half_ref.refs_0_, bf16[8192,128]{1,0:T(8,128)(2,1)} %collective-permute-done.2.refs_1_, s32[8192]{0:T(1024)S(1)} %get-tuple-element.20.refs_2_.refs_0_, ...), custom_call_target="tpu_custom_call", output_to_operand_aliasing={{0}: (6, {})} | custom-call | flops 10000000 | bytes 10000000 | tf_op jit(solution)/shard_map/decode/pallas_call | solution.py:213
  19.4 0.0 copy-start.2
  19.4 3.2 %copy-done.2 = f32[16384,128]{1,0:T(8,128)} copy-done((f32[16384,128]{1,0:T(8,128)}, f32[16384,128]{1,0:T(8,128)S(1)}, u32[]{:S(2)}) %copy-start.2) | copy-done | bytes 8388632
  22.6 0.0 collective-permute-done.1
  22.7 1.9 %collective-permute-start.3 = (bf16[4,1,32,128]{3,2,1,0:T(8,128)(2,1)S(1)}, bf16[4,1,32,128]{3,2,1,0:T(8,128)(2,1)S(1)}, u32[]{:S(2)}, u32[]{:S(2)}) collective-permute-start(bf16[4,1,32,128]{3,2,1,0:T(8,128)(2,1)S(1)} %bitcast.26), channel_id=1, source_target_pairs={{0,2},{1,3},{2,0},{3,1},{4,6},{5,7},{6,4},{7,5},{8,10},{9,11},{10,... | collective-permute-start | bytes 98312 | tf_op jit(solution)/shard_map/ppermute | solution.py:384
  24.5 0.0 copy-start.3
  24.5 3.4 %copy-done.3 = f32[16384,128]{1,0:T(8,128)S(1)} copy-done((f32[16384,128]{1,0:T(8,128)S(1)}, f32[16384,128]{1,0:T(8,128)}, u32[]{:S(2)}) %copy-start.3) | copy-done | bytes 8388632
  27.9 0.0 copy-start.4
  27.9 3.2 %decode.4 = (bf16[8192,128]{1,0:T(8,128)(2,1)S(1)}, bf16[16,128]{1,0:T(8,128)(2,1)S(1)}) custom-call(s32[8192]{0:T(1024)S(1)} %get-tuple-element.20.refs_2_.refs_0_, s32[1024]{0:T(1024)S(1)} %get-tuple-element.18.refs_3_.refs_1_.starts, s32[1024]{0:T(1024)S(1)} %get-tuple-element.21.refs_4_.refs_2_, ...), custom_call_target="tpu_custom_call", output_to_operand_aliasing={{0}: (5, {})} | custom-call | flops 10000000 | bytes 10000000 | tf_op jit(solution)/shard_map/decode/pallas_call | solution.py:213
  31.2 0.0 collective-permute-done.3
  31.2 0.1 collective-permute-start.4
  31.3 0.0 copy-done.4
  31.3 3.2 %decode.5 = (bf16[8192,128]{1,0:T(8,128)(2,1)S(1)}, bf16[16,128]{1,0:T(8,128)(2,1)S(1)}) custom-call(s32[8192]{0:T(1024)S(1)} %get-tuple-element.20.refs_2_.refs_0_, s32[1024]{0:T(1024)S(1)} %get-tuple-element.18.refs_3_.refs_1_.starts, s32[1024]{0:T(1024)S(1)} %get-tuple-element.21.refs_4_.refs_2_, ...), custom_call_target="tpu_custom_call", output_to_operand_aliasing={{0}: (5, {})} | custom-call | flops 10000000 | bytes 10000000 | tf_op jit(solution)/shard_map/decode/pallas_call | solution.py:213
  34.5 0.0 copy-start.5
  34.6 0.0 collective-permute-done.4
  34.6 3.0 %score.1 = f32[16,64]{1,0:T(8,128)S(1)} custom-call(s32[1]{0:T(128)} %bitcast.me_ref, s32[1024]{0:T(1024)S(1)} %get-tuple-element.18.refs_3_.refs_1_.starts, bf16[512,128]{1,0:T(8,128)(2,1)S(1)} %bitcast.25, bf16[8192,128]{1,0:T(8,128)(2,1)S(1)} %get-tuple-element.30.embedded), custom_call_target="tpu_custom_call" | custom-call | tf_op jit(solution)/shard_map/score/pallas_call | solution.py:318
  37.6 9.0 %all_to_all.11 = f32[16,1,64]{2,1,0:T(1,128)S(1)} all-to-all(f32[16,1,64]{2,1,0:T(1,128)S(1)} %bitcast.29), channel_id=1, replica_groups=mesh['groups'=2,'shard'=8,'sub'=2] {'shard','sub'}, dimensions={0} | all-to-all | bytes 8192 | tf_op jit(solution)/shard_map/all_to_all | solution.py:400
  46.6 0.0 copy-done.5
  46.6 0.7 %pick.1 = f32[1,62]{1,0:T(1,128)} custom-call(s32[1,62]{1,0:T(1,128)S(1)} %copy-done.5, f32[16,64]{1,0:T(8,128)S(1)} %bitcast.30), custom_call_target="tpu_custom_call" | custom-call | tf_op jit(solution)/shard_map/pick/pallas_call | solution.py:359
  (12 shorter events, 0.1 us)
Async XLA Ops:
  0.0 11.5 %collective-permute-start.2 = (bf16[8192,128]{1,0:T(8,128)(2,1)}, bf16[8192,128]{1,0:T(8,128)(2,1)}, u32[]{:S(2)}, u32[]{:S(2)}) collective-permute-start(bf16[8192,128]{1,0:T(8,128)(2,1)} %own_hbm.1), channel_id=1, source_target_pairs={{0,1},{1,0},{2,3},{3,2},{4,5},{5,4},{6,7},{7,6},{8,9},{9,8},{10,11... | collective-permute-start | bytes 6291464 | tf_op jit(solution)/shard_map/ppermute | solution.py:377
  0.5 9.4 %collective-permute-start = (bf16[1,1,32,128]{3,2,1,0:T(8,128)(2,1)}, bf16[1,1,32,128]{3,2,1,0:T(8,128)(2,1)S(1)}, u32[]{:S(2)}, u32[]{:S(2)}) collective-permute-start(bf16[1,1,32,128]{3,2,1,0:T(8,128)(2,1)} %bitcast.33), channel_id=1, source_target_pairs={{0,8},{1,9},{2,10},{3,11},{4,12},{5,13},{6,14},{7,15},{8,0},{9,1},... | collective-permute-start | bytes 24584 | tf_op jit(solution)/shard_map/ppermute | solution.py:384
  4.0 5.8 %copy-start.6 = (bf16[1,32,128]{2,1,0:T(8,128)(2,1)S(1)}, bf16[1,32,128]{2,1,0:T(8,128)(2,1)}, u32[]{:S(2)}) copy-start(bf16[1,32,128]{2,1,0:T(8,128)(2,1)} %param.6) | copy-start | bytes 24580
  6.6 3.2 %copy-start = (f32[16384,128]{1,0:T(8,128)}, f32[16384,128]{1,0:T(8,128)S(1)}, u32[]{:S(2)}) copy-start(f32[16384,128]{1,0:T(8,128)S(1)} %get-tuple-element.23.refs_6_) | copy-start | bytes 25165828
  9.9 12.7 %collective-permute-start.1 = (bf16[2,1,32,128]{3,2,1,0:T(8,128)(2,1)S(1)}, bf16[2,1,32,128]{3,2,1,0:T(8,128)(2,1)S(1)}, u32[]{:S(2)}, u32[]{:S(2)}) collective-permute-start(bf16[2,1,32,128]{3,2,1,0:T(8,128)(2,1)S(1)} %maximum_bitcast_fusion.refs_7_), channel_id=1, source_target_pairs={{0,4},{1,5},{2,6},{3,7},{4,0},{5,1},{6,2},{7,3},{8,12},{9,13},{10,... | collective-permute-start | bytes 49160 | tf_op jit(solution)/shard_map/ppermute | solution.py:384
  11.5 3.4 %copy-start.1 = (f32[16384,128]{1,0:T(8,128)S(1)}, f32[16384,128]{1,0:T(8,128)}, u32[]{:S(2)}) copy-start(f32[16384,128]{1,0:T(8,128)} %copy-done) | copy-start | bytes 25165828
  19.4 3.2 %copy-start.2 = (f32[16384,128]{1,0:T(8,128)}, f32[16384,128]{1,0:T(8,128)S(1)}, u32[]{:S(2)}) copy-start(f32[16384,128]{1,0:T(8,128)S(1)} %get-tuple-element.25.refs_4_) | copy-start | bytes 25165828
  22.7 8.5 %collective-permute-start.3 = (bf16[4,1,32,128]{3,2,1,0:T(8,128)(2,1)S(1)}, bf16[4,1,32,128]{3,2,1,0:T(8,128)(2,1)S(1)}, u32[]{:S(2)}, u32[]{:S(2)}) collective-permute-start(bf16[4,1,32,128]{3,2,1,0:T(8,128)(2,1)S(1)} %bitcast.26), channel_id=1, source_target_pairs={{0,2},{1,3},{2,0},{3,1},{4,6},{5,7},{6,4},{7,5},{8,10},{9,11},{10,... | collective-permute-start | bytes 98312 | tf_op jit(solution)/shard_map/ppermute | solution.py:384
  24.5 3.4 %copy-start.3 = (f32[16384,128]{1,0:T(8,128)S(1)}, f32[16384,128]{1,0:T(8,128)}, u32[]{:S(2)}) copy-start(f32[16384,128]{1,0:T(8,128)} %copy-done.2) | copy-start | bytes 25165828
  27.9 3.4 %copy-start.4 = (f32[16384,128]{1,0:T(8,128)S(1)}, f32[16384,128]{1,0:T(8,128)}, u32[]{:S(2)}) copy-start(f32[16384,128]{1,0:T(8,128)} %copy-done.2) | copy-start | bytes 25165828
  31.2 3.4 %collective-permute-start.4 = (bf16[8,1,32,128]{3,2,1,0:T(8,128)(2,1)S(1)}, bf16[8,1,32,128]{3,2,1,0:T(8,128)(2,1)S(1)}, u32[]{:S(2)}, u32[]{:S(2)}) collective-permute-start(bf16[8,1,32,128]{3,2,1,0:T(8,128)(2,1)S(1)} %bitcast.22), channel_id=1, source_target_pairs={{0,1},{1,0},{2,3},{3,2},{4,5},{5,4},{6,7},{7,6},{8,9},{9,8},{10,11... | collective-permute-start | bytes 196616 | tf_op jit(solution)/shard_map/ppermute | solution.py:384
  34.5 12.1 %copy-start.5 = (s32[1,62]{1,0:T(1,128)S(1)}, s32[1,62]{1,0:T(1,128)}, u32[]{:S(2)}) copy-start(s32[1,62]{1,0:T(1,128)} %candidates_ref.1) | copy-start | bytes 748

commit v17 on v16

--- a/solution.py
+++ b/solution.py
@@ -38,13 +38,19 @@
     return pltpu.CompilerParams(vmem_limit_bytes=mebibytes * 1024 * 1024)
 
 
+def shares_of(passages):
+    units = -(-passages // 8)
+    edges = [units * step // STEPS * 8 for step in range(STEPS)] + [passages]
+    return list(zip(edges[:-1], edges[1:]))
+
+
 def prepare_kernel(
-    half_ref,
+    me_ref,
     lengths_hbm,
     codes_hbm,
     own_hbm,
     residuals_hbm,
-    table,
+    staged,
     residuals,
     codes,
     starts,
@@ -53,27 +59,22 @@
     lengths_ref,
     starts_ref,
     lives_ref,
-    staged,
     sems,
 ):
+    del me_ref
     passages = lengths_ref.shape[0]
     slots = codes_hbm.shape[0] // passages
-    half_rows = own_hbm.shape[0]
     moves = []
 
     def move(source, to):
         moves.append(pltpu.make_async_copy(source, to, sems.at[len(moves)]))
         moves[-1].start()
-        return moves[-1]
-
-    lengths_copy = move(lengths_hbm, lengths_ref)
-    piece = half_rows // PIECES
-    copies = []
-    for k in range(PIECES):
-        at = pl.ds(k * piece, piece)
-        copies.append(move(own_hbm.at[at], staged.at[at]))
-    codes_copy = move(codes_hbm, codes)
-    residual_copy = move(residuals_hbm, residuals)
+
+    lengths_copy = pltpu.make_async_copy(lengths_hbm, lengths_ref, sems.at[5])
+    lengths_copy.start()
+    move(codes_hbm, codes)
+    move(own_hbm, staged)
+    move(residuals_hbm, residuals)
     nothing[...] = jnp.zeros(nothing.shape, nothing.dtype)
     lengths_copy.wait()
 
@@ -84,31 +85,38 @@
             lives_ref[chunks + k] = length - k * CHUNK
         return chunks + quotient(length + CHUNK - 1, CHUNK)
 
-    chunks = lax.fori_loop(0, passages, listing, 0, unroll=4)
+    last = starts_ref.shape[0] - 1
+    chunks = jnp.int32(0)
+    for step, (low, high) in enumerate(shares_of(passages)):
+        chunks = lax.fori_loop(low, high, listing, chunks, unroll=4)
+        for k in range(GROUP):
+            starts_ref[chunks + k] = passages * slots
+            lives_ref[chunks + k] = 0
+        chunks = quotient(chunks + GROUP - 1, GROUP) * GROUP
+        starts_ref[last - STEPS + step] = quotient(chunks, GROUP)
     for k in range(SCORE_GROUP):
         starts_ref[chunks + k] = passages * slots
-        lives_ref[chunks + k] = 0
-    starts_ref[starts_ref.shape[0] - 1] = chunks
-    starts_copy = move(starts_ref, starts)
-    lives_copy = move(lives_ref, lives)
-    for k in range(PIECES):
-        copies[k].wait()
-        to = pl.ds(pl.multiple_of(half_ref[0] * half_rows + k * piece, piece), piece)
-        table[to, :] = staged[pl.ds(k * piece, piece), :].astype(jnp.float32)
-    for copy in (codes_copy, starts_copy, lives_copy, residual_copy):
+    starts_ref[last] = chunks
+    move(starts_ref, starts)
+    move(lives_ref, lives)
+    for copy in moves:
         copy.wait()
 
 
-def prepare(half, lengths, token_codes, own, residuals):
-    half_rows, width = own.shape
+def list_size(passages, slots):
+    most = passages * (slots // CHUNK) + STEPS * GROUP + SCORE_GROUP + STEPS + 1
+    return -(-most // 1024) * 1024
+
+
+def prepare(me, lengths, token_codes, own, residuals):
+    width = own.shape[1]
     passages = lengths.shape[0]
     slots = token_codes.shape[0] // passages
-    most = passages * (slots // CHUNK) + SCORE_GROUP + slots // CHUNK
-    most = -(-most // 1024) * 1024
+    most = list_size(passages, slots)
     return pl.pallas_call(
         prepare_kernel,
         out_shape=(
-            pltpu.VMEM((2 * half_rows, width), jnp.float32),
+            pltpu.VMEM(own.shape, jnp.bfloat16),
             pltpu.VMEM(residuals.shape, jnp.bfloat16),
             pltpu.VMEM(token_codes.shape, jnp.int32),
             pltpu.VMEM((most,), jnp.int32),
@@ -121,25 +129,27 @@
             pltpu.SMEM(lengths.shape, jnp.int32),
             pltpu.SMEM((most,), jnp.int32),
             pltpu.SMEM((most,), jnp.int32),
-            pltpu.VMEM((half_rows, width), jnp.bfloat16),
-            pltpu.SemaphoreType.DMA((5 + PIECES,)),
+            pltpu.SemaphoreType.DMA((6,)),
         ],
         compiler_params=granted(4),
         cost_estimate=pl.CostEstimate(flops=10**7, bytes_accessed=8 * 10**6, transcendentals=0),
         name="prepare",
-    )(half, pinned(lengths), pinned(token_codes), pinned(own), pinned(residuals))
-
-
-def decode_kernel(step, *refs):
+    )(me, pinned(lengths), pinned(token_codes), pinned(own), pinned(residuals))
+
+
+def decode_kernel(step, passages, *refs):
     if step == 0:
-        half_ref, other_ref, codes, starts, lives, residuals, _, _, table, embedded = refs[:10]
+        half_ref, own_ref, other_ref, codes, starts, lives, residuals, _, table, embedded = refs[:10]
     else:
         codes, starts, lives, residuals, table, _, _, embedded = refs[:8]
     nothing, codes_ref, starts_ref, lives_ref, rows, sems = refs[-6:]
     tokens = codes_ref.shape[0]
+    slots = tokens // passages
     width = rows.shape[1]
     moves = []
-    pairs = ((starts, starts_ref), (lives, lives_ref), (codes, codes_ref))
+    first, after = shares_of(passages)[step]
+    part = pl.ds(first * slots, (after - first) * slots)
+    pairs = ((starts, starts_ref), (lives, lives_ref), (codes.at[part], codes_ref.at[part]))
     for k, (source, to) in enumerate(pairs):
         moves.append(pltpu.make_async_copy(source, to, sems.at[k]))
         moves[-1].start()
@@ -147,9 +157,10 @@
     if step == 0:
         half_rows = other_ref.shape[0]
         piece = half_rows // PIECES
-        for k in range(PIECES):
-            to = pl.ds(pl.multiple_of((1 - half_ref[0]) * half_rows + k * piece, piece), piece)
-            table[to, :] = other_ref[pl.ds(k * piece, piece), :].astype(jnp.float32)
+        for source, base in ((own_ref, half_ref[0]), (other_ref, 1 - half_ref[0])):
+            for k in range(PIECES):
+                to = pl.ds(pl.multiple_of(base * half_rows + k * piece, piece), piece)
+                table[to, :] = source[pl.ds(k * piece, piece), :].astype(jnp.float32)
 
     slot_numbers = lax.broadcasted_iota(jnp.int32, (CHUNK, width), 0)
     table_single = table.reshape(table.shape[0], 1, width)
@@ -157,7 +168,7 @@
 
     def fetch(g):
         for k in range(GROUP):
-            at = jnp.minimum(starts_ref[g * GROUP + k], tokens - CHUNK)
+            at = jnp.minimum(starts_ref[g * GROUP + k], after * slots - CHUNK)
             for j in range(CHUNK):
                 rows_single[k * CHUNK + j] = table_single[codes_ref[at + j]]
 
@@ -177,10 +188,9 @@
 
     for move in moves:
         move.wait()
-    groups = quotient(starts_ref[starts_ref.shape[0] - 1] + GROUP - 1, GROUP)
-    groups = jnp.maximum(groups, STEPS)
-    low = quotient(groups * (65536 * step // STEPS + 1), 65536)
-    high = quotient(groups * (65536 * (step + 1) // STEPS + 1), 65536)
+    last = starts_ref.shape[0] - 1
+    low = starts_ref[last - STEPS + step - 1] if step > 0 else 0
+    high = starts_ref[last - STEPS + step]
     fetch(low)
 
     def decode(g, carry):
@@ -193,25 +203,28 @@
     keep(high - 1, finish(high - 1))
 
 
-def decode_step(step, half, other, codes, starts, lives, residuals, table, embedded, held):
+def decode_step(
+    step, passages, half, own, other, codes, starts, lives, residuals, table, embedded, held
+):
     tokens, width = residuals.shape
     rounding = SCORE_GROUP * CHUNK
-    space = (-(-tokens // rounding) * rounding, width)
+    space = (-(-(tokens + STEPS * GROUP * CHUNK) // rounding) * rounding, width)
     inside = lambda array: pinned(array, pltpu.VMEM)
-    shared = [inside(codes), inside(starts), inside(lives), inside(residuals), inside(table)]
+    shared = [inside(codes), inside(starts), inside(lives), inside(residuals)]
     if step == 0:
-        operands = [half, inside(other)] + shared + [inside(held)]
+        operands = [half, inside(own), inside(other)] + shared + [inside(held)]
         in_specs = [SMEM] + [VMEM] * 7
-        out_shape = [pltpu.VMEM(table.shape, table.dtype), pltpu.VMEM(space, jnp.bfloat16)]
-        aliases = {6: 0}
+        whole = (2 * own.shape[0], width)
+        out_shape = [pltpu.VMEM(whole, jnp.float32), pltpu.VMEM(space, jnp.bfloat16)]
+        aliases = {}
     else:
-        operands = shared + [inside(embedded), inside(held)]
+        operands = shared + [inside(table), inside(embedded), inside(held)]
         in_specs = [VMEM] * 7
         out_shape = [pltpu.VMEM(space, jnp.bfloat16)]
         aliases = {5: 0}
     out_shape.append(pltpu.VMEM((16, width), jnp.bfloat16))
     results = pl.pallas_call(
-        functools.partial(decode_kernel, step),
+        functools.partial(decode_kernel, step, passages),
         out_shape=tuple(out_shape),
         in_specs=in_specs,
         out_specs=(VMEM,) * len(out_shape),
@@ -373,6 +386,7 @@
     half = lax.axis_index("sub").astype(jnp.int32)
     me = lax.axis_index("shard").astype(jnp.int32) * lax.axis_size("sub") + half
     half = half.reshape(1)
+    me = me.reshape(1)
     near = residuals.reshape(passages * slots, width)
     other = lax.ppermute(centroids, "sub", [(0, 1), (1, 0)])
 
@@ -383,11 +397,23 @@
         pairs = [(device, device ^ (1 << first)) for device in range(targets)]
         received = lax.ppermute(held, ("shard", "sub"), pairs)
         if turn == 0:
-            ready = prepare(half, lengths, token_codes.reshape(passages * slots), centroids, near)
-            table, near, codes, starts, lives, nothing = ready
+            ready = prepare(me, lengths, token_codes.reshape(passages * slots), centroids, near)
+            own, near, codes, starts, lives, nothing = ready
+            table = None
         elif turn <= STEPS:
             table, embedded, nothing = decode_step(
-                turn - 1, half, other, codes, starts, lives, near, table, embedded, held
+                turn - 1,
+                passages,
+                half,
+                own,
+                other,
+                codes,
+                starts,
+                lives,
+                near,
+                table,
+                embedded,
+                held,
             )
         received = received + nothing[0:1, :]
         held = jnp.concatenate([held, received], axis=1)
@@ -395,7 +421,7 @@
             held = held.reshape((-1, 1) + held.shape[2:])
     query_rows = held.reshape(targets * local_queries * token_count, width)
     scores = score_all(
-        me.reshape(1), starts, query_rows, embedded, passages, slots, token_count, local_queries
+        me, starts, query_rows, embedded, passages, slots, token_count, local_queries
     )
     returned = lax.all_to_all(
         scores.reshape(targets, local_queries * passages),

time: 47.7 us -> 34.3 us (0.72)
  local copies, waits for them, and re-layouts: 13.2 us -> 0.02 us
  blocking collectives: 8.98 us -> 10.1 us
  Pallas kernels: 17.2 us -> 16.3 us
    unnamed x14 -> x4, local copies, waits for them, and re-layouts: 13.2 us -> 0.01 us
    pallas_call x4, Pallas kernels: 13.5 us -> 12.2 us  [the longest x3 9.57 us: decode_step(): pl.pallas_call(functools.partial(decode_kernel, step, passages), out_shap...]
    all_to_all x1, blocking collectives: 8.98 us -> 10.1 us  [body(): lax.all_to_all(scores.reshape(targets, local_queries * passages), ('shard...]
  transfers between devices with their start and end apart: 5 -> 5, of which waited for: 0 -> 0; matrix products, arithmetic and copies ran while one was open for 0% -> 0% of each run, Pallas kernels for 29% -> 36%
where the time goes in v17:
time: 34.3 us; the launch traced here: 34 us
  Pallas kernels  16.3 us (48%)
  blocking collectives  10.1 us (29%)
  starting transfers between devices  7.31 us (21%)
    all_to_all x1, blocking collectives, body(): lax.all_to_all(scores.reshape(targets, local_queries * passages), ('shard...  10.1 us
    pallas_call x3, Pallas kernels, decode_step(): pl.pallas_call(functools.partial(decode_kernel, step, passages), out_shap...  9.57 us
    ppermute x4, starting transfers between devices, body(): received = lax.ppermute(held, ('shard', 'sub'), pairs)  6.86 us
    pallas_call x1, Pallas kernels, score_all(): pl.pallas_call(functools.partial(score_kernel, token_count, local_queries...  3.44 us
    pallas_call x1, Pallas kernels, prepare(): pl.pallas_call(prepare_kernel, out_shape=(pltpu.VMEM(own.shape, jnp.bfloa...  2.6 us
  transfers between devices with their start and end apart: 5, of which 0 were waited for; matrix products, arithmetic and copies ran while one was open for 0% of the time, Pallas kernels for 36%

profile of v17, /device:TPU:0, one launch (start us, length us, event | category | flops | bytes accessed | tf_op | source)
XLA Modules:
  0.0 34.0 jit_solution(8112122939568467975)
XLA Ops:
  0.0 0.5 %collective-permute-start.2 = (bf16[8192,128]{1,0:T(8,128)(2,1)}, bf16[8192,128]{1,0:T(8,128)(2,1)S(1)}, u32[]{:S(2)}, u32[]{:S(2)}) collective-permute-start(bf16[8192,128]{1,0:T(8,128)(2,1)} %own_hbm.1), channel_id=1, source_target_pairs={{0,1},{1,0},{2,3},{3,2},{4,5},{5,4},{6,7},{7,6},{8,9},{9,8},{10,11... | collective-permute-start | bytes 6291464 | tf_op jit(solution)/shard_map/ppermute | solution.py:391
  0.5 3.6 %collective-permute-start = (bf16[1,1,32,128]{3,2,1,0:T(8,128)(2,1)}, bf16[1,1,32,128]{3,2,1,0:T(8,128)(2,1)S(1)}, u32[]{:S(2)}, u32[]{:S(2)}) collective-permute-start(bf16[1,1,32,128]{3,2,1,0:T(8,128)(2,1)} %bitcast.33), channel_id=1, source_target_pairs={{0,8},{1,9},{2,10},{3,11},{4,12},{5,13},{6,14},{7,15},{8,0},{9,1},... | collective-permute-start | bytes 24584 | tf_op jit(solution)/shard_map/ppermute | solution.py:398
  4.0 0.0 copy-start.1
  4.0 2.6 %prepare.1 = (bf16[8192,128]{1,0:T(8,128)(2,1)S(1)}, bf16[8192,128]{1,0:T(8,128)(2,1)S(1)}, s32[8192]{0:T(1024)S(1)}, s32[1024]{0:T(1024)S(1)}, s32[1024]{0:T(1024)S(1)}, /*index=5*/bf16[16,128]{1,0:T(8,128)(2,1)S(1)}) custom-call(s32[1]{0:T(128)} %bitcast.me_ref, s32[64]{0:T(128)} %lengths_hbm.1, s32[8192]{0:T(1024)} %bitcast.32, ...), custom_call_target="tpu_custom_call" | custom-call | flops 10000000 | bytes 8000000 | tf_op jit(solution)/shard_map/prepare/pallas_call | solution.py:116
  6.7 0.0 collective-permute-done
  6.7 0.0 copy-done.1
  6.7 1.6 %collective-permute-start.1 = (bf16[2,1,32,128]{3,2,1,0:T(8,128)(2,1)S(1)}, bf16[2,1,32,128]{3,2,1,0:T(8,128)(2,1)S(1)}, u32[]{:S(2)}, u32[]{:S(2)}) collective-permute-start(bf16[2,1,32,128]{3,2,1,0:T(8,128)(2,1)S(1)} %maximum_bitcast_fusion.refs_7_), channel_id=1, source_target_pairs={{0,4},{1,5},{2,6},{3,7},{4,0},{5,1},{6,2},{7,3},{8,12},{9,13},{10,... | collective-permute-start | bytes 49160 | tf_op jit(solution)/shard_map/ppermute | solution.py:398
  8.3 0.0 collective-permute-done.2.refs_2_
  8.3 2.8 %decode.3 = (f32[16384,128]{1,0:T(8,128)S(1)}, bf16[9216,128]{1,0:T(8,128)(2,1)S(1)}, bf16[16,128]{1,0:T(8,128)(2,1)S(1)}) custom-call(s32[1]{0:T(128)} %bitcast.6.refs_0_, bf16[8192,128]{1,0:T(8,128)(2,1)S(1)} %get-tuple-element.20.refs_1_, bf16[8192,128]{1,0:T(8,128)(2,1)S(1)} %collective-permute-done.2.refs_2_, ...), custom_call_target="tpu_custom_call" | custom-call | flops 10000000 | bytes 10000000 | tf_op jit(solution)/shard_map/decode/pallas_call | solution.py:226
  11.2 0.0 collective-permute-done.1
  11.2 1.6 %collective-permute-start.3 = (bf16[4,1,32,128]{3,2,1,0:T(8,128)(2,1)S(1)}, bf16[4,1,32,128]{3,2,1,0:T(8,128)(2,1)S(1)}, u32[]{:S(2)}, u32[]{:S(2)}) collective-permute-start(bf16[4,1,32,128]{3,2,1,0:T(8,128)(2,1)S(1)} %bitcast.26), channel_id=1, source_target_pairs={{0,2},{1,3},{2,0},{3,1},{4,6},{5,7},{6,4},{7,5},{8,10},{9,11},{10,... | collective-permute-start | bytes 98312 | tf_op jit(solution)/shard_map/ppermute | solution.py:398
  12.8 3.5 %decode.4 = (bf16[9216,128]{1,0:T(8,128)(2,1)S(1)}, bf16[16,128]{1,0:T(8,128)(2,1)S(1)}) custom-call(s32[8192]{0:T(1024)S(1)} %get-tuple-element.21.refs_3_.refs_0_, s32[1024]{0:T(1024)S(1)} %get-tuple-element.18.refs_4_.refs_1_.starts, s32[1024]{0:T(1024)S(1)} %get-tuple-element.22.refs_5_.refs_2_, ...), custom_call_target="tpu_custom_call", output_to_operand_aliasing={{0}: (5, {})} | custom-call | flops 10000000 | bytes 10000000 | tf_op jit(solution)/shard_map/decode/pallas_call | solution.py:226
  16.3 0.0 collective-permute-done.3
  16.4 0.1 collective-permute-start.4
  16.5 3.2 %decode.5 = (bf16[9216,128]{1,0:T(8,128)(2,1)S(1)}, bf16[16,128]{1,0:T(8,128)(2,1)S(1)}) custom-call(s32[8192]{0:T(1024)S(1)} %get-tuple-element.21.refs_3_.refs_0_, s32[1024]{0:T(1024)S(1)} %get-tuple-element.18.refs_4_.refs_1_.starts, s32[1024]{0:T(1024)S(1)} %get-tuple-element.22.refs_5_.refs_2_, ...), custom_call_target="tpu_custom_call", output_to_operand_aliasing={{0}: (5, {})} | custom-call | flops 10000000 | bytes 10000000 | tf_op jit(solution)/shard_map/decode/pallas_call | solution.py:226
  19.7 0.0 copy-start
  19.7 0.0 collective-permute-done.4
  19.8 3.4 %score.1 = f32[16,64]{1,0:T(8,128)S(1)} custom-call(s32[1]{0:T(128)} %bitcast.me_ref, s32[1024]{0:T(1024)S(1)} %get-tuple-element.18.refs_4_.refs_1_.starts, bf16[512,128]{1,0:T(8,128)(2,1)S(1)} %bitcast.25, bf16[9216,128]{1,0:T(8,128)(2,1)S(1)} %get-tuple-element.30.embedded), custom_call_target="tpu_custom_call" | custom-call | tf_op jit(solution)/shard_map/score/pallas_call | solution.py:331
  23.2 10.1 %all_to_all.11 = f32[16,1,64]{2,1,0:T(1,128)S(1)} all-to-all(f32[16,1,64]{2,1,0:T(1,128)S(1)} %bitcast.29), channel_id=1, replica_groups=mesh['groups'=2,'shard'=8,'sub'=2] {'shard','sub'}, dimensions={0} | all-to-all | bytes 8192 | tf_op jit(solution)/shard_map/all_to_all | solution.py:426
  33.3 0.0 copy-done
  33.3 0.7 %pick.1 = f32[1,62]{1,0:T(1,128)} custom-call(s32[1,62]{1,0:T(1,128)S(1)} %copy-done, f32[16,64]{1,0:T(8,128)S(1)} %bitcast.30), custom_call_target="tpu_custom_call" | custom-call | tf_op jit(solution)/shard_map/pick/pallas_call | solution.py:372
  (12 shorter events, 0.1 us)
Async XLA Ops:
  0.0 8.3 %collective-permute-start.2 = (bf16[8192,128]{1,0:T(8,128)(2,1)}, bf16[8192,128]{1,0:T(8,128)(2,1)S(1)}, u32[]{:S(2)}, u32[]{:S(2)}) collective-permute-start(bf16[8192,128]{1,0:T(8,128)(2,1)} %own_hbm.1), channel_id=1, source_target_pairs={{0,1},{1,0},{2,3},{3,2},{4,5},{5,4},{6,7},{7,6},{8,9},{9,8},{10,11... | collective-permute-start | bytes 6291464 | tf_op jit(solution)/shard_map/ppermute | solution.py:391
  0.5 6.2 %collective-permute-start = (bf16[1,1,32,128]{3,2,1,0:T(8,128)(2,1)}, bf16[1,1,32,128]{3,2,1,0:T(8,128)(2,1)S(1)}, u32[]{:S(2)}, u32[]{:S(2)}) collective-permute-start(bf16[1,1,32,128]{3,2,1,0:T(8,128)(2,1)} %bitcast.33), channel_id=1, source_target_pairs={{0,8},{1,9},{2,10},{3,11},{4,12},{5,13},{6,14},{7,15},{8,0},{9,1},... | collective-permute-start | bytes 24584 | tf_op jit(solution)/shard_map/ppermute | solution.py:398
  4.0 2.6 %copy-start.1 = (bf16[1,32,128]{2,1,0:T(8,128)(2,1)S(1)}, bf16[1,32,128]{2,1,0:T(8,128)(2,1)}, u32[]{:S(2)}) copy-start(bf16[1,32,128]{2,1,0:T(8,128)(2,1)} %param.6) | copy-start | bytes 24580
  6.7 4.5 %collective-permute-start.1 = (bf16[2,1,32,128]{3,2,1,0:T(8,128)(2,1)S(1)}, bf16[2,1,32,128]{3,2,1,0:T(8,128)(2,1)S(1)}, u32[]{:S(2)}, u32[]{:S(2)}) collective-permute-start(bf16[2,1,32,128]{3,2,1,0:T(8,128)(2,1)S(1)} %maximum_bitcast_fusion.refs_7_), channel_id=1, source_target_pairs={{0,4},{1,5},{2,6},{3,7},{4,0},{5,1},{6,2},{7,3},{8,12},{9,13},{10,... | collective-permute-start | bytes 49160 | tf_op jit(solution)/shard_map/ppermute | solution.py:398
  11.2 5.1 %collective-permute-start.3 = (bf16[4,1,32,128]{3,2,1,0:T(8,128)(2,1)S(1)}, bf16[4,1,32,128]{3,2,1,0:T(8,128)(2,1)S(1)}, u32[]{:S(2)}, u32[]{:S(2)}) collective-permute-start(bf16[4,1,32,128]{3,2,1,0:T(8,128)(2,1)S(1)} %bitcast.26), channel_id=1, source_target_pairs={{0,2},{1,3},{2,0},{3,1},{4,6},{5,7},{6,4},{7,5},{8,10},{9,11},{10,... | collective-permute-start | bytes 98312 | tf_op jit(solution)/shard_map/ppermute | solution.py:398
  16.4 3.3 %collective-permute-start.4 = (bf16[8,1,32,128]{3,2,1,0:T(8,128)(2,1)S(1)}, bf16[8,1,32,128]{3,2,1,0:T(8,128)(2,1)S(1)}, u32[]{:S(2)}, u32[]{:S(2)}) collective-permute-start(bf16[8,1,32,128]{3,2,1,0:T(8,128)(2,1)S(1)} %bitcast.22), channel_id=1, source_target_pairs={{0,1},{1,0},{2,3},{3,2},{4,5},{5,4},{6,7},{7,6},{8,9},{9,8},{10,11... | collective-permute-start | bytes 196616 | tf_op jit(solution)/shard_map/ppermute | solution.py:398
  19.7 13.7 %copy-start = (s32[1,62]{1,0:T(1,128)S(1)}, s32[1,62]{1,0:T(1,128)}, u32[]{:S(2)}) copy-start(s32[1,62]{1,0:T(1,128)} %candidates_ref.1) | copy-start | bytes 748

commit v18 on v17

--- a/solution.py
+++ b/solution.py
@@ -39,9 +39,8 @@
 
 
 def shares_of(passages):
-    units = -(-passages // 8)
-    edges = [units * step // STEPS * 8 for step in range(STEPS)] + [passages]
-    return list(zip(edges[:-1], edges[1:]))
+    edges = [0, passages * 11 // 32, passages * 21 // 32]
+    return tuple(zip(edges, edges[1:] + [passages]))
 
 
 def prepare_kernel(
@@ -139,16 +138,17 @@
 
 def decode_kernel(step, passages, *refs):
     if step == 0:
-        half_ref, own_ref, other_ref, codes, starts, lives, residuals, _, table, embedded = refs[:10]
+        half_ref, own_ref, other_ref, codes, starts, lives, residuals, _, table = refs[:9]
     else:
-        codes, starts, lives, residuals, table, _, _, embedded = refs[:8]
-    nothing, codes_ref, starts_ref, lives_ref, rows, sems = refs[-6:]
+        codes, starts, lives, residuals, table = refs[:5]
+    embedded, rows, nothing, codes_ref, starts_ref, lives_ref, sems = refs[-7:]
     tokens = codes_ref.shape[0]
     slots = tokens // passages
     width = rows.shape[1]
     moves = []
     first, after = shares_of(passages)[step]
-    part = pl.ds(first * slots, (after - first) * slots)
+    first_move, after_move = first // 8 * 8, min(-(-after // 8) * 8, passages)
+    part = pl.ds(first_move * slots, (after_move - first_move) * slots)
     pairs = ((starts, starts_ref), (lives, lives_ref), (codes.at[part], codes_ref.at[part]))
     for k, (source, to) in enumerate(pairs):
         moves.append(pltpu.make_async_copy(source, to, sems.at[k]))
@@ -191,20 +191,21 @@
     last = starts_ref.shape[0] - 1
     low = starts_ref[last - STEPS + step - 1] if step > 0 else 0
     high = starts_ref[last - STEPS + step]
-    fetch(low)
-
     def decode(g, carry):
         done = finish(g - 1)
         fetch(g)
         keep(g - 1, done)
         return carry
 
-    lax.fori_loop(low + 1, high, decode, 0)
-    keep(high - 1, finish(high - 1))
+    if step == 0:
+        fetch(low)
+    lax.fori_loop(low + (step == 0), high, decode, 0)
+    if step == STEPS - 1:
+        keep(high - 1, finish(high - 1))
 
 
 def decode_step(
-    step, passages, half, own, other, codes, starts, lives, residuals, table, embedded, held
+    step, passages, half, own, other, codes, starts, lives, residuals, table, carried, held
 ):
     tokens, width = residuals.shape
     rounding = SCORE_GROUP * CHUNK
@@ -215,13 +216,15 @@
         operands = [half, inside(own), inside(other)] + shared + [inside(held)]
         in_specs = [SMEM] + [VMEM] * 7
         whole = (2 * own.shape[0], width)
-        out_shape = [pltpu.VMEM(whole, jnp.float32), pltpu.VMEM(space, jnp.bfloat16)]
+        out_shape = [pltpu.VMEM(whole, jnp.float32)]
         aliases = {}
     else:
-        operands = shared + [inside(table), inside(embedded), inside(held)]
-        in_specs = [VMEM] * 7
-        out_shape = [pltpu.VMEM(space, jnp.bfloat16)]
-        aliases = {5: 0}
+        operands = shared + [inside(table), inside(held)] + [inside(array) for array in carried]
+        in_specs = [VMEM] * 8
+        out_shape = []
+        aliases = {6: 0, 7: 1}
+    out_shape.append(pltpu.VMEM(space, jnp.bfloat16))
+    out_shape.append(pltpu.VMEM((GROUP * CHUNK, width), jnp.float32))
     out_shape.append(pltpu.VMEM((16, width), jnp.bfloat16))
     results = pl.pallas_call(
         functools.partial(decode_kernel, step, passages),
@@ -233,7 +236,6 @@
             pltpu.SMEM((tokens,), jnp.int32),
             pltpu.SMEM(starts.shape, jnp.int32),
             pltpu.SMEM(lives.shape, jnp.int32),
-            pltpu.VMEM((GROUP * CHUNK, width), jnp.float32),
             pltpu.SemaphoreType.DMA((3,)),
         ],
         compiler_params=granted(4),
@@ -241,8 +243,8 @@
         name="decode",
     )(*operands)
     if step == 0:
-        return results
-    return (table,) + tuple(results)
+        table, results = results[0], results[1:]
+    return table, results[:2], results[2]
 
 
 def score_kernel(
@@ -280,29 +282,36 @@
         vectors = normalized(queries_ref[at, :].astype(jnp.float32))
         turned[...] = vectors.astype(jnp.float32).T.astype(jnp.bfloat16)
 
-        def score(g, so_far):
-            count = SCORE_GROUP // SCORE_PARTS
-            size = count * CHUNK
+        count = SCORE_GROUP // SCORE_PARTS
+        size = count * CHUNK
+
+        def score(first, so_far):
+            at = pl.ds(pl.multiple_of(first * size, size), size)
+            similar = jnp.dot(embedded[at, :], turned[...], preferred_element_type=jnp.float32)
+            parts = jnp.max(similar.reshape(count, CHUNK // 8, 8, block), axis=1)
+            for k in range(count):
+                start = at_ref[first * count + k]
+                p = quotient(start, slots)
+                so_far = jnp.where(start == p * slots, parts[k], jnp.maximum(so_far, parts[k]))
+                to = pl.multiple_of(p * 8, 8)
+                for lane in range(block // 128):
+                    largest[lane, pl.ds(to, 8), :] = so_far[:, lane * 128 : (lane + 1) * 128]
+            return so_far
+
+        def score_parts(g, so_far):
             for part in range(SCORE_PARTS):
-                first = g * SCORE_PARTS + part
-                at = pl.ds(pl.multiple_of(first * size, size), size)
-                similar = jnp.dot(embedded[at, :], turned[...], preferred_element_type=jnp.float32)
-                parts = jnp.max(similar.reshape(count, CHUNK // 8, 8, block), axis=1)
-                for k in range(count):
-                    start = at_ref[first * count + k]
-                    p = quotient(start, slots)
-                    so_far = jnp.where(start == p * slots, parts[k], jnp.maximum(so_far, parts[k]))
-                    to = pl.multiple_of(p * 8, 8)
-                    for lane in range(block // 128):
-                        largest[lane, pl.ds(to, 8), :] = so_far[:, lane * 128 : (lane + 1) * 128]
+                so_far = score(g * SCORE_PARTS + part, so_far)
             return so_far
 
         @pl.when(b == 0)
         def arrived():
             starts_copy.wait()
 
-        groups = quotient(at_ref[at_ref.shape[0] - 1] + SCORE_GROUP - 1, SCORE_GROUP)
-        lax.fori_loop(0, groups, score, jnp.zeros((8, block), jnp.float32))
+        parts_used = quotient(at_ref[at_ref.shape[0] - 1] + count - 1, count)
+        whole = quotient(parts_used, SCORE_PARTS)
+        so_far = jnp.zeros((8, block), jnp.float32)
+        so_far = lax.fori_loop(0, whole, score_parts, so_far)
+        lax.fori_loop(whole * SCORE_PARTS, parts_used, score, so_far)
         kept = []
         for lane in range(block // 128):
             best = largest[lane, pl.ds(0, passages, stride=8), :]
@@ -392,7 +401,7 @@
 
     held = queries.reshape(1, 1, local_queries * token_count, width)
     bits = targets.bit_length() - 1
-    embedded = None
+    carried = None
     for turn, first in enumerate(range(bits - 1, -1, -1)):
         pairs = [(device, device ^ (1 << first)) for device in range(targets)]
         received = lax.ppermute(held, ("shard", "sub"), pairs)
@@ -401,7 +410,7 @@
             own, near, codes, starts, lives, nothing = ready
             table = None
         elif turn <= STEPS:
-            table, embedded, nothing = decode_step(
+            table, carried, nothing = decode_step(
                 turn - 1,
                 passages,
                 half,
@@ -412,7 +421,7 @@
                 lives,
                 near,
                 table,
-                embedded,
+                carried,
                 held,
             )
         received = received + nothing[0:1, :]
@@ -421,7 +430,7 @@
             held = held.reshape((-1, 1) + held.shape[2:])
     query_rows = held.reshape(targets * local_queries * token_count, width)
     scores = score_all(
-        me, starts, query_rows, embedded, passages, slots, token_count, local_queries
+        me, starts, query_rows, carried[0], passages, slots, token_count, local_queries
     )
     returned = lax.all_to_all(
         scores.reshape(targets, local_queries * passages),

time: 34.3 us -> 34.1 us (level)
  blocking collectives: 10.1 us -> 10.5 us
    all_to_all x1, blocking collectives: 10.1 us -> 10.5 us  [body(): lax.all_to_all(scores.reshape(targets, local_queries * passages), ('shard...]
where the time goes in v18:
time: 34.1 us; the launch traced here: 34 us
  Pallas kernels  16.2 us (48%)
  blocking collectives  10.5 us (31%)
  starting transfers between devices  6.98 us (20%)
    all_to_all x1, blocking collectives, body(): lax.all_to_all(scores.reshape(targets, local_queries * passages), ('shard...  10.5 us
    pallas_call x3, Pallas kernels, decode_step(): pl.pallas_call(functools.partial(decode_kernel, step, passages), out_shap...  9.68 us
    ppermute x4, starting transfers between devices, body(): received = lax.ppermute(held, ('shard', 'sub'), pairs)  6.53 us
    pallas_call x1, Pallas kernels, score_all(): pl.pallas_call(functools.partial(score_kernel, token_count, local_queries...  3.3 us
    pallas_call x1, Pallas kernels, prepare(): pl.pallas_call(prepare_kernel, out_shape=(pltpu.VMEM(own.shape, jnp.bfloa...  2.61 us
  transfers between devices with their start and end apart: 5, of which 0 were waited for; matrix products, arithmetic and copies ran while one was open for 0% of the time, Pallas kernels for 36%

profile of v18, /device:TPU:0, one launch (start us, length us, event | category | flops | bytes accessed | tf_op | source)
XLA Modules:
  0.0 34.0 jit_solution(6075295126836234106)
XLA Ops:
  0.0 0.5 %collective-permute-start.2 = (bf16[8192,128]{1,0:T(8,128)(2,1)}, bf16[8192,128]{1,0:T(8,128)(2,1)S(1)}, u32[]{:S(2)}, u32[]{:S(2)}) collective-permute-start(bf16[8192,128]{1,0:T(8,128)(2,1)} %own_hbm.1), channel_id=1, source_target_pairs={{0,1},{1,0},{2,3},{3,2},{4,5},{5,4},{6,7},{7,6},{8,9},{9,8},{10,11... | collective-permute-start | bytes 6291464 | tf_op jit(solution)/shard_map/ppermute | solution.py:400
  0.5 3.6 %collective-permute-start = (bf16[1,1,32,128]{3,2,1,0:T(8,128)(2,1)}, bf16[1,1,32,128]{3,2,1,0:T(8,128)(2,1)S(1)}, u32[]{:S(2)}, u32[]{:S(2)}) collective-permute-start(bf16[1,1,32,128]{3,2,1,0:T(8,128)(2,1)} %bitcast.33), channel_id=1, source_target_pairs={{0,8},{1,9},{2,10},{3,11},{4,12},{5,13},{6,14},{7,15},{8,0},{9,1},... | collective-permute-start | bytes 24584 | tf_op jit(solution)/shard_map/ppermute | solution.py:407
  4.0 0.0 copy-start.1
  4.0 2.6 %prepare.1 = (bf16[8192,128]{1,0:T(8,128)(2,1)S(1)}, bf16[8192,128]{1,0:T(8,128)(2,1)S(1)}, s32[8192]{0:T(1024)S(1)}, s32[1024]{0:T(1024)S(1)}, s32[1024]{0:T(1024)S(1)}, /*index=5*/bf16[16,128]{1,0:T(8,128)(2,1)S(1)}) custom-call(s32[1]{0:T(128)} %bitcast.me_ref, s32[64]{0:T(128)} %lengths_hbm.1, s32[8192]{0:T(1024)} %bitcast.32, ...), custom_call_target="tpu_custom_call" | custom-call | flops 10000000 | bytes 8000000 | tf_op jit(solution)/shard_map/prepare/pallas_call | solution.py:115
  6.7 0.0 collective-permute-done
  6.7 0.0 copy-done.1
  6.7 1.6 %collective-permute-start.1 = (bf16[2,1,32,128]{3,2,1,0:T(8,128)(2,1)S(1)}, bf16[2,1,32,128]{3,2,1,0:T(8,128)(2,1)S(1)}, u32[]{:S(2)}, u32[]{:S(2)}) collective-permute-start(bf16[2,1,32,128]{3,2,1,0:T(8,128)(2,1)S(1)} %maximum_bitcast_fusion.refs_7_), channel_id=1, source_target_pairs={{0,4},{1,5},{2,6},{3,7},{4,0},{5,1},{6,2},{7,3},{8,12},{9,13},{10,... | collective-permute-start | bytes 49160 | tf_op jit(solution)/shard_map/ppermute | solution.py:407
  8.4 0.0 collective-permute-done.2.refs_2_
  8.4 3.4 %decode.3 = (f32[16384,128]{1,0:T(8,128)S(1)}, bf16[9216,128]{1,0:T(8,128)(2,1)S(1)}, f32[256,128]{1,0:T(8,128)S(1)}, bf16[16,128]{1,0:T(8,128)(2,1)S(1)}) custom-call(s32[1]{0:T(128)} %bitcast.6.refs_0_, bf16[8192,128]{1,0:T(8,128)(2,1)S(1)} %get-tuple-element.22.refs_1_, bf16[8192,128]{1,0:T(8,128)(2,1)S(1)} %collective-permute-done.2.refs_2_, ...), custom_call_target="tpu_custom_call" | custom-call | flops 10000000 | bytes 10000000 | tf_op jit(solution)/shard_map/decode/pallas_call | solution.py:229
  11.8 0.0 collective-permute-done.1
  11.8 1.2 %collective-permute-start.3 = (bf16[4,1,32,128]{3,2,1,0:T(8,128)(2,1)S(1)}, bf16[4,1,32,128]{3,2,1,0:T(8,128)(2,1)S(1)}, u32[]{:S(2)}, u32[]{:S(2)}) collective-permute-start(bf16[4,1,32,128]{3,2,1,0:T(8,128)(2,1)S(1)} %bitcast.26), channel_id=1, source_target_pairs={{0,2},{1,3},{2,0},{3,1},{4,6},{5,7},{6,4},{7,5},{8,10},{9,11},{10,... | collective-permute-start | bytes 98312 | tf_op jit(solution)/shard_map/ppermute | solution.py:407
  13.1 2.9 %decode.4 = (bf16[9216,128]{1,0:T(8,128)(2,1)S(1)}, f32[256,128]{1,0:T(8,128)S(1)}, bf16[16,128]{1,0:T(8,128)(2,1)S(1)}) custom-call(s32[8192]{0:T(1024)S(1)} %get-tuple-element.23.refs_3_.refs_0_, s32[1024]{0:T(1024)S(1)} %get-tuple-element.20.refs_4_.refs_1_.starts, ...), custom_call_target="tpu_custom_call", output_to_operand_aliasing={{0}: (6, {}), {1}: (7, {})} | custom-call | flops 10000000 | bytes 10000000 | tf_op jit(solution)/shard_map/decode/pallas_call | solution.py:229
  16.0 0.0 collective-permute-done.3
  16.1 0.1 collective-permute-start.4
  16.1 3.3 %decode.5 = (bf16[9216,128]{1,0:T(8,128)(2,1)S(1)}, f32[256,128]{1,0:T(8,128)S(1)}, bf16[16,128]{1,0:T(8,128)(2,1)S(1)}) custom-call(s32[8192]{0:T(1024)S(1)} %get-tuple-element.23.refs_3_.refs_0_, s32[1024]{0:T(1024)S(1)} %get-tuple-element.20.refs_4_.refs_1_.starts, ...), custom_call_target="tpu_custom_call", output_to_operand_aliasing={{0}: (6, {}), {1}: (7, {})} | custom-call | flops 10000000 | bytes 10000000 | tf_op jit(solution)/shard_map/decode/pallas_call | solution.py:229
  19.5 0.0 copy-start
  19.5 0.0 collective-permute-done.4
  19.5 3.3 %score.1 = f32[16,64]{1,0:T(8,128)S(1)} custom-call(s32[1]{0:T(128)} %bitcast.me_ref, s32[1024]{0:T(1024)S(1)} %get-tuple-element.20.refs_4_.refs_1_.starts, bf16[512,128]{1,0:T(8,128)(2,1)S(1)} %bitcast.25, bf16[9216,128]{1,0:T(8,128)(2,1)S(1)} %get-tuple-element.34.embedded), custom_call_target="tpu_custom_call" | custom-call | tf_op jit(solution)/shard_map/score/pallas_call | solution.py:340
  22.9 10.5 %all_to_all.11 = f32[16,1,64]{2,1,0:T(1,128)S(1)} all-to-all(f32[16,1,64]{2,1,0:T(1,128)S(1)} %bitcast.29), channel_id=1, replica_groups=mesh['groups'=2,'shard'=8,'sub'=2] {'shard','sub'}, dimensions={0} | all-to-all | bytes 8192 | tf_op jit(solution)/shard_map/all_to_all | solution.py:435
  33.4 0.0 copy-done
  33.4 0.7 %pick.1 = f32[1,62]{1,0:T(1,128)} custom-call(s32[1,62]{1,0:T(1,128)S(1)} %copy-done, f32[16,64]{1,0:T(8,128)S(1)} %bitcast.30), custom_call_target="tpu_custom_call" | custom-call | tf_op jit(solution)/shard_map/pick/pallas_call | solution.py:381
  (12 shorter events, 0.1 us)
Async XLA Ops:
  0.0 8.4 %collective-permute-start.2 = (bf16[8192,128]{1,0:T(8,128)(2,1)}, bf16[8192,128]{1,0:T(8,128)(2,1)S(1)}, u32[]{:S(2)}, u32[]{:S(2)}) collective-permute-start(bf16[8192,128]{1,0:T(8,128)(2,1)} %own_hbm.1), channel_id=1, source_target_pairs={{0,1},{1,0},{2,3},{3,2},{4,5},{5,4},{6,7},{7,6},{8,9},{9,8},{10,11... | collective-permute-start | bytes 6291464 | tf_op jit(solution)/shard_map/ppermute | solution.py:400
  0.5 6.2 %collective-permute-start = (bf16[1,1,32,128]{3,2,1,0:T(8,128)(2,1)}, bf16[1,1,32,128]{3,2,1,0:T(8,128)(2,1)S(1)}, u32[]{:S(2)}, u32[]{:S(2)}) collective-permute-start(bf16[1,1,32,128]{3,2,1,0:T(8,128)(2,1)} %bitcast.33), channel_id=1, source_target_pairs={{0,8},{1,9},{2,10},{3,11},{4,12},{5,13},{6,14},{7,15},{8,0},{9,1},... | collective-permute-start | bytes 24584 | tf_op jit(solution)/shard_map/ppermute | solution.py:407
  4.0 2.7 %copy-start.1 = (bf16[1,32,128]{2,1,0:T(8,128)(2,1)S(1)}, bf16[1,32,128]{2,1,0:T(8,128)(2,1)}, u32[]{:S(2)}) copy-start(bf16[1,32,128]{2,1,0:T(8,128)(2,1)} %param.6) | copy-start | bytes 24580
  6.7 5.1 %collective-permute-start.1 = (bf16[2,1,32,128]{3,2,1,0:T(8,128)(2,1)S(1)}, bf16[2,1,32,128]{3,2,1,0:T(8,128)(2,1)S(1)}, u32[]{:S(2)}, u32[]{:S(2)}) collective-permute-start(bf16[2,1,32,128]{3,2,1,0:T(8,128)(2,1)S(1)} %maximum_bitcast_fusion.refs_7_), channel_id=1, source_target_pairs={{0,4},{1,5},{2,6},{3,7},{4,0},{5,1},{6,2},{7,3},{8,12},{9,13},{10,... | collective-permute-start | bytes 49160 | tf_op jit(solution)/shard_map/ppermute | solution.py:407
  11.8 4.2 %collective-permute-start.3 = (bf16[4,1,32,128]{3,2,1,0:T(8,128)(2,1)S(1)}, bf16[4,1,32,128]{3,2,1,0:T(8,128)(2,1)S(1)}, u32[]{:S(2)}, u32[]{:S(2)}) collective-permute-start(bf16[4,1,32,128]{3,2,1,0:T(8,128)(2,1)S(1)} %bitcast.26), channel_id=1, source_target_pairs={{0,2},{1,3},{2,0},{3,1},{4,6},{5,7},{6,4},{7,5},{8,10},{9,11},{10,... | collective-permute-start | bytes 98312 | tf_op jit(solution)/shard_map/ppermute | solution.py:407
  16.1 3.4 %collective-permute-start.4 = (bf16[8,1,32,128]{3,2,1,0:T(8,128)(2,1)S(1)}, bf16[8,1,32,128]{3,2,1,0:T(8,128)(2,1)S(1)}, u32[]{:S(2)}, u32[]{:S(2)}) collective-permute-start(bf16[8,1,32,128]{3,2,1,0:T(8,128)(2,1)S(1)} %bitcast.22), channel_id=1, source_target_pairs={{0,1},{1,0},{2,3},{3,2},{4,5},{5,4},{6,7},{7,6},{8,9},{9,8},{10,11... | collective-permute-start | bytes 196616 | tf_op jit(solution)/shard_map/ppermute | solution.py:407
  19.5 13.9 %copy-start = (s32[1,62]{1,0:T(1,128)S(1)}, s32[1,62]{1,0:T(1,128)}, u32[]{:S(2)}) copy-start(s32[1,62]{1,0:T(1,128)} %candidates_ref.1) | copy-start | bytes 748

commit v19 on v18

--- a/solution.py
+++ b/solution.py
@@ -50,38 +50,39 @@
     own_hbm,
     residuals_hbm,
     staged,
-    residuals,
+    near,
     codes,
     starts,
-    lives,
+    cleans,
     nothing,
     lengths_ref,
     starts_ref,
-    lives_ref,
+    cleans_ref,
+    length_rows,
+    drawn,
+    residuals,
     sems,
 ):
     del me_ref
-    passages = lengths_ref.shape[0]
-    slots = codes_hbm.shape[0] // passages
-    moves = []
-
-    def move(source, to):
-        moves.append(pltpu.make_async_copy(source, to, sems.at[len(moves)]))
-        moves[-1].start()
-
-    lengths_copy = pltpu.make_async_copy(lengths_hbm, lengths_ref, sems.at[5])
+    passages, slots = codes_hbm.shape
+    width = own_hbm.shape[1]
+    lengths_copy = pltpu.make_async_copy(lengths_hbm, lengths_ref, sems.at[0])
+    codes_copy = pltpu.make_async_copy(codes_hbm, drawn, sems.at[1])
+    residual_copy = pltpu.make_async_copy(residuals_hbm, residuals, sems.at[2])
+    own_copy = pltpu.make_async_copy(own_hbm, staged, sems.at[3])
     lengths_copy.start()
-    move(codes_hbm, codes)
-    move(own_hbm, staged)
-    move(residuals_hbm, residuals)
+    codes_copy.start()
+    residual_copy.start()
+    own_copy.start()
     nothing[...] = jnp.zeros(nothing.shape, nothing.dtype)
     lengths_copy.wait()
 
     def listing(p, chunks):
         length = lengths_ref[p]
+        length_rows[pl.ds(p, 1), :] = jnp.full((1, slots), length, jnp.int32)
         for k in range(slots // CHUNK):
             starts_ref[chunks + k] = p * slots + k * CHUNK
-            lives_ref[chunks + k] = length - k * CHUNK
+            cleans_ref[chunks + k] = p * slots + k * CHUNK
         return chunks + quotient(length + CHUNK - 1, CHUNK)
 
     last = starts_ref.shape[0] - 1
@@ -90,16 +91,38 @@
         chunks = lax.fori_loop(low, high, listing, chunks, unroll=4)
         for k in range(GROUP):
             starts_ref[chunks + k] = passages * slots
-            lives_ref[chunks + k] = 0
+            cleans_ref[chunks + k] = low * slots
         chunks = quotient(chunks + GROUP - 1, GROUP) * GROUP
-        starts_ref[last - STEPS + step] = quotient(chunks, GROUP)
+        cleans_ref[last - STEPS + step] = quotient(chunks, GROUP)
     for k in range(SCORE_GROUP):
         starts_ref[chunks + k] = passages * slots
     starts_ref[last] = chunks
-    move(starts_ref, starts)
-    move(lives_ref, lives)
-    for copy in moves:
-        copy.wait()
+    starts_copy = pltpu.make_async_copy(starts_ref, starts, sems.at[4])
+    cleans_copy = pltpu.make_async_copy(cleans_ref, cleans, sems.at[5])
+    starts_copy.start()
+    cleans_copy.start()
+    codes_copy.wait()
+    lanes = lax.broadcasted_iota(jnp.int32, (passages, slots), 1)
+    codes[...] = jnp.where(lanes < length_rows[...], drawn[...], drawn[:, 0:1])
+    residual_copy.wait()
+    slot_numbers = lax.broadcasted_iota(jnp.int32, (CHUNK, width), 0)
+
+    def place(g, carry):
+        for k in range(GROUP):
+            at = cleans_ref[g * GROUP + k]
+            p = quotient(at, slots)
+            live = lengths_ref[p] - (at - p * slots)
+            first = residuals[pl.ds(pl.multiple_of(p * slots, CHUNK), CHUNK), :]
+            rows = residuals[pl.ds(pl.multiple_of(at, CHUNK), CHUNK), :].astype(jnp.float32)
+            rows = jnp.where(slot_numbers < live, rows, first.astype(jnp.float32)[0:1, :])
+            to = pl.multiple_of((g * GROUP + k) * CHUNK, CHUNK)
+            near[pl.ds(to, CHUNK), :] = rows
+        return carry
+
+    lax.fori_loop(0, quotient(chunks, GROUP), place, 0)
+    own_copy.wait()
+    starts_copy.wait()
+    cleans_copy.wait()
 
 
 def list_size(passages, slots):
@@ -107,16 +130,20 @@
     return -(-most // 1024) * 1024
 
 
+def list_rows(passages, slots):
+    rounding = SCORE_GROUP * CHUNK
+    return -(-(passages * slots + STEPS * GROUP * CHUNK) // rounding) * rounding
+
+
 def prepare(me, lengths, token_codes, own, residuals):
     width = own.shape[1]
-    passages = lengths.shape[0]
-    slots = token_codes.shape[0] // passages
+    passages, slots = token_codes.shape
     most = list_size(passages, slots)
     return pl.pallas_call(
         prepare_kernel,
         out_shape=(
             pltpu.VMEM(own.shape, jnp.bfloat16),
-            pltpu.VMEM(residuals.shape, jnp.bfloat16),
+            pltpu.VMEM((list_rows(passages, slots), width), jnp.float32),
             pltpu.VMEM(token_codes.shape, jnp.int32),
             pltpu.VMEM((most,), jnp.int32),
             pltpu.VMEM((most,), jnp.int32),
@@ -128,6 +155,9 @@
             pltpu.SMEM(lengths.shape, jnp.int32),
             pltpu.SMEM((most,), jnp.int32),
             pltpu.SMEM((most,), jnp.int32),
+            pltpu.VMEM(token_codes.shape, jnp.int32),
+            pltpu.VMEM(token_codes.shape, jnp.int32),
+            pltpu.VMEM(residuals.shape, jnp.bfloat16),
             pltpu.SemaphoreType.DMA((6,)),
         ],
         compiler_params=granted(4),
@@ -138,18 +168,18 @@
 
 def decode_kernel(step, passages, *refs):
     if step == 0:
-        half_ref, own_ref, other_ref, codes, starts, lives, residuals, _, table = refs[:9]
+        half_ref, own_ref, other_ref, codes, cleans, near, _, table = refs[:8]
     else:
-        codes, starts, lives, residuals, table = refs[:5]
-    embedded, rows, nothing, codes_ref, starts_ref, lives_ref, sems = refs[-7:]
-    tokens = codes_ref.shape[0]
-    slots = tokens // passages
+        codes, cleans, near, table = refs[:4]
+    embedded, rows, nothing, codes_smem, cleans_ref, sems = refs[-6:]
+    slots = codes.shape[1]
     width = rows.shape[1]
+    codes_ref = codes_smem.reshape(passages * slots)
     moves = []
     first, after = shares_of(passages)[step]
     first_move, after_move = first // 8 * 8, min(-(-after // 8) * 8, passages)
-    part = pl.ds(first_move * slots, (after_move - first_move) * slots)
-    pairs = ((starts, starts_ref), (lives, lives_ref), (codes.at[part], codes_ref.at[part]))
+    part = pl.ds(first_move, after_move - first_move)
+    pairs = ((cleans, cleans_ref), (codes.at[part], codes_smem.at[part]))
     for k, (source, to) in enumerate(pairs):
         moves.append(pltpu.make_async_copy(source, to, sems.at[k]))
         moves[-1].start()
@@ -162,25 +192,18 @@
                 to = pl.ds(pl.multiple_of(base * half_rows + k * piece, piece), piece)
                 table[to, :] = source[pl.ds(k * piece, piece), :].astype(jnp.float32)
 
-    slot_numbers = lax.broadcasted_iota(jnp.int32, (CHUNK, width), 0)
     table_single = table.reshape(table.shape[0], 1, width)
     rows_single = rows.reshape(rows.shape[0], 1, width)
 
     def fetch(g):
         for k in range(GROUP):
-            at = jnp.minimum(starts_ref[g * GROUP + k], after * slots - CHUNK)
+            at = cleans_ref[g * GROUP + k]
             for j in range(CHUNK):
                 rows_single[k * CHUNK + j] = table_single[codes_ref[at + j]]
 
     def finish(g):
-        summed = []
-        for k in range(GROUP):
-            at = jnp.minimum(starts_ref[g * GROUP + k], tokens - CHUNK)
-            near = residuals[pl.ds(pl.multiple_of(at, CHUNK), CHUNK), :]
-            vectors = rows[pl.ds(k * CHUNK, CHUNK), :] + near.astype(jnp.float32)
-            live = slot_numbers < lives_ref[g * GROUP + k]
-            summed.append(jnp.where(live, vectors, vectors[0:1, :]))
-        return normalized(jnp.concatenate(summed, axis=0))
+        size = GROUP * CHUNK
+        return normalized(rows[...] + near[pl.ds(pl.multiple_of(g * size, size), size), :])
 
     def keep(g, done):
         size = GROUP * CHUNK
@@ -188,9 +211,9 @@
 
     for move in moves:
         move.wait()
-    last = starts_ref.shape[0] - 1
-    low = starts_ref[last - STEPS + step - 1] if step > 0 else 0
-    high = starts_ref[last - STEPS + step]
+    last = cleans_ref.shape[0] - 1
+    low = cleans_ref[last - STEPS + step - 1] if step > 0 else 0
+    high = cleans_ref[last - STEPS + step]
     def decode(g, carry):
         done = finish(g - 1)
         fetch(g)
@@ -205,24 +228,24 @@
 
 
 def decode_step(
-    step, passages, half, own, other, codes, starts, lives, residuals, table, carried, held
+    step, half, own, other, codes, cleans, near, table, carried, held
 ):
-    tokens, width = residuals.shape
-    rounding = SCORE_GROUP * CHUNK
-    space = (-(-(tokens + STEPS * GROUP * CHUNK) // rounding) * rounding, width)
+    passages, slots = codes.shape
+    width = near.shape[1]
+    space = near.shape
     inside = lambda array: pinned(array, pltpu.VMEM)
-    shared = [inside(codes), inside(starts), inside(lives), inside(residuals)]
+    shared = [inside(codes), inside(cleans), inside(near)]
     if step == 0:
         operands = [half, inside(own), inside(other)] + shared + [inside(held)]
-        in_specs = [SMEM] + [VMEM] * 7
+        in_specs = [SMEM] + [VMEM] * 6
         whole = (2 * own.shape[0], width)
         out_shape = [pltpu.VMEM(whole, jnp.float32)]
         aliases = {}
     else:
         operands = shared + [inside(table), inside(held)] + [inside(array) for array in carried]
-        in_specs = [VMEM] * 8
+        in_specs = [VMEM] * 7
         out_shape = []
-        aliases = {6: 0, 7: 1}
+        aliases = {5: 0, 6: 1}
     out_shape.append(pltpu.VMEM(space, jnp.bfloat16))
     out_shape.append(pltpu.VMEM((GROUP * CHUNK, width), jnp.float32))
     out_shape.append(pltpu.VMEM((16, width), jnp.bfloat16))
@@ -233,10 +256,9 @@
         out_specs=(VMEM,) * len(out_shape),
         input_output_aliases=aliases,
         scratch_shapes=[
-            pltpu.SMEM((tokens,), jnp.int32),
-            pltpu.SMEM(starts.shape, jnp.int32),
-            pltpu.SMEM(lives.shape, jnp.int32),
-            pltpu.SemaphoreType.DMA((3,)),
+            pltpu.SMEM(codes.shape, jnp.int32),
+            pltpu.SMEM(cleans.shape, jnp.int32),
+            pltpu.SemaphoreType.DMA((2,)),
         ],
         compiler_params=granted(4),
         cost_estimate=pl.CostEstimate(flops=10**7, bytes_accessed=10**7, transcendentals=0),
@@ -396,7 +418,7 @@
     me = lax.axis_index("shard").astype(jnp.int32) * lax.axis_size("sub") + half
     half = half.reshape(1)
     me = me.reshape(1)
-    near = residuals.reshape(passages * slots, width)
+    flat = residuals.reshape(passages * slots, width)
     other = lax.ppermute(centroids, "sub", [(0, 1), (1, 0)])
 
     held = queries.reshape(1, 1, local_queries * token_count, width)
@@ -406,23 +428,12 @@
         pairs = [(device, device ^ (1 << first)) for device in range(targets)]
         received = lax.ppermute(held, ("shard", "sub"), pairs)
         if turn == 0:
-            ready = prepare(me, lengths, token_codes.reshape(passages * slots), centroids, near)
-            own, near, codes, starts, lives, nothing = ready
+            ready = prepare(me, lengths, token_codes, centroids, flat)
+            own, near, codes, starts, cleans, nothing = ready
             table = None
         elif turn <= STEPS:
             table, carried, nothing = decode_step(
-                turn - 1,
-                passages,
-                half,
-                own,
-                other,
-                codes,
-                starts,
-                lives,
-                near,
-                table,
-                carried,
-                held,
+                turn - 1, half, own, other, codes, cleans, near, table, carried, held
             )
         received = received + nothing[0:1, :]
         held = jnp.concatenate([held, received], axis=1)

time: 34.1 us -> 32.9 us (0.965)
  Pallas kernels: 16.2 us -> 13.1 us
  blocking collectives: 10.5 us -> 11.7 us
  starting transfers between devices: 6.98 us -> 7.45 us
    pallas_call x3, Pallas kernels: 9.68 us -> 6.69 us  [decode_step(): pl.pallas_call(functools.partial(decode_kernel, step, passages), out_shap...]
    all_to_all x1, blocking collectives: 10.5 us -> 11.7 us  [body(): lax.all_to_all(scores.reshape(targets, local_queries * passages), ('shard...]
    ppermute x4, starting transfers between devices: 6.53 us -> 7 us  [body(): received = lax.ppermute(held, ('shard', 'sub'), pairs)]
    pallas_call x1, Pallas kernels: 3.3 us -> 2.89 us  [score_all(): pl.pallas_call(functools.partial(score_kernel, token_count, local_queries...]
  transfers between devices with their start and end apart: 5 -> 5, of which waited for: 0 -> 1; matrix products, arithmetic and copies ran while one was open for 0% -> 0% of each run, Pallas kernels for 36% -> 29%
where the time goes in v19:
time: 32.9 us; the launch traced here: 32.7 us
  Pallas kernels  13.1 us (40%)
  blocking collectives  11.7 us (36%)
  starting transfers between devices  7.45 us (23%)
    all_to_all x1, blocking collectives, body(): lax.all_to_all(scores.reshape(targets, local_queries * passages), ('shard...  11.7 us
    ppermute x4, starting transfers between devices, body(): received = lax.ppermute(held, ('shard', 'sub'), pairs)  7 us
    pallas_call x3, Pallas kernels, decode_step(): pl.pallas_call(functools.partial(decode_kernel, step, passages), out_shap...  6.69 us
    pallas_call x1, Pallas kernels, score_all(): pl.pallas_call(functools.partial(score_kernel, token_count, local_queries...  2.89 us
    pallas_call x1, Pallas kernels, prepare(): pl.pallas_call(prepare_kernel, out_shape=(pltpu.VMEM(own.shape, jnp.bfloa...  2.82 us
  transfers between devices with their start and end apart: 5, of which 1 were waited for; matrix products, arithmetic and copies ran while one was open for 0% of the time, Pallas kernels for 29%

profile of v19, /device:TPU:0, one launch (start us, length us, event | category | flops | bytes accessed | tf_op | source)
XLA Modules:
  0.0 32.7 jit_solution(10050582987683340397)
XLA Ops:
  0.0 0.0 copy-start.1
  0.0 0.5 %collective-permute-start.2 = (bf16[8192,128]{1,0:T(8,128)(2,1)}, bf16[8192,128]{1,0:T(8,128)(2,1)S(1)}, u32[]{:S(2)}, u32[]{:S(2)}) collective-permute-start(bf16[8192,128]{1,0:T(8,128)(2,1)} %own_hbm.1), channel_id=1, source_target_pairs={{0,1},{1,0},{2,3},{3,2},{4,5},{5,4},{6,7},{7,6},{8,9},{9,8},{10,11... | collective-permute-start | bytes 6291464 | tf_op jit(solution)/shard_map/ppermute | solution.py:422
  0.5 3.6 %collective-permute-start = (bf16[1,1,32,128]{3,2,1,0:T(8,128)(2,1)}, bf16[1,1,32,128]{3,2,1,0:T(8,128)(2,1)S(1)}, u32[]{:S(2)}, u32[]{:S(2)}) collective-permute-start(bf16[1,1,32,128]{3,2,1,0:T(8,128)(2,1)} %bitcast.31), channel_id=1, source_target_pairs={{0,8},{1,9},{2,10},{3,11},{4,12},{5,13},{6,14},{7,15},{8,0},{9,1},... | collective-permute-start | bytes 24584 | tf_op jit(solution)/shard_map/ppermute | solution.py:429
  4.1 2.8 %prepare.1 = (bf16[8192,128]{1,0:T(8,128)(2,1)S(1)}, f32[9216,128]{1,0:T(8,128)S(1)}, s32[64,128]{1,0:T(8,128)S(1)}, s32[1024]{0:T(1024)S(1)}, s32[1024]{0:T(1024)S(1)}, /*index=5*/bf16[16,128]{1,0:T(8,128)(2,1)S(1)}) custom-call(s32[1]{0:T(128)} %bitcast.me_ref, s32[64]{0:T(128)} %lengths_hbm.1, s32[64,128]{1,0:T(8,128)} %codes_hbm.1, ...), custom_call_target="tpu_custom_call" | custom-call | flops 10000000 | bytes 8000000 | tf_op jit(solution)/shard_map/prepare/pallas_call | solution.py:142
  6.9 0.0 collective-permute-done
  7.0 0.0 copy-done.1
  7.0 1.8 %collective-permute-start.1 = (bf16[2,1,32,128]{3,2,1,0:T(8,128)(2,1)S(1)}, bf16[2,1,32,128]{3,2,1,0:T(8,128)(2,1)S(1)}, u32[]{:S(2)}, u32[]{:S(2)}) collective-permute-start(bf16[2,1,32,128]{3,2,1,0:T(8,128)(2,1)S(1)} %maximum_bitcast_fusion.refs_6_), channel_id=1, source_target_pairs={{0,4},{1,5},{2,6},{3,7},{4,0},{5,1},{6,2},{7,3},{8,12},{9,13},{10,... | collective-permute-start | bytes 49160 | tf_op jit(solution)/shard_map/ppermute | solution.py:429
  8.7 0.0 collective-permute-done.2.refs_2_
  8.8 2.2 %decode.3 = (f32[16384,128]{1,0:T(8,128)S(1)}, bf16[9216,128]{1,0:T(8,128)(2,1)S(1)}, f32[256,128]{1,0:T(8,128)S(1)}, bf16[16,128]{1,0:T(8,128)(2,1)S(1)}) custom-call(s32[1]{0:T(128)} %bitcast.5.refs_0_, bf16[8192,128]{1,0:T(8,128)(2,1)S(1)} %get-tuple-element.22.refs_1_, bf16[8192,128]{1,0:T(8,128)(2,1)S(1)} %collective-permute-done.2.refs_2_, ...), custom_call_target="tpu_custom_call" | custom-call | flops 10000000 | bytes 10000000 | tf_op jit(solution)/shard_map/decode/pallas_call | solution.py:252
  10.9 0.0 collective-permute-done.1
  11.0 1.5 %collective-permute-start.3 = (bf16[4,1,32,128]{3,2,1,0:T(8,128)(2,1)S(1)}, bf16[4,1,32,128]{3,2,1,0:T(8,128)(2,1)S(1)}, u32[]{:S(2)}, u32[]{:S(2)}) collective-permute-start(bf16[4,1,32,128]{3,2,1,0:T(8,128)(2,1)S(1)} %bitcast.25), channel_id=1, source_target_pairs={{0,2},{1,3},{2,0},{3,1},{4,6},{5,7},{6,4},{7,5},{8,10},{9,11},{10,... | collective-permute-start | bytes 98312 | tf_op jit(solution)/shard_map/ppermute | solution.py:429
  12.5 2.2 %decode.4 = (bf16[9216,128]{1,0:T(8,128)(2,1)S(1)}, f32[256,128]{1,0:T(8,128)S(1)}, bf16[16,128]{1,0:T(8,128)(2,1)S(1)}) custom-call(s32[64,128]{1,0:T(8,128)S(1)} %get-tuple-element.23.refs_3_.refs_0_, s32[1024]{0:T(1024)S(1)} %get-tuple-element.24.refs_4_.refs_1_, ...), custom_call_target="tpu_custom_call", output_to_operand_aliasing={{0}: (5, {}), {1}: (6, {})} | custom-call | flops 10000000 | bytes 10000000 | tf_op jit(solution)/shard_map/decode/pallas_call | solution.py:252
  14.7 0.2 collective-permute-done.3
  15.0 0.1 collective-permute-start.4
  15.0 2.3 %decode.5 = (bf16[9216,128]{1,0:T(8,128)(2,1)S(1)}, f32[256,128]{1,0:T(8,128)S(1)}, bf16[16,128]{1,0:T(8,128)(2,1)S(1)}) custom-call(s32[64,128]{1,0:T(8,128)S(1)} %get-tuple-element.23.refs_3_.refs_0_, s32[1024]{0:T(1024)S(1)} %get-tuple-element.24.refs_4_.refs_1_, ...), custom_call_target="tpu_custom_call", output_to_operand_aliasing={{0}: (5, {}), {1}: (6, {})} | custom-call | flops 10000000 | bytes 10000000 | tf_op jit(solution)/shard_map/decode/pallas_call | solution.py:252
  17.3 0.0 copy-start
  17.4 0.0 collective-permute-done.4
  17.4 2.9 %score.1 = f32[16,64]{1,0:T(8,128)S(1)} custom-call(s32[1]{0:T(128)} %bitcast.me_ref, s32[1024]{0:T(1024)S(1)} %get-tuple-element.20.starts, bf16[512,128]{1,0:T(8,128)(2,1)S(1)} %bitcast.24, bf16[9216,128]{1,0:T(8,128)(2,1)S(1)} %get-tuple-element.34.embedded), custom_call_target="tpu_custom_call" | custom-call | tf_op jit(solution)/shard_map/score/pallas_call | solution.py:362
  20.3 11.7 %all_to_all.11 = f32[16,1,64]{2,1,0:T(1,128)S(1)} all-to-all(f32[16,1,64]{2,1,0:T(1,128)S(1)} %bitcast.28), channel_id=1, replica_groups=mesh['groups'=2,'shard'=8,'sub'=2] {'shard','sub'}, dimensions={0} | all-to-all | bytes 8192 | tf_op jit(solution)/shard_map/all_to_all | solution.py:446
  32.0 0.0 copy-done
  32.0 0.7 %pick.1 = f32[1,62]{1,0:T(1,128)} custom-call(s32[1,62]{1,0:T(1,128)S(1)} %copy-done, f32[16,64]{1,0:T(8,128)S(1)} %bitcast.29), custom_call_target="tpu_custom_call" | custom-call | tf_op jit(solution)/shard_map/pick/pallas_call | solution.py:403
  (12 shorter events, 0.1 us)
Async XLA Ops:
  0.0 7.0 %copy-start.1 = (bf16[1,32,128]{2,1,0:T(8,128)(2,1)S(1)}, bf16[1,32,128]{2,1,0:T(8,128)(2,1)}, u32[]{:S(2)}) copy-start(bf16[1,32,128]{2,1,0:T(8,128)(2,1)} %param.6) | copy-start | bytes 24580
  0.0 8.7 %collective-permute-start.2 = (bf16[8192,128]{1,0:T(8,128)(2,1)}, bf16[8192,128]{1,0:T(8,128)(2,1)S(1)}, u32[]{:S(2)}, u32[]{:S(2)}) collective-permute-start(bf16[8192,128]{1,0:T(8,128)(2,1)} %own_hbm.1), channel_id=1, source_target_pairs={{0,1},{1,0},{2,3},{3,2},{4,5},{5,4},{6,7},{7,6},{8,9},{9,8},{10,11... | collective-permute-start | bytes 6291464 | tf_op jit(solution)/shard_map/ppermute | solution.py:422
  0.5 6.5 %collective-permute-start = (bf16[1,1,32,128]{3,2,1,0:T(8,128)(2,1)}, bf16[1,1,32,128]{3,2,1,0:T(8,128)(2,1)S(1)}, u32[]{:S(2)}, u32[]{:S(2)}) collective-permute-start(bf16[1,1,32,128]{3,2,1,0:T(8,128)(2,1)} %bitcast.31), channel_id=1, source_target_pairs={{0,8},{1,9},{2,10},{3,11},{4,12},{5,13},{6,14},{7,15},{8,0},{9,1},... | collective-permute-start | bytes 24584 | tf_op jit(solution)/shard_map/ppermute | solution.py:429
  7.0 3.9 %collective-permute-start.1 = (bf16[2,1,32,128]{3,2,1,0:T(8,128)(2,1)S(1)}, bf16[2,1,32,128]{3,2,1,0:T(8,128)(2,1)S(1)}, u32[]{:S(2)}, u32[]{:S(2)}) collective-permute-start(bf16[2,1,32,128]{3,2,1,0:T(8,128)(2,1)S(1)} %maximum_bitcast_fusion.refs_6_), channel_id=1, source_target_pairs={{0,4},{1,5},{2,6},{3,7},{4,0},{5,1},{6,2},{7,3},{8,12},{9,13},{10,... | collective-permute-start | bytes 49160 | tf_op jit(solution)/shard_map/ppermute | solution.py:429
  11.0 4.0 %collective-permute-start.3 = (bf16[4,1,32,128]{3,2,1,0:T(8,128)(2,1)S(1)}, bf16[4,1,32,128]{3,2,1,0:T(8,128)(2,1)S(1)}, u32[]{:S(2)}, u32[]{:S(2)}) collective-permute-start(bf16[4,1,32,128]{3,2,1,0:T(8,128)(2,1)S(1)} %bitcast.25), channel_id=1, source_target_pairs={{0,2},{1,3},{2,0},{3,1},{4,6},{5,7},{6,4},{7,5},{8,10},{9,11},{10,... | collective-permute-start | bytes 98312 | tf_op jit(solution)/shard_map/ppermute | solution.py:429
  15.0 2.4 %collective-permute-start.4 = (bf16[8,1,32,128]{3,2,1,0:T(8,128)(2,1)S(1)}, bf16[8,1,32,128]{3,2,1,0:T(8,128)(2,1)S(1)}, u32[]{:S(2)}, u32[]{:S(2)}) collective-permute-start(bf16[8,1,32,128]{3,2,1,0:T(8,128)(2,1)S(1)} %bitcast.21), channel_id=1, source_target_pairs={{0,1},{1,0},{2,3},{3,2},{4,5},{5,4},{6,7},{7,6},{8,9},{9,8},{10,11... | collective-permute-start | bytes 196616 | tf_op jit(solution)/shard_map/ppermute | solution.py:429
  17.3 14.7 %copy-start = (s32[1,62]{1,0:T(1,128)S(1)}, s32[1,62]{1,0:T(1,128)}, u32[]{:S(2)}) copy-start(s32[1,62]{1,0:T(1,128)} %candidates_ref.1) | copy-start | bytes 748

commit v20 on v19

--- a/solution.py
+++ b/solution.py
@@ -11,7 +11,7 @@
 GROUP = 16
 SCORE_GROUP = 64
 SCORE_PARTS = 2
-STEPS = 3
+STEPS = 2
 PIECES = 4
 QUERY_BLOCK = 512
 SMEM = pl.BlockSpec(memory_space=pltpu.SMEM)
@@ -39,7 +39,7 @@
 
 
 def shares_of(passages):
-    edges = [0, passages * 11 // 32, passages * 21 // 32]
+    edges = [0, passages * 15 // 32]
     return tuple(zip(edges, edges[1:] + [passages]))
 
 
@@ -270,6 +270,7 @@
 
 
 def score_kernel(
+    bit,
     token_count,
     local_queries,
     slots,
@@ -277,6 +278,7 @@
     starts,
     queries_ref,
     embedded,
+    before_ref,
     out_ref,
     at_ref,
     turned,
@@ -289,23 +291,24 @@
     query_tokens = queries_ref.shape[0]
     block = min(QUERY_BLOCK, query_tokens)
     blocks = query_tokens // block
-    per_block = block // token_count
-    owner = lax.broadcasted_iota(jnp.int32, (per_block, block), 0)
-    token_of = quotient(lax.broadcasted_iota(jnp.int32, (per_block, block), 1), token_count)
-    block_targets = per_block // local_queries
-    near_me = me_ref[0] & (block_targets - 1)
-    far_me = quotient(me_ref[0], block_targets)
+    window = 2 * block // token_count
+    window_targets = window // local_queries
+    near_me = me_ref[0] & (window_targets - 1)
+    far_me = quotient(me_ref[0], window_targets)
+    owner = lax.broadcasted_iota(jnp.int32, (window, block), 0)
     owner_target = quotient(owner, local_queries)
-    relative = (owner_target ^ near_me) * local_queries + owner - owner_target * local_queries
-    summing = (relative == token_of).astype(jnp.bfloat16)
+    owner_row = (owner_target ^ near_me) * local_queries + owner - owner_target * local_queries
+    query_of = quotient(lax.broadcasted_iota(jnp.int32, (window, block), 1), token_count)
+    target_of = quotient(query_of, local_queries)
+    row_of = query_of + (target_of + bit) * local_queries
+    summing = (owner_row == row_of).astype(jnp.bfloat16)
+    count = SCORE_GROUP // SCORE_PARTS
+    size = count * CHUNK
 
     def score_block(b, carry):
         at = pl.ds(pl.multiple_of(b * block, block), block)
         vectors = normalized(queries_ref[at, :].astype(jnp.float32))
         turned[...] = vectors.astype(jnp.float32).T.astype(jnp.bfloat16)
-
-        count = SCORE_GROUP // SCORE_PARTS
-        size = count * CHUNK
 
         def score(first, so_far):
             at = pl.ds(pl.multiple_of(first * size, size), size)
@@ -340,29 +343,30 @@
             for k in range(1, 8):
                 best = jnp.maximum(best, largest[lane, pl.ds(k, passages, stride=8), :])
             kept.append(best)
-        best = jnp.concatenate(kept, axis=1)
-        sums = jnp.zeros((per_block, passages), jnp.float32)
+        left = jnp.concatenate(kept, axis=1)
+        to = pl.ds(pl.multiple_of((b ^ far_me) * window, window), window)
+        sums = before_ref[to, :] if bit else jnp.zeros((window, passages), jnp.float32)
         for _ in range(3):
-            part = best.astype(jnp.bfloat16)
-            best = best - part.astype(jnp.float32)
+            part = left.astype(jnp.bfloat16)
+            left = left - part.astype(jnp.float32)
             sums = sums + lax.dot_general(
                 summing, part, (((1,), (1,)), ((), ())), preferred_element_type=jnp.float32
             )
-        to = pl.multiple_of((b ^ far_me) * per_block, per_block)
-        out_ref[pl.ds(to, per_block), :] = sums
+        out_ref[to, :] = sums
         return carry
 
     lax.fori_loop(0, blocks, score_block, 0)
 
 
-def score_all(me, starts, query_rows, embedded, passages, slots, token_count, local_queries):
+def score_half(bit, me, starts, query_rows, embedded, before, passages, slots, shape):
+    token_count, local_queries = shape
     query_tokens, width = query_rows.shape
     block = min(QUERY_BLOCK, query_tokens)
     blocks = query_tokens // block
     return pl.pallas_call(
-        functools.partial(score_kernel, token_count, local_queries, slots),
-        out_shape=jax.ShapeDtypeStruct((query_tokens // token_count, passages), jnp.float32),
-        in_specs=[SMEM, VMEM, VMEM, VMEM],
+        functools.partial(score_kernel, bit, token_count, local_queries, slots),
+        out_shape=pltpu.VMEM((2 * query_tokens // token_count, passages), jnp.float32),
+        in_specs=[SMEM] + [VMEM] * 4,
         out_specs=VMEM,
         scratch_shapes=[
             pltpu.SMEM(starts.shape, jnp.int32),
@@ -370,13 +374,15 @@
             pltpu.VMEM((block // 128, (passages + 1) * 8, 128), jnp.float32),
             pltpu.SemaphoreType.DMA,
         ],
-        compiler_params=granted(8 + 2 * blocks),
+        compiler_params=granted(4),
+        cost_estimate=pl.CostEstimate(flops=10**7, bytes_accessed=8 * 10**6, transcendentals=0),
         name="score",
     )(
         me,
         pinned(starts, pltpu.VMEM),
         pinned(query_rows, pltpu.VMEM),
         pinned(embedded, pltpu.VMEM),
+        pinned(before, pltpu.VMEM),
     )
 
 
@@ -435,14 +441,15 @@
             table, carried, nothing = decode_step(
                 turn - 1, half, own, other, codes, cleans, near, table, carried, held
             )
-        received = received + nothing[0:1, :]
-        held = jnp.concatenate([held, received], axis=1)
         if first > 0:
+            received = received + nothing[0:1, :]
+            held = jnp.concatenate([held, received], axis=1)
             held = held.reshape((-1, 1) + held.shape[2:])
-    query_rows = held.reshape(targets * local_queries * token_count, width)
-    scores = score_all(
-        me, starts, query_rows, carried[0], passages, slots, token_count, local_queries
-    )
+    shape = (token_count, local_queries)
+    scores = carried[1]
+    for bit, half_rows in enumerate((held, received)):
+        rows = half_rows.reshape(targets // 2 * local_queries * token_count, width)
+        scores = score_half(bit, me, starts, rows, carried[0], scores, passages, slots, shape)
     returned = lax.all_to_all(
         scores.reshape(targets, local_queries * passages),
         ("shard", "sub"),

time: 32.9 us -> 32.7 us (level)
  Pallas kernels: 13.1 us -> 16 us
  blocking collectives: 11.7 us -> 9.08 us
  starting transfers between devices: 7.45 us -> 7.08 us
    all_to_all x1, blocking collectives: 11.7 us -> 9.08 us  [body(): lax.all_to_all(scores.reshape(targets, local_queries * passages), ('shard...]
    pallas_call x1 -> x2, Pallas kernels: 2.89 us -> 5.43 us  [score_half(): pl.pallas_call(functools.partial(score_kernel, bit, token_count, local_qu...]
    ppermute x4, starting transfers between devices: 7 us -> 6.63 us  [body(): received = lax.ppermute(held, ('shard', 'sub'), pairs)]
    pallas_call x3 -> x2, Pallas kernels: 6.69 us -> 6.91 us  [decode_step(): pl.pallas_call(functools.partial(decode_kernel, step, passages), out_shap...]
  transfers between devices with their start and end apart: 5 -> 5, of which waited for: 1 -> 0; matrix products, arithmetic and copies ran while one was open for 0% -> 0% of each run, Pallas kernels for 29% -> 39%
where the time goes in v20:
time: 32.7 us; the launch traced here: 32.4 us
  Pallas kernels  16 us (49%)
  blocking collectives  9.08 us (28%)
  starting transfers between devices  7.08 us (22%)
    all_to_all x1, blocking collectives, body(): lax.all_to_all(scores.reshape(targets, local_queries * passages), ('shard...  9.08 us
    pallas_call x2, Pallas kernels, decode_step(): pl.pallas_call(functools.partial(decode_kernel, step, passages), out_shap...  6.91 us
    ppermute x4, starting transfers between devices, body(): received = lax.ppermute(held, ('shard', 'sub'), pairs)  6.63 us
    pallas_call x2, Pallas kernels, score_half(): pl.pallas_call(functools.partial(score_kernel, bit, token_count, local_qu...  5.43 us
    pallas_call x1, Pallas kernels, prepare(): pl.pallas_call(prepare_kernel, out_shape=(pltpu.VMEM(own.shape, jnp.bfloa...  3.04 us
    pallas_call x1, Pallas kernels, pick(): pl.pallas_call(functools.partial(pick_kernel, passages), out_shape=jax.Sh...  0.66 us
  transfers between devices with their start and end apart: 5, of which 0 were waited for; matrix products, arithmetic and copies ran while one was open for 0% of the time, Pallas kernels for 39%

profile of v20, /device:TPU:0, one launch (start us, length us, event | category | flops | bytes accessed | tf_op | source)
XLA Modules:
  0.0 32.4 jit_solution(11610791512891910540)
XLA Ops:
  0.0 0.0 copy-start.1
  0.0 0.5 %collective-permute-start.2 = (bf16[8192,128]{1,0:T(8,128)(2,1)}, bf16[8192,128]{1,0:T(8,128)(2,1)S(1)}, u32[]{:S(2)}, u32[]{:S(2)}) collective-permute-start(bf16[8192,128]{1,0:T(8,128)(2,1)} %own_hbm.1), channel_id=1, source_target_pairs={{0,1},{1,0},{2,3},{3,2},{4,5},{5,4},{6,7},{7,6},{8,9},{9,8},{10,11... | collective-permute-start | bytes 6291464 | tf_op jit(solution)/shard_map/ppermute | solution.py:428
  0.5 3.6 %collective-permute-start = (bf16[1,1,32,128]{3,2,1,0:T(8,128)(2,1)}, bf16[1,1,32,128]{3,2,1,0:T(8,128)(2,1)S(1)}, u32[]{:S(2)}, u32[]{:S(2)}) collective-permute-start(bf16[1,1,32,128]{3,2,1,0:T(8,128)(2,1)} %bitcast.29), channel_id=1, source_target_pairs={{0,8},{1,9},{2,10},{3,11},{4,12},{5,13},{6,14},{7,15},{8,0},{9,1},... | collective-permute-start | bytes 24584 | tf_op jit(solution)/shard_map/ppermute | solution.py:435
  4.1 3.0 %prepare.1 = (bf16[8192,128]{1,0:T(8,128)(2,1)S(1)}, f32[9216,128]{1,0:T(8,128)S(1)}, s32[64,128]{1,0:T(8,128)S(1)}, s32[1024]{0:T(1024)S(1)}, s32[1024]{0:T(1024)S(1)}, /*index=5*/bf16[16,128]{1,0:T(8,128)(2,1)S(1)}) custom-call(s32[1]{0:T(128)} %bitcast.me_ref, s32[64]{0:T(128)} %lengths_hbm.1, s32[64,128]{1,0:T(8,128)} %codes_hbm.1, ...), custom_call_target="tpu_custom_call" | custom-call | flops 10000000 | bytes 8000000 | tf_op jit(solution)/shard_map/prepare/pallas_call | solution.py:142
  7.2 0.0 collective-permute-done
  7.2 0.0 copy-done.1
  7.2 1.5 %collective-permute-start.1 = (bf16[2,1,32,128]{3,2,1,0:T(8,128)(2,1)S(1)}, bf16[2,1,32,128]{3,2,1,0:T(8,128)(2,1)S(1)}, u32[]{:S(2)}, u32[]{:S(2)}) collective-permute-start(bf16[2,1,32,128]{3,2,1,0:T(8,128)(2,1)S(1)} %maximum_bitcast_fusion.refs_6_), channel_id=1, source_target_pairs={{0,4},{1,5},{2,6},{3,7},{4,0},{5,1},{6,2},{7,3},{8,12},{9,13},{10,... | collective-permute-start | bytes 49160 | tf_op jit(solution)/shard_map/ppermute | solution.py:435
  8.7 0.0 collective-permute-done.2.refs_2_
  8.7 3.1 %decode.2 = (f32[16384,128]{1,0:T(8,128)S(1)}, bf16[9216,128]{1,0:T(8,128)(2,1)S(1)}, f32[256,128]{1,0:T(8,128)S(1)}, bf16[16,128]{1,0:T(8,128)(2,1)S(1)}) custom-call(s32[1]{0:T(128)} %bitcast.5.refs_0_, bf16[8192,128]{1,0:T(8,128)(2,1)S(1)} %get-tuple-element.20.refs_1_, bf16[8192,128]{1,0:T(8,128)(2,1)S(1)} %collective-permute-done.2.refs_2_, ...), custom_call_target="tpu_custom_call" | custom-call | flops 10000000 | bytes 10000000 | tf_op jit(solution)/shard_map/decode/pallas_call | solution.py:252
  11.9 0.0 collective-permute-done.1
  11.9 1.4 %collective-permute-start.3 = (bf16[4,1,32,128]{3,2,1,0:T(8,128)(2,1)S(1)}, bf16[4,1,32,128]{3,2,1,0:T(8,128)(2,1)S(1)}, u32[]{:S(2)}, u32[]{:S(2)}) collective-permute-start(bf16[4,1,32,128]{3,2,1,0:T(8,128)(2,1)S(1)} %bitcast.20), channel_id=1, source_target_pairs={{0,2},{1,3},{2,0},{3,1},{4,6},{5,7},{6,4},{7,5},{8,10},{9,11},{10,... | collective-permute-start | bytes 98312 | tf_op jit(solution)/shard_map/ppermute | solution.py:435
  13.3 3.8 %decode.3 = (bf16[9216,128]{1,0:T(8,128)(2,1)S(1)}, f32[256,128]{1,0:T(8,128)S(1)}, bf16[16,128]{1,0:T(8,128)(2,1)S(1)}) custom-call(s32[64,128]{1,0:T(8,128)S(1)} %get-tuple-element.21.refs_3_.refs_0_, s32[1024]{0:T(1024)S(1)} %get-tuple-element.22.refs_4_.refs_1_, ...), custom_call_target="tpu_custom_call", output_to_operand_aliasing={{0}: (5, {}), {1}: (6, {})} | custom-call | flops 10000000 | bytes 10000000 | tf_op jit(solution)/shard_map/decode/pallas_call | solution.py:252
  17.1 0.0 collective-permute-done.3
  17.2 0.1 collective-permute-start.4
  17.2 0.0 copy-start
  17.2 2.7 %score.2.before_ref = f32[16,64]{1,0:T(8,128)S(1)} custom-call(s32[1]{0:T(128)} %bitcast.me_ref, s32[1024]{0:T(1024)S(1)} %get-tuple-element.18.starts, bf16[256,128]{1,0:T(8,128)(2,1)S(1)} %bitcast.24, bf16[9216,128]{1,0:T(8,128)(2,1)S(1)} %get-tuple-element.29.embedded, f32[256,128]{1,0:T(8,128)S(1)} %get-tuple-element.30.before_ref), custom_call_target="tpu_custom_call" | custom-call | flops 10000000 | bytes 8000000 | tf_op jit(solution)/shard_map/score/pallas_call | solution.py:366
  20.0 0.0 collective-permute-done.4
  20.0 2.7 %score.3 = f32[16,64]{1,0:T(8,128)S(1)} custom-call(s32[1]{0:T(128)} %bitcast.me_ref, s32[1024]{0:T(1024)S(1)} %get-tuple-element.18.starts, bf16[256,128]{1,0:T(8,128)(2,1)S(1)} %bitcast.25, bf16[9216,128]{1,0:T(8,128)(2,1)S(1)} %get-tuple-element.29.embedded, f32[16,64]{1,0:T(8,128)S(1)} %score.2.before_ref), custom_call_target="tpu_custom_call" | custom-call | flops 10000000 | bytes 8000000 | tf_op jit(solution)/shard_map/score/pallas_call | solution.py:366
  22.7 9.1 %all_to_all.11 = f32[16,1,64]{2,1,0:T(1,128)S(1)} all-to-all(f32[16,1,64]{2,1,0:T(1,128)S(1)} %bitcast.26), channel_id=1, replica_groups=mesh['groups'=2,'shard'=8,'sub'=2] {'shard','sub'}, dimensions={0} | all-to-all | bytes 8192 | tf_op jit(solution)/shard_map/all_to_all | solution.py:453
  31.8 0.0 copy-done
  31.8 0.7 %pick.1 = f32[1,62]{1,0:T(1,128)} custom-call(s32[1,62]{1,0:T(1,128)S(1)} %copy-done, f32[16,64]{1,0:T(8,128)S(1)} %bitcast.27), custom_call_target="tpu_custom_call" | custom-call | tf_op jit(solution)/shard_map/pick/pallas_call | solution.py:409
  (9 shorter events, 0.1 us)
Async XLA Ops:
  0.0 7.2 %copy-start.1 = (bf16[1,32,128]{2,1,0:T(8,128)(2,1)S(1)}, bf16[1,32,128]{2,1,0:T(8,128)(2,1)}, u32[]{:S(2)}) copy-start(bf16[1,32,128]{2,1,0:T(8,128)(2,1)} %param.6) | copy-start | bytes 24580
  0.0 8.7 %collective-permute-start.2 = (bf16[8192,128]{1,0:T(8,128)(2,1)}, bf16[8192,128]{1,0:T(8,128)(2,1)S(1)}, u32[]{:S(2)}, u32[]{:S(2)}) collective-permute-start(bf16[8192,128]{1,0:T(8,128)(2,1)} %own_hbm.1), channel_id=1, source_target_pairs={{0,1},{1,0},{2,3},{3,2},{4,5},{5,4},{6,7},{7,6},{8,9},{9,8},{10,11... | collective-permute-start | bytes 6291464 | tf_op jit(solution)/shard_map/ppermute | solution.py:428
  0.5 6.7 %collective-permute-start = (bf16[1,1,32,128]{3,2,1,0:T(8,128)(2,1)}, bf16[1,1,32,128]{3,2,1,0:T(8,128)(2,1)S(1)}, u32[]{:S(2)}, u32[]{:S(2)}) collective-permute-start(bf16[1,1,32,128]{3,2,1,0:T(8,128)(2,1)} %bitcast.29), channel_id=1, source_target_pairs={{0,8},{1,9},{2,10},{3,11},{4,12},{5,13},{6,14},{7,15},{8,0},{9,1},... | collective-permute-start | bytes 24584 | tf_op jit(solution)/shard_map/ppermute | solution.py:435
  7.2 4.7 %collective-permute-start.1 = (bf16[2,1,32,128]{3,2,1,0:T(8,128)(2,1)S(1)}, bf16[2,1,32,128]{3,2,1,0:T(8,128)(2,1)S(1)}, u32[]{:S(2)}, u32[]{:S(2)}) collective-permute-start(bf16[2,1,32,128]{3,2,1,0:T(8,128)(2,1)S(1)} %maximum_bitcast_fusion.refs_6_), channel_id=1, source_target_pairs={{0,4},{1,5},{2,6},{3,7},{4,0},{5,1},{6,2},{7,3},{8,12},{9,13},{10,... | collective-permute-start | bytes 49160 | tf_op jit(solution)/shard_map/ppermute | solution.py:435
  11.9 5.2 %collective-permute-start.3 = (bf16[4,1,32,128]{3,2,1,0:T(8,128)(2,1)S(1)}, bf16[4,1,32,128]{3,2,1,0:T(8,128)(2,1)S(1)}, u32[]{:S(2)}, u32[]{:S(2)}) collective-permute-start(bf16[4,1,32,128]{3,2,1,0:T(8,128)(2,1)S(1)} %bitcast.20), channel_id=1, source_target_pairs={{0,2},{1,3},{2,0},{3,1},{4,6},{5,7},{6,4},{7,5},{8,10},{9,11},{10,... | collective-permute-start | bytes 98312 | tf_op jit(solution)/shard_map/ppermute | solution.py:435
  17.2 2.8 %collective-permute-start.4 = (bf16[8,1,32,128]{3,2,0,1:T(8,128)(2,1)S(1)}, bf16[8,1,32,128]{3,2,0,1:T(8,128)(2,1)S(1)}, u32[]{:S(2)}, u32[]{:S(2)}) collective-permute-start(bf16[8,1,32,128]{3,2,0,1:T(8,128)(2,1)S(1)} %bitcast.23), channel_id=1, source_target_pairs={{0,1},{1,0},{2,3},{3,2},{4,5},{5,4},{6,7},{7,6},{8,9},{9,8},{10,11... | collective-permute-start | bytes 196616 | tf_op jit(solution)/shard_map/ppermute | solution.py:435
  17.2 14.5 %copy-start = (s32[1,62]{1,0:T(1,128)S(1)}, s32[1,62]{1,0:T(1,128)}, u32[]{:S(2)}) copy-start(s32[1,62]{1,0:T(1,128)} %candidates_ref.1) | copy-start | bytes 748

commit v21 on v20

--- a/solution.py
+++ b/solution.py
@@ -39,27 +39,39 @@
 
 
 def shares_of(passages):
-    edges = [0, passages * 15 // 32]
+    edges = [0, passages // 2]
     return tuple(zip(edges, edges[1:] + [passages]))
+
+
+def widened(table, half, source):
+    half_rows = source.shape[0]
+    piece = half_rows // PIECES
+    for k in range(PIECES):
+        to = pl.ds(pl.multiple_of(half * half_rows + k * piece, piece), piece)
+        table[to, :] = source[pl.ds(k * piece, piece), :].astype(jnp.float32)
 
 
 def prepare_kernel(
     me_ref,
+    half_ref,
     lengths_hbm,
     codes_hbm,
     own_hbm,
     residuals_hbm,
-    staged,
+    table,
     near,
     codes,
-    starts,
+    marks,
+    resets,
     cleans,
     nothing,
     lengths_ref,
-    starts_ref,
+    marks_ref,
+    resets_ref,
     cleans_ref,
     length_rows,
     drawn,
+    staged,
     residuals,
     sems,
 ):
@@ -81,26 +93,29 @@
         length = lengths_ref[p]
         length_rows[pl.ds(p, 1), :] = jnp.full((1, slots), length, jnp.int32)
         for k in range(slots // CHUNK):
-            starts_ref[chunks + k] = p * slots + k * CHUNK
+            marks_ref[chunks + k] = p
+            resets_ref[chunks + k] = -jnp.inf if k == 0 else 0.0
             cleans_ref[chunks + k] = p * slots + k * CHUNK
         return chunks + quotient(length + CHUNK - 1, CHUNK)
 
-    last = starts_ref.shape[0] - 1
+    last = marks_ref.shape[0] - 1
     chunks = jnp.int32(0)
     for step, (low, high) in enumerate(shares_of(passages)):
         chunks = lax.fori_loop(low, high, listing, chunks, unroll=4)
         for k in range(GROUP):
-            starts_ref[chunks + k] = passages * slots
+            marks_ref[chunks + k] = passages
+            resets_ref[chunks + k] = -jnp.inf
             cleans_ref[chunks + k] = low * slots
         chunks = quotient(chunks + GROUP - 1, GROUP) * GROUP
         cleans_ref[last - STEPS + step] = quotient(chunks, GROUP)
     for k in range(SCORE_GROUP):
-        starts_ref[chunks + k] = passages * slots
-    starts_ref[last] = chunks
-    starts_copy = pltpu.make_async_copy(starts_ref, starts, sems.at[4])
-    cleans_copy = pltpu.make_async_copy(cleans_ref, cleans, sems.at[5])
-    starts_copy.start()
-    cleans_copy.start()
+        marks_ref[chunks + k] = passages
+        resets_ref[chunks + k] = -jnp.inf
+    marks_ref[last] = chunks
+    lists = []
+    for source, to in ((marks_ref, marks), (resets_ref, resets), (cleans_ref, cleans)):
+        lists.append(pltpu.make_async_copy(source, to, sems.at[4 + len(lists)]))
+        lists[-1].start()
     codes_copy.wait()
     lanes = lax.broadcasted_iota(jnp.int32, (passages, slots), 1)
     codes[...] = jnp.where(lanes < length_rows[...], drawn[...], drawn[:, 0:1])
@@ -121,8 +136,9 @@
 
     lax.fori_loop(0, quotient(chunks, GROUP), place, 0)
     own_copy.wait()
-    starts_copy.wait()
-    cleans_copy.wait()
+    widened(table, half_ref[0], staged)
+    for copy in lists:
+        copy.wait()
 
 
 def list_size(passages, slots):
@@ -135,40 +151,43 @@
     return -(-(passages * slots + STEPS * GROUP * CHUNK) // rounding) * rounding
 
 
-def prepare(me, lengths, token_codes, own, residuals):
-    width = own.shape[1]
+def prepare(me, half, lengths, token_codes, own, residuals):
+    half_rows, width = own.shape
     passages, slots = token_codes.shape
     most = list_size(passages, slots)
     return pl.pallas_call(
         prepare_kernel,
         out_shape=(
-            pltpu.VMEM(own.shape, jnp.bfloat16),
+            pltpu.VMEM((2 * half_rows, width), jnp.float32),
             pltpu.VMEM((list_rows(passages, slots), width), jnp.float32),
             pltpu.VMEM(token_codes.shape, jnp.int32),
             pltpu.VMEM((most,), jnp.int32),
+            pltpu.VMEM((most,), jnp.float32),
             pltpu.VMEM((most,), jnp.int32),
             pltpu.VMEM((16, width), jnp.bfloat16),
         ),
-        in_specs=[SMEM, HBM, HBM, HBM, HBM],
-        out_specs=(VMEM,) * 6,
+        in_specs=[SMEM, SMEM, HBM, HBM, HBM, HBM],
+        out_specs=(VMEM,) * 7,
         scratch_shapes=[
             pltpu.SMEM(lengths.shape, jnp.int32),
             pltpu.SMEM((most,), jnp.int32),
+            pltpu.SMEM((most,), jnp.float32),
             pltpu.SMEM((most,), jnp.int32),
             pltpu.VMEM(token_codes.shape, jnp.int32),
             pltpu.VMEM(token_codes.shape, jnp.int32),
+            pltpu.VMEM(own.shape, jnp.bfloat16),
             pltpu.VMEM(residuals.shape, jnp.bfloat16),
-            pltpu.SemaphoreType.DMA((6,)),
+            pltpu.SemaphoreType.DMA((7,)),
         ],
-        compiler_params=granted(4),
+        compiler_params=granted(6),
         cost_estimate=pl.CostEstimate(flops=10**7, bytes_accessed=8 * 10**6, transcendentals=0),
         name="prepare",
-    )(me, pinned(lengths), pinned(token_codes), pinned(own), pinned(residuals))
+    )(me, half, pinned(lengths), pinned(token_codes), pinned(own), pinned(residuals))
 
 
 def decode_kernel(step, passages, *refs):
     if step == 0:
-        half_ref, own_ref, other_ref, codes, cleans, near, _, table = refs[:8]
+        half_ref, other_ref, codes, cleans, near, _, _, table = refs[:8]
     else:
         codes, cleans, near, table = refs[:4]
     embedded, rows, nothing, codes_smem, cleans_ref, sems = refs[-6:]
@@ -185,12 +204,7 @@
         moves[-1].start()
     nothing[...] = jnp.zeros(nothing.shape, nothing.dtype)
     if step == 0:
-        half_rows = other_ref.shape[0]
-        piece = half_rows // PIECES
-        for source, base in ((own_ref, half_ref[0]), (other_ref, 1 - half_ref[0])):
-            for k in range(PIECES):
-                to = pl.ds(pl.multiple_of(base * half_rows + k * piece, piece), piece)
-                table[to, :] = source[pl.ds(k * piece, piece), :].astype(jnp.float32)
+        widened(table, 1 - half_ref[0], other_ref)
 
     table_single = table.reshape(table.shape[0], 1, width)
     rows_single = rows.reshape(rows.shape[0], 1, width)
@@ -228,7 +242,7 @@
 
 
 def decode_step(
-    step, half, own, other, codes, cleans, near, table, carried, held
+    step, half, other, codes, cleans, near, table, carried, held
 ):
     passages, slots = codes.shape
     width = near.shape[1]
@@ -236,11 +250,10 @@
     inside = lambda array: pinned(array, pltpu.VMEM)
     shared = [inside(codes), inside(cleans), inside(near)]
     if step == 0:
-        operands = [half, inside(own), inside(other)] + shared + [inside(held)]
+        operands = [half, inside(other)] + shared + [inside(held), inside(table)]
         in_specs = [SMEM] + [VMEM] * 6
-        whole = (2 * own.shape[0], width)
-        out_shape = [pltpu.VMEM(whole, jnp.float32)]
-        aliases = {}
+        out_shape = [pltpu.VMEM(table.shape, jnp.float32)]
+        aliases = {6: 0}
     else:
         operands = shared + [inside(table), inside(held)] + [inside(array) for array in carried]
         in_specs = [VMEM] * 7
@@ -273,20 +286,23 @@
     bit,
     token_count,
     local_queries,
-    slots,
     me_ref,
-    starts,
+    marks,
+    resets,
     queries_ref,
     embedded,
     before_ref,
     out_ref,
-    at_ref,
+    marks_ref,
+    resets_ref,
     turned,
     largest,
-    sem,
+    sems,
 ):
-    starts_copy = pltpu.make_async_copy(starts, at_ref, sem)
-    starts_copy.start()
+    lists = []
+    for k, (source, to) in enumerate(((marks, marks_ref), (resets, resets_ref))):
+        lists.append(pltpu.make_async_copy(source, to, sems.at[k]))
+        lists[-1].start()
     passages = out_ref.shape[1]
     query_tokens = queries_ref.shape[0]
     block = min(QUERY_BLOCK, query_tokens)
@@ -315,12 +331,10 @@
             similar = jnp.dot(embedded[at, :], turned[...], preferred_element_type=jnp.float32)
             parts = jnp.max(similar.reshape(count, CHUNK // 8, 8, block), axis=1)
             for k in range(count):
-                start = at_ref[first * count + k]
-                p = quotient(start, slots)
-                so_far = jnp.where(start == p * slots, parts[k], jnp.maximum(so_far, parts[k]))
-                to = pl.multiple_of(p * 8, 8)
+                so_far = jnp.maximum(so_far + resets_ref[first * count + k], parts[k])
+                p = marks_ref[first * count + k]
                 for lane in range(block // 128):
-                    largest[lane, pl.ds(to, 8), :] = so_far[:, lane * 128 : (lane + 1) * 128]
+                    largest[lane, p] = so_far[:, lane * 128 : (lane + 1) * 128]
             return so_far
 
         def score_parts(g, so_far):
@@ -330,18 +344,20 @@
 
         @pl.when(b == 0)
         def arrived():
-            starts_copy.wait()
-
-        parts_used = quotient(at_ref[at_ref.shape[0] - 1] + count - 1, count)
+            for copy in lists:
+                copy.wait()
+
+        parts_used = quotient(marks_ref[marks_ref.shape[0] - 1] + count - 1, count)
         whole = quotient(parts_used, SCORE_PARTS)
         so_far = jnp.zeros((8, block), jnp.float32)
         so_far = lax.fori_loop(0, whole, score_parts, so_far)
         lax.fori_loop(whole * SCORE_PARTS, parts_used, score, so_far)
         kept = []
         for lane in range(block // 128):
-            best = largest[lane, pl.ds(0, passages, stride=8), :]
+            flat = largest.at[lane].reshape(8 * largest.shape[1], 128)
+            best = flat[pl.ds(0, passages, stride=8), :]
             for k in range(1, 8):
-                best = jnp.maximum(best, largest[lane, pl.ds(k, passages, stride=8), :])
+                best = jnp.maximum(best, flat[pl.ds(k, passages, stride=8), :])
             kept.append(best)
         left = jnp.concatenate(kept, axis=1)
         to = pl.ds(pl.multiple_of((b ^ far_me) * window, window), window)
@@ -358,28 +374,30 @@
     lax.fori_loop(0, blocks, score_block, 0)
 
 
-def score_half(bit, me, starts, query_rows, embedded, before, passages, slots, shape):
+def score_half(bit, me, marks, resets, query_rows, embedded, before, passages, shape):
     token_count, local_queries = shape
     query_tokens, width = query_rows.shape
     block = min(QUERY_BLOCK, query_tokens)
     blocks = query_tokens // block
     return pl.pallas_call(
-        functools.partial(score_kernel, bit, token_count, local_queries, slots),
+        functools.partial(score_kernel, bit, token_count, local_queries),
         out_shape=pltpu.VMEM((2 * query_tokens // token_count, passages), jnp.float32),
-        in_specs=[SMEM] + [VMEM] * 4,
+        in_specs=[SMEM] + [VMEM] * 5,
         out_specs=VMEM,
         scratch_shapes=[
-            pltpu.SMEM(starts.shape, jnp.int32),
+            pltpu.SMEM(marks.shape, jnp.int32),
+            pltpu.SMEM(resets.shape, jnp.float32),
             pltpu.VMEM((width, block), jnp.bfloat16),
-            pltpu.VMEM((block // 128, (passages + 1) * 8, 128), jnp.float32),
-            pltpu.SemaphoreType.DMA,
+            pltpu.VMEM((block // 128, passages + 1, 8, 128), jnp.float32),
+            pltpu.SemaphoreType.DMA((2,)),
         ],
         compiler_params=granted(4),
         cost_estimate=pl.CostEstimate(flops=10**7, bytes_accessed=8 * 10**6, transcendentals=0),
         name="score",
     )(
         me,
-        pinned(starts, pltpu.VMEM),
+        pinned(marks, pltpu.VMEM),
+        pinned(resets, pltpu.VMEM),
         pinned(query_rows, pltpu.VMEM),
         pinned(embedded, pltpu.VMEM),
         pinned(before, pltpu.VMEM),
@@ -434,12 +452,11 @@
         pairs = [(device, device ^ (1 << first)) for device in range(targets)]
         received = lax.ppermute(held, ("shard", "sub"), pairs)
         if turn == 0:
-            ready = prepare(me, lengths, token_codes, centroids, flat)
-            own, near, codes, starts, cleans, nothing = ready
-            table = None
+            ready = prepare(me, half, lengths, token_codes, centroids, flat)
+            table, near, codes, marks, resets, cleans, nothing = ready
         elif turn <= STEPS:
             table, carried, nothing = decode_step(
-                turn - 1, half, own, other, codes, cleans, near, table, carried, held
+                turn - 1, half, other, codes, cleans, near, table, carried, held
             )
         if first > 0:
             received = received + nothing[0:1, :]
@@ -449,7 +466,7 @@
     scores = carried[1]
     for bit, half_rows in enumerate((held, received)):
         rows = half_rows.reshape(targets // 2 * local_queries * token_count, width)
-        scores = score_half(bit, me, starts, rows, carried[0], scores, passages, slots, shape)
+        scores = score_half(bit, me, marks, resets, rows, carried[0], scores, passages, shape)
     returned = lax.all_to_all(
         scores.reshape(targets, local_queries * passages),
         ("shard", "sub"),

time: 32.7 us -> 33.1 us (1.012)
  blocking collectives: 9.08 us -> 9.47 us
    pallas_call x2, Pallas kernels: 6.91 us -> 6.39 us  [decode_step(): pl.pallas_call(functools.partial(decode_kernel, step, passages), out_shap...]
    pallas_call x1, Pallas kernels: 3.04 us -> 3.5 us  [prepare(): pl.pallas_call(prepare_kernel, out_shape=(pltpu.VMEM((2 * half_rows, widt...]
    all_to_all x1, blocking collectives: 9.08 us -> 9.47 us  [body(): lax.all_to_all(scores.reshape(targets, local_queries * passages), ('shard...]
  transfers between devices with their start and end apart: 5 -> 5, of which waited for: 0 -> 0; matrix products, arithmetic and copies ran while one was open for 0% -> 0% of each run, Pallas kernels for 39% -> 38%
where the time goes in v21:
time: 33.1 us; the launch traced here: 32.7 us
  Pallas kernels  15.8 us (48%)
  blocking collectives  9.47 us (29%)
  starting transfers between devices  7.2 us (22%)
    all_to_all x1, blocking collectives, body(): lax.all_to_all(scores.reshape(targets, local_queries * passages), ('shard...  9.47 us
    ppermute x4, starting transfers between devices, body(): received = lax.ppermute(held, ('shard', 'sub'), pairs)  6.75 us
    pallas_call x2, Pallas kernels, decode_step(): pl.pallas_call(functools.partial(decode_kernel, step, passages), out_shap...  6.39 us
    pallas_call x2, Pallas kernels, score_half(): pl.pallas_call(functools.partial(score_kernel, bit, token_count, local_qu...  5.26 us
    pallas_call x1, Pallas kernels, prepare(): pl.pallas_call(prepare_kernel, out_shape=(pltpu.VMEM((2 * half_rows, widt...  3.5 us
  transfers between devices with their start and end apart: 5, of which 0 were waited for; matrix products, arithmetic and copies ran while one was open for 0% of the time, Pallas kernels for 38%

profile of v21, /device:TPU:0, one launch (start us, length us, event | category | flops | bytes accessed | tf_op | source)
XLA Modules:
  0.0 32.7 jit_solution(4073193551547867977)
XLA Ops:
  0.0 0.0 copy-start.1
  0.0 0.5 %collective-permute-start.2 = (bf16[8192,128]{1,0:T(8,128)(2,1)}, bf16[8192,128]{1,0:T(8,128)(2,1)S(1)}, u32[]{:S(2)}, u32[]{:S(2)}) collective-permute-start(bf16[8192,128]{1,0:T(8,128)(2,1)} %own_hbm.1), channel_id=1, source_target_pairs={{0,1},{1,0},{2,3},{3,2},{4,5},{5,4},{6,7},{7,6},{8,9},{9,8},{10,11... | collective-permute-start | bytes 6291464 | tf_op jit(solution)/shard_map/ppermute | solution.py:446
  0.5 3.6 %collective-permute-start = (bf16[1,1,32,128]{3,2,1,0:T(8,128)(2,1)}, bf16[1,1,32,128]{3,2,1,0:T(8,128)(2,1)S(1)}, u32[]{:S(2)}, u32[]{:S(2)}) collective-permute-start(bf16[1,1,32,128]{3,2,1,0:T(8,128)(2,1)} %bitcast.29), channel_id=1, source_target_pairs={{0,8},{1,9},{2,10},{3,11},{4,12},{5,13},{6,14},{7,15},{8,0},{9,1},... | collective-permute-start | bytes 24584 | tf_op jit(solution)/shard_map/ppermute | solution.py:453
  4.1 3.5 %prepare.1 = (f32[16384,128]{1,0:T(8,128)S(1)}, f32[9216,128]{1,0:T(8,128)S(1)}, s32[64,128]{1,0:T(8,128)S(1)}, s32[1024]{0:T(1024)S(1)}, f32[1024]{0:T(1024)S(1...) custom-call(s32[1]{0:T(128)} %bitcast.me_ref, s32[1]{0:T(128)} %bitcast.1.half_ref.refs_0_, s32[64]{0:T(128)} %lengths_hbm.1, ...), custom_call_target="tpu_custom_call" | custom-call | flops 10000000 | bytes 8000000 | tf_op jit(solution)/shard_map/prepare/pallas_call | solution.py:158
  7.6 0.0 collective-permute-done
  7.6 0.0 copy-done.1
  7.7 1.5 %collective-permute-start.1 = (bf16[2,1,32,128]{3,2,1,0:T(8,128)(2,1)S(1)}, bf16[2,1,32,128]{3,2,1,0:T(8,128)(2,1)S(1)}, u32[]{:S(2)}, u32[]{:S(2)}) collective-permute-start(bf16[2,1,32,128]{3,2,1,0:T(8,128)(2,1)S(1)} %maximum_bitcast_fusion.refs_5_), channel_id=1, source_target_pairs={{0,4},{1,5},{2,6},{3,7},{4,0},{5,1},{6,2},{7,3},{8,12},{9,13},{10,... | collective-permute-start | bytes 49160 | tf_op jit(solution)/shard_map/ppermute | solution.py:453
  9.2 0.0 collective-permute-done.2.refs_1_
  9.2 3.1 %decode.2 = (f32[16384,128]{1,0:T(8,128)S(1)}, bf16[9216,128]{1,0:T(8,128)(2,1)S(1)}, f32[256,128]{1,0:T(8,128)S(1)}, bf16[16,128]{1,0:T(8,128)(2,1)S(1)}) custom-call(s32[1]{0:T(128)} %bitcast.1.half_ref.refs_0_, bf16[8192,128]{1,0:T(8,128)(2,1)S(1)} %collective-permute-done.2.refs_1_, ...), custom_call_target="tpu_custom_call", output_to_operand_aliasing={{0}: (6, {})} | custom-call | flops 10000000 | bytes 10000000 | tf_op jit(solution)/shard_map/decode/pallas_call | solution.py:265
  12.3 0.0 collective-permute-done.1
  12.4 1.5 %collective-permute-start.3 = (bf16[4,1,32,128]{3,2,1,0:T(8,128)(2,1)S(1)}, bf16[4,1,32,128]{3,2,1,0:T(8,128)(2,1)S(1)}, u32[]{:S(2)}, u32[]{:S(2)}) collective-permute-start(bf16[4,1,32,128]{3,2,1,0:T(8,128)(2,1)S(1)} %bitcast.20), channel_id=1, source_target_pairs={{0,2},{1,3},{2,0},{3,1},{4,6},{5,7},{6,4},{7,5},{8,10},{9,11},{10,... | collective-permute-start | bytes 98312 | tf_op jit(solution)/shard_map/ppermute | solution.py:453
  13.9 3.3 %decode.3 = (bf16[9216,128]{1,0:T(8,128)(2,1)S(1)}, f32[256,128]{1,0:T(8,128)S(1)}, bf16[16,128]{1,0:T(8,128)(2,1)S(1)}) custom-call(s32[64,128]{1,0:T(8,128)S(1)} %get-tuple-element.22.refs_2_.refs_0_, s32[1024]{0:T(1024)S(1)} %get-tuple-element.23.refs_3_.refs_1_, ...), custom_call_target="tpu_custom_call", output_to_operand_aliasing={{0}: (5, {}), {1}: (6, {})} | custom-call | flops 10000000 | bytes 10000000 | tf_op jit(solution)/shard_map/decode/pallas_call | solution.py:265
  17.2 0.0 collective-permute-done.3
  17.2 0.1 collective-permute-start.4
  17.3 0.0 copy-start
  17.3 2.6 %score.2.before_ref = f32[16,64]{1,0:T(8,128)S(1)} custom-call(s32[1]{0:T(128)} %bitcast.me_ref, s32[1024]{0:T(1024)S(1)} %get-tuple-element.19.marks, f32[1024]{0:T(1024)S(1)} %get-tuple-element.20.resets, bf16[256,128]{1,0:T(8,128)(2,1)S(1)} %bitcast.24, bf16[9216,128]{1,0:T(8,128)(2,1)S(1)} %get-tuple-element.31.embedded, ...), custom_call_target="tpu_custom_call" | custom-call | flops 10000000 | bytes 8000000 | tf_op jit(solution)/shard_map/score/pallas_call | solution.py:382
  19.9 0.0 collective-permute-done.4
  20.0 2.6 %score.3 = f32[16,64]{1,0:T(8,128)S(1)} custom-call(s32[1]{0:T(128)} %bitcast.me_ref, s32[1024]{0:T(1024)S(1)} %get-tuple-element.19.marks, f32[1024]{0:T(1024)S(1)} %get-tuple-element.20.resets, bf16[256,128]{1,0:T(8,128)(2,1)S(1)} %bitcast.25, bf16[9216,128]{1,0:T(8,128)(2,1)S(1)} %get-tuple-element.31.embedded, f32[16,64]{1,0:T(8,128)S(1)} %score.2.before_ref), custom_call_target="tpu_custom_call" | custom-call | flops 10000000 | bytes 8000000 | tf_op jit(solution)/shard_map/score/pallas_call | solution.py:382
  22.6 9.5 %all_to_all.11 = f32[16,1,64]{2,1,0:T(1,128)S(1)} all-to-all(f32[16,1,64]{2,1,0:T(1,128)S(1)} %bitcast.26), channel_id=1, replica_groups=mesh['groups'=2,'shard'=8,'sub'=2] {'shard','sub'}, dimensions={0} | all-to-all | bytes 8192 | tf_op jit(solution)/shard_map/all_to_all | solution.py:470
  32.1 0.0 copy-done
  32.1 0.7 %pick.1 = f32[1,62]{1,0:T(1,128)} custom-call(s32[1,62]{1,0:T(1,128)S(1)} %copy-done, f32[16,64]{1,0:T(8,128)S(1)} %bitcast.27), custom_call_target="tpu_custom_call" | custom-call | tf_op jit(solution)/shard_map/pick/pallas_call | solution.py:427
  (9 shorter events, 0.1 us)
Async XLA Ops:
  0.0 7.7 %copy-start.1 = (bf16[1,32,128]{2,1,0:T(8,128)(2,1)S(1)}, bf16[1,32,128]{2,1,0:T(8,128)(2,1)}, u32[]{:S(2)}) copy-start(bf16[1,32,128]{2,1,0:T(8,128)(2,1)} %param.6) | copy-start | bytes 24580
  0.0 9.2 %collective-permute-start.2 = (bf16[8192,128]{1,0:T(8,128)(2,1)}, bf16[8192,128]{1,0:T(8,128)(2,1)S(1)}, u32[]{:S(2)}, u32[]{:S(2)}) collective-permute-start(bf16[8192,128]{1,0:T(8,128)(2,1)} %own_hbm.1), channel_id=1, source_target_pairs={{0,1},{1,0},{2,3},{3,2},{4,5},{5,4},{6,7},{7,6},{8,9},{9,8},{10,11... | collective-permute-start | bytes 6291464 | tf_op jit(solution)/shard_map/ppermute | solution.py:446
  0.5 7.2 %collective-permute-start = (bf16[1,1,32,128]{3,2,1,0:T(8,128)(2,1)}, bf16[1,1,32,128]{3,2,1,0:T(8,128)(2,1)S(1)}, u32[]{:S(2)}, u32[]{:S(2)}) collective-permute-start(bf16[1,1,32,128]{3,2,1,0:T(8,128)(2,1)} %bitcast.29), channel_id=1, source_target_pairs={{0,8},{1,9},{2,10},{3,11},{4,12},{5,13},{6,14},{7,15},{8,0},{9,1},... | collective-permute-start | bytes 24584 | tf_op jit(solution)/shard_map/ppermute | solution.py:453
  7.7 4.7 %collective-permute-start.1 = (bf16[2,1,32,128]{3,2,1,0:T(8,128)(2,1)S(1)}, bf16[2,1,32,128]{3,2,1,0:T(8,128)(2,1)S(1)}, u32[]{:S(2)}, u32[]{:S(2)}) collective-permute-start(bf16[2,1,32,128]{3,2,1,0:T(8,128)(2,1)S(1)} %maximum_bitcast_fusion.refs_5_), channel_id=1, source_target_pairs={{0,4},{1,5},{2,6},{3,7},{4,0},{5,1},{6,2},{7,3},{8,12},{9,13},{10,... | collective-permute-start | bytes 49160 | tf_op jit(solution)/shard_map/ppermute | solution.py:453
  12.4 4.8 %collective-permute-start.3 = (bf16[4,1,32,128]{3,2,1,0:T(8,128)(2,1)S(1)}, bf16[4,1,32,128]{3,2,1,0:T(8,128)(2,1)S(1)}, u32[]{:S(2)}, u32[]{:S(2)}) collective-permute-start(bf16[4,1,32,128]{3,2,1,0:T(8,128)(2,1)S(1)} %bitcast.20), channel_id=1, source_target_pairs={{0,2},{1,3},{2,0},{3,1},{4,6},{5,7},{6,4},{7,5},{8,10},{9,11},{10,... | collective-permute-start | bytes 98312 | tf_op jit(solution)/shard_map/ppermute | solution.py:453
  17.2 2.7 %collective-permute-start.4 = (bf16[8,1,32,128]{3,2,0,1:T(8,128)(2,1)S(1)}, bf16[8,1,32,128]{3,2,0,1:T(8,128)(2,1)S(1)}, u32[]{:S(2)}, u32[]{:S(2)}) collective-permute-start(bf16[8,1,32,128]{3,2,0,1:T(8,128)(2,1)S(1)} %bitcast.23), channel_id=1, source_target_pairs={{0,1},{1,0},{2,3},{3,2},{4,5},{5,4},{6,7},{7,6},{8,9},{9,8},{10,11... | collective-permute-start | bytes 196616 | tf_op jit(solution)/shard_map/ppermute | solution.py:453
  17.3 14.8 %copy-start = (s32[1,62]{1,0:T(1,128)S(1)}, s32[1,62]{1,0:T(1,128)}, u32[]{:S(2)}) copy-start(s32[1,62]{1,0:T(1,128)} %candidates_ref.1) | copy-start | bytes 748

commit v22 on v20

--- a/solution.py
+++ b/solution.py
@@ -22,6 +22,14 @@
 def normalized(vectors):
     total = jnp.sum(vectors * vectors, axis=-1, keepdims=True)
     return (vectors * lax.rsqrt(total + 1e-06)).astype(jnp.bfloat16)
+
+
+def thirds(values):
+    parts = []
+    for _ in range(3):
+        parts.append(values.astype(jnp.bfloat16))
+        values = values - parts[-1].astype(jnp.float32)
+    return parts
 
 
 def quotient(number, divisor):
@@ -127,7 +135,7 @@
 
 def list_size(passages, slots):
     most = passages * (slots // CHUNK) + STEPS * GROUP + SCORE_GROUP + STEPS + 1
-    return -(-most // 1024) * 1024
+    return -(-most // 128) * 128
 
 
 def list_rows(passages, slots):
@@ -301,7 +309,7 @@
     query_of = quotient(lax.broadcasted_iota(jnp.int32, (window, block), 1), token_count)
     target_of = quotient(query_of, local_queries)
     row_of = query_of + (target_of + bit) * local_queries
-    summing = (owner_row == row_of).astype(jnp.bfloat16)
+    summing = jnp.concatenate([(owner_row == row_of).astype(jnp.bfloat16)] * 3, axis=1)
     count = SCORE_GROUP // SCORE_PARTS
     size = count * CHUNK
 
@@ -345,13 +353,14 @@
             kept.append(best)
         left = jnp.concatenate(kept, axis=1)
         to = pl.ds(pl.multiple_of((b ^ far_me) * window, window), window)
-        sums = before_ref[to, :] if bit else jnp.zeros((window, passages), jnp.float32)
-        for _ in range(3):
-            part = left.astype(jnp.bfloat16)
-            left = left - part.astype(jnp.float32)
-            sums = sums + lax.dot_general(
-                summing, part, (((1,), (1,)), ((), ())), preferred_element_type=jnp.float32
-            )
+        sums = lax.dot_general(
+            summing,
+            jnp.concatenate(thirds(left), axis=1),
+            (((1,), (1,)), ((), ())),
+            preferred_element_type=jnp.float32,
+        )
+        if bit:
+            sums = sums + before_ref[to, :]
         out_ref[to, :] = sums
         return carry
 
@@ -396,11 +405,11 @@
         target = quotient(wanted, passages)
         hits = (passage_numbers == wanted - target * passages).astype(jnp.bfloat16)
         left = returned_ref[:, q * passages : (q + 1) * passages]
-        picked = jnp.zeros((targets, count), jnp.float32)
-        for _ in range(3):
-            part = left.astype(jnp.bfloat16)
-            left = left - part.astype(jnp.float32)
-            picked = picked + jnp.dot(part, hits, preferred_element_type=jnp.float32)
+        picked = jnp.dot(
+            jnp.concatenate(thirds(left), axis=1),
+            jnp.concatenate([hits] * 3, axis=0),
+            preferred_element_type=jnp.float32,
+        )
         kept = jnp.where(target_numbers == target, picked, 0.0)
         out_ref[q : q + 1, :] = jnp.sum(kept, axis=0, keepdims=True)
 

time: 32.7 us -> 33.1 us (1.012)
  Pallas kernels: 16 us -> 14.7 us
  blocking collectives: 9.08 us -> 10.1 us
  starting transfers between devices: 7.08 us -> 7.88 us
    all_to_all x1, blocking collectives: 9.08 us -> 10.1 us  [body(): lax.all_to_all(scores.reshape(targets, local_queries * passages), ('shard...]
    ppermute x4, starting transfers between devices: 6.63 us -> 7.43 us  [body(): received = lax.ppermute(held, ('shard', 'sub'), pairs)]
    pallas_call x2, Pallas kernels: 6.91 us -> 6.18 us  [decode_step(): pl.pallas_call(functools.partial(decode_kernel, step, passages), out_shap...]
    pallas_call x2, Pallas kernels: 5.43 us -> 4.91 us  [score_half(): pl.pallas_call(functools.partial(score_kernel, bit, token_count, local_qu...]
  transfers between devices with their start and end apart: 5 -> 5, of which waited for: 0 -> 0; matrix products, arithmetic and copies ran while one was open for 0% -> 0% of each run, Pallas kernels for 39% -> 35%
where the time goes in v22:
time: 33.1 us; the launch traced here: 32.9 us
  Pallas kernels  14.7 us (44%)
  blocking collectives  10.1 us (31%)
  starting transfers between devices  7.88 us (24%)
    all_to_all x1, blocking collectives, body(): lax.all_to_all(scores.reshape(targets, local_queries * passages), ('shard...  10.1 us
    ppermute x4, starting transfers between devices, body(): received = lax.ppermute(held, ('shard', 'sub'), pairs)  7.43 us
    pallas_call x2, Pallas kernels, decode_step(): pl.pallas_call(functools.partial(decode_kernel, step, passages), out_shap...  6.18 us
    pallas_call x2, Pallas kernels, score_half(): pl.pallas_call(functools.partial(score_kernel, bit, token_count, local_qu...  4.91 us
    pallas_call x1, Pallas kernels, prepare(): pl.pallas_call(prepare_kernel, out_shape=(pltpu.VMEM(own.shape, jnp.bfloa...  2.86 us
    pallas_call x1, Pallas kernels, pick(): pl.pallas_call(functools.partial(pick_kernel, passages), out_shape=jax.Sh...  0.71 us
  transfers between devices with their start and end apart: 5, of which 0 were waited for; matrix products, arithmetic and copies ran while one was open for 0% of the time, Pallas kernels for 35%

profile of v22, /device:TPU:0, one launch (start us, length us, event | category | flops | bytes accessed | tf_op | source)
XLA Modules:
  0.0 32.9 jit_solution(7810844917868305235)
XLA Ops:
  0.0 0.0 copy-start.1
  0.0 0.5 %collective-permute-start.2 = (bf16[8192,128]{1,0:T(8,128)(2,1)}, bf16[8192,128]{1,0:T(8,128)(2,1)S(1)}, u32[]{:S(2)}, u32[]{:S(2)}) collective-permute-start(bf16[8192,128]{1,0:T(8,128)(2,1)} %own_hbm.1), channel_id=1, source_target_pairs={{0,1},{1,0},{2,3},{3,2},{4,5},{5,4},{6,7},{7,6},{8,9},{9,8},{10,11... | collective-permute-start | bytes 6291464 | tf_op jit(solution)/shard_map/ppermute | solution.py:437
  0.5 3.6 %collective-permute-start = (bf16[1,1,32,128]{3,2,1,0:T(8,128)(2,1)}, bf16[1,1,32,128]{3,2,1,0:T(8,128)(2,1)S(1)}, u32[]{:S(2)}, u32[]{:S(2)}) collective-permute-start(bf16[1,1,32,128]{3,2,1,0:T(8,128)(2,1)} %bitcast.29), channel_id=1, source_target_pairs={{0,8},{1,9},{2,10},{3,11},{4,12},{5,13},{6,14},{7,15},{8,0},{9,1},... | collective-permute-start | bytes 24584 | tf_op jit(solution)/shard_map/ppermute | solution.py:444
  4.1 2.9 %prepare.1 = (bf16[8192,128]{1,0:T(8,128)(2,1)S(1)}, f32[9216,128]{1,0:T(8,128)S(1)}, s32[64,128]{1,0:T(8,128)S(1)}, s32[640]{0:T(1024)S(1)}, s32[640]{0:T(1024)S(1)}, /*index=5*/bf16[16,128]{1,0:T(8,128)(2,1)S(1)}) custom-call(s32[1]{0:T(128)} %bitcast.me_ref, s32[64]{0:T(128)} %lengths_hbm.1, s32[64,128]{1,0:T(8,128)} %codes_hbm.1, ...), custom_call_target="tpu_custom_call" | custom-call | flops 10000000 | bytes 8000000 | tf_op jit(solution)/shard_map/prepare/pallas_call | solution.py:150
  7.0 0.0 collective-permute-done
  7.0 0.0 copy-done.1
  7.0 1.8 %collective-permute-start.1 = (bf16[2,1,32,128]{3,2,1,0:T(8,128)(2,1)S(1)}, bf16[2,1,32,128]{3,2,1,0:T(8,128)(2,1)S(1)}, u32[]{:S(2)}, u32[]{:S(2)}) collective-permute-start(bf16[2,1,32,128]{3,2,1,0:T(8,128)(2,1)S(1)} %maximum_bitcast_fusion.refs_6_), channel_id=1, source_target_pairs={{0,4},{1,5},{2,6},{3,7},{4,0},{5,1},{6,2},{7,3},{8,12},{9,13},{10,... | collective-permute-start | bytes 49160 | tf_op jit(solution)/shard_map/ppermute | solution.py:444
  8.8 0.0 collective-permute-done.2.refs_2_
  8.8 2.6 %decode.2 = (f32[16384,128]{1,0:T(8,128)S(1)}, bf16[9216,128]{1,0:T(8,128)(2,1)S(1)}, f32[256,128]{1,0:T(8,128)S(1)}, bf16[16,128]{1,0:T(8,128)(2,1)S(1)}) custom-call(s32[1]{0:T(128)} %bitcast.5.refs_0_, bf16[8192,128]{1,0:T(8,128)(2,1)S(1)} %get-tuple-element.20.refs_1_, bf16[8192,128]{1,0:T(8,128)(2,1)S(1)} %collective-permute-done.2.refs_2_, ...), custom_call_target="tpu_custom_call" | custom-call | flops 10000000 | bytes 10000000 | tf_op jit(solution)/shard_map/decode/pallas_call | solution.py:260
  11.5 0.0 collective-permute-done.1
  11.5 1.9 %collective-permute-start.3 = (bf16[4,1,32,128]{3,2,1,0:T(8,128)(2,1)S(1)}, bf16[4,1,32,128]{3,2,1,0:T(8,128)(2,1)S(1)}, u32[]{:S(2)}, u32[]{:S(2)}) collective-permute-start(bf16[4,1,32,128]{3,2,1,0:T(8,128)(2,1)S(1)} %bitcast.20), channel_id=1, source_target_pairs={{0,2},{1,3},{2,0},{3,1},{4,6},{5,7},{6,4},{7,5},{8,10},{9,11},{10,... | collective-permute-start | bytes 98312 | tf_op jit(solution)/shard_map/ppermute | solution.py:444
  13.4 3.5 %decode.3 = (bf16[9216,128]{1,0:T(8,128)(2,1)S(1)}, f32[256,128]{1,0:T(8,128)S(1)}, bf16[16,128]{1,0:T(8,128)(2,1)S(1)}) custom-call(s32[64,128]{1,0:T(8,128)S(1)} %get-tuple-element.21.refs_3_.refs_0_, s32[640]{0:T(1024)S(1)} %get-tuple-element.22.refs_4_.refs_1_, ...), custom_call_target="tpu_custom_call", output_to_operand_aliasing={{0}: (5, {}), {1}: (6, {})} | custom-call | flops 10000000 | bytes 10000000 | tf_op jit(solution)/shard_map/decode/pallas_call | solution.py:260
  17.0 0.0 collective-permute-done.3
  17.0 0.1 collective-permute-start.4
  17.1 0.0 copy-start
  17.1 2.5 %score.2.before_ref = f32[16,64]{1,0:T(8,128)S(1)} custom-call(s32[1]{0:T(128)} %bitcast.me_ref, s32[640]{0:T(1024)S(1)} %get-tuple-element.18.starts, bf16[256,128]{1,0:T(8,128)(2,1)S(1)} %bitcast.24, bf16[9216,128]{1,0:T(8,128)(2,1)S(1)} %get-tuple-element.29.embedded, f32[256,128]{1,0:T(8,128)S(1)} %get-tuple-element.30.before_ref), custom_call_target="tpu_custom_call" | custom-call | flops 10000000 | bytes 8000000 | tf_op jit(solution)/shard_map/score/pallas_call | solution.py:375
  19.6 0.0 collective-permute-done.4
  19.6 2.5 %score.3 = f32[16,64]{1,0:T(8,128)S(1)} custom-call(s32[1]{0:T(128)} %bitcast.me_ref, s32[640]{0:T(1024)S(1)} %get-tuple-element.18.starts, bf16[256,128]{1,0:T(8,128)(2,1)S(1)} %bitcast.25, bf16[9216,128]{1,0:T(8,128)(2,1)S(1)} %get-tuple-element.29.embedded, f32[16,64]{1,0:T(8,128)S(1)} %score.2.before_ref), custom_call_target="tpu_custom_call" | custom-call | flops 10000000 | bytes 8000000 | tf_op jit(solution)/shard_map/score/pallas_call | solution.py:375
  22.1 10.1 %all_to_all.11 = f32[16,1,64]{2,1,0:T(1,128)S(1)} all-to-all(f32[16,1,64]{2,1,0:T(1,128)S(1)} %bitcast.26), channel_id=1, replica_groups=mesh['groups'=2,'shard'=8,'sub'=2] {'shard','sub'}, dimensions={0} | all-to-all | bytes 8192 | tf_op jit(solution)/shard_map/all_to_all | solution.py:462
  32.2 0.0 copy-done
  32.2 0.7 %pick.1 = f32[1,62]{1,0:T(1,128)} custom-call(s32[1,62]{1,0:T(1,128)S(1)} %copy-done, f32[16,64]{1,0:T(8,128)S(1)} %bitcast.27), custom_call_target="tpu_custom_call" | custom-call | tf_op jit(solution)/shard_map/pick/pallas_call | solution.py:418
  (9 shorter events, 0.1 us)
Async XLA Ops:
  0.0 7.0 %copy-start.1 = (bf16[1,32,128]{2,1,0:T(8,128)(2,1)S(1)}, bf16[1,32,128]{2,1,0:T(8,128)(2,1)}, u32[]{:S(2)}) copy-start(bf16[1,32,128]{2,1,0:T(8,128)(2,1)} %param.6) | copy-start | bytes 24580
  0.0 8.8 %collective-permute-start.2 = (bf16[8192,128]{1,0:T(8,128)(2,1)}, bf16[8192,128]{1,0:T(8,128)(2,1)S(1)}, u32[]{:S(2)}, u32[]{:S(2)}) collective-permute-start(bf16[8192,128]{1,0:T(8,128)(2,1)} %own_hbm.1), channel_id=1, source_target_pairs={{0,1},{1,0},{2,3},{3,2},{4,5},{5,4},{6,7},{7,6},{8,9},{9,8},{10,11... | collective-permute-start | bytes 6291464 | tf_op jit(solution)/shard_map/ppermute | solution.py:437
  0.5 6.5 %collective-permute-start = (bf16[1,1,32,128]{3,2,1,0:T(8,128)(2,1)}, bf16[1,1,32,128]{3,2,1,0:T(8,128)(2,1)S(1)}, u32[]{:S(2)}, u32[]{:S(2)}) collective-permute-start(bf16[1,1,32,128]{3,2,1,0:T(8,128)(2,1)} %bitcast.29), channel_id=1, source_target_pairs={{0,8},{1,9},{2,10},{3,11},{4,12},{5,13},{6,14},{7,15},{8,0},{9,1},... | collective-permute-start | bytes 24584 | tf_op jit(solution)/shard_map/ppermute | solution.py:444
  7.0 4.4 %collective-permute-start.1 = (bf16[2,1,32,128]{3,2,1,0:T(8,128)(2,1)S(1)}, bf16[2,1,32,128]{3,2,1,0:T(8,128)(2,1)S(1)}, u32[]{:S(2)}, u32[]{:S(2)}) collective-permute-start(bf16[2,1,32,128]{3,2,1,0:T(8,128)(2,1)S(1)} %maximum_bitcast_fusion.refs_6_), channel_id=1, source_target_pairs={{0,4},{1,5},{2,6},{3,7},{4,0},{5,1},{6,2},{7,3},{8,12},{9,13},{10,... | collective-permute-start | bytes 49160 | tf_op jit(solution)/shard_map/ppermute | solution.py:444
  11.5 5.5 %collective-permute-start.3 = (bf16[4,1,32,128]{3,2,1,0:T(8,128)(2,1)S(1)}, bf16[4,1,32,128]{3,2,1,0:T(8,128)(2,1)S(1)}, u32[]{:S(2)}, u32[]{:S(2)}) collective-permute-start(bf16[4,1,32,128]{3,2,1,0:T(8,128)(2,1)S(1)} %bitcast.20), channel_id=1, source_target_pairs={{0,2},{1,3},{2,0},{3,1},{4,6},{5,7},{6,4},{7,5},{8,10},{9,11},{10,... | collective-permute-start | bytes 98312 | tf_op jit(solution)/shard_map/ppermute | solution.py:444
  17.0 2.6 %collective-permute-start.4 = (bf16[8,1,32,128]{3,2,0,1:T(8,128)(2,1)S(1)}, bf16[8,1,32,128]{3,2,0,1:T(8,128)(2,1)S(1)}, u32[]{:S(2)}, u32[]{:S(2)}) collective-permute-start(bf16[8,1,32,128]{3,2,0,1:T(8,128)(2,1)S(1)} %bitcast.23), channel_id=1, source_target_pairs={{0,1},{1,0},{2,3},{3,2},{4,5},{5,4},{6,7},{7,6},{8,9},{9,8},{10,11... | collective-permute-start | bytes 196616 | tf_op jit(solution)/shard_map/ppermute | solution.py:444
  17.1 15.1 %copy-start = (s32[1,62]{1,0:T(1,128)S(1)}, s32[1,62]{1,0:T(1,128)}, u32[]{:S(2)}) copy-start(s32[1,62]{1,0:T(1,128)} %candidates_ref.1) | copy-start | bytes 748

commit v23 on v22

--- a/solution.py
+++ b/solution.py
@@ -11,6 +11,7 @@
 GROUP = 16
 SCORE_GROUP = 64
 SCORE_PARTS = 2
+SCORE_RUNS = (4, 2, 1)
 STEPS = 2
 PIECES = 4
 QUERY_BLOCK = 512
@@ -47,7 +48,7 @@
 
 
 def shares_of(passages):
-    edges = [0, passages * 15 // 32]
+    edges = [0, passages // 2]
     return tuple(zip(edges, edges[1:] + [passages]))
 
 
@@ -331,20 +332,23 @@
                     largest[lane, pl.ds(to, 8), :] = so_far[:, lane * 128 : (lane + 1) * 128]
             return so_far
 
-        def score_parts(g, so_far):
-            for part in range(SCORE_PARTS):
-                so_far = score(g * SCORE_PARTS + part, so_far)
-            return so_far
-
         @pl.when(b == 0)
         def arrived():
             starts_copy.wait()
 
         parts_used = quotient(at_ref[at_ref.shape[0] - 1] + count - 1, count)
-        whole = quotient(parts_used, SCORE_PARTS)
         so_far = jnp.zeros((8, block), jnp.float32)
-        so_far = lax.fori_loop(0, whole, score_parts, so_far)
-        lax.fori_loop(whole * SCORE_PARTS, parts_used, score, so_far)
+        done = jnp.int32(0)
+        for run in SCORE_RUNS:
+
+            def score_run(g, so_far, run=run, done=done):
+                for part in range(run):
+                    so_far = score(done + g * run + part, so_far)
+                return so_far
+
+            runs = quotient(parts_used - done, run)
+            so_far = lax.fori_loop(0, runs, score_run, so_far)
+            done = done + runs * run
         kept = []
         for lane in range(block // 128):
             best = largest[lane, pl.ds(0, passages, stride=8), :]
@@ -405,11 +409,9 @@
         target = quotient(wanted, passages)
         hits = (passage_numbers == wanted - target * passages).astype(jnp.bfloat16)
         left = returned_ref[:, q * passages : (q + 1) * passages]
-        picked = jnp.dot(
-            jnp.concatenate(thirds(left), axis=1),
-            jnp.concatenate([hits] * 3, axis=0),
-            preferred_element_type=jnp.float32,
-        )
+        picked = jnp.zeros((targets, count), jnp.float32)
+        for part in thirds(left):
+            picked = picked + jnp.dot(part, hits, preferred_element_type=jnp.float32)
         kept = jnp.where(target_numbers == target, picked, 0.0)
         out_ref[q : q + 1, :] = jnp.sum(kept, axis=0, keepdims=True)
 

time: 33.1 us -> 32.1 us (0.970)
  Pallas kernels: 14.7 us -> 13.5 us
    pallas_call x2, Pallas kernels: 4.91 us -> 4.15 us  [score_half(): pl.pallas_call(functools.partial(score_kernel, bit, token_count, local_qu...]
  transfers between devices with their start and end apart: 5 -> 5, of which waited for: 0 -> 0; matrix products, arithmetic and copies ran while one was open for 0% -> 0% of each run, Pallas kernels for 35% -> 34%
where the time goes in v23:
time: 32.1 us; the launch traced here: 31.8 us
  Pallas kernels  13.5 us (42%)
  blocking collectives  10.4 us (32%)
  starting transfers between devices  7.71 us (24%)
    all_to_all x1, blocking collectives, body(): lax.all_to_all(scores.reshape(targets, local_queries * passages), ('shard...  10.4 us
    ppermute x4, starting transfers between devices, body(): received = lax.ppermute(held, ('shard', 'sub'), pairs)  7.26 us
    pallas_call x2, Pallas kernels, decode_step(): pl.pallas_call(functools.partial(decode_kernel, step, passages), out_shap...  5.89 us
    pallas_call x2, Pallas kernels, score_half(): pl.pallas_call(functools.partial(score_kernel, bit, token_count, local_qu...  4.15 us
    pallas_call x1, Pallas kernels, prepare(): pl.pallas_call(prepare_kernel, out_shape=(pltpu.VMEM(own.shape, jnp.bfloa...  2.79 us
    pallas_call x1, Pallas kernels, pick(): pl.pallas_call(functools.partial(pick_kernel, passages), out_shape=jax.Sh...  0.66 us
  transfers between devices with their start and end apart: 5, of which 0 were waited for; matrix products, arithmetic and copies ran while one was open for 0% of the time, Pallas kernels for 34%

profile of v23, /device:TPU:0, one launch (start us, length us, event | category | flops | bytes accessed | tf_op | source)
XLA Modules:
  0.0 31.8 jit_solution(2797963787937484408)
XLA Ops:
  0.0 0.0 copy-start.1
  0.0 0.5 %collective-permute-start.2 = (bf16[8192,128]{1,0:T(8,128)(2,1)}, bf16[8192,128]{1,0:T(8,128)(2,1)S(1)}, u32[]{:S(2)}, u32[]{:S(2)}) collective-permute-start(bf16[8192,128]{1,0:T(8,128)(2,1)} %own_hbm.1), channel_id=1, source_target_pairs={{0,1},{1,0},{2,3},{3,2},{4,5},{5,4},{6,7},{7,6},{8,9},{9,8},{10,11... | collective-permute-start | bytes 6291464 | tf_op jit(solution)/shard_map/ppermute | solution.py:439
  0.5 3.6 %collective-permute-start = (bf16[1,1,32,128]{3,2,1,0:T(8,128)(2,1)}, bf16[1,1,32,128]{3,2,1,0:T(8,128)(2,1)S(1)}, u32[]{:S(2)}, u32[]{:S(2)}) collective-permute-start(bf16[1,1,32,128]{3,2,1,0:T(8,128)(2,1)} %bitcast.29), channel_id=1, source_target_pairs={{0,8},{1,9},{2,10},{3,11},{4,12},{5,13},{6,14},{7,15},{8,0},{9,1},... | collective-permute-start | bytes 24584 | tf_op jit(solution)/shard_map/ppermute | solution.py:446
  4.1 2.8 %prepare.1 = (bf16[8192,128]{1,0:T(8,128)(2,1)S(1)}, f32[9216,128]{1,0:T(8,128)S(1)}, s32[64,128]{1,0:T(8,128)S(1)}, s32[640]{0:T(1024)S(1)}, s32[640]{0:T(1024)S(1)}, /*index=5*/bf16[16,128]{1,0:T(8,128)(2,1)S(1)}) custom-call(s32[1]{0:T(128)} %bitcast.me_ref, s32[64]{0:T(128)} %lengths_hbm.1, s32[64,128]{1,0:T(8,128)} %codes_hbm.1, ...), custom_call_target="tpu_custom_call" | custom-call | flops 10000000 | bytes 8000000 | tf_op jit(solution)/shard_map/prepare/pallas_call | solution.py:151
  6.9 0.0 collective-permute-done
  6.9 0.0 copy-done.1
  7.0 1.7 %collective-permute-start.1 = (bf16[2,1,32,128]{3,2,1,0:T(8,128)(2,1)S(1)}, bf16[2,1,32,128]{3,2,1,0:T(8,128)(2,1)S(1)}, u32[]{:S(2)}, u32[]{:S(2)}) collective-permute-start(bf16[2,1,32,128]{3,2,1,0:T(8,128)(2,1)S(1)} %maximum_bitcast_fusion.refs_6_), channel_id=1, source_target_pairs={{0,4},{1,5},{2,6},{3,7},{4,0},{5,1},{6,2},{7,3},{8,12},{9,13},{10,... | collective-permute-start | bytes 49160 | tf_op jit(solution)/shard_map/ppermute | solution.py:446
  8.7 0.0 collective-permute-done.2.refs_2_
  8.7 2.9 %decode.2 = (f32[16384,128]{1,0:T(8,128)S(1)}, bf16[9216,128]{1,0:T(8,128)(2,1)S(1)}, f32[256,128]{1,0:T(8,128)S(1)}, bf16[16,128]{1,0:T(8,128)(2,1)S(1)}) custom-call(s32[1]{0:T(128)} %bitcast.5.refs_0_, bf16[8192,128]{1,0:T(8,128)(2,1)S(1)} %get-tuple-element.20.refs_1_, bf16[8192,128]{1,0:T(8,128)(2,1)S(1)} %collective-permute-done.2.refs_2_, ...), custom_call_target="tpu_custom_call" | custom-call | flops 10000000 | bytes 10000000 | tf_op jit(solution)/shard_map/decode/pallas_call | solution.py:261
  11.6 0.0 collective-permute-done.1
  11.6 1.6 %collective-permute-start.3 = (bf16[4,1,32,128]{3,2,1,0:T(8,128)(2,1)S(1)}, bf16[4,1,32,128]{3,2,1,0:T(8,128)(2,1)S(1)}, u32[]{:S(2)}, u32[]{:S(2)}) collective-permute-start(bf16[4,1,32,128]{3,2,1,0:T(8,128)(2,1)S(1)} %bitcast.20), channel_id=1, source_target_pairs={{0,2},{1,3},{2,0},{3,1},{4,6},{5,7},{6,4},{7,5},{8,10},{9,11},{10,... | collective-permute-start | bytes 98312 | tf_op jit(solution)/shard_map/ppermute | solution.py:446
  13.2 3.0 %decode.3 = (bf16[9216,128]{1,0:T(8,128)(2,1)S(1)}, f32[256,128]{1,0:T(8,128)S(1)}, bf16[16,128]{1,0:T(8,128)(2,1)S(1)}) custom-call(s32[64,128]{1,0:T(8,128)S(1)} %get-tuple-element.21.refs_3_.refs_0_, s32[640]{0:T(1024)S(1)} %get-tuple-element.22.refs_4_.refs_1_, ...), custom_call_target="tpu_custom_call", output_to_operand_aliasing={{0}: (5, {}), {1}: (6, {})} | custom-call | flops 10000000 | bytes 10000000 | tf_op jit(solution)/shard_map/decode/pallas_call | solution.py:261
  16.2 0.0 collective-permute-done.3
  16.3 0.3 collective-permute-start.4
  16.6 0.0 copy-start
  16.6 2.1 %score.2.before_ref = f32[16,64]{1,0:T(8,128)S(1)} custom-call(s32[1]{0:T(128)} %bitcast.me_ref, s32[640]{0:T(1024)S(1)} %get-tuple-element.18.starts, bf16[256,128]{1,0:T(8,128)(2,1)S(1)} %bitcast.24, bf16[9216,128]{1,0:T(8,128)(2,1)S(1)} %get-tuple-element.29.embedded, f32[256,128]{1,0:T(8,128)S(1)} %get-tuple-element.30.before_ref), custom_call_target="tpu_custom_call" | custom-call | flops 10000000 | bytes 8000000 | tf_op jit(solution)/shard_map/score/pallas_call | solution.py:379
  18.7 0.0 collective-permute-done.4
  18.7 2.1 %score.3 = f32[16,64]{1,0:T(8,128)S(1)} custom-call(s32[1]{0:T(128)} %bitcast.me_ref, s32[640]{0:T(1024)S(1)} %get-tuple-element.18.starts, bf16[256,128]{1,0:T(8,128)(2,1)S(1)} %bitcast.25, bf16[9216,128]{1,0:T(8,128)(2,1)S(1)} %get-tuple-element.29.embedded, f32[16,64]{1,0:T(8,128)S(1)} %score.2.before_ref), custom_call_target="tpu_custom_call" | custom-call | flops 10000000 | bytes 8000000 | tf_op jit(solution)/shard_map/score/pallas_call | solution.py:379
  20.8 10.4 %all_to_all.11 = f32[16,1,64]{2,1,0:T(1,128)S(1)} all-to-all(f32[16,1,64]{2,1,0:T(1,128)S(1)} %bitcast.26), channel_id=1, replica_groups=mesh['groups'=2,'shard'=8,'sub'=2] {'shard','sub'}, dimensions={0} | all-to-all | bytes 8192 | tf_op jit(solution)/shard_map/all_to_all | solution.py:464
  31.2 0.0 copy-done
  31.2 0.7 %pick.1 = f32[1,62]{1,0:T(1,128)} custom-call(s32[1,62]{1,0:T(1,128)S(1)} %copy-done, f32[16,64]{1,0:T(8,128)S(1)} %bitcast.27), custom_call_target="tpu_custom_call" | custom-call | tf_op jit(solution)/shard_map/pick/pallas_call | solution.py:420
  (9 shorter events, 0.1 us)
Async XLA Ops:
  0.0 6.9 %copy-start.1 = (bf16[1,32,128]{2,1,0:T(8,128)(2,1)S(1)}, bf16[1,32,128]{2,1,0:T(8,128)(2,1)}, u32[]{:S(2)}) copy-start(bf16[1,32,128]{2,1,0:T(8,128)(2,1)} %param.6) | copy-start | bytes 24580
  0.0 8.7 %collective-permute-start.2 = (bf16[8192,128]{1,0:T(8,128)(2,1)}, bf16[8192,128]{1,0:T(8,128)(2,1)S(1)}, u32[]{:S(2)}, u32[]{:S(2)}) collective-permute-start(bf16[8192,128]{1,0:T(8,128)(2,1)} %own_hbm.1), channel_id=1, source_target_pairs={{0,1},{1,0},{2,3},{3,2},{4,5},{5,4},{6,7},{7,6},{8,9},{9,8},{10,11... | collective-permute-start | bytes 6291464 | tf_op jit(solution)/shard_map/ppermute | solution.py:439
  0.5 6.5 %collective-permute-start = (bf16[1,1,32,128]{3,2,1,0:T(8,128)(2,1)}, bf16[1,1,32,128]{3,2,1,0:T(8,128)(2,1)S(1)}, u32[]{:S(2)}, u32[]{:S(2)}) collective-permute-start(bf16[1,1,32,128]{3,2,1,0:T(8,128)(2,1)} %bitcast.29), channel_id=1, source_target_pairs={{0,8},{1,9},{2,10},{3,11},{4,12},{5,13},{6,14},{7,15},{8,0},{9,1},... | collective-permute-start | bytes 24584 | tf_op jit(solution)/shard_map/ppermute | solution.py:446
  7.0 4.6 %collective-permute-start.1 = (bf16[2,1,32,128]{3,2,1,0:T(8,128)(2,1)S(1)}, bf16[2,1,32,128]{3,2,1,0:T(8,128)(2,1)S(1)}, u32[]{:S(2)}, u32[]{:S(2)}) collective-permute-start(bf16[2,1,32,128]{3,2,1,0:T(8,128)(2,1)S(1)} %maximum_bitcast_fusion.refs_6_), channel_id=1, source_target_pairs={{0,4},{1,5},{2,6},{3,7},{4,0},{5,1},{6,2},{7,3},{8,12},{9,13},{10,... | collective-permute-start | bytes 49160 | tf_op jit(solution)/shard_map/ppermute | solution.py:446
  11.6 4.7 %collective-permute-start.3 = (bf16[4,1,32,128]{3,2,1,0:T(8,128)(2,1)S(1)}, bf16[4,1,32,128]{3,2,1,0:T(8,128)(2,1)S(1)}, u32[]{:S(2)}, u32[]{:S(2)}) collective-permute-start(bf16[4,1,32,128]{3,2,1,0:T(8,128)(2,1)S(1)} %bitcast.20), channel_id=1, source_target_pairs={{0,2},{1,3},{2,0},{3,1},{4,6},{5,7},{6,4},{7,5},{8,10},{9,11},{10,... | collective-permute-start | bytes 98312 | tf_op jit(solution)/shard_map/ppermute | solution.py:446
  16.3 2.4 %collective-permute-start.4 = (bf16[8,1,32,128]{3,2,0,1:T(8,128)(2,1)S(1)}, bf16[8,1,32,128]{3,2,0,1:T(8,128)(2,1)S(1)}, u32[]{:S(2)}, u32[]{:S(2)}) collective-permute-start(bf16[8,1,32,128]{3,2,0,1:T(8,128)(2,1)S(1)} %bitcast.23), channel_id=1, source_target_pairs={{0,1},{1,0},{2,3},{3,2},{4,5},{5,4},{6,7},{7,6},{8,9},{9,8},{10,11... | collective-permute-start | bytes 196616 | tf_op jit(solution)/shard_map/ppermute | solution.py:446
  16.6 14.6 %copy-start = (s32[1,62]{1,0:T(1,128)S(1)}, s32[1,62]{1,0:T(1,128)}, u32[]{:S(2)}) copy-start(s32[1,62]{1,0:T(1,128)} %candidates_ref.1) | copy-start | bytes 748

commit v24 on v23

--- a/solution.py
+++ b/solution.py
@@ -12,6 +12,7 @@
 SCORE_GROUP = 64
 SCORE_PARTS = 2
 SCORE_RUNS = (4, 2, 1)
+WIDE_BITS = 2
 STEPS = 2
 PIECES = 4
 QUERY_BLOCK = 512
@@ -279,7 +280,6 @@
 
 
 def score_kernel(
-    bit,
     token_count,
     local_queries,
     slots,
@@ -287,7 +287,6 @@
     starts,
     queries_ref,
     embedded,
-    before_ref,
     out_ref,
     at_ref,
     turned,
@@ -300,7 +299,7 @@
     query_tokens = queries_ref.shape[0]
     block = min(QUERY_BLOCK, query_tokens)
     blocks = query_tokens // block
-    window = 2 * block // token_count
+    window = block // token_count
     window_targets = window // local_queries
     near_me = me_ref[0] & (window_targets - 1)
     far_me = quotient(me_ref[0], window_targets)
@@ -308,9 +307,7 @@
     owner_target = quotient(owner, local_queries)
     owner_row = (owner_target ^ near_me) * local_queries + owner - owner_target * local_queries
     query_of = quotient(lax.broadcasted_iota(jnp.int32, (window, block), 1), token_count)
-    target_of = quotient(query_of, local_queries)
-    row_of = query_of + (target_of + bit) * local_queries
-    summing = jnp.concatenate([(owner_row == row_of).astype(jnp.bfloat16)] * 3, axis=1)
+    summing = jnp.concatenate([(owner_row == query_of).astype(jnp.bfloat16)] * 3, axis=1)
     count = SCORE_GROUP // SCORE_PARTS
     size = count * CHUNK
 
@@ -363,23 +360,21 @@
             (((1,), (1,)), ((), ())),
             preferred_element_type=jnp.float32,
         )
-        if bit:
-            sums = sums + before_ref[to, :]
         out_ref[to, :] = sums
         return carry
 
     lax.fori_loop(0, blocks, score_block, 0)
 
 
-def score_half(bit, me, starts, query_rows, embedded, before, passages, slots, shape):
+def score_all(me, starts, query_rows, embedded, passages, slots, shape):
     token_count, local_queries = shape
     query_tokens, width = query_rows.shape
     block = min(QUERY_BLOCK, query_tokens)
     blocks = query_tokens // block
     return pl.pallas_call(
-        functools.partial(score_kernel, bit, token_count, local_queries, slots),
-        out_shape=pltpu.VMEM((2 * query_tokens // token_count, passages), jnp.float32),
-        in_specs=[SMEM] + [VMEM] * 4,
+        functools.partial(score_kernel, token_count, local_queries, slots),
+        out_shape=pltpu.VMEM((query_tokens // token_count, passages), jnp.float32),
+        in_specs=[SMEM] + [VMEM] * 3,
         out_specs=VMEM,
         scratch_shapes=[
             pltpu.SMEM(starts.shape, jnp.int32),
@@ -395,7 +390,6 @@
         pinned(starts, pltpu.VMEM),
         pinned(query_rows, pltpu.VMEM),
         pinned(embedded, pltpu.VMEM),
-        pinned(before, pltpu.VMEM),
     )
 
 
@@ -441,9 +435,12 @@
     held = queries.reshape(1, 1, local_queries * token_count, width)
     bits = targets.bit_length() - 1
     carried = None
-    for turn, first in enumerate(range(bits - 1, -1, -1)):
-        pairs = [(device, device ^ (1 << first)) for device in range(targets)]
-        received = lax.ppermute(held, ("shard", "sub"), pairs)
+    rounds = [(bits - WIDE_BITS, WIDE_BITS)] + [(k, 1) for k in range(bits - WIDE_BITS - 1, -1, -1)]
+    for turn, (first, taken) in enumerate(rounds):
+        received = []
+        for value in range(1, 1 << taken):
+            pairs = [(device, device ^ (value << first)) for device in range(targets)]
+            received.append(lax.ppermute(held, ("shard", "sub"), pairs))
         if turn == 0:
             ready = prepare(me, lengths, token_codes, centroids, flat)
             own, near, codes, starts, cleans, nothing = ready
@@ -452,15 +449,12 @@
             table, carried, nothing = decode_step(
                 turn - 1, half, own, other, codes, cleans, near, table, carried, held
             )
-        if first > 0:
-            received = received + nothing[0:1, :]
-            held = jnp.concatenate([held, received], axis=1)
-            held = held.reshape((-1, 1) + held.shape[2:])
+        received = [block + nothing[0:1, :] for block in received]
+        held = jnp.concatenate([held] + received, axis=1)
+        held = held.reshape((-1, 1) + held.shape[2:])
     shape = (token_count, local_queries)
-    scores = carried[1]
-    for bit, half_rows in enumerate((held, received)):
-        rows = half_rows.reshape(targets // 2 * local_queries * token_count, width)
-        scores = score_half(bit, me, starts, rows, carried[0], scores, passages, slots, shape)
+    rows = held.reshape(targets * local_queries * token_count, width)
+    scores = score_all(me, starts, rows, carried[0], passages, slots, shape)
     returned = lax.all_to_all(
         scores.reshape(targets, local_queries * passages),
         ("shard", "sub"),

time: 32.1 us -> 32.6 us (1.016)
  waiting for transfers between devices: 0.01 us -> 2.72 us
  Pallas kernels: 13.5 us -> 12.6 us
  blocking collectives: 10.4 us -> 9.57 us
  starting transfers between devices: 7.71 us -> 7.31 us
    ppermute x4 -> x5, waiting for transfers between devices: 0.01 us -> 2.72 us  [body(): received.append(lax.ppermute(held, ('shard', 'sub'), pairs))]
    pallas_call x2 -> x1, Pallas kernels: 4.15 us -> 2.7 us  [score_all(): pl.pallas_call(functools.partial(score_kernel, token_count, local_queries...]
    all_to_all x1, blocking collectives: 10.4 us -> 9.57 us  [body(): lax.all_to_all(scores.reshape(targets, local_queries * passages), ('shard...]
    pallas_call x2, Pallas kernels: 5.89 us -> 6.35 us  [decode_step(): pl.pallas_call(functools.partial(decode_kernel, step, passages), out_shap...]
    ppermute x4 -> x5, starting transfers between devices: 7.26 us -> 6.85 us  [body(): received.append(lax.ppermute(held, ('shard', 'sub'), pairs))]
  transfers between devices with their start and end apart: 5 -> 6, of which waited for: 0 -> 1; matrix products, arithmetic and copies ran while one was open for 0% -> 0% of each run, Pallas kernels for 34% -> 29%
where the time goes in v24:
time: 32.6 us; the launch traced here: 32.4 us
  Pallas kernels  12.6 us (39%)
  blocking collectives  9.57 us (29%)
  starting transfers between devices  7.31 us (22%)
  waiting for transfers between devices  2.72 us (8%)
    all_to_all x1, blocking collectives, body(): lax.all_to_all(scores.reshape(targets, local_queries * passages), ('shard...  9.57 us
    ppermute x5, starting transfers between devices, body(): received.append(lax.ppermute(held, ('shard', 'sub'), pairs))  6.85 us
    pallas_call x2, Pallas kernels, decode_step(): pl.pallas_call(functools.partial(decode_kernel, step, passages), out_shap...  6.35 us
    pallas_call x1, Pallas kernels, prepare(): pl.pallas_call(prepare_kernel, out_shape=(pltpu.VMEM(own.shape, jnp.bfloa...  2.91 us
    ppermute x5, waiting for transfers between devices, body(): received.append(lax.ppermute(held, ('shard', 'sub'), pairs))  2.72 us
    pallas_call x1, Pallas kernels, score_all(): pl.pallas_call(functools.partial(score_kernel, token_count, local_queries...  2.7 us
    pallas_call x1, Pallas kernels, pick(): pl.pallas_call(functools.partial(pick_kernel, passages), out_shape=jax.Sh...  0.66 us
  transfers between devices with their start and end apart: 6, of which 1 were waited for; matrix products, arithmetic and copies ran while one was open for 0% of the time, Pallas kernels for 29%

profile of v24, /device:TPU:0, one launch (start us, length us, event | category | flops | bytes accessed | tf_op | source)
XLA Modules:
  0.0 32.4 jit_solution(18201142039937816336)
XLA Ops:
  0.0 0.0 copy-start.1
  0.0 0.5 %collective-permute-start.4 = (bf16[8192,128]{1,0:T(8,128)(2,1)}, bf16[8192,128]{1,0:T(8,128)(2,1)S(1)}, u32[]{:S(2)}, u32[]{:S(2)}) collective-permute-start(bf16[8192,128]{1,0:T(8,128)(2,1)} %own_hbm.1), channel_id=1, source_target_pairs={{0,1},{1,0},{2,3},{3,2},{4,5},{5,4},{6,7},{7,6},{8,9},{9,8},{10,11... | collective-permute-start | bytes 6291464 | tf_op jit(solution)/shard_map/ppermute | solution.py:433
  0.5 2.6 %collective-permute-start = (bf16[1,1,32,128]{3,2,1,0:T(8,128)(2,1)}, bf16[1,1,32,128]{3,2,1,0:T(8,128)(2,1)S(1)}, u32[]{:S(2)}, u32[]{:S(2)}) collective-permute-start(bf16[1,1,32,128]{3,2,1,0:T(8,128)(2,1)} %bitcast.25), channel_id=1, source_target_pairs={{0,4},{1,5},{2,6},{3,7},{4,0},{5,1},{6,2},{7,3},{8,12},{9,13},{10,... | collective-permute-start | bytes 24584 | tf_op jit(solution)/shard_map/ppermute | solution.py:443
  3.1 2.6 %collective-permute-start.1 = (bf16[1,1,32,128]{3,2,1,0:T(8,128)(2,1)}, bf16[1,1,32,128]{3,2,1,0:T(8,128)(2,1)S(1)}, u32[]{:S(2)}, u32[]{:S(2)}) collective-permute-start(bf16[1,1,32,128]{3,2,1,0:T(8,128)(2,1)} %bitcast.26), channel_id=1, source_target_pairs={{0,8},{1,9},{2,10},{3,11},{4,12},{5,13},{6,14},{7,15},{8,0},{9,1},... | collective-permute-start | bytes 24584 | tf_op jit(solution)/shard_map/ppermute | solution.py:443
  5.7 0.0 collective-permute-start.2
  5.7 2.9 %prepare.1 = (bf16[8192,128]{1,0:T(8,128)(2,1)S(1)}, f32[9216,128]{1,0:T(8,128)S(1)}, s32[64,128]{1,0:T(8,128)S(1)}, s32[640]{0:T(1024)S(1)}, s32[640]{0:T(1024)S(1)}, /*index=5*/bf16[16,128]{1,0:T(8,128)(2,1)S(1)}) custom-call(s32[1]{0:T(128)} %bitcast.me_ref, s32[64]{0:T(128)} %lengths_hbm.1, s32[64,128]{1,0:T(8,128)} %codes_hbm.1, ...), custom_call_target="tpu_custom_call" | custom-call | flops 10000000 | bytes 8000000 | tf_op jit(solution)/shard_map/prepare/pallas_call | solution.py:152
  8.6 0.0 collective-permute-done
  8.6 0.0 collective-permute-done.1
  8.6 2.7 %collective-permute-done.2 = bf16[1,1,32,128]{3,2,1,0:T(8,128)(2,1)S(1)} collective-permute-done((bf16[1,1,32,128]{3,2,1,0:T(8,128)(2,1)}, bf16[1,1,32,128]{3,2,1,0:T(8,128)(2,1)S(1)}, u32[]{:S(2)}, u32[]{:S(2)}) %collective-permute-start.2) | collective-permute-done | bytes 8224 | tf_op jit(solution)/shard_map/ppermute | solution.py:443
  11.3 0.0 copy-done.1
  11.4 1.6 %collective-permute-start.3 = (bf16[4,1,32,128]{3,2,1,0:T(8,128)(2,1)S(1)}, bf16[4,1,32,128]{3,2,1,0:T(8,128)(2,1)S(1)}, u32[]{:S(2)}, u32[]{:S(2)}) collective-permute-start(bf16[4,1,32,128]{3,2,1,0:T(8,128)(2,1)S(1)} %maximum_bitcast_fusion.refs_6_), channel_id=1, source_target_pairs={{0,2},{1,3},{2,0},{3,1},{4,6},{5,7},{6,4},{7,5},{8,10},{9,11},{10,... | collective-permute-start | bytes 98312 | tf_op jit(solution)/shard_map/ppermute | solution.py:443
  12.9 0.0 collective-permute-done.4.refs_2_
  12.9 2.9 %decode.2 = (f32[16384,128]{1,0:T(8,128)S(1)}, bf16[9216,128]{1,0:T(8,128)(2,1)S(1)}, f32[256,128]{1,0:T(8,128)S(1)}, bf16[16,128]{1,0:T(8,128)(2,1)S(1)}) custom-call(s32[1]{0:T(128)} %bitcast.5.refs_0_, bf16[8192,128]{1,0:T(8,128)(2,1)S(1)} %get-tuple-element.19.refs_1_, bf16[8192,128]{1,0:T(8,128)(2,1)S(1)} %collective-permute-done.4.refs_2_, ...), custom_call_target="tpu_custom_call" | custom-call | flops 10000000 | bytes 10000000 | tf_op jit(solution)/shard_map/decode/pallas_call | solution.py:262
  15.8 0.0 collective-permute-done.3
  15.9 0.1 collective-permute-start.5
  15.9 3.5 %decode.3 = (bf16[9216,128]{1,0:T(8,128)(2,1)S(1)}, f32[256,128]{1,0:T(8,128)S(1)}, bf16[16,128]{1,0:T(8,128)(2,1)S(1)}) custom-call(s32[64,128]{1,0:T(8,128)S(1)} %get-tuple-element.20.refs_3_.refs_0_, s32[640]{0:T(1024)S(1)} %get-tuple-element.21.refs_4_.refs_1_, ...), custom_call_target="tpu_custom_call", output_to_operand_aliasing={{0}: (5, {}), {1}: (6, {})} | custom-call | flops 10000000 | bytes 10000000 | tf_op jit(solution)/shard_map/decode/pallas_call | solution.py:262
  19.4 0.0 copy-start
  19.4 0.0 collective-permute-done.5
  19.5 2.7 %score.1 = f32[16,64]{1,0:T(8,128)S(1)} custom-call(s32[1]{0:T(128)} %bitcast.me_ref, s32[640]{0:T(1024)S(1)} %get-tuple-element.17.starts, bf16[512,128]{1,0:T(8,128)(2,1)S(1)} %bitcast.21, bf16[9216,128]{1,0:T(8,128)(2,1)S(1)} %get-tuple-element.28.embedded), custom_call_target="tpu_custom_call" | custom-call | flops 10000000 | bytes 8000000 | tf_op jit(solution)/shard_map/score/pallas_call | solution.py:374
  22.2 9.6 %all_to_all.11 = f32[16,1,64]{2,1,0:T(1,128)S(1)} all-to-all(f32[16,1,64]{2,1,0:T(1,128)S(1)} %bitcast.22), channel_id=1, replica_groups=mesh['groups'=2,'shard'=8,'sub'=2] {'shard','sub'}, dimensions={0} | all-to-all | bytes 8192 | tf_op jit(solution)/shard_map/all_to_all | solution.py:458
  31.8 0.0 copy-done
  31.8 0.7 %pick.1 = f32[1,62]{1,0:T(1,128)} custom-call(s32[1,62]{1,0:T(1,128)S(1)} %copy-done, f32[16,64]{1,0:T(8,128)S(1)} %bitcast.23), custom_call_target="tpu_custom_call" | custom-call | tf_op jit(solution)/shard_map/pick/pallas_call | solution.py:414
  (9 shorter events, 0.1 us)
Async XLA Ops:
  0.0 11.3 %copy-start.1 = (bf16[1,32,128]{2,1,0:T(8,128)(2,1)S(1)}, bf16[1,32,128]{2,1,0:T(8,128)(2,1)}, u32[]{:S(2)}) copy-start(bf16[1,32,128]{2,1,0:T(8,128)(2,1)} %param.6) | copy-start | bytes 24580
  0.0 12.9 %collective-permute-start.4 = (bf16[8192,128]{1,0:T(8,128)(2,1)}, bf16[8192,128]{1,0:T(8,128)(2,1)S(1)}, u32[]{:S(2)}, u32[]{:S(2)}) collective-permute-start(bf16[8192,128]{1,0:T(8,128)(2,1)} %own_hbm.1), channel_id=1, source_target_pairs={{0,1},{1,0},{2,3},{3,2},{4,5},{5,4},{6,7},{7,6},{8,9},{9,8},{10,11... | collective-permute-start | bytes 6291464 | tf_op jit(solution)/shard_map/ppermute | solution.py:433
  0.5 8.2 %collective-permute-start = (bf16[1,1,32,128]{3,2,1,0:T(8,128)(2,1)}, bf16[1,1,32,128]{3,2,1,0:T(8,128)(2,1)S(1)}, u32[]{:S(2)}, u32[]{:S(2)}) collective-permute-start(bf16[1,1,32,128]{3,2,1,0:T(8,128)(2,1)} %bitcast.25), channel_id=1, source_target_pairs={{0,4},{1,5},{2,6},{3,7},{4,0},{5,1},{6,2},{7,3},{8,12},{9,13},{10,... | collective-permute-start | bytes 24584 | tf_op jit(solution)/shard_map/ppermute | solution.py:443
  3.1 5.5 %collective-permute-start.1 = (bf16[1,1,32,128]{3,2,1,0:T(8,128)(2,1)}, bf16[1,1,32,128]{3,2,1,0:T(8,128)(2,1)S(1)}, u32[]{:S(2)}, u32[]{:S(2)}) collective-permute-start(bf16[1,1,32,128]{3,2,1,0:T(8,128)(2,1)} %bitcast.26), channel_id=1, source_target_pairs={{0,8},{1,9},{2,10},{3,11},{4,12},{5,13},{6,14},{7,15},{8,0},{9,1},... | collective-permute-start | bytes 24584 | tf_op jit(solution)/shard_map/ppermute | solution.py:443
  5.7 5.7 %collective-permute-start.2 = (bf16[1,1,32,128]{3,2,1,0:T(8,128)(2,1)}, bf16[1,1,32,128]{3,2,1,0:T(8,128)(2,1)S(1)}, u32[]{:S(2)}, u32[]{:S(2)}) collective-permute-start(bf16[1,1,32,128]{3,2,1,0:T(8,128)(2,1)} %bitcast.27), channel_id=1, source_target_pairs={{0,12},{1,13},{2,14},{3,15},{4,8},{5,9},{6,10},{7,11},{8,4},{9,5},... | collective-permute-start | bytes 24584 | tf_op jit(solution)/shard_map/ppermute | solution.py:443
  11.4 4.5 %collective-permute-start.3 = (bf16[4,1,32,128]{3,2,1,0:T(8,128)(2,1)S(1)}, bf16[4,1,32,128]{3,2,1,0:T(8,128)(2,1)S(1)}, u32[]{:S(2)}, u32[]{:S(2)}) collective-permute-start(bf16[4,1,32,128]{3,2,1,0:T(8,128)(2,1)S(1)} %maximum_bitcast_fusion.refs_6_), channel_id=1, source_target_pairs={{0,2},{1,3},{2,0},{3,1},{4,6},{5,7},{6,4},{7,5},{8,10},{9,11},{10,... | collective-permute-start | bytes 98312 | tf_op jit(solution)/shard_map/ppermute | solution.py:443
  15.9 3.6 %collective-permute-start.5 = (bf16[8,1,32,128]{3,2,1,0:T(8,128)(2,1)S(1)}, bf16[8,1,32,128]{3,2,1,0:T(8,128)(2,1)S(1)}, u32[]{:S(2)}, u32[]{:S(2)}) collective-permute-start(bf16[8,1,32,128]{3,2,1,0:T(8,128)(2,1)S(1)} %bitcast.18), channel_id=1, source_target_pairs={{0,1},{1,0},{2,3},{3,2},{4,5},{5,4},{6,7},{7,6},{8,9},{9,8},{10,11... | collective-permute-start | bytes 196616 | tf_op jit(solution)/shard_map/ppermute | solution.py:443
  19.4 12.4 %copy-start = (s32[1,62]{1,0:T(1,128)S(1)}, s32[1,62]{1,0:T(1,128)}, u32[]{:S(2)}) copy-start(s32[1,62]{1,0:T(1,128)} %candidates_ref.1) | copy-start | bytes 748

commit v25 on v23

--- a/solution.py
+++ b/solution.py
@@ -11,7 +11,7 @@
 GROUP = 16
 SCORE_GROUP = 64
 SCORE_PARTS = 2
-SCORE_RUNS = (4, 2, 1)
+SCORE_RUNS = (8, 4, 2, 1)
 STEPS = 2
 PIECES = 4
 QUERY_BLOCK = 512

time: 32.1 us -> 32 us (level)
  Pallas kernels: 13.5 us -> 14.9 us
  blocking collectives: 10.4 us -> 9.33 us
  starting transfers between devices: 7.71 us -> 7.37 us
    all_to_all x1, blocking collectives: 10.4 us -> 9.33 us  [body(): lax.all_to_all(scores.reshape(targets, local_queries * passages), ('shard...]
    pallas_call x2, Pallas kernels: 5.89 us -> 6.57 us  [decode_step(): pl.pallas_call(functools.partial(decode_kernel, step, passages), out_shap...]
    pallas_call x2, Pallas kernels: 4.15 us -> 4.67 us  [score_half(): pl.pallas_call(functools.partial(score_kernel, bit, token_count, local_qu...]
    ppermute x4, starting transfers between devices: 7.26 us -> 6.92 us  [body(): received = lax.ppermute(held, ('shard', 'sub'), pairs)]
  transfers between devices with their start and end apart: 5 -> 5, of which waited for: 0 -> 0; matrix products, arithmetic and copies ran while one was open for 0% -> 0% of each run, Pallas kernels for 34% -> 37%
where the time goes in v25:
time: 32 us; the launch traced here: 31.8 us
  Pallas kernels  14.9 us (47%)
  blocking collectives  9.33 us (29%)
  starting transfers between devices  7.37 us (23%)
    all_to_all x1, blocking collectives, body(): lax.all_to_all(scores.reshape(targets, local_queries * passages), ('shard...  9.33 us
    ppermute x4, starting transfers between devices, body(): received = lax.ppermute(held, ('shard', 'sub'), pairs)  6.92 us
    pallas_call x2, Pallas kernels, decode_step(): pl.pallas_call(functools.partial(decode_kernel, step, passages), out_shap...  6.57 us
    pallas_call x2, Pallas kernels, score_half(): pl.pallas_call(functools.partial(score_kernel, bit, token_count, local_qu...  4.67 us
    pallas_call x1, Pallas kernels, prepare(): pl.pallas_call(prepare_kernel, out_shape=(pltpu.VMEM(own.shape, jnp.bfloa...  2.97 us
    pallas_call x1, Pallas kernels, pick(): pl.pallas_call(functools.partial(pick_kernel, passages), out_shape=jax.Sh...  0.66 us
  transfers between devices with their start and end apart: 5, of which 0 were waited for; matrix products, arithmetic and copies ran while one was open for 0% of the time, Pallas kernels for 37%

profile of v25, /device:TPU:0, one launch (start us, length us, event | category | flops | bytes accessed | tf_op | source)
XLA Modules:
  0.0 31.8 jit_solution(12811931500633699163)
XLA Ops:
  0.0 0.0 copy-start.1
  0.0 0.5 %collective-permute-start.2 = (bf16[8192,128]{1,0:T(8,128)(2,1)}, bf16[8192,128]{1,0:T(8,128)(2,1)S(1)}, u32[]{:S(2)}, u32[]{:S(2)}) collective-permute-start(bf16[8192,128]{1,0:T(8,128)(2,1)} %own_hbm.1), channel_id=1, source_target_pairs={{0,1},{1,0},{2,3},{3,2},{4,5},{5,4},{6,7},{7,6},{8,9},{9,8},{10,11... | collective-permute-start | bytes 6291464 | tf_op jit(solution)/shard_map/ppermute | solution.py:439
  0.5 3.6 %collective-permute-start = (bf16[1,1,32,128]{3,2,1,0:T(8,128)(2,1)}, bf16[1,1,32,128]{3,2,1,0:T(8,128)(2,1)S(1)}, u32[]{:S(2)}, u32[]{:S(2)}) collective-permute-start(bf16[1,1,32,128]{3,2,1,0:T(8,128)(2,1)} %bitcast.29), channel_id=1, source_target_pairs={{0,8},{1,9},{2,10},{3,11},{4,12},{5,13},{6,14},{7,15},{8,0},{9,1},... | collective-permute-start | bytes 24584 | tf_op jit(solution)/shard_map/ppermute | solution.py:446
  4.1 3.0 %prepare.1 = (bf16[8192,128]{1,0:T(8,128)(2,1)S(1)}, f32[9216,128]{1,0:T(8,128)S(1)}, s32[64,128]{1,0:T(8,128)S(1)}, s32[640]{0:T(1024)S(1)}, s32[640]{0:T(1024)S(1)}, /*index=5*/bf16[16,128]{1,0:T(8,128)(2,1)S(1)}) custom-call(s32[1]{0:T(128)} %bitcast.me_ref, s32[64]{0:T(128)} %lengths_hbm.1, s32[64,128]{1,0:T(8,128)} %codes_hbm.1, ...), custom_call_target="tpu_custom_call" | custom-call | flops 10000000 | bytes 8000000 | tf_op jit(solution)/shard_map/prepare/pallas_call | solution.py:151
  7.1 0.0 collective-permute-done
  7.1 0.0 copy-done.1
  7.1 1.5 %collective-permute-start.1 = (bf16[2,1,32,128]{3,2,1,0:T(8,128)(2,1)S(1)}, bf16[2,1,32,128]{3,2,1,0:T(8,128)(2,1)S(1)}, u32[]{:S(2)}, u32[]{:S(2)}) collective-permute-start(bf16[2,1,32,128]{3,2,1,0:T(8,128)(2,1)S(1)} %maximum_bitcast_fusion.refs_6_), channel_id=1, source_target_pairs={{0,4},{1,5},{2,6},{3,7},{4,0},{5,1},{6,2},{7,3},{8,12},{9,13},{10,... | collective-permute-start | bytes 49160 | tf_op jit(solution)/shard_map/ppermute | solution.py:446
  8.6 0.0 collective-permute-done.2.refs_2_
  8.6 3.1 %decode.2 = (f32[16384,128]{1,0:T(8,128)S(1)}, bf16[9216,128]{1,0:T(8,128)(2,1)S(1)}, f32[256,128]{1,0:T(8,128)S(1)}, bf16[16,128]{1,0:T(8,128)(2,1)S(1)}) custom-call(s32[1]{0:T(128)} %bitcast.5.refs_0_, bf16[8192,128]{1,0:T(8,128)(2,1)S(1)} %get-tuple-element.20.refs_1_, bf16[8192,128]{1,0:T(8,128)(2,1)S(1)} %collective-permute-done.2.refs_2_, ...), custom_call_target="tpu_custom_call" | custom-call | flops 10000000 | bytes 10000000 | tf_op jit(solution)/shard_map/decode/pallas_call | solution.py:261
  11.7 0.0 collective-permute-done.1
  11.8 1.7 %collective-permute-start.3 = (bf16[4,1,32,128]{3,2,1,0:T(8,128)(2,1)S(1)}, bf16[4,1,32,128]{3,2,1,0:T(8,128)(2,1)S(1)}, u32[]{:S(2)}, u32[]{:S(2)}) collective-permute-start(bf16[4,1,32,128]{3,2,1,0:T(8,128)(2,1)S(1)} %bitcast.20), channel_id=1, source_target_pairs={{0,2},{1,3},{2,0},{3,1},{4,6},{5,7},{6,4},{7,5},{8,10},{9,11},{10,... | collective-permute-start | bytes 98312 | tf_op jit(solution)/shard_map/ppermute | solution.py:446
  13.5 3.5 %decode.3 = (bf16[9216,128]{1,0:T(8,128)(2,1)S(1)}, f32[256,128]{1,0:T(8,128)S(1)}, bf16[16,128]{1,0:T(8,128)(2,1)S(1)}) custom-call(s32[64,128]{1,0:T(8,128)S(1)} %get-tuple-element.21.refs_3_.refs_0_, s32[640]{0:T(1024)S(1)} %get-tuple-element.22.refs_4_.refs_1_, ...), custom_call_target="tpu_custom_call", output_to_operand_aliasing={{0}: (5, {}), {1}: (6, {})} | custom-call | flops 10000000 | bytes 10000000 | tf_op jit(solution)/shard_map/decode/pallas_call | solution.py:261
  17.0 0.0 collective-permute-done.3
  17.0 0.1 collective-permute-start.4
  17.1 0.0 copy-start
  17.1 2.3 %score.2.before_ref = f32[16,64]{1,0:T(8,128)S(1)} custom-call(s32[1]{0:T(128)} %bitcast.me_ref, s32[640]{0:T(1024)S(1)} %get-tuple-element.18.starts, bf16[256,128]{1,0:T(8,128)(2,1)S(1)} %bitcast.24, bf16[9216,128]{1,0:T(8,128)(2,1)S(1)} %get-tuple-element.29.embedded, f32[256,128]{1,0:T(8,128)S(1)} %get-tuple-element.30.before_ref), custom_call_target="tpu_custom_call" | custom-call | flops 10000000 | bytes 8000000 | tf_op jit(solution)/shard_map/score/pallas_call | solution.py:379
  19.5 0.0 collective-permute-done.4
  19.5 2.3 %score.3 = f32[16,64]{1,0:T(8,128)S(1)} custom-call(s32[1]{0:T(128)} %bitcast.me_ref, s32[640]{0:T(1024)S(1)} %get-tuple-element.18.starts, bf16[256,128]{1,0:T(8,128)(2,1)S(1)} %bitcast.25, bf16[9216,128]{1,0:T(8,128)(2,1)S(1)} %get-tuple-element.29.embedded, f32[16,64]{1,0:T(8,128)S(1)} %score.2.before_ref), custom_call_target="tpu_custom_call" | custom-call | flops 10000000 | bytes 8000000 | tf_op jit(solution)/shard_map/score/pallas_call | solution.py:379
  21.8 9.3 %all_to_all.11 = f32[16,1,64]{2,1,0:T(1,128)S(1)} all-to-all(f32[16,1,64]{2,1,0:T(1,128)S(1)} %bitcast.26), channel_id=1, replica_groups=mesh['groups'=2,'shard'=8,'sub'=2] {'shard','sub'}, dimensions={0} | all-to-all | bytes 8192 | tf_op jit(solution)/shard_map/all_to_all | solution.py:464
  31.1 0.0 copy-done
  31.2 0.7 %pick.1 = f32[1,62]{1,0:T(1,128)} custom-call(s32[1,62]{1,0:T(1,128)S(1)} %copy-done, f32[16,64]{1,0:T(8,128)S(1)} %bitcast.27), custom_call_target="tpu_custom_call" | custom-call | tf_op jit(solution)/shard_map/pick/pallas_call | solution.py:420
  (9 shorter events, 0.1 us)
Async XLA Ops:
  0.0 7.1 %copy-start.1 = (bf16[1,32,128]{2,1,0:T(8,128)(2,1)S(1)}, bf16[1,32,128]{2,1,0:T(8,128)(2,1)}, u32[]{:S(2)}) copy-start(bf16[1,32,128]{2,1,0:T(8,128)(2,1)} %param.6) | copy-start | bytes 24580
  0.0 8.6 %collective-permute-start.2 = (bf16[8192,128]{1,0:T(8,128)(2,1)}, bf16[8192,128]{1,0:T(8,128)(2,1)S(1)}, u32[]{:S(2)}, u32[]{:S(2)}) collective-permute-start(bf16[8192,128]{1,0:T(8,128)(2,1)} %own_hbm.1), channel_id=1, source_target_pairs={{0,1},{1,0},{2,3},{3,2},{4,5},{5,4},{6,7},{7,6},{8,9},{9,8},{10,11... | collective-permute-start | bytes 6291464 | tf_op jit(solution)/shard_map/ppermute | solution.py:439
  0.5 6.6 %collective-permute-start = (bf16[1,1,32,128]{3,2,1,0:T(8,128)(2,1)}, bf16[1,1,32,128]{3,2,1,0:T(8,128)(2,1)S(1)}, u32[]{:S(2)}, u32[]{:S(2)}) collective-permute-start(bf16[1,1,32,128]{3,2,1,0:T(8,128)(2,1)} %bitcast.29), channel_id=1, source_target_pairs={{0,8},{1,9},{2,10},{3,11},{4,12},{5,13},{6,14},{7,15},{8,0},{9,1},... | collective-permute-start | bytes 24584 | tf_op jit(solution)/shard_map/ppermute | solution.py:446
  7.1 4.6 %collective-permute-start.1 = (bf16[2,1,32,128]{3,2,1,0:T(8,128)(2,1)S(1)}, bf16[2,1,32,128]{3,2,1,0:T(8,128)(2,1)S(1)}, u32[]{:S(2)}, u32[]{:S(2)}) collective-permute-start(bf16[2,1,32,128]{3,2,1,0:T(8,128)(2,1)S(1)} %maximum_bitcast_fusion.refs_6_), channel_id=1, source_target_pairs={{0,4},{1,5},{2,6},{3,7},{4,0},{5,1},{6,2},{7,3},{8,12},{9,13},{10,... | collective-permute-start | bytes 49160 | tf_op jit(solution)/shard_map/ppermute | solution.py:446
  11.8 5.2 %collective-permute-start.3 = (bf16[4,1,32,128]{3,2,1,0:T(8,128)(2,1)S(1)}, bf16[4,1,32,128]{3,2,1,0:T(8,128)(2,1)S(1)}, u32[]{:S(2)}, u32[]{:S(2)}) collective-permute-start(bf16[4,1,32,128]{3,2,1,0:T(8,128)(2,1)S(1)} %bitcast.20), channel_id=1, source_target_pairs={{0,2},{1,3},{2,0},{3,1},{4,6},{5,7},{6,4},{7,5},{8,10},{9,11},{10,... | collective-permute-start | bytes 98312 | tf_op jit(solution)/shard_map/ppermute | solution.py:446
  17.0 2.4 %collective-permute-start.4 = (bf16[8,1,32,128]{3,2,0,1:T(8,128)(2,1)S(1)}, bf16[8,1,32,128]{3,2,0,1:T(8,128)(2,1)S(1)}, u32[]{:S(2)}, u32[]{:S(2)}) collective-permute-start(bf16[8,1,32,128]{3,2,0,1:T(8,128)(2,1)S(1)} %bitcast.23), channel_id=1, source_target_pairs={{0,1},{1,0},{2,3},{3,2},{4,5},{5,4},{6,7},{7,6},{8,9},{9,8},{10,11... | collective-permute-start | bytes 196616 | tf_op jit(solution)/shard_map/ppermute | solution.py:446
  17.1 14.0 %copy-start = (s32[1,62]{1,0:T(1,128)S(1)}, s32[1,62]{1,0:T(1,128)}, u32[]{:S(2)}) copy-start(s32[1,62]{1,0:T(1,128)} %candidates_ref.1) | copy-start | bytes 748

commit v26 on v23

--- a/solution.py
+++ b/solution.py
@@ -10,7 +10,7 @@
 CHUNK = 16
 GROUP = 16
 SCORE_GROUP = 64
-SCORE_PARTS = 2
+PART = 32
 SCORE_RUNS = (4, 2, 1)
 STEPS = 2
 PIECES = 4
@@ -98,14 +98,12 @@
     chunks = jnp.int32(0)
     for step, (low, high) in enumerate(shares_of(passages)):
         chunks = lax.fori_loop(low, high, listing, chunks, unroll=4)
-        for k in range(GROUP):
+        for k in range(PART):
             starts_ref[chunks + k] = passages * slots
             cleans_ref[chunks + k] = low * slots
-        chunks = quotient(chunks + GROUP - 1, GROUP) * GROUP
+        chunks = quotient(chunks + PART - 1, PART) * PART
         cleans_ref[last - STEPS + step] = quotient(chunks, GROUP)
-    for k in range(SCORE_GROUP):
-        starts_ref[chunks + k] = passages * slots
-    starts_ref[last] = chunks
+        starts_ref[last - STEPS + step] = chunks
     starts_copy = pltpu.make_async_copy(starts_ref, starts, sems.at[4])
     cleans_copy = pltpu.make_async_copy(cleans_ref, cleans, sems.at[5])
     starts_copy.start()
@@ -135,13 +133,13 @@
 
 
 def list_size(passages, slots):
-    most = passages * (slots // CHUNK) + STEPS * GROUP + SCORE_GROUP + STEPS + 1
+    most = passages * (slots // CHUNK) + STEPS * PART + PART + STEPS + 1
     return -(-most // 128) * 128
 
 
 def list_rows(passages, slots):
     rounding = SCORE_GROUP * CHUNK
-    return -(-(passages * slots + STEPS * GROUP * CHUNK) // rounding) * rounding
+    return -(-(passages * slots + STEPS * PART * CHUNK) // rounding) * rounding
 
 
 def prepare(me, lengths, token_codes, own, residuals):
@@ -311,8 +309,7 @@
     target_of = quotient(query_of, local_queries)
     row_of = query_of + (target_of + bit) * local_queries
     summing = jnp.concatenate([(owner_row == row_of).astype(jnp.bfloat16)] * 3, axis=1)
-    count = SCORE_GROUP // SCORE_PARTS
-    size = count * CHUNK
+    size = PART * CHUNK
 
     def score_block(b, carry):
         at = pl.ds(pl.multiple_of(b * block, block), block)
@@ -322,9 +319,9 @@
         def score(first, so_far):
             at = pl.ds(pl.multiple_of(first * size, size), size)
             similar = jnp.dot(embedded[at, :], turned[...], preferred_element_type=jnp.float32)
-            parts = jnp.max(similar.reshape(count, CHUNK // 8, 8, block), axis=1)
-            for k in range(count):
-                start = at_ref[first * count + k]
+            parts = jnp.max(similar.reshape(PART, CHUNK // 8, 8, block), axis=1)
+            for k in range(PART):
+                start = at_ref[first * PART + k]
                 p = quotient(start, slots)
                 so_far = jnp.where(start == p * slots, parts[k], jnp.maximum(so_far, parts[k]))
                 to = pl.multiple_of(p * 8, 8)
@@ -336,19 +333,27 @@
         def arrived():
             starts_copy.wait()
 
-        parts_used = quotient(at_ref[at_ref.shape[0] - 1] + count - 1, count)
-        so_far = jnp.zeros((8, block), jnp.float32)
+        last = at_ref.shape[0] - 1
+        edge = quotient(at_ref[last - STEPS], PART)
+        after = quotient(at_ref[last - STEPS + 1], PART)
+        common = jnp.minimum(edge, after - edge)
+        chains = (jnp.zeros((8, block), jnp.float32),) * 2
         done = jnp.int32(0)
         for run in SCORE_RUNS:
 
-            def score_run(g, so_far, run=run, done=done):
+            def score_run(g, chains, run=run, done=done):
+                first, second = chains
                 for part in range(run):
-                    so_far = score(done + g * run + part, so_far)
-                return so_far
-
-            runs = quotient(parts_used - done, run)
-            so_far = lax.fori_loop(0, runs, score_run, so_far)
+                    i = done + g * run + part
+                    first = score(i, first)
+                    second = score(edge + i, second)
+                return first, second
+
+            runs = quotient(common - done, run)
+            chains = lax.fori_loop(0, runs, score_run, chains)
             done = done + runs * run
+        lax.fori_loop(common, edge, score, chains[0])
+        lax.fori_loop(edge + common, after, score, chains[1])
         kept = []
         for lane in range(block // 128):
             best = largest[lane, pl.ds(0, passages, stride=8), :]

time: 32.1 us -> 32.3 us (level); the launches traced: 31.8 us -> 32.4 us
  Pallas kernels: 13.5 us -> 13.9 us
    pallas_call x2, Pallas kernels: 5.89 us -> 6.34 us  [decode_step(): pl.pallas_call(functools.partial(decode_kernel, step, passages), out_shap...]
  transfers between devices with their start and end apart: 5 -> 5, of which waited for: 0 -> 0; matrix products, arithmetic and copies ran while one was open for 0% -> 0% of each run, Pallas kernels for 34% -> 35%
where the time goes in v26:
time: 32.3 us; the launch traced here: 32.4 us
  Pallas kernels  13.9 us (43%)
  blocking collectives  10.7 us (33%)
  starting transfers between devices  7.54 us (23%)
    all_to_all x1, blocking collectives, body(): lax.all_to_all(scores.reshape(targets, local_queries * passages), ('shard...  10.7 us
    ppermute x4, starting transfers between devices, body(): received = lax.ppermute(held, ('shard', 'sub'), pairs)  7.09 us
    pallas_call x2, Pallas kernels, decode_step(): pl.pallas_call(functools.partial(decode_kernel, step, passages), out_shap...  6.34 us
    pallas_call x2, Pallas kernels, score_half(): pl.pallas_call(functools.partial(score_kernel, bit, token_count, local_qu...  4.03 us
    pallas_call x1, Pallas kernels, prepare(): pl.pallas_call(prepare_kernel, out_shape=(pltpu.VMEM(own.shape, jnp.bfloa...  2.91 us
    pallas_call x1, Pallas kernels, pick(): pl.pallas_call(functools.partial(pick_kernel, passages), out_shape=jax.Sh...  0.66 us
  transfers between devices with their start and end apart: 5, of which 0 were waited for; matrix products, arithmetic and copies ran while one was open for 0% of the time, Pallas kernels for 35%

profile of v26, /device:TPU:0, one launch (start us, length us, event | category | flops | bytes accessed | tf_op | source)
XLA Modules:
  0.0 32.4 jit_solution(1509060525442087811)
XLA Ops:
  0.0 0.0 copy-start.1
  0.0 0.5 %collective-permute-start.2 = (bf16[8192,128]{1,0:T(8,128)(2,1)}, bf16[8192,128]{1,0:T(8,128)(2,1)S(1)}, u32[]{:S(2)}, u32[]{:S(2)}) collective-permute-start(bf16[8192,128]{1,0:T(8,128)(2,1)} %own_hbm.1), channel_id=1, source_target_pairs={{0,1},{1,0},{2,3},{3,2},{4,5},{5,4},{6,7},{7,6},{8,9},{9,8},{10,11... | collective-permute-start | bytes 6291464 | tf_op jit(solution)/shard_map/ppermute | solution.py:444
  0.5 3.6 %collective-permute-start = (bf16[1,1,32,128]{3,2,1,0:T(8,128)(2,1)}, bf16[1,1,32,128]{3,2,1,0:T(8,128)(2,1)S(1)}, u32[]{:S(2)}, u32[]{:S(2)}) collective-permute-start(bf16[1,1,32,128]{3,2,1,0:T(8,128)(2,1)} %bitcast.29), channel_id=1, source_target_pairs={{0,8},{1,9},{2,10},{3,11},{4,12},{5,13},{6,14},{7,15},{8,0},{9,1},... | collective-permute-start | bytes 24584 | tf_op jit(solution)/shard_map/ppermute | solution.py:451
  4.1 2.9 %prepare.1 = (bf16[8192,128]{1,0:T(8,128)(2,1)S(1)}, f32[9216,128]{1,0:T(8,128)S(1)}, s32[64,128]{1,0:T(8,128)S(1)}, s32[640]{0:T(1024)S(1)}, s32[640]{0:T(1024)S(1)}, /*index=5*/bf16[16,128]{1,0:T(8,128)(2,1)S(1)}) custom-call(s32[1]{0:T(128)} %bitcast.me_ref, s32[64]{0:T(128)} %lengths_hbm.1, s32[64,128]{1,0:T(8,128)} %codes_hbm.1, ...), custom_call_target="tpu_custom_call" | custom-call | flops 10000000 | bytes 8000000 | tf_op jit(solution)/shard_map/prepare/pallas_call | solution.py:149
  7.0 0.0 collective-permute-done
  7.1 0.0 copy-done.1
  7.1 1.6 %collective-permute-start.1 = (bf16[2,1,32,128]{3,2,1,0:T(8,128)(2,1)S(1)}, bf16[2,1,32,128]{3,2,1,0:T(8,128)(2,1)S(1)}, u32[]{:S(2)}, u32[]{:S(2)}) collective-permute-start(bf16[2,1,32,128]{3,2,1,0:T(8,128)(2,1)S(1)} %maximum_bitcast_fusion.refs_6_), channel_id=1, source_target_pairs={{0,4},{1,5},{2,6},{3,7},{4,0},{5,1},{6,2},{7,3},{8,12},{9,13},{10,... | collective-permute-start | bytes 49160 | tf_op jit(solution)/shard_map/ppermute | solution.py:451
  8.7 0.0 collective-permute-done.2.refs_2_
  8.7 3.1 %decode.2 = (f32[16384,128]{1,0:T(8,128)S(1)}, bf16[9216,128]{1,0:T(8,128)(2,1)S(1)}, f32[256,128]{1,0:T(8,128)S(1)}, bf16[16,128]{1,0:T(8,128)(2,1)S(1)}) custom-call(s32[1]{0:T(128)} %bitcast.5.refs_0_, bf16[8192,128]{1,0:T(8,128)(2,1)S(1)} %get-tuple-element.20.refs_1_, bf16[8192,128]{1,0:T(8,128)(2,1)S(1)} %collective-permute-done.2.refs_2_, ...), custom_call_target="tpu_custom_call" | custom-call | flops 10000000 | bytes 10000000 | tf_op jit(solution)/shard_map/decode/pallas_call | solution.py:259
  11.8 0.0 collective-permute-done.1
  11.9 1.6 %collective-permute-start.3 = (bf16[4,1,32,128]{3,2,1,0:T(8,128)(2,1)S(1)}, bf16[4,1,32,128]{3,2,1,0:T(8,128)(2,1)S(1)}, u32[]{:S(2)}, u32[]{:S(2)}) collective-permute-start(bf16[4,1,32,128]{3,2,1,0:T(8,128)(2,1)S(1)} %bitcast.20), channel_id=1, source_target_pairs={{0,2},{1,3},{2,0},{3,1},{4,6},{5,7},{6,4},{7,5},{8,10},{9,11},{10,... | collective-permute-start | bytes 98312 | tf_op jit(solution)/shard_map/ppermute | solution.py:451
  13.4 3.2 %decode.3 = (bf16[9216,128]{1,0:T(8,128)(2,1)S(1)}, f32[256,128]{1,0:T(8,128)S(1)}, bf16[16,128]{1,0:T(8,128)(2,1)S(1)}) custom-call(s32[64,128]{1,0:T(8,128)S(1)} %get-tuple-element.21.refs_3_.refs_0_, s32[640]{0:T(1024)S(1)} %get-tuple-element.22.refs_4_.refs_1_, ...), custom_call_target="tpu_custom_call", output_to_operand_aliasing={{0}: (5, {}), {1}: (6, {})} | custom-call | flops 10000000 | bytes 10000000 | tf_op jit(solution)/shard_map/decode/pallas_call | solution.py:259
  16.7 0.0 collective-permute-done.3
  16.7 0.2 collective-permute-start.4
  17.0 0.0 copy-start
  17.0 2.0 %score.2.before_ref = f32[16,64]{1,0:T(8,128)S(1)} custom-call(s32[1]{0:T(128)} %bitcast.me_ref, s32[640]{0:T(1024)S(1)} %get-tuple-element.18.starts, bf16[256,128]{1,0:T(8,128)(2,1)S(1)} %bitcast.24, bf16[9216,128]{1,0:T(8,128)(2,1)S(1)} %get-tuple-element.29.embedded, f32[256,128]{1,0:T(8,128)S(1)} %get-tuple-element.30.before_ref), custom_call_target="tpu_custom_call" | custom-call | flops 10000000 | bytes 8000000 | tf_op jit(solution)/shard_map/score/pallas_call | solution.py:384
  19.0 0.0 collective-permute-done.4
  19.0 2.0 %score.3 = f32[16,64]{1,0:T(8,128)S(1)} custom-call(s32[1]{0:T(128)} %bitcast.me_ref, s32[640]{0:T(1024)S(1)} %get-tuple-element.18.starts, bf16[256,128]{1,0:T(8,128)(2,1)S(1)} %bitcast.25, bf16[9216,128]{1,0:T(8,128)(2,1)S(1)} %get-tuple-element.29.embedded, f32[16,64]{1,0:T(8,128)S(1)} %score.2.before_ref), custom_call_target="tpu_custom_call" | custom-call | flops 10000000 | bytes 8000000 | tf_op jit(solution)/shard_map/score/pallas_call | solution.py:384
  21.0 10.7 %all_to_all.11 = f32[16,1,64]{2,1,0:T(1,128)S(1)} all-to-all(f32[16,1,64]{2,1,0:T(1,128)S(1)} %bitcast.26), channel_id=1, replica_groups=mesh['groups'=2,'shard'=8,'sub'=2] {'shard','sub'}, dimensions={0} | all-to-all | bytes 8192 | tf_op jit(solution)/shard_map/all_to_all | solution.py:469
  31.7 0.0 copy-done
  31.7 0.7 %pick.1 = f32[1,62]{1,0:T(1,128)} custom-call(s32[1,62]{1,0:T(1,128)S(1)} %copy-done, f32[16,64]{1,0:T(8,128)S(1)} %bitcast.27), custom_call_target="tpu_custom_call" | custom-call | tf_op jit(solution)/shard_map/pick/pallas_call | solution.py:425
  (9 shorter events, 0.1 us)
Async XLA Ops:
  0.0 7.1 %copy-start.1 = (bf16[1,32,128]{2,1,0:T(8,128)(2,1)S(1)}, bf16[1,32,128]{2,1,0:T(8,128)(2,1)}, u32[]{:S(2)}) copy-start(bf16[1,32,128]{2,1,0:T(8,128)(2,1)} %param.6) | copy-start | bytes 24580
  0.0 8.7 %collective-permute-start.2 = (bf16[8192,128]{1,0:T(8,128)(2,1)}, bf16[8192,128]{1,0:T(8,128)(2,1)S(1)}, u32[]{:S(2)}, u32[]{:S(2)}) collective-permute-start(bf16[8192,128]{1,0:T(8,128)(2,1)} %own_hbm.1), channel_id=1, source_target_pairs={{0,1},{1,0},{2,3},{3,2},{4,5},{5,4},{6,7},{7,6},{8,9},{9,8},{10,11... | collective-permute-start | bytes 6291464 | tf_op jit(solution)/shard_map/ppermute | solution.py:444
  0.5 6.6 %collective-permute-start = (bf16[1,1,32,128]{3,2,1,0:T(8,128)(2,1)}, bf16[1,1,32,128]{3,2,1,0:T(8,128)(2,1)S(1)}, u32[]{:S(2)}, u32[]{:S(2)}) collective-permute-start(bf16[1,1,32,128]{3,2,1,0:T(8,128)(2,1)} %bitcast.29), channel_id=1, source_target_pairs={{0,8},{1,9},{2,10},{3,11},{4,12},{5,13},{6,14},{7,15},{8,0},{9,1},... | collective-permute-start | bytes 24584 | tf_op jit(solution)/shard_map/ppermute | solution.py:451
  7.1 4.8 %collective-permute-start.1 = (bf16[2,1,32,128]{3,2,1,0:T(8,128)(2,1)S(1)}, bf16[2,1,32,128]{3,2,1,0:T(8,128)(2,1)S(1)}, u32[]{:S(2)}, u32[]{:S(2)}) collective-permute-start(bf16[2,1,32,128]{3,2,1,0:T(8,128)(2,1)S(1)} %maximum_bitcast_fusion.refs_6_), channel_id=1, source_target_pairs={{0,4},{1,5},{2,6},{3,7},{4,0},{5,1},{6,2},{7,3},{8,12},{9,13},{10,... | collective-permute-start | bytes 49160 | tf_op jit(solution)/shard_map/ppermute | solution.py:451
  11.9 4.8 %collective-permute-start.3 = (bf16[4,1,32,128]{3,2,1,0:T(8,128)(2,1)S(1)}, bf16[4,1,32,128]{3,2,1,0:T(8,128)(2,1)S(1)}, u32[]{:S(2)}, u32[]{:S(2)}) collective-permute-start(bf16[4,1,32,128]{3,2,1,0:T(8,128)(2,1)S(1)} %bitcast.20), channel_id=1, source_target_pairs={{0,2},{1,3},{2,0},{3,1},{4,6},{5,7},{6,4},{7,5},{8,10},{9,11},{10,... | collective-permute-start | bytes 98312 | tf_op jit(solution)/shard_map/ppermute | solution.py:451
  16.7 2.3 %collective-permute-start.4 = (bf16[8,1,32,128]{3,2,0,1:T(8,128)(2,1)S(1)}, bf16[8,1,32,128]{3,2,0,1:T(8,128)(2,1)S(1)}, u32[]{:S(2)}, u32[]{:S(2)}) collective-permute-start(bf16[8,1,32,128]{3,2,0,1:T(8,128)(2,1)S(1)} %bitcast.23), channel_id=1, source_target_pairs={{0,1},{1,0},{2,3},{3,2},{4,5},{5,4},{6,7},{7,6},{8,9},{9,8},{10,11... | collective-permute-start | bytes 196616 | tf_op jit(solution)/shard_map/ppermute | solution.py:451
  17.0 14.7 %copy-start = (s32[1,62]{1,0:T(1,128)S(1)}, s32[1,62]{1,0:T(1,128)}, u32[]{:S(2)}) copy-start(s32[1,62]{1,0:T(1,128)} %candidates_ref.1) | copy-start | bytes 748

commit v27 on v26

--- a/solution.py
+++ b/solution.py
@@ -8,7 +8,7 @@
 from jax.sharding import PartitionSpec as P
 
 CHUNK = 16
-GROUP = 16
+GROUP = 32
 SCORE_GROUP = 64
 PART = 32
 SCORE_RUNS = (4, 2, 1)

time: 32.3 us -> 31.8 us (0.985)
  blocking collectives: 10.7 us -> 9.5 us
  Pallas kernels: 13.9 us -> 14.7 us
    all_to_all x1, blocking collectives: 10.7 us -> 9.5 us  [body(): lax.all_to_all(scores.reshape(targets, local_queries * passages), ('shard...]
    pallas_call x2, Pallas kernels: 4.03 us -> 4.51 us  [score_half(): pl.pallas_call(functools.partial(score_kernel, bit, token_count, local_qu...]
  transfers between devices with their start and end apart: 5 -> 5, of which waited for: 0 -> 0; matrix products, arithmetic and copies ran while one was open for 0% -> 0% of each run, Pallas kernels for 35% -> 37%
where the time goes in v27:
time: 31.8 us; the launch traced here: 31.7 us
  Pallas kernels  14.7 us (46%)
  blocking collectives  9.5 us (30%)
  starting transfers between devices  7.25 us (23%)
    all_to_all x1, blocking collectives, body(): lax.all_to_all(scores.reshape(targets, local_queries * passages), ('shard...  9.5 us
    ppermute x4, starting transfers between devices, body(): received = lax.ppermute(held, ('shard', 'sub'), pairs)  6.8 us
    pallas_call x2, Pallas kernels, decode_step(): pl.pallas_call(functools.partial(decode_kernel, step, passages), out_shap...  6.59 us
    pallas_call x2, Pallas kernels, score_half(): pl.pallas_call(functools.partial(score_kernel, bit, token_count, local_qu...  4.51 us
    pallas_call x1, Pallas kernels, prepare(): pl.pallas_call(prepare_kernel, out_shape=(pltpu.VMEM(own.shape, jnp.bfloa...  2.97 us
    pallas_call x1, Pallas kernels, pick(): pl.pallas_call(functools.partial(pick_kernel, passages), out_shape=jax.Sh...  0.66 us
  transfers between devices with their start and end apart: 5, of which 0 were waited for; matrix products, arithmetic and copies ran while one was open for 0% of the time, Pallas kernels for 37%

profile of v27, /device:TPU:0, one launch (start us, length us, event | category | flops | bytes accessed | tf_op | source)
XLA Modules:
  0.0 31.7 jit_solution(7941496774993932460)
XLA Ops:
  0.0 0.0 copy-start.1
  0.0 0.5 %collective-permute-start.2 = (bf16[8192,128]{1,0:T(8,128)(2,1)}, bf16[8192,128]{1,0:T(8,128)(2,1)S(1)}, u32[]{:S(2)}, u32[]{:S(2)}) collective-permute-start(bf16[8192,128]{1,0:T(8,128)(2,1)} %own_hbm.1), channel_id=1, source_target_pairs={{0,1},{1,0},{2,3},{3,2},{4,5},{5,4},{6,7},{7,6},{8,9},{9,8},{10,11... | collective-permute-start | bytes 6291464 | tf_op jit(solution)/shard_map/ppermute | solution.py:444
  0.5 3.6 %collective-permute-start = (bf16[1,1,32,128]{3,2,1,0:T(8,128)(2,1)}, bf16[1,1,32,128]{3,2,1,0:T(8,128)(2,1)S(1)}, u32[]{:S(2)}, u32[]{:S(2)}) collective-permute-start(bf16[1,1,32,128]{3,2,1,0:T(8,128)(2,1)} %bitcast.29), channel_id=1, source_target_pairs={{0,8},{1,9},{2,10},{3,11},{4,12},{5,13},{6,14},{7,15},{8,0},{9,1},... | collective-permute-start | bytes 24584 | tf_op jit(solution)/shard_map/ppermute | solution.py:451
  4.1 3.0 %prepare.1 = (bf16[8192,128]{1,0:T(8,128)(2,1)S(1)}, f32[9216,128]{1,0:T(8,128)S(1)}, s32[64,128]{1,0:T(8,128)S(1)}, s32[640]{0:T(1024)S(1)}, s32[640]{0:T(1024)S(1)}, /*index=5*/bf16[16,128]{1,0:T(8,128)(2,1)S(1)}) custom-call(s32[1]{0:T(128)} %bitcast.me_ref, s32[64]{0:T(128)} %lengths_hbm.1, s32[64,128]{1,0:T(8,128)} %codes_hbm.1, ...), custom_call_target="tpu_custom_call" | custom-call | flops 10000000 | bytes 8000000 | tf_op jit(solution)/shard_map/prepare/pallas_call | solution.py:149
  7.1 0.0 collective-permute-done
  7.1 0.0 copy-done.1
  7.1 1.5 %collective-permute-start.1 = (bf16[2,1,32,128]{3,2,1,0:T(8,128)(2,1)S(1)}, bf16[2,1,32,128]{3,2,1,0:T(8,128)(2,1)S(1)}, u32[]{:S(2)}, u32[]{:S(2)}) collective-permute-start(bf16[2,1,32,128]{3,2,1,0:T(8,128)(2,1)S(1)} %maximum_bitcast_fusion.refs_6_), channel_id=1, source_target_pairs={{0,4},{1,5},{2,6},{3,7},{4,0},{5,1},{6,2},{7,3},{8,12},{9,13},{10,... | collective-permute-start | bytes 49160 | tf_op jit(solution)/shard_map/ppermute | solution.py:451
  8.7 0.0 collective-permute-done.2.refs_2_
  8.7 3.0 %decode.2 = (f32[16384,128]{1,0:T(8,128)S(1)}, bf16[9216,128]{1,0:T(8,128)(2,1)S(1)}, f32[512,128]{1,0:T(8,128)S(1)}, bf16[16,128]{1,0:T(8,128)(2,1)S(1)}) custom-call(s32[1]{0:T(128)} %bitcast.5.refs_0_, bf16[8192,128]{1,0:T(8,128)(2,1)S(1)} %get-tuple-element.20.refs_1_, bf16[8192,128]{1,0:T(8,128)(2,1)S(1)} %collective-permute-done.2.refs_2_, ...), custom_call_target="tpu_custom_call" | custom-call | flops 10000000 | bytes 10000000 | tf_op jit(solution)/shard_map/decode/pallas_call | solution.py:259
  11.7 0.0 collective-permute-done.1
  11.7 1.6 %collective-permute-start.3 = (bf16[4,1,32,128]{3,2,1,0:T(8,128)(2,1)S(1)}, bf16[4,1,32,128]{3,2,1,0:T(8,128)(2,1)S(1)}, u32[]{:S(2)}, u32[]{:S(2)}) collective-permute-start(bf16[4,1,32,128]{3,2,1,0:T(8,128)(2,1)S(1)} %bitcast.20), channel_id=1, source_target_pairs={{0,2},{1,3},{2,0},{3,1},{4,6},{5,7},{6,4},{7,5},{8,10},{9,11},{10,... | collective-permute-start | bytes 98312 | tf_op jit(solution)/shard_map/ppermute | solution.py:451
  13.3 3.6 %decode.3 = (bf16[9216,128]{1,0:T(8,128)(2,1)S(1)}, f32[512,128]{1,0:T(8,128)S(1)}, bf16[16,128]{1,0:T(8,128)(2,1)S(1)}) custom-call(s32[64,128]{1,0:T(8,128)S(1)} %get-tuple-element.21.refs_3_.refs_0_, s32[640]{0:T(1024)S(1)} %get-tuple-element.22.refs_4_.refs_1_, ...), custom_call_target="tpu_custom_call", output_to_operand_aliasing={{0}: (5, {}), {1}: (6, {})} | custom-call | flops 10000000 | bytes 10000000 | tf_op jit(solution)/shard_map/decode/pallas_call | solution.py:259
  16.9 0.0 collective-permute-done.3
  16.9 0.1 collective-permute-start.4
  17.0 0.0 copy-start
  17.0 2.3 %score.2.before_ref = f32[16,64]{1,0:T(8,128)S(1)} custom-call(s32[1]{0:T(128)} %bitcast.me_ref, s32[640]{0:T(1024)S(1)} %get-tuple-element.18.starts, bf16[256,128]{1,0:T(8,128)(2,1)S(1)} %bitcast.24, bf16[9216,128]{1,0:T(8,128)(2,1)S(1)} %get-tuple-element.29.embedded, f32[512,128]{1,0:T(8,128)S(1)} %get-tuple-element.30.before_ref), custom_call_target="tpu_custom_call" | custom-call | flops 10000000 | bytes 8000000 | tf_op jit(solution)/shard_map/score/pallas_call | solution.py:384
  19.3 0.0 collective-permute-done.4
  19.3 2.2 %score.3 = f32[16,64]{1,0:T(8,128)S(1)} custom-call(s32[1]{0:T(128)} %bitcast.me_ref, s32[640]{0:T(1024)S(1)} %get-tuple-element.18.starts, bf16[256,128]{1,0:T(8,128)(2,1)S(1)} %bitcast.25, bf16[9216,128]{1,0:T(8,128)(2,1)S(1)} %get-tuple-element.29.embedded, f32[16,64]{1,0:T(8,128)S(1)} %score.2.before_ref), custom_call_target="tpu_custom_call" | custom-call | flops 10000000 | bytes 8000000 | tf_op jit(solution)/shard_map/score/pallas_call | solution.py:384
  21.6 9.5 %all_to_all.11 = f32[16,1,64]{2,1,0:T(1,128)S(1)} all-to-all(f32[16,1,64]{2,1,0:T(1,128)S(1)} %bitcast.26), channel_id=1, replica_groups=mesh['groups'=2,'shard'=8,'sub'=2] {'shard','sub'}, dimensions={0} | all-to-all | bytes 8192 | tf_op jit(solution)/shard_map/all_to_all | solution.py:469
  31.1 0.0 copy-done
  31.1 0.7 %pick.1 = f32[1,62]{1,0:T(1,128)} custom-call(s32[1,62]{1,0:T(1,128)S(1)} %copy-done, f32[16,64]{1,0:T(8,128)S(1)} %bitcast.27), custom_call_target="tpu_custom_call" | custom-call | tf_op jit(solution)/shard_map/pick/pallas_call | solution.py:425
  (9 shorter events, 0.1 us)
Async XLA Ops:
  0.0 7.1 %copy-start.1 = (bf16[1,32,128]{2,1,0:T(8,128)(2,1)S(1)}, bf16[1,32,128]{2,1,0:T(8,128)(2,1)}, u32[]{:S(2)}) copy-start(bf16[1,32,128]{2,1,0:T(8,128)(2,1)} %param.6) | copy-start | bytes 24580
  0.0 8.7 %collective-permute-start.2 = (bf16[8192,128]{1,0:T(8,128)(2,1)}, bf16[8192,128]{1,0:T(8,128)(2,1)S(1)}, u32[]{:S(2)}, u32[]{:S(2)}) collective-permute-start(bf16[8192,128]{1,0:T(8,128)(2,1)} %own_hbm.1), channel_id=1, source_target_pairs={{0,1},{1,0},{2,3},{3,2},{4,5},{5,4},{6,7},{7,6},{8,9},{9,8},{10,11... | collective-permute-start | bytes 6291464 | tf_op jit(solution)/shard_map/ppermute | solution.py:444
  0.5 6.6 %collective-permute-start = (bf16[1,1,32,128]{3,2,1,0:T(8,128)(2,1)}, bf16[1,1,32,128]{3,2,1,0:T(8,128)(2,1)S(1)}, u32[]{:S(2)}, u32[]{:S(2)}) collective-permute-start(bf16[1,1,32,128]{3,2,1,0:T(8,128)(2,1)} %bitcast.29), channel_id=1, source_target_pairs={{0,8},{1,9},{2,10},{3,11},{4,12},{5,13},{6,14},{7,15},{8,0},{9,1},... | collective-permute-start | bytes 24584 | tf_op jit(solution)/shard_map/ppermute | solution.py:451
  7.1 4.5 %collective-permute-start.1 = (bf16[2,1,32,128]{3,2,1,0:T(8,128)(2,1)S(1)}, bf16[2,1,32,128]{3,2,1,0:T(8,128)(2,1)S(1)}, u32[]{:S(2)}, u32[]{:S(2)}) collective-permute-start(bf16[2,1,32,128]{3,2,1,0:T(8,128)(2,1)S(1)} %maximum_bitcast_fusion.refs_6_), channel_id=1, source_target_pairs={{0,4},{1,5},{2,6},{3,7},{4,0},{5,1},{6,2},{7,3},{8,12},{9,13},{10,... | collective-permute-start | bytes 49160 | tf_op jit(solution)/shard_map/ppermute | solution.py:451
  11.7 5.2 %collective-permute-start.3 = (bf16[4,1,32,128]{3,2,1,0:T(8,128)(2,1)S(1)}, bf16[4,1,32,128]{3,2,1,0:T(8,128)(2,1)S(1)}, u32[]{:S(2)}, u32[]{:S(2)}) collective-permute-start(bf16[4,1,32,128]{3,2,1,0:T(8,128)(2,1)S(1)} %bitcast.20), channel_id=1, source_target_pairs={{0,2},{1,3},{2,0},{3,1},{4,6},{5,7},{6,4},{7,5},{8,10},{9,11},{10,... | collective-permute-start | bytes 98312 | tf_op jit(solution)/shard_map/ppermute | solution.py:451
  16.9 2.4 %collective-permute-start.4 = (bf16[8,1,32,128]{3,2,0,1:T(8,128)(2,1)S(1)}, bf16[8,1,32,128]{3,2,0,1:T(8,128)(2,1)S(1)}, u32[]{:S(2)}, u32[]{:S(2)}) collective-permute-start(bf16[8,1,32,128]{3,2,0,1:T(8,128)(2,1)S(1)} %bitcast.23), channel_id=1, source_target_pairs={{0,1},{1,0},{2,3},{3,2},{4,5},{5,4},{6,7},{7,6},{8,9},{9,8},{10,11... | collective-permute-start | bytes 196616 | tf_op jit(solution)/shard_map/ppermute | solution.py:451
  17.0 14.1 %copy-start = (s32[1,62]{1,0:T(1,128)S(1)}, s32[1,62]{1,0:T(1,128)}, u32[]{:S(2)}) copy-start(s32[1,62]{1,0:T(1,128)} %candidates_ref.1) | copy-start | bytes 748
